TPU v7x, 32 devices: a whole 2x2x4 slice. The times are simulated.
32 devices in a mesh: head: 4 (over y, core), doc: 8 (over z, x).
Axes of the slice: x: 2, y: 2, z: 4, core: 2. Of those that a mesh axis runs over, the one named last changes fastest.
Arguments:
- tokens: bfloat16 [3072, 1024], P('doc'), may hold values from -6 to 6
- w_qkv: bfloat16 [1024, 3, 1024], P(None, None, 'head'), may hold values from -0.1875 to 0.1875
- w_out: bfloat16 [1024, 1024], P('head'), may hold values from -0.1875 to 0.1875
- w_up: bfloat16 [1024, 4096], P(None, 'head'), may hold values from -0.1875 to 0.1875
- w_down: bfloat16 [4096, 1024], P('head'), may hold values from -0.09375 to 0.09375
- gain_one: float32 [1024], replicated, may hold values from 0.5 to 1.5
- gain_two: float32 [1024], replicated, may hold values from 0.5 to 1.5
- rel_table: bfloat16 [512, 1024], replicated, may hold values from -6 to 6
- prompt_cache: bfloat16 [2, 1024, 1024], P(None, 'doc', 'head'), may hold values from -480 to 480
- w_proj: bfloat16 [1024, 128], replicated, may hold values from -0.1875 to 0.1875
- doc_vectors: bfloat16 [512, 256, 128], P('doc'), may hold values from -0.5 to 0.5
- doc_lengths: int32 [512], P('doc'), may hold values from 8 to 256, as said below
- group_ids: int32 [96], P('doc'), may hold values from 0 to 15
- candidates: int32 [96, 32], P('doc', 'head'), may hold values from 0 to 511, as said below
Outputs:
- query_vectors: bfloat16 [3072, 128], P('doc')
- scores: float32 [96, 32], P('doc', 'head')
Inputs may be any that keep to these rules, and one draw needn't show every extreme that they name: Split candidates into aligned blocks of 12 requests by 8 columns (one index of doc with one of head). Index o of doc holds documents o * 64 to o * 64 + 63. In each block at most 24 entries name documents held by one index of doc, and one index of doc, the same for all blocks, is named by exactly 24 entries of every block. The documents named within one block are distinct. Some document has exactly 256 tokens; token slots from doc_lengths on are padding.
All inputs are finite; a program needn't handle non-finite values.
Results may differ from a plain program's by a relative error of at most 0.02.
Values may be sent and summed in bfloat16 or wider, within the bound.
No kernel may reach another device: no remote copies, remote signals or barrier semaphores. Data moves between devices by JAX's collectives and lax.ppermute only.
A program may use at most 128 MiB of HBM per device.

v0:
```python
import math

import jax
import jax.numpy as jnp
from jax import lax
from jax.sharding import PartitionSpec as P

HD = 64
RELS = 512
QLEN = 32
PLEN = 64
DOC_DEV = 64


def layer_norm(values, gain):
    centre = values - jnp.mean(values, axis=-1, keepdims=True)
    spread = jnp.mean(centre * centre, axis=-1, keepdims=True)
    return centre * lax.rsqrt(spread + 1e-07) * gain


def slot_order(holders):
    count = holders.shape[0]
    same = holders[:, None] == holders[None, :]
    earlier = jnp.arange(count)[:, None] > jnp.arange(count)[None, :]
    return jnp.sum(same & earlier, axis=1)


def rate_slots(slot_query, slot_doc, doc_vectors, doc_lengths):
    shape = slot_doc.shape
    flat_doc = slot_doc.reshape(-1)
    flat_query = slot_query.reshape((flat_doc.shape[0],) + slot_query.shape[-2:])
    safe_doc = jnp.maximum(flat_doc, 0)
    documents = doc_vectors[safe_doc]
    lengths = doc_lengths[safe_doc]
    sims = jnp.einsum("sqe,sje->sqj", flat_query, documents, preferred_element_type=jnp.float32)
    live = jnp.arange(documents.shape[1], dtype=jnp.int32)[None, None, :] < lengths[:, None, None]
    best = jnp.max(jnp.where(live, sims, -jnp.inf), axis=2)
    totals = jnp.where(flat_doc >= 0, jnp.sum(best, axis=1), 0.0)
    return totals.reshape(shape)


def body(
    tokens,
    w_qkv,
    w_out,
    w_up,
    w_down,
    gain_one,
    gain_two,
    rel_table,
    prompt_cache,
    w_proj,
    doc_vectors,
    doc_lengths,
    group_ids,
    candidates,
):
    rows_dev = tokens.shape[0]
    req_dev = rows_dev // QLEN
    width = w_qkv.shape[2]
    heads_loc = width // HD
    half = RELS // 2
    scale_root = math.sqrt(3 * HD)
    gathered = lax.all_gather(prompt_cache, "doc", axis=1, tiled=True)
    weights_split = w_qkv.reshape(w_qkv.shape[0], 3, heads_loc, HD)
    projected_all = jnp.einsum(
        "td,dchf->chtf", tokens, weights_split, preferred_element_type=jnp.float32
    ).astype(jnp.bfloat16)
    rel_both = jnp.einsum(
        "rd,dchf->chrf", rel_table, weights_split[:, :2], preferred_element_type=jnp.float32
    ).astype(jnp.bfloat16)
    head_shape = (heads_loc, req_dev, QLEN, HD)
    query_four = projected_all[0].reshape(head_shape)
    keys_four = projected_all[1].reshape(head_shape)
    values_four = projected_all[2].reshape(head_shape)
    groups_all = gathered.shape[1] // PLEN
    cache_all = gathered.reshape(2, groups_all, PLEN, heads_loc, HD)
    picked = jnp.transpose(cache_all[:, group_ids], (0, 3, 1, 2, 4))
    keys = jnp.concatenate([keys_four, picked[0]], axis=2)
    values = jnp.concatenate([values_four, picked[1]], axis=2)
    pos_query = PLEN + jnp.arange(QLEN, dtype=jnp.int32)
    pos_key = jnp.concatenate([pos_query, jnp.arange(PLEN, dtype=jnp.int32)])
    index_one = pos_query[:, None] - pos_key[None, :] + half
    index_two = pos_key[:, None] - pos_query[None, :] + half
    rel_k_rows = rel_both[1][:, index_one]
    rel_q_rows = rel_both[0][:, index_two]
    c2p = jnp.einsum("hrqd,hqkd->hrqk", query_four, rel_k_rows, preferred_element_type=jnp.float32)
    p2c = jnp.einsum("hrkd,hkqd->hrqk", keys, rel_q_rows, preferred_element_type=jnp.float32)
    content = jnp.einsum("hrqd,hrkd->hrqk", query_four, keys, preferred_element_type=jnp.float32)
    logits = (content + c2p + p2c) / scale_root
    largest = jnp.max(logits, axis=-1, keepdims=True)
    weights = jnp.exp(logits - largest)
    denominator = jnp.sum(weights, axis=-1)
    summed = jnp.einsum(
        "hrqk,hrkd->hrqd", weights.astype(jnp.bfloat16), values, preferred_element_type=jnp.float32
    )
    attended = (summed / denominator[..., None]).astype(jnp.bfloat16)
    out_split = w_out.reshape(heads_loc, HD, w_out.shape[1])
    attn_part = jnp.einsum(
        "hrqd,hde->rqe", attended, out_split, preferred_element_type=jnp.float32
    ).reshape(rows_dev, w_out.shape[1])
    attn_total = lax.psum(attn_part.astype(jnp.bfloat16), "head").astype(jnp.float32)
    hidden_one = layer_norm(tokens.astype(jnp.float32) + attn_total, gain_one).astype(jnp.bfloat16)
    inner = jax.nn.gelu(
        jnp.dot(hidden_one, w_up, preferred_element_type=jnp.float32), approximate=False
    ).astype(jnp.bfloat16)
    ffn_total = lax.psum(
        jnp.dot(inner, w_down, preferred_element_type=jnp.float32).astype(jnp.bfloat16), "head"
    ).astype(jnp.float32)
    hidden_two = layer_norm(hidden_one.astype(jnp.float32) + ffn_total, gain_two).astype(
        jnp.bfloat16
    )
    projected = jnp.dot(hidden_two, w_proj, preferred_element_type=jnp.float32)
    query_vectors = (
        projected * lax.rsqrt(jnp.sum(projected * projected, axis=-1, keepdims=True) + 1e-06)
    ).astype(jnp.bfloat16)
    shards = lax.axis_size("doc")
    cand_dev = candidates.shape[1]
    pairs = req_dev * cand_dev
    capacity = max(2, 2 * pairs // shards)
    flat_cand = candidates.reshape(-1)
    holders = flat_cand // DOC_DEV
    request_of = jnp.arange(pairs, dtype=jnp.int32) // cand_dev
    slot_rank = slot_order(holders)
    copies, cand_copies = (
        lax.all_gather(query_vectors, "doc", axis=0, tiled=True),
        lax.all_gather(candidates, "doc", axis=0, tiled=True),
    )
    all_query = copies.reshape(shards, req_dev, QLEN, copies.shape[1])
    all_cand = cand_copies.reshape(shards, pairs)
    holder_all = all_cand // DOC_DEV
    local_all = all_cand % DOC_DEV
    rank_all = jax.vmap(slot_order)(holder_all)
    own_index = lax.axis_index("doc")
    chosen = (holder_all[:, None, :] == own_index) & (
        rank_all[:, None, :] == jnp.arange(capacity, dtype=jnp.int32)[None, :, None]
    )
    filled = jnp.any(chosen, axis=2)
    slot_request = jnp.sum(jnp.where(chosen, request_of[None, None, :], 0), axis=2)
    slot_doc = jnp.where(
        filled, jnp.sum(jnp.where(chosen, local_all[:, None, :], 0), axis=2), -1
    ).astype(jnp.int32)
    slot_query = all_query[jnp.arange(shards)[:, None], slot_request]
    slot_scores = rate_slots(slot_query, slot_doc, doc_vectors, doc_lengths)
    returned = lax.all_to_all(slot_scores, "doc", split_axis=0, concat_axis=0, tiled=True)
    scores = returned.reshape(-1)[holders * capacity + slot_rank].reshape(candidates.shape)
    return (query_vectors, scores)


def solution(mesh):
    placed = (
        P("doc", None),
        P(None, None, "head"),
        P("head", None),
        P(None, "head"),
        P("head", None),
        P(),
        P(),
        P(),
        P(None, "doc", "head"),
        P(),
        P("doc", None, None),
        P("doc"),
        P("doc"),
        P("doc", "head"),
    )
    return jax.shard_map(
        body,
        mesh=mesh,
        in_specs=placed,
        out_specs=(P("doc", None), P("doc", "head")),
        check_vma=False,
    )
```

profile of v0, /device:TPU:0, one launch (start us, length us, event | category | flops | bytes accessed | tf_op | source)
XLA Modules:
  0.0 305.4 jit_solution(2043249529237896893)
XLA Ops:
  7.2 0.7 all-gather.3.cloned.1.call-update
  8.3 2.6 copy.151
  10.9 2.4 fusion.21
  13.3 0.9 slice_bitcast_fusion.3
  14.2 1.0 fusion.20
  15.2 0.8 fusion.103
  16.2 32.3 %all-gather = s32[8,12,8]{1,2,0:T(8,128)S(1)} all-gather(s32[1,12,8]{1,2,0:T(8,128)S(1)} %bitcast.93), channel_id=1, replica_groups=mesh['head'=4,'doc'=8] {'doc'}, dimensions={0}, use_global_device_ids=true | all-gather | bytes 3456 | tf_op jit(solution)/shard_map/all_gather | solution.py:127
  48.7 1.3 copy.162
  50.0 21.5 %gather_fusion.2 = bf16[3072,4,64]{2,1,0:T(4,128)(2,1)} fusion(bf16[4,512,64]{2,0,1:T(4,128)(2,1)S(1)} %copy.162, s32[3072]{0:T(1024)S(1)} %broadcast_clamp_fusion), kind=kCustom, calls=%fused_computation.2 | custom fusion | bytes 3158016 | tf_op jit(solution)/shard_map/gather | solution.py:86
  71.5 4.0 %copy.163 = bf16[3072,4,64]{2,0,1:T(8,128)(2,1)} copy(bf16[3072,4,64]{2,1,0:T(4,128)(2,1)} %gather_fusion.2) | data formatting | bytes 3145728 | tf_op jit(solution)/shard_map/gather | solution.py:86
  75.4 1.1 copy.153
  76.6 1.2 copy.157
  77.8 1.3 copy.158
  79.0 21.5 %gather_fusion.1 = bf16[3072,4,64]{2,1,0:T(4,128)(2,1)} fusion(bf16[4,512,64]{2,0,1:T(4,128)(2,1)S(1)} %copy.158, s32[3072]{0:T(1024)S(1)} %broadcast_clamp_fusion.1), kind=kCustom, calls=%fused_computation.1 | custom fusion | bytes 3158016 | tf_op jit(solution)/shard_map/gather | solution.py:85
  100.5 5.5 %copy.159 = bf16[32,96,4,64]{1,3,0,2:T(8,128)(2,1)} copy(bf16[32,96,4,64]{3,2,1,0:T(4,128)(2,1)} %bitcast.82) | data formatting | bytes 3145728 | tf_op jit(solution)/shard_map/gather | solution.py:85
  106.1 1.2 copy.152
  107.3 1.8 copy.166
  109.1 2.2 copy.167
  112.4 3.2 %fusion = f32[4,32,96,12]{2,3,1,0:T(8,128)} fusion(bf16[32,96,4,64]{1,3,0,2:T(8,128)(2,1)} %copy.159, bf16[4,12,32,64]{3,2,1,0:T(8,128)(2,1)S(1)} %bitcast.86), kind=kOutput, calls=%fused_computation.9 | convolution fusion | flops 18874368 | bytes 2359296 | tf_op jit(solution)/shard_map/hrqd,hqkd->hrqk/dot_general | solution.py:87
  115.6 4.4 %reshape.599 = bf16[2,16,64,4,64]{4,3,2,1,0:T(4,128)(2,1)} reshape(bf16[2,1024,256]{2,1,0:T(8,128)(2,1)} %all-gather.3.cloned.1.call-done) | data formatting | bytes 2097152 | tf_op jit(solution)/shard_map/reshape | solution.py:77
  120.0 3.5 %copy.155 = bf16[2,16,64,4,64]{4,2,3,1,0:T(8,128)(2,1)} copy(bf16[2,16,64,4,64]{4,3,2,1,0:T(4,128)(2,1)} %reshape.599) | data formatting | bytes 2097152 | tf_op jit(solution)/shard_map/reshape | solution.py:77
  123.5 3.5 %gather_fusion = bf16[12,2,64,4,64]{4,2,3,1,0:T(8,128)(2,1)} fusion(bf16[2,16,64,4,64]{4,2,3,1,0:T(8,128)(2,1)} %copy.155, s32[1024]{0:T(1024)S(1)} %pad_clamp_fusion.2), kind=kCustom, calls=%fused_computation | custom fusion | bytes 1572912 | tf_op jit(solution)/shard_map/gather | solution.py:78
  127.1 2.6 copy.156
  129.7 2.5 slice_bitcast_fusion.1
  132.2 1.4 pad_maximum_fusion
  133.6 3.0 copy.164
  136.6 5.8 %fusion.107 = f32[4,96,32,12]{2,3,1,0:T(8,128)} fusion(bf16[4,96,32,64]{3,2,1,0:T(8,128)(2,1)} %bitcast.83, bf16[4,12,96,64]{3,1,2,0:T(8,128)(2,1)} %copy.164), kind=kOutput, calls=%fused_computation.191 | convolution fusion | flops 18874368 | bytes 2752512 | tf_op jit(solution)/shard_map/hrkd,hkqd->hrqk/dot_general | solution.py:88
  142.5 3.1 %copy.165 = f32[4,96,32,12]{1,2,3,0:T(8,128)} copy(f32[4,96,32,12]{2,3,1,0:T(8,128)} %fusion.107) | data formatting | bytes 1179648 | tf_op jit(solution)/shard_map/hrkd,hkqd->hrqk/dot_general | solution.py:88
  145.5 2.3 fusion.104
  148.4 0.8 fusion.19
  149.4 1.3 bitcast_convert_fusion
  151.3 10.3 %gather_fusion.5 = bf16[192,256,128]{2,1,0:T(8,128)(2,1)} fusion(bf16[64,256,128]{2,1,0:T(8,128)(2,1)} %param.24, s32[1024]{0:T(1024)S(1)} %pad_clamp_fusion.1), kind=kCustom, calls=%fused_computation.5 | custom fusion | bytes 25166592 | tf_op jit(solution)/shard_map/gather | solution.py:33
  161.7 1.5 gather_fusion.3
  163.4 23.1 %all-reduce.3.cloned.1.call-done = bf16[384,1024]{1,0:T(8,128)(2,1)} async-done(((bf16[384,1024]{1,0:T(8,128)(2,1)}), bf16[384,1024]{1,0:T(8,128)(2,1)}) %all-reduce.3.cloned.1.call-update) | async-done | bytes 786448 | tf_op jit(solution)/shard_map/psum | solution.py:102
  186.5 1.5 fusion.13
  188.4 1.3 multiply_convert_fusion.1
  189.7 7.6 %convolution_convert_fusion = bf16[384,1024]{1,0:T(8,128)(2,1)} fusion(bf16[1024,1024]{1,0:T(8,128)(2,1)S(1)} %copy-done, bf16[384,1024]{1,0:T(8,128)(2,1)} %multiply_convert_fusion.1, bf16[1024,1024]{1,0:T(8,128)(2,1)} %param.17), kind=kOutput, calls=%fused_computation.40 | convolution fusion | flops 1636564992 | bytes 5767168 | tf_op jit(solution)/shard_map/dot_general | solution.py:108
  197.5 34.7 %all-reduce.5.cloned.1.call-done = bf16[384,1024]{1,0:T(8,128)(2,1)} async-done(((bf16[384,1024]{1,0:T(8,128)(2,1)}), bf16[384,1024]{1,0:T(8,128)(2,1)}) %all-reduce.5.cloned.1.call-update) | async-done | bytes 786448 | tf_op jit(solution)/shard_map/psum | solution.py:107
  232.2 1.5 fusion.15
  234.7 34.9 %all_gather.11 = bf16[3072,128]{0,1:T(8,128)(2,1)} all-gather(bf16[384,128]{0,1:T(8,128)(2,1)S(1)} %multiply_convert_fusion.3), channel_id=1, replica_groups=mesh['head'=4,'doc'=8] {'doc'}, dimensions={0}, use_global_device_ids=true | all-gather | bytes 884736 | tf_op jit(solution)/shard_map/all_gather | solution.py:126
  269.6 1.5 copy.170
  271.1 3.0 gather_fusion.4
  274.1 9.6 %select_reduce_fusion = f32[192,32]{1,0:T(8,128)S(1)} fusion(pred[192,256]{1,0:T(8,128)(4,1)S(1)} %iota_compare_fusion, bf16[192,32,128]{2,1,0:T(8,128)(2,1)} %gather_fusion.4, bf16[192,256,128]{2,1,0:T(8,128)(2,1)} %gather_fusion.5), kind=kOutput, calls=%fused_computation.7 | convolution fusion | flops 405792768 | bytes 14229504 | tf_op jit(solution)/shard_map/sqe,sje->sqj/dot_general | solution.py:35
  284.5 4.8 %all-to-all-start = ((f32[8,1,24]{2,1,0:T(1,128)}), f32[8,1,24]{2,1,0:T(1,128)S(1)}, u32[]{:S(2)}, u32[]{:S(2)}) async-start(f32[8,1,24]{2,1,0:T(1,128)} %bitcast.30), calls=%async_computation | async-start | bytes 8192 | tf_op jit(solution)/shard_map/all_to_all | solution.py:145
  289.2 0.8 copy.175
  290.0 5.6 %all-to-all-done = f32[8,1,24]{2,1,0:T(1,128)S(1)} async-done(((f32[8,1,24]{2,1,0:T(1,128)}), f32[8,1,24]{2,1,0:T(1,128)S(1)}, u32[]{:S(2)}, u32[]{:S(2)}) %all-to-all-start) | async-done | bytes 800 | tf_op jit(solution)/shard_map/all_to_all | solution.py:145
  296.9 1.3 gather_fusion.6
  298.2 0.7 copy.176
  (88 shorter events, 7.1 us)
Async XLA Ops:
  7.2 182.6 %copy-start = (bf16[1024,1024]{1,0:T(8,128)(2,1)S(1)}, bf16[1024,1024]{1,0:T(8,128)(2,1)}, u32[]{:S(2)}) copy-start(bf16[1024,1024]{1,0:T(8,128)(2,1)} %param.18) | copy-start | bytes 6291460
  7.2 108.4 %all-gather.3.cloned.1.call-start = ((), (), s32[]{:S(2)}) async-start(), calls=%async_computation.1 | async-start | bytes 1179648 | tf_op jit(solution)/shard_map/all_gather | solution.py:64
  7.9 178.6 %all-reduce.3.cloned.1.call-start = ((), (), s32[]{:S(2)}) async-start(), calls=%async_computation.2 | async-start | bytes 1572864 | tf_op jit(solution)/shard_map/psum | solution.py:102
  10.9 3.3 %copy-start.2 = (bf16[384,1024]{1,0:T(8,128)(2,1)S(1)}, bf16[384,1024]{1,0:T(8,128)(2,1)}, u32[]{:S(2)}) copy-start(bf16[384,1024]{1,0:T(8,128)(2,1)} %param.14) | copy-start | bytes 2359300
  10.9 3.3 %copy-start.7 = (bf16[1024,3,256]{0,2,1:T(8,128)(2,1)S(1)}, bf16[1024,3,256]{0,2,1:T(8,128)(2,1)}, u32[]{:S(2)}) copy-start(bf16[1024,3,256]{0,2,1:T(8,128)(2,1)} %copy.151) | copy-start | bytes 4718596
  14.2 1.9 copy-start.10
  106.1 6.2 %copy-start.15 = (s32[12]{0:T(128)S(1)}, s32[12]{0:T(128)}, u32[]{:S(2)}) copy-start(s32[12]{0:T(128)} %param.26) | copy-start | bytes 148
  129.7 2.5 copy-start.6
  145.5 2.9 copy-start.8
  145.5 2.9 copy-start.9
  148.4 1.0 copy-start.12
  150.8 81.4 %all-reduce.5.cloned.1.call-start = ((), (), s32[]{:S(2)}) async-start(), calls=%async_computation.3 | async-start | bytes 1572864 | tf_op jit(solution)/shard_map/psum | solution.py:107
  151.3 10.3 %copy-start.1 = (s32[64]{0:T(128)S(1)}, s32[64]{0:T(128)}, u32[]{:S(2)}) copy-start(s32[64]{0:T(128)} %param.25) | copy-start | bytes 772
  163.4 25.0 %copy-start.11 = (f32[1024]{0:T(1024)S(1)}, f32[1024]{0:T(1024)}, u32[]{:S(2)}) copy-start(f32[1024]{0:T(1024)} %param.19) | copy-start | bytes 12292
  186.5 1.5 copy-start.3
  189.7 42.4 %copy-start.4 = (bf16[384,1024]{1,0:T(8,128)(2,1)S(1)}, bf16[384,1024]{1,0:T(8,128)(2,1)}, u32[]{:S(2)}) copy-start(bf16[384,1024]{1,0:T(8,128)(2,1)} %multiply_convert_fusion.1) | copy-start | bytes 2359300
  197.5 36.6 %copy-start.13 = (bf16[1024,128]{1,0:T(8,128)(2,1)S(1)}, bf16[1024,128]{1,0:T(8,128)(2,1)}, u32[]{:S(2)}) copy-start(bf16[1024,128]{1,0:T(8,128)(2,1)} %param.23) | copy-start | bytes 786436
  197.5 36.6 %copy-start.14 = (f32[1024]{0:T(1024)S(1)}, f32[1024]{0:T(1024)}, u32[]{:S(2)}) copy-start(f32[1024]{0:T(1024)} %param.20) | copy-start | bytes 12292
  232.2 1.5 copy-start.5
  284.5 11.1 %all-to-all-start = ((f32[8,1,24]{2,1,0:T(1,128)}), f32[8,1,24]{2,1,0:T(1,128)S(1)}, u32[]{:S(2)}, u32[]{:S(2)}) async-start(f32[8,1,24]{2,1,0:T(1,128)} %bitcast.30), calls=%async_computation | async-start | bytes 8192 | tf_op jit(solution)/shard_map/all_to_all | solution.py:145
Sparse Core Ops, SparseCore 0:
  10.2 42.8 all-gather.2
  150.9 35.5 all-reduce.2
  197.5 34.6 all-reduce.4
where the time goes:
time: 306 us; the launch traced here: 305 us
  local copies, waits for them, and re-layouts  110 us (36%)
  blocking collectives  67.1 us (22%)
  waiting for transfers between devices  64.1 us (21%)
  matrix products  34.6 us (11%)
  between operations  14.1 us (5%)
  other arithmetic  9.98 us (3%)
  starting transfers between devices  5.06 us (2%)
    all_gather x1, blocking collectives, body(): lax.all_gather(query_vectors, 'doc', axis=0, tiled=True)  34.9 us
    psum x1, waiting for transfers between devices, body(): lax.psum(jnp.dot(inner, w_down, preferred_element_type=jnp.float32).astyp...  34.7 us
    all_gather x1, blocking collectives, body(): lax.all_gather(candidates, 'doc', axis=0, tiled=True)  32.3 us
    gather x2, local copies, waits for them, and re-layouts, body(): rel_k_rows = rel_both[1][:, index_one]  27 us
    gather x2, local copies, waits for them, and re-layouts, body(): rel_q_rows = rel_both[0][:, index_two]  25.5 us
    psum x1, waiting for transfers between devices, body(): lax.psum(attn_part.astype(jnp.bfloat16), 'head').astype(jnp.float32)  23.1 us
    gather x1, local copies, waits for them, and re-layouts, rate_slots(): documents = doc_vectors[safe_doc]  10.3 us
    dot_general x1, matrix products, rate_slots(): jnp.einsum('sqe,sje->sqj', flat_query, documents, preferred_element_type=...  9.57 us
  transfers between devices with their start and end apart: 4, of which 3 were waited for; matrix products, arithmetic and copies ran while one was open for 29% of the time, Pallas kernels for 0%

commit v1 on v0

--- a/solution.py
+++ b/solution.py
@@ -1,8 +1,11 @@
+import functools
 import math
 
 import jax
 import jax.numpy as jnp
 from jax import lax
+from jax.experimental import pallas as pl
+from jax.experimental.pallas import tpu as pltpu
 from jax.sharding import PartitionSpec as P
 
 HD = 64
@@ -39,7 +42,7 @@
     return totals.reshape(shape)
 
 
-def body(
+def body_any(
     tokens,
     w_qkv,
     w_out,
@@ -147,6 +150,352 @@
     return (query_vectors, scores)
 
 
+LANES = 128
+MIB = 1 << 20
+
+
+def full_specs(count):
+    return [pl.BlockSpec(memory_space=pltpu.VMEM)] * count
+
+
+def params():
+    return pltpu.CompilerParams(vmem_limit_bytes=48 * MIB)
+
+
+def attend_kernel(
+    krow, vrow, qkv, relq, relk, k_zero, k_one, k_two, k_three, v_zero, v_one, att, k_all, v_all
+):
+    width = att.shape[1]
+    heads = width // HD
+    for place, piece in enumerate((k_zero, k_one, k_two, k_three)):
+        k_all[place * piece.shape[0] : (place + 1) * piece.shape[0], :] = piece[...]
+    for place, piece in enumerate((v_zero, v_one)):
+        v_all[place * piece.shape[0] : (place + 1) * piece.shape[0], :] = piece[...]
+    zero = jnp.bfloat16(0)
+    turn = (
+        lax.broadcasted_iota(jnp.int32, (LANES, LANES), 0)
+        + lax.broadcasted_iota(jnp.int32, (LANES, LANES), 1)
+        == LANES - 1
+    )
+    flip = jnp.where(turn, 1.0, 0.0).astype(jnp.bfloat16)
+    rel_k = jnp.dot(flip, relk[...], preferred_element_type=jnp.float32).astype(jnp.bfloat16)
+    rel_q = jnp.dot(flip, relq[...], preferred_element_type=jnp.float32).astype(jnp.bfloat16)
+    head_of = lax.broadcasted_iota(jnp.int32, (LANES, width), 1) // HD
+    rel_q_heads = jnp.concatenate([jnp.where(head_of == h, rel_q, zero) for h in range(heads)], axis=0)
+    small_head = lax.broadcasted_iota(jnp.int32, (QLEN, width), 1) // HD
+    slot = lax.broadcasted_iota(jnp.int32, (LANES, LANES), 1) // QLEN
+    live = lax.broadcasted_iota(jnp.int32, (heads * QLEN, LANES), 1) < PLEN + QLEN
+    padding = jnp.zeros((LANES - PLEN - QLEN, width), jnp.bfloat16)
+    scale = 1.0 / math.sqrt(3 * HD)
+
+    def one_request(r, carry):
+        rows = pl.ds(pl.multiple_of(r * QLEN, QLEN), QLEN)
+        q = qkv[rows, 0:width]
+        k_own = qkv[rows, width : 2 * width]
+        v_own = qkv[rows, 2 * width : 3 * width]
+        k_group = k_all[pl.ds(pl.multiple_of(krow[r], PLEN), PLEN), :]
+        v_group = v_all[pl.ds(pl.multiple_of(vrow[r], PLEN), PLEN), :]
+        keys = jnp.concatenate([k_group, k_own, padding], axis=0)
+        values = jnp.concatenate([v_group, v_own, padding], axis=0)
+        q_heads = jnp.concatenate([jnp.where(small_head == h, q, zero) for h in range(heads)], axis=0)
+        both = lax.dot_general(
+            q_heads,
+            jnp.concatenate([keys, rel_k], axis=0),
+            (((1,), (1,)), ((), ())),
+            preferred_element_type=jnp.float32,
+        )
+        content = both[:, :LANES]
+        query_rel = both[:, LANES:]
+        c2p = jnp.concatenate(
+            [
+                pltpu.roll(
+                    query_rel[h * QLEN : (h + 1) * QLEN], 97, 1, stride=1, stride_axis=0
+                )
+                for h in range(heads)
+            ],
+            axis=0,
+        )
+        key_rel = lax.dot_general(
+            keys, rel_q_heads, (((1,), (1,)), ((), ())), preferred_element_type=jnp.float32
+        )
+        turned = jnp.zeros((LANES, LANES), jnp.float32)
+        for h in range(heads):
+            rolled = pltpu.roll(
+                key_rel[:, h * LANES : (h + 1) * LANES],
+                (32 + h * QLEN) % LANES,
+                1,
+                stride=1,
+                stride_axis=0,
+            )
+            turned = jnp.where(slot == h, rolled, turned)
+        p2c = turned.T[: heads * QLEN]
+        logits = jnp.where(live, (content + c2p + p2c) * scale, -jnp.inf)
+        largest = jnp.max(logits, axis=1, keepdims=True)
+        weights = jnp.exp(logits - largest)
+        denominator = jnp.sum(weights, axis=1, keepdims=True)
+        summed = jnp.dot(weights.astype(jnp.bfloat16), values, preferred_element_type=jnp.float32)
+        summed = summed / denominator
+        out = summed[:QLEN]
+        for h in range(1, heads):
+            out = jnp.where(small_head == h, summed[h * QLEN : (h + 1) * QLEN], out)
+        att[rows, :] = out.astype(jnp.bfloat16)
+        return carry
+
+    lax.fori_loop(0, att.shape[0] // QLEN, one_request, 0, unroll=2)
+
+
+def attend(krow, vrow, qkv, relq, relk, k_pieces, v_pieces):
+    rows = qkv.shape[0]
+    width = qkv.shape[1] // 3
+    cached = sum(piece.shape[0] for piece in v_pieces)
+    return pl.pallas_call(
+        attend_kernel,
+        out_shape=jax.ShapeDtypeStruct((rows, width), jnp.bfloat16),
+        in_specs=[pl.BlockSpec(memory_space=pltpu.SMEM)] * 2 + full_specs(9),
+        out_specs=pl.BlockSpec(memory_space=pltpu.VMEM),
+        scratch_shapes=[
+            pltpu.VMEM((cached, width), jnp.bfloat16),
+            pltpu.VMEM((cached, width), jnp.bfloat16),
+        ],
+        compiler_params=params(),
+        cost_estimate=pl.CostEstimate(flops=400 * MIB, bytes_accessed=2 * MIB, transcendentals=0),
+        name="attend",
+    )(krow, vrow, qkv, relq, relk, *k_pieces, *v_pieces)
+
+
+def norm_rows(values, gain):
+    centre = values - jnp.mean(values, axis=-1, keepdims=True)
+    spread = jnp.mean(centre * centre, axis=-1, keepdims=True)
+    return centre * lax.rsqrt(spread + 1e-07) * gain
+
+
+def feed_rows(start, count, a, w, tokens, gain, w_up, w_down):
+    rows = pl.ds(pl.multiple_of(start, 32), count)
+    mixed = tokens[rows, :].astype(jnp.float32)
+    for piece, weight in zip(a, w):
+        mixed = mixed + jnp.dot(piece[rows, :], weight[...], preferred_element_type=jnp.float32)
+    hidden = norm_rows(mixed, gain[...]).astype(jnp.bfloat16)
+    total = None
+    step = 256
+    for at in range(0, w_up.shape[1], step):
+        up = jnp.dot(hidden, w_up[:, at : at + step], preferred_element_type=jnp.float32)
+        inner = (0.5 * up * (1.0 + lax.erf(up * math.sqrt(0.5)))).astype(jnp.bfloat16)
+        part = jnp.dot(inner, w_down[at : at + step, :], preferred_element_type=jnp.float32)
+        total = part if total is None else total + part
+    return hidden, total
+
+
+def feed_other_kernel(start, a0, a1, a2, a3, w0, w1, w2, w3, tokens, gain, w_up, w_down, out):
+    _, total = feed_rows(
+        start[0], out.shape[0], (a0, a1, a2, a3), (w0, w1, w2, w3), tokens, gain, w_up, w_down
+    )
+    out[...] = total.astype(out.dtype)
+
+
+def feed_own_kernel(start, a0, a1, a2, a3, w0, w1, w2, w3, tokens, gain, w_up, w_down, out, own):
+    pieces, weights = (a0, a1, a2, a3), (w0, w1, w2, w3)
+    _, total = feed_rows(start[0], out.shape[0], pieces, weights, tokens, gain, w_up, w_down)
+    out[...] = total
+    hidden, total = feed_rows(start[1], own.shape[0], pieces, weights, tokens, gain, w_up, w_down)
+    own[...] = hidden.astype(jnp.float32) + total
+
+
+def feed(kernel, start, pieces, weights, tokens, gain, w_up, w_down, outs, name):
+    return pl.pallas_call(
+        kernel,
+        out_shape=outs,
+        in_specs=[pl.BlockSpec(memory_space=pltpu.SMEM)] + full_specs(12),
+        out_specs=full_specs(len(outs)),
+        compiler_params=params(),
+        cost_estimate=pl.CostEstimate(flops=1600 * MIB, bytes_accessed=6 * MIB, transcendentals=0),
+        name=name,
+    )(start, *pieces, *weights, tokens, gain, w_up, w_down)
+
+
+def project_kernel(own, from_core, from_y, gain, w_proj, out):
+    after = own[...] + from_core[...].astype(jnp.float32) + from_y[...].astype(jnp.float32)
+    hidden = norm_rows(after, gain[...]).astype(jnp.bfloat16)
+    projected = jnp.dot(hidden, w_proj[...], preferred_element_type=jnp.float32)
+    length = jnp.sum(projected * projected, axis=-1, keepdims=True)
+    vectors = (projected * lax.rsqrt(length + 1e-06)).astype(jnp.bfloat16)
+    for place in range(out.shape[0]):
+        out[place] = vectors
+
+
+def score_kernel(slots, count, lengths, queries, docs, out):
+    lanes = out.shape[1]
+    flat = (
+        lax.broadcasted_iota(jnp.int32, out.shape, 0) * lanes
+        + lax.broadcasted_iota(jnp.int32, out.shape, 1)
+    )
+    slots_doc = docs.shape[1]
+    position = lax.broadcasted_iota(jnp.int32, (QLEN, slots_doc), 1)
+    unroll = 4
+
+    def some(i, totals):
+        for u in range(unroll):
+            packed = slots[i * unroll + u]
+            entry = packed & 4095
+            group = (packed >> 12) & 255
+            doc = packed >> 20
+            query = queries[pl.ds(pl.multiple_of(group * QLEN, QLEN), QLEN), :]
+            sims = lax.dot_general(
+                query, docs[doc], (((1,), (1,)), ((), ())), preferred_element_type=jnp.float32
+            )
+            sims = jnp.where(position < lengths[doc], sims, -jnp.inf)
+            best = jnp.max(sims, axis=1, keepdims=True)
+            total = jnp.sum(best, axis=0, keepdims=True)
+            totals = jnp.where(flat == entry, total, totals)
+        return totals
+
+    out[...] = lax.fori_loop(
+        0, (count[0] + unroll - 1) // unroll, some, jnp.zeros(out.shape, jnp.float32)
+    )
+
+
+def body(
+    tokens,
+    w_qkv,
+    w_out,
+    w_up,
+    w_down,
+    gain_one,
+    gain_two,
+    rel_table,
+    prompt_cache,
+    w_proj,
+    doc_vectors,
+    doc_lengths,
+    group_ids,
+    candidates,
+):
+    rows = tokens.shape[0]
+    width = w_qkv.shape[2]
+    n_doc = lax.axis_size("doc")
+    n_head = lax.axis_size("head")
+    me = lax.axis_index("doc")
+    place = lax.axis_index("head")
+    own_y, own_c = place // 2, place % 2
+    half, quarter = rows // 2, rows // 4
+
+    def over_doc(x, k):
+        return lax.ppermute(x, "doc", [(i, i ^ k) for i in range(n_doc)])
+
+    def over_head(x, k):
+        return lax.ppermute(x, "head", [(i, i ^ k) for i in range(n_head)])
+
+    keys, values = prompt_cache[0], prompt_cache[1]
+    keys_two = jnp.concatenate([keys, over_doc(keys, 1)], axis=0)
+    values_four = jnp.concatenate([values] + [over_doc(values, k) for k in (2, 4, 6)], axis=0)
+    key_pieces = [keys_two] + [over_doc(keys_two, k) for k in (2, 4, 6)]
+    value_pieces = [values_four, over_doc(values_four, 1)]
+    groups_dev = keys.shape[0] // PLEN
+    relative = (group_ids // groups_dev) ^ me
+    within = group_ids % groups_dev * PLEN
+    krow = relative * keys.shape[0] + within
+    vrow = (relative // 2 + relative % 2 * (n_doc // 2)) * keys.shape[0] + within
+
+    weight = w_qkv.reshape(w_qkv.shape[0], 3 * width)
+    qkv = jnp.dot(tokens, weight, preferred_element_type=jnp.float32).astype(jnp.bfloat16)
+    low_q = RELS // 2 - PLEN - QLEN + 1
+    low_k = RELS // 2 - QLEN
+    relq = jnp.dot(
+        rel_table[low_q : low_q + LANES], weight[:, :width], preferred_element_type=jnp.float32
+    ).astype(jnp.bfloat16)
+    relk = jnp.dot(
+        rel_table[low_k : low_k + LANES],
+        weight[:, width : 2 * width],
+        preferred_element_type=jnp.float32,
+    ).astype(jnp.bfloat16)
+
+    reqs = candidates.shape[0] // n_head
+    cols = candidates.shape[1]
+    sent = candidates.reshape(2, 2, reqs * cols).transpose(1, 0, 2).reshape(1, n_head, reqs * cols)
+    sent = jnp.broadcast_to(sent, (n_doc, n_head, reqs * cols)).reshape(n_doc * n_head, reqs * cols)
+    entries = lax.all_to_all(sent, ("doc", "head"), 0, 0, tiled=True).reshape(n_doc, n_head * reqs * cols)
+    block = n_head * reqs * cols
+    doc_at = jnp.arange(n_doc, dtype=jnp.int32)[:, None]
+    entry_at = jnp.arange(block, dtype=jnp.int32)[None, :]
+    group_at = doc_at * reqs + entry_at // cols % reqs
+    packed = (doc_at * LANES + entry_at) | (group_at << 12) | ((entries % DOC_DEV) << 20)
+    packed = packed.reshape(-1)
+    mine = (entries // DOC_DEV == me).reshape(-1)
+    rank = jnp.cumsum(mine.astype(jnp.int32)) - 1
+    total_slots = n_doc * block
+    chosen = mine[None, :] & (rank[None, :] == jnp.arange(total_slots, dtype=jnp.int32)[:, None])
+    slots = jnp.sum(jnp.where(chosen, packed[None, :], 0), axis=1)
+    count = jnp.sum(mine.astype(jnp.int32))
+    slots = jnp.where(jnp.arange(total_slots) < count, slots, LANES - 1)
+
+    out_one = over_head(w_out, 2)
+    out_pieces = [w_out, over_head(w_out, 1), out_one, over_head(out_one, 1)]
+
+    att = attend(krow, vrow, qkv, relq, relk, key_pieces, value_pieces)
+    att_y = over_head(att, 2)
+    att_pieces = [att, over_head(att, 1), att_y, over_head(att_y, 1)]
+
+    gain_rows = gain_one.reshape(1, -1)
+    common = (att_pieces, out_pieces, tokens, gain_rows, w_up, w_down)
+    start_other = ((1 - own_c) * half).astype(jnp.int32).reshape(1)
+    other = feed(
+        feed_other_kernel,
+        start_other,
+        *common,
+        [jax.ShapeDtypeStruct((half, tokens.shape[1]), jnp.bfloat16)],
+        "feed_other",
+    )[0]
+    from_core = over_head(other, 1)
+    start_own = jnp.stack(
+        [own_c * half + (1 - own_y) * quarter, own_c * half + own_y * quarter]
+    ).astype(jnp.int32)
+    for_y, own = feed(
+        feed_own_kernel,
+        start_own,
+        *common,
+        [jax.ShapeDtypeStruct((quarter, tokens.shape[1]), jnp.float32)] * 2,
+        "feed_own",
+    )
+    core_y = lax.dynamic_slice_in_dim(from_core, (1 - own_y) * quarter, quarter, 0)
+    core_own = lax.dynamic_slice_in_dim(from_core, own_y * quarter, quarter, 0)
+    from_y = over_head((for_y + core_y.astype(jnp.float32)).astype(jnp.bfloat16), 2)
+
+    emb = w_proj.shape[1]
+    vectors = pl.pallas_call(
+        project_kernel,
+        out_shape=jax.ShapeDtypeStruct((n_doc, quarter, emb), jnp.bfloat16),
+        in_specs=full_specs(5),
+        out_specs=full_specs(1)[0],
+        compiler_params=params(),
+        name="project",
+    )(own, core_own, from_y, gain_two.reshape(1, -1), w_proj)
+    queries = lax.all_to_all(vectors, "doc", 0, 0, tiled=True).reshape(n_doc * quarter, emb)
+
+    mine_rows = vectors[0]
+    y_rows = over_head(mine_rows, 2)
+    pair = jnp.where(
+        own_y == 0, jnp.concatenate([mine_rows, y_rows]), jnp.concatenate([y_rows, mine_rows])
+    )
+    core_pair = over_head(pair, 1)
+    query_vectors = jnp.where(
+        own_c == 0, jnp.concatenate([pair, core_pair]), jnp.concatenate([core_pair, pair])
+    )
+
+    smem = pl.BlockSpec(memory_space=pltpu.SMEM)
+    rated = pl.pallas_call(
+        score_kernel,
+        out_shape=jax.ShapeDtypeStruct((n_doc, LANES), jnp.float32),
+        in_specs=[smem, smem, smem] + full_specs(2),
+        out_specs=full_specs(1)[0],
+        compiler_params=params(),
+        name="rate",
+    )(slots, count.reshape(1), doc_lengths, queries, doc_vectors)
+    tiles = rated[:, :block].reshape(n_doc * n_head, reqs * cols)
+    back = lax.all_to_all(tiles, ("doc", "head"), 0, 0, tiled=True)
+    scores = jnp.sum(back.reshape(n_doc, n_head, reqs, cols), axis=0)
+    scores = scores.reshape(2, 2, reqs, cols).transpose(1, 0, 2, 3).reshape(n_head * reqs, cols)
+    return (query_vectors, scores)
+
+
 def solution(mesh):
     placed = (
         P("doc", None),
@@ -164,8 +513,9 @@
         P("doc"),
         P("doc", "head"),
     )
+    fits = mesh.shape["head"] == 4 and mesh.shape["doc"] == 8
     return jax.shard_map(
-        body,
+        body if fits else body_any,
         mesh=mesh,
         in_specs=placed,
         out_specs=(P("doc", None), P("doc", "head")),

time: 306 us -> 124 us (0.41)
  local copies, waits for them, and re-layouts: 110 us -> 16 us
  blocking collectives: 67.1 us -> 0 us
  waiting for transfers between devices: 64.1 us -> 22.2 us
  starting transfers between devices: 5.06 us -> 40 us
  matrix products: 34.6 us -> 5.54 us
  Pallas kernels: 0 us -> 28.7 us
  between operations: 14.1 us -> 0.95 us
    gather x10 -> x0, local copies, waits for them, and re-layouts: 74.8 us -> none  [the longest x2 27 us: body(): rel_k_rows = rel_both[1][:, index_one]]
    all_gather x2 -> x0, blocking collectives: 67.1 us -> none  [the longest x1 34.9 us: body(): lax.all_gather(query_vectors, 'doc', axis=0, tiled=True)]
    psum x2 -> x0, waiting for transfers between devices: 57.8 us -> none  [the longest x1 34.7 us: body(): lax.psum(jnp.dot(inner, w_down, preferred_element_type=jnp.float32).astyp...]
    dot_general x10 -> x3, matrix products: 34.6 us -> 5.54 us  [the longest x1 1.96 us: body(): jnp.dot(rel_table[low_k:low_k + LANES], weight[:, width:2 * width], prefe...]
    pallas_call x0 -> x5, Pallas kernels: none -> 28.7 us  [the longest x2 10.9 us: feed(): pl.pallas_call(kernel, out_shape=outs, in_specs=[pl.BlockSpec(memory_spac...]
    ppermute x0 -> x18, starting transfers between devices: none -> 20.3 us  [the longest x8 13.5 us: over_doc(): return lax.ppermute(x, 'doc', [(i, i ^ k) for i in range(n_doc)])]
    all_to_all x1 -> x3, starting transfers between devices: 4.76 us -> 19.6 us  [the longest x1 9.92 us: body(): back = lax.all_to_all(tiles, ('doc', 'head'), 0, 0, tiled=True)]
    ppermute x0 -> x18, waiting for transfers between devices: none -> 13.2 us  [the longest x10 9.11 us: over_head(): return lax.ppermute(x, 'head', [(i, i ^ k) for i in range(n_head)])]
  transfers between devices with their start and end apart: 4 -> 21, of which waited for: 3 -> 7; matrix products, arithmetic and copies ran while one was open for 29% -> 17% of each run, Pallas kernels for 0% -> 19%
where the time goes in v1:
time: 124 us; the launch traced here: 122 us
  starting transfers between devices  40 us (32%)
  Pallas kernels  28.7 us (23%)
  waiting for transfers between devices  22.2 us (18%)
  local copies, waits for them, and re-layouts  16 us (13%)
  other arithmetic  9.11 us (7%)
  matrix products  5.54 us (4%)
    ppermute x8, starting transfers between devices, over_doc(): return lax.ppermute(x, 'doc', [(i, i ^ k) for i in range(n_doc)])  13.5 us
    pallas_call x2, Pallas kernels, feed(): pl.pallas_call(kernel, out_shape=outs, in_specs=[pl.BlockSpec(memory_spac...  10.9 us
    all_to_all x1, starting transfers between devices, body(): back = lax.all_to_all(tiles, ('doc', 'head'), 0, 0, tiled=True)  9.92 us
    pallas_call x1, Pallas kernels, attend(): pl.pallas_call(attend_kernel, out_shape=jax.ShapeDtypeStruct((rows, width...  9.41 us
    ppermute x10, waiting for transfers between devices, over_head(): return lax.ppermute(x, 'head', [(i, i ^ k) for i in range(n_head)])  9.11 us
    unnamed x36, local copies, waits for them, and re-layouts  8.26 us
    pallas_call x1, Pallas kernels, body(): pl.pallas_call(score_kernel, out_shape=jax.ShapeDtypeStruct((n_doc, LANES...  7.26 us
    ppermute x10, starting transfers between devices, over_head(): return lax.ppermute(x, 'head', [(i, i ^ k) for i in range(n_head)])  6.87 us
  transfers between devices with their start and end apart: 21, of which 7 were waited for; matrix products, arithmetic and copies ran while one was open for 17% of the time, Pallas kernels for 19%

profile of v1, /device:TPU:0, one launch (start us, length us, event | category | flops | bytes accessed | tf_op | source)
XLA Modules:
  0.0 122.4 jit_solution(9111139528838009396)
XLA Ops:
  0.6 1.5 %slice_bitcast_fusion = (bf16[128,256]{1,0:T(8,128)(2,1)}, bf16[128,256]{1,0:T(8,128)(2,1)S(1)}) fusion(bf16[2,128,256]{2,1,0:T(8,128)(2,1)} %param.22), kind=kLoop, calls=%fused_computation.14 | loop fusion | bytes 262144 | tf_op jit(solution)/shard_map/squeeze | solution.py:387
  2.1 3.0 %collective-permute-start.4 = (bf16[128,256]{1,0:T(8,128)(2,1)}, bf16[128,256]{1,0:T(8,128)(2,1)}, u32[]{:S(2)}, u32[]{:S(2)}) collective-permute-start(bf16[128,256]{1,0:T(8,128)(2,1)} %get-tuple-element.17), channel_id=1, source_target_pairs={{0,2},{1,3},{2,0},{3,1},{4,6},{5,7},{6,4},{7,5},{8,10},{9,11},{10,... | collective-permute-start | bytes 196616 | tf_op jit(solution)/shard_map/ppermute | solution.py:382
  5.2 2.6 %collective-permute-start.5 = (bf16[128,256]{1,0:T(8,128)(2,1)}, bf16[128,256]{1,0:T(8,128)(2,1)}, u32[]{:S(2)}, u32[]{:S(2)}) collective-permute-start(bf16[128,256]{1,0:T(8,128)(2,1)} %get-tuple-element.17), channel_id=1, source_target_pairs={{0,4},{1,5},{2,6},{3,7},{4,0},{5,1},{6,2},{7,3},{8,12},{9,13},{10,... | collective-permute-start | bytes 196616 | tf_op jit(solution)/shard_map/ppermute | solution.py:382
  7.8 1.7 %collective-permute-start = (bf16[128,256]{1,0:T(8,128)(2,1)S(1)}, bf16[128,256]{1,0:T(8,128)(2,1)}, u32[]{:S(2)}, u32[]{:S(2)}) collective-permute-start(bf16[128,256]{1,0:T(8,128)(2,1)S(1)} %get-tuple-element.18), channel_id=1, source_target_pairs={{0,1},{1,0},{2,3},{3,2},{4,5},{5,4},{6,7},{7,6},{8,9},{9,8},{10,11... | collective-permute-start | bytes 196616 | tf_op jit(solution)/shard_map/ppermute | solution.py:382
  9.5 1.5 %collective-permute-start.12 = (bf16[256,1024]{1,0:T(8,128)(2,1)}, bf16[256,1024]{1,0:T(8,128)(2,1)}, u32[]{:S(2)}, u32[]{:S(2)}) collective-permute-start(bf16[256,1024]{1,0:T(8,128)(2,1)} %w0.3), channel_id=1, source_target_pairs={{0,16},{8,24},{16,0},{24,8},{1,17},{9,25},{17,1},{25,9},{2,18},{10... | collective-permute-start | bytes 1572872 | tf_op jit(solution)/shard_map/ppermute | solution.py:385
  11.0 0.8 copy.33
  12.4 4.1 %all-to-all-start = ((s32[32,1,24]{2,1,0:T(1,128)}), s32[32,1,24]{2,1,0:T(1,128)}, u32[]{:S(2)}, u32[]{:S(2)}) async-start(s32[32,1,24]{2,1,0:T(1,128)} %bitcast.11), calls=%async_computation | async-start | bytes 32768 | tf_op jit(solution)/shard_map/all_to_all | solution.py:415
  16.5 1.7 %copy.32 = bf16[1024,3,256]{0,2,1:T(8,128)(2,1)S(1)} copy(bf16[1024,3,256]{2,0,1:T(8,128)(2,1)} %param.15) | data formatting | bytes 3145728 | tf_op args[1]
  18.3 2.0 %convolution_convert_fusion.1.relk = bf16[128,256]{1,0:T(8,128)(2,1)} fusion(bf16[1024,768]{0,1:T(8,128)(2,1)S(1)} %bitcast.35, bf16[512,1024]{1,0:T(8,128)(2,1)} %param.21), kind=kOutput, calls=%fused_computation.4 | convolution fusion | flops 67141632 | bytes 851968 | tf_op jit(solution)/shard_map/dot_general | solution.py:405
  20.3 1.9 %convolution_convert_fusion.2.relq = bf16[128,256]{1,0:T(8,128)(2,1)} fusion(bf16[1024,768]{0,1:T(8,128)(2,1)S(1)} %bitcast.36, bf16[512,1024]{1,0:T(8,128)(2,1)} %param.21), kind=kOutput, calls=%fused_computation.5 | convolution fusion | flops 67141632 | bytes 851968 | tf_op jit(solution)/shard_map/dot_general | solution.py:402
  22.2 1.7 %convolution_convert_fusion.qkv = bf16[384,768]{1,0:T(8,128)(2,1)} fusion(bf16[384,1024]{1,0:T(8,128)(2,1)S(1)} %copy-done.2, bf16[1024,768]{0,1:T(8,128)(2,1)S(1)} %bitcast.37), kind=kOutput, calls=%fused_computation.3 | convolution fusion | flops 604274688 | bytes 2949120 | tf_op jit(solution)/shard_map/dot_general | solution.py:399
  23.9 0.7 shift-left_or_fusion
  24.6 0.9 pad_maximum_fusion.1.k_zero
  25.5 1.8 %collective-permute-start.1 = (bf16[256,256]{1,0:T(8,128)(2,1)S(1)}, bf16[256,256]{1,0:T(8,128)(2,1)}, u32[]{:S(2)}, u32[]{:S(2)}) collective-permute-start(bf16[256,256]{1,0:T(8,128)(2,1)S(1)} %pad_maximum_fusion.1.k_zero), channel_id=1, source_target_pairs={{0,2},{1,3},{2,0},{3,1},{4,6},{5,7},{6,4},{7,5},{8,10},{9,11},{10,... | collective-permute-start | bytes 393224 | tf_op jit(solution)/shard_map/ppermute | solution.py:382
  27.2 2.4 %collective-permute-start.2 = (bf16[256,256]{1,0:T(8,128)(2,1)S(1)}, bf16[256,256]{1,0:T(8,128)(2,1)}, u32[]{:S(2)}, u32[]{:S(2)}) collective-permute-start(bf16[256,256]{1,0:T(8,128)(2,1)S(1)} %pad_maximum_fusion.1.k_zero), channel_id=1, source_target_pairs={{0,4},{1,5},{2,6},{3,7},{4,0},{5,1},{6,2},{7,3},{8,12},{9,13},{10,... | collective-permute-start | bytes 393224 | tf_op jit(solution)/shard_map/ppermute | solution.py:382
  29.9 1.7 %pad_maximum_fusion.v_zero = bf16[512,256]{1,0:T(8,128)(2,1)} fusion(bf16[128,256]{1,0:T(8,128)(2,1)} %collective-permute-done.6, bf16[128,256]{1,0:T(8,128)(2,1)} %collective-permute-done.5, bf16[128,256]{1,0:T(8,128)(2,1)} %collective-permute-done.4, bf16[128,256]{1,0:T(8,128)(2,1)} %get-tuple-element.17), kind=kLoop, calls=%fused_computation.9 | loop fusion | flops 1048576 | bytes 524288 | tf_op jit(solution)/shard_map/concatenate | solution.py:389
  31.6 1.7 %collective-permute-start.7 = (bf16[512,256]{1,0:T(8,128)(2,1)}, bf16[512,256]{1,0:T(8,128)(2,1)}, u32[]{:S(2)}, u32[]{:S(2)}) collective-permute-start(bf16[512,256]{1,0:T(8,128)(2,1)} %pad_maximum_fusion.v_zero), channel_id=1, source_target_pairs={{0,1},{1,0},{2,3},{3,2},{4,5},{5,4},{6,7},{7,6},{8,9},{9,8},{10,11... | collective-permute-start | bytes 786440 | tf_op jit(solution)/shard_map/ppermute | solution.py:382
  33.4 1.3 %or.18 = s32[768]{0:T(1024)} reshape(s32[8,96]{1,0:T(8,128)} %shift-left_or_fusion) | data formatting | bytes 6144 | tf_op jit(solution)/shard_map/or | solution.py:420
  34.7 1.4 %reshape.238 = s32[6,128]{1,0:T(8,128)} reshape(s32[32,24]{1,0:T(8,128)} %bitcast.12) | data formatting | bytes 6144 | tf_op jit(solution)/shard_map/reshape | solution.py:415
  36.1 4.1 %collective-permute-done.2.k_two = bf16[256,256]{1,0:T(8,128)(2,1)} collective-permute-done((bf16[256,256]{1,0:T(8,128)(2,1)S(1)}, bf16[256,256]{1,0:T(8,128)(2,1)}, u32[]{:S(2)}, u32[]{:S(2)}) %collective-permute-start.2) | collective-permute-done | bytes 131104 | tf_op jit(solution)/shard_map/ppermute | solution.py:382
  40.3 1.1 copy-done.4
  41.3 0.8 copy-done.6
  42.2 0.8 copy-done.7
  43.0 9.4 %attend.1.a0 = bf16[384,256]{1,0:T(8,128)(2,1)} custom-call(s32[12]{0:T(128)S(1)} %multiply_add_fusion.1.krow, s32[12]{0:T(128)S(1)} %get-tuple-element.14.vrow, bf16[384,768]{1,0:T(8,128)(2,1)S(1)} %copy-done.4, bf16[128,256]{1,0:T(8,128)(2,1)S(1)} %copy-done.7, bf16[128,256]{1,0:T(8,128)(2,1)S(1)} %copy-done.6, ...), custom_call_target="tpu_custom_call" | custom-call | flops 419430400 | bytes 2097152 | tf_op jit(solution)/shard_map/attend/pallas_call | solution.py:251
  52.4 1.5 %collective-permute-start.9 = (bf16[384,256]{1,0:T(8,128)(2,1)}, bf16[384,256]{1,0:T(8,128)(2,1)}, u32[]{:S(2)}, u32[]{:S(2)}) collective-permute-start(bf16[384,256]{1,0:T(8,128)(2,1)} %attend.1.a0), channel_id=1, source_target_pairs={{0,16},{8,24},{16,0},{24,8},{1,17},{9,25},{17,1},{25,9},{2,18},{10... | collective-permute-start | bytes 589832 | tf_op jit(solution)/shard_map/ppermute | solution.py:385
  54.8 1.4 %reduce.11 = s32[32,24]{1,0:T(8,128)S(1)} reduce(s32[32,1,24]{2,1,0:T(1,128)} %all-to-all-done, s32[]{:T(128)} %broadcast.291), dimensions={1}, to_apply=%all_to_all.18.reduce_sub_computation.5 | reduce | bytes 6148 | tf_op jit(solution)/shard_map/all_to_all | solution.py:415
  57.0 1.4 %collective-permute-done.9.a2 = bf16[384,256]{1,0:T(8,128)(2,1)} collective-permute-done((bf16[384,256]{1,0:T(8,128)(2,1)}, bf16[384,256]{1,0:T(8,128)(2,1)}, u32[]{:S(2)}, u32[]{:S(2)}) %collective-permute-start.9) | collective-permute-done | bytes 196640 | tf_op jit(solution)/shard_map/ppermute | solution.py:385
  58.5 1.6 %collective-permute-done.10.a3 = bf16[384,256]{1,0:T(8,128)(2,1)S(1)} collective-permute-done((bf16[384,256]{1,0:T(8,128)(2,1)}, bf16[384,256]{1,0:T(8,128)(2,1)S(1)}, u32[]{:S(2)}, u32[]{:S(2)}) %collective-permute-start.10) | collective-permute-done | bytes 196640 | tf_op jit(solution)/shard_map/ppermute | solution.py:385
  60.1 4.5 %feed_other.1 = bf16[192,1024]{1,0:T(8,128)(2,1)S(1)} custom-call(s32[1]{0:T(128)} %bitcast.6.start, bf16[384,256]{1,0:T(8,128)(2,1)} %attend.1.a0, bf16[384,256]{1,0:T(8,128)(2,1)S(1)} %collective-permute-done.8.a1, bf16[384,256]{1,0:T(8,128)(2,1)} %collective-permute-done.9.a2, bf16[384,256]{1,0:T(8,128)(2,1)S(1)} %collective-permute-done.10.a3, ...), custom_call_target="tpu_custom_call" | custom-call | flops 1677721600 | bytes 6291456 | tf_op jit(solution)/shard_map/feed_other/pallas_call | solution.py:304
  64.8 6.4 %feed_own.1 = (f32[96,1024]{1,0:T(8,128)S(1)}, f32[96,1024]{1,0:T(8,128)S(1)}) custom-call(s32[2]{0:T(128)S(1)} %pad_add_fusion.start, bf16[384,256]{1,0:T(8,128)(2,1)} %attend.1.a0, bf16[384,256]{1,0:T(8,128)(2,1)S(1)} %collective-permute-done.8.a1, bf16[384,256]{1,0:T(8,128)(2,1)} %collective-permute-done.9.a2, ...), custom_call_target="tpu_custom_call" | custom-call | flops 1677721600 | bytes 6291456 | tf_op jit(solution)/shard_map/feed_own/pallas_call | solution.py:304
  71.3 1.5 %collective-permute-start.15 = (bf16[96,1024]{1,0:T(8,128)(2,1)S(1)}, bf16[96,1024]{1,0:T(8,128)(2,1)S(1)}, u32[]{:S(2)}, u32[]{:S(2)}) collective-permute-start(bf16[96,1024]{1,0:T(8,128)(2,1)S(1)} %add_convert_fusion), channel_id=1, source_target_pairs={{0,16},{8,24},{16,0},{24,8},{1,17},{9,25},{17,1},{25,9},{2,18},{10... | collective-permute-start | bytes 589832 | tf_op jit(solution)/shard_map/ppermute | solution.py:385
  73.4 5.1 %collective-permute-done.15.from_y = bf16[96,1024]{1,0:T(8,128)(2,1)S(1)} collective-permute-done((bf16[96,1024]{1,0:T(8,128)(2,1)S(1)}, bf16[96,1024]{1,0:T(8,128)(2,1)S(1)}, u32[]{:S(2)}, u32[]{:S(2)}) %collective-permute-start.15) | collective-permute-done | bytes 196640 | tf_op jit(solution)/shard_map/ppermute | solution.py:385
  78.6 1.2 project.1
  79.7 5.6 %all-to-all-start.1 = ((bf16[8,96,128]{2,1,0:T(8,128)(2,1)}), bf16[8,96,128]{2,1,0:T(8,128)(2,1)S(1)}, u32[]{:S(2)}, u32[]{:S(2)}) async-start(bf16[8,96,128]{2,1,0:T(8,128)(2,1)} %project.1), calls=%async_computation.1 | async-start | bytes 393216 | tf_op jit(solution)/shard_map/all_to_all | solution.py:471
  85.3 0.7 slice_bitcast_fusion.2
  86.1 1.5 %collective-permute-start.16 = (bf16[96,128]{1,0:T(8,128)(2,1)S(1)}, bf16[96,128]{1,0:T(8,128)(2,1)S(1)}, u32[]{:S(2)}, u32[]{:S(2)}) collective-permute-start(bf16[96,128]{1,0:T(8,128)(2,1)S(1)} %slice_bitcast_fusion.2), channel_id=1, source_target_pairs={{0,16},{8,24},{16,0},{24,8},{1,17},{9,25},{17,1},{25,9},{2,18},{10... | collective-permute-start | bytes 73736 | tf_op jit(solution)/shard_map/ppermute | solution.py:385
  87.5 1.4 %convert_reduce_fusion = s32[]{:T(128)} fusion(s32[32,24]{1,0:T(8,128)} %bitcast.12, s32[]{:T(128)S(6)} %axis_index.25), kind=kLoop, calls=%fused_computation.24 | loop fusion | flops 13823 | bytes 3080 | tf_op jit(solution)/shard_map/reduce_sum | solution.py:427
  88.9 1.0 collective-permute-done.16
  90.0 0.7 fusion.13.slots
  90.6 2.5 %all-to-all-done.1 = bf16[8,96,128]{2,1,0:T(8,128)(2,1)S(1)} async-done(((bf16[8,96,128]{2,1,0:T(8,128)(2,1)}), bf16[8,96,128]{2,1,0:T(8,128)(2,1)S(1)}, u32[]{:S(2)}, u32[]{:S(2)}) %all-to-all-start.1) | async-done | bytes 196640 | tf_op jit(solution)/shard_map/all_to_all | solution.py:471
  93.1 2.2 %copy-done.1 = bf16[64,256,128]{2,1,0:T(8,128)(2,1)S(1)} copy-done((bf16[64,256,128]{2,1,0:T(8,128)(2,1)S(1)}, bf16[64,256,128]{2,1,0:T(8,128)(2,1)}, u32[]{:S(2)}) %copy-start.1) | copy-done | bytes 4194328
  95.3 7.3 %rate.1 = f32[8,128]{1,0:T(8,128)S(1)} custom-call(s32[768]{0:T(1024)S(1)} %fusion.13.slots, s32[1]{0:T(128)} %bitcast.14.count, s32[64]{0:T(128)S(1)} %copy-done.10, bf16[768,128]{1,0:T(8,128)(2,1)S(1)} %bitcast.30, bf16[64,256,128]{2,1,0:T(8,128)(2,1)S(1)} %copy-done.1), custom_call_target="tpu_custom_call" | custom-call | tf_op jit(solution)/shard_map/rate/pallas_call | solution.py:484
  102.6 0.7 all_to_all.21
  103.2 9.9 %all-to-all-start.2 = ((f32[32,1,24]{2,1,0:T(1,128)}), f32[32,1,24]{2,1,0:T(1,128)S(1)}, u32[]{:S(2)}, u32[]{:S(2)}) async-start(f32[32,1,24]{2,1,0:T(1,128)} %bitcast.16), calls=%async_computation.2 | async-start | bytes 32768 | tf_op jit(solution)/shard_map/all_to_all | solution.py:493
  113.2 0.7 maximum_select_fusion
  113.8 6.5 %all-to-all-done.2 = f32[32,1,24]{2,1,0:T(1,128)S(1)} async-done(((f32[32,1,24]{2,1,0:T(1,128)}), f32[32,1,24]{2,1,0:T(1,128)S(1)}, u32[]{:S(2)}, u32[]{:S(2)}) %all-to-all-start.2) | async-done | bytes 3104 | tf_op jit(solution)/shard_map/all_to_all | solution.py:493
  120.8 0.7 reduce.12
  121.8 0.7 reshape.245
  (77 shorter events, 4.6 us)
Async XLA Ops:
  2.1 16.1 %copy-start.11 = (bf16[128,256]{1,0:T(8,128)(2,1)}, bf16[128,256]{1,0:T(8,128)(2,1)S(1)}, u32[]{:S(2)}) copy-start(bf16[128,256]{1,0:T(8,128)(2,1)S(1)} %get-tuple-element.18) | copy-start | bytes 196612
  2.1 25.1 %collective-permute-start.4 = (bf16[128,256]{1,0:T(8,128)(2,1)}, bf16[128,256]{1,0:T(8,128)(2,1)}, u32[]{:S(2)}, u32[]{:S(2)}) collective-permute-start(bf16[128,256]{1,0:T(8,128)(2,1)} %get-tuple-element.17), channel_id=1, source_target_pairs={{0,2},{1,3},{2,0},{3,1},{4,6},{5,7},{6,4},{7,5},{8,10},{9,11},{10,... | collective-permute-start | bytes 196616 | tf_op jit(solution)/shard_map/ppermute | solution.py:382
  5.2 24.5 %collective-permute-start.5 = (bf16[128,256]{1,0:T(8,128)(2,1)}, bf16[128,256]{1,0:T(8,128)(2,1)}, u32[]{:S(2)}, u32[]{:S(2)}) collective-permute-start(bf16[128,256]{1,0:T(8,128)(2,1)} %get-tuple-element.17), channel_id=1, source_target_pairs={{0,4},{1,5},{2,6},{3,7},{4,0},{5,1},{6,2},{7,3},{8,12},{9,13},{10,... | collective-permute-start | bytes 196616 | tf_op jit(solution)/shard_map/ppermute | solution.py:382
  7.8 22.2 %collective-permute-start.6 = (bf16[128,256]{1,0:T(8,128)(2,1)}, bf16[128,256]{1,0:T(8,128)(2,1)}, u32[]{:S(2)}, u32[]{:S(2)}) collective-permute-start(bf16[128,256]{1,0:T(8,128)(2,1)} %get-tuple-element.17), channel_id=1, source_target_pairs={{0,6},{1,7},{2,4},{3,5},{4,2},{5,3},{6,0},{7,1},{8,14},{9,15},{10,... | collective-permute-start | bytes 196616 | tf_op jit(solution)/shard_map/ppermute | solution.py:382
  7.8 16.8 %collective-permute-start = (bf16[128,256]{1,0:T(8,128)(2,1)S(1)}, bf16[128,256]{1,0:T(8,128)(2,1)}, u32[]{:S(2)}, u32[]{:S(2)}) collective-permute-start(bf16[128,256]{1,0:T(8,128)(2,1)S(1)} %get-tuple-element.18), channel_id=1, source_target_pairs={{0,1},{1,0},{2,3},{3,2},{4,5},{5,4},{6,7},{7,6},{8,9},{9,8},{10,11... | collective-permute-start | bytes 196616 | tf_op jit(solution)/shard_map/ppermute | solution.py:382
  9.5 44.4 %collective-permute-start.12 = (bf16[256,1024]{1,0:T(8,128)(2,1)}, bf16[256,1024]{1,0:T(8,128)(2,1)}, u32[]{:S(2)}, u32[]{:S(2)}) collective-permute-start(bf16[256,1024]{1,0:T(8,128)(2,1)} %w0.3), channel_id=1, source_target_pairs={{0,16},{8,24},{16,0},{24,8},{1,17},{9,25},{17,1},{25,9},{2,18},{10... | collective-permute-start | bytes 1572872 | tf_op jit(solution)/shard_map/ppermute | solution.py:385
  12.4 22.3 %all-to-all-start = ((s32[32,1,24]{2,1,0:T(1,128)}), s32[32,1,24]{2,1,0:T(1,128)}, u32[]{:S(2)}, u32[]{:S(2)}) async-start(s32[32,1,24]{2,1,0:T(1,128)} %bitcast.11), calls=%async_computation | async-start | bytes 32768 | tf_op jit(solution)/shard_map/all_to_all | solution.py:415
  18.3 3.9 %copy-start.2 = (bf16[384,1024]{1,0:T(8,128)(2,1)S(1)}, bf16[384,1024]{1,0:T(8,128)(2,1)}, u32[]{:S(2)}) copy-start(bf16[384,1024]{1,0:T(8,128)(2,1)} %tokens.3) | copy-start | bytes 2359300
  22.2 2.4 %copy-start.15 = (s32[12]{0:T(128)S(1)}, s32[12]{0:T(128)}, u32[]{:S(2)}) copy-start(s32[12]{0:T(128)} %param.26) | copy-start | bytes 148
  22.2 2.4 %copy-start.12 = (bf16[128,256]{1,0:T(8,128)(2,1)S(1)}, bf16[128,256]{1,0:T(8,128)(2,1)}, u32[]{:S(2)}) copy-start(bf16[128,256]{1,0:T(8,128)(2,1)} %copy-done.11) | copy-start | bytes 196612
  22.2 13.9 %copy-start.3 = (bf16[256,1024]{1,0:T(8,128)(2,1)S(1)}, bf16[256,1024]{1,0:T(8,128)(2,1)}, u32[]{:S(2)}) copy-start(bf16[256,1024]{1,0:T(8,128)(2,1)} %w0.3) | copy-start | bytes 1572868
  22.2 37.8 %copy-start.8 = (f32[1024]{0:T(1024)S(1)}, f32[1024]{0:T(1024)}, u32[]{:S(2)}) copy-start(f32[1024]{0:T(1024)} %param.19) | copy-start | bytes 12292
  23.9 36.2 %copy-start = (bf16[1024,1024]{1,0:T(8,128)(2,1)S(1)}, bf16[1024,1024]{1,0:T(8,128)(2,1)}, u32[]{:S(2)}) copy-start(bf16[1024,1024]{1,0:T(8,128)(2,1)} %w_up.3) | copy-start | bytes 6291460
  25.5 10.6 %collective-permute-start.1 = (bf16[256,256]{1,0:T(8,128)(2,1)S(1)}, bf16[256,256]{1,0:T(8,128)(2,1)}, u32[]{:S(2)}, u32[]{:S(2)}) collective-permute-start(bf16[256,256]{1,0:T(8,128)(2,1)S(1)} %pad_maximum_fusion.1.k_zero), channel_id=1, source_target_pairs={{0,2},{1,3},{2,0},{3,1},{4,6},{5,7},{6,4},{7,5},{8,10},{9,11},{10,... | collective-permute-start | bytes 393224 | tf_op jit(solution)/shard_map/ppermute | solution.py:382
  27.2 13.0 %collective-permute-start.2 = (bf16[256,256]{1,0:T(8,128)(2,1)S(1)}, bf16[256,256]{1,0:T(8,128)(2,1)}, u32[]{:S(2)}, u32[]{:S(2)}) collective-permute-start(bf16[256,256]{1,0:T(8,128)(2,1)S(1)} %pad_maximum_fusion.1.k_zero), channel_id=1, source_target_pairs={{0,4},{1,5},{2,6},{3,7},{4,0},{5,1},{6,2},{7,3},{8,12},{9,13},{10,... | collective-permute-start | bytes 393224 | tf_op jit(solution)/shard_map/ppermute | solution.py:382
  29.7 10.6 %collective-permute-start.3 = (bf16[256,256]{1,0:T(8,128)(2,1)S(1)}, bf16[256,256]{1,0:T(8,128)(2,1)}, u32[]{:S(2)}, u32[]{:S(2)}) collective-permute-start(bf16[256,256]{1,0:T(8,128)(2,1)S(1)} %pad_maximum_fusion.1.k_zero), channel_id=1, source_target_pairs={{0,6},{1,7},{2,4},{3,5},{4,2},{5,3},{6,0},{7,1},{8,14},{9,15},{10,... | collective-permute-start | bytes 393224 | tf_op jit(solution)/shard_map/ppermute | solution.py:382
  31.6 8.6 %collective-permute-start.7 = (bf16[512,256]{1,0:T(8,128)(2,1)}, bf16[512,256]{1,0:T(8,128)(2,1)}, u32[]{:S(2)}, u32[]{:S(2)}) collective-permute-start(bf16[512,256]{1,0:T(8,128)(2,1)} %pad_maximum_fusion.v_zero), channel_id=1, source_target_pairs={{0,1},{1,0},{2,3},{3,2},{4,5},{5,4},{6,7},{7,6},{8,9},{9,8},{10,11... | collective-permute-start | bytes 786440 | tf_op jit(solution)/shard_map/ppermute | solution.py:382
  36.1 22.4 %collective-permute-start.11 = (bf16[256,1024]{1,0:T(8,128)(2,1)S(1)}, bf16[256,1024]{1,0:T(8,128)(2,1)}, u32[]{:S(2)}, u32[]{:S(2)}) collective-permute-start(bf16[256,1024]{1,0:T(8,128)(2,1)S(1)} %copy-done.3), channel_id=1, source_target_pairs={{0,8},{8,0},{16,24},{24,16},{1,9},{9,1},{17,25},{25,17},{2,10},{10... | collective-permute-start | bytes 1572872 | tf_op jit(solution)/shard_map/ppermute | solution.py:385
  40.2 1.1 copy-start.4
  41.3 0.8 copy-start.6
  42.2 0.8 copy-start.7
  43.0 10.9 %copy-start.14 = (s32[6,128]{1,0:T(8,128)S(1)}, s32[6,128]{1,0:T(8,128)}, u32[]{:S(2)}) copy-start(s32[6,128]{1,0:T(8,128)} %reshape.238) | copy-start | bytes 9220
  52.4 6.0 %collective-permute-start.9 = (bf16[384,256]{1,0:T(8,128)(2,1)}, bf16[384,256]{1,0:T(8,128)(2,1)}, u32[]{:S(2)}, u32[]{:S(2)}) collective-permute-start(bf16[384,256]{1,0:T(8,128)(2,1)} %attend.1.a0), channel_id=1, source_target_pairs={{0,16},{8,24},{16,0},{24,8},{1,17},{9,25},{17,1},{25,9},{2,18},{10... | collective-permute-start | bytes 589832 | tf_op jit(solution)/shard_map/ppermute | solution.py:385
  53.9 6.2 %collective-permute-start.13 = (bf16[256,1024]{1,0:T(8,128)(2,1)}, bf16[256,1024]{1,0:T(8,128)(2,1)}, u32[]{:S(2)}, u32[]{:S(2)}) collective-permute-start(bf16[256,1024]{1,0:T(8,128)(2,1)} %collective-permute-done.12.w2), channel_id=1, source_target_pairs={{0,8},{8,0},{16,24},{24,16},{1,9},{9,1},{17,25},{25,17},{2,10},{10... | collective-permute-start | bytes 1572872 | tf_op jit(solution)/shard_map/ppermute | solution.py:385
  56.4 2.1 %collective-permute-start.8 = (bf16[384,256]{1,0:T(8,128)(2,1)}, bf16[384,256]{1,0:T(8,128)(2,1)S(1)}, u32[]{:S(2)}, u32[]{:S(2)}) collective-permute-start(bf16[384,256]{1,0:T(8,128)(2,1)} %attend.1.a0), channel_id=1, source_target_pairs={{0,8},{8,0},{16,24},{24,16},{1,9},{9,1},{17,25},{25,17},{2,10},{10... | collective-permute-start | bytes 589832 | tf_op jit(solution)/shard_map/ppermute | solution.py:385
  58.4 1.7 %collective-permute-start.10 = (bf16[384,256]{1,0:T(8,128)(2,1)}, bf16[384,256]{1,0:T(8,128)(2,1)S(1)}, u32[]{:S(2)}, u32[]{:S(2)}) collective-permute-start(bf16[384,256]{1,0:T(8,128)(2,1)} %collective-permute-done.9.a2), channel_id=1, source_target_pairs={{0,8},{8,0},{16,24},{24,16},{1,9},{9,1},{17,25},{25,17},{2,10},{10... | collective-permute-start | bytes 589832 | tf_op jit(solution)/shard_map/ppermute | solution.py:385
  60.1 4.7 %copy-start.13 = (s32[768]{0:T(1024)S(1)}, s32[768]{0:T(1024)}, u32[]{:S(2)}) copy-start(s32[768]{0:T(1024)} %or.18) | copy-start | bytes 9220
  64.6 6.7 %collective-permute-start.14 = (bf16[192,1024]{1,0:T(8,128)(2,1)S(1)}, bf16[192,1024]{1,0:T(8,128)(2,1)S(1)}, u32[]{:S(2)}, u32[]{:S(2)}) collective-permute-start(bf16[192,1024]{1,0:T(8,128)(2,1)S(1)} %feed_other.1), channel_id=1, source_target_pairs={{0,8},{8,0},{16,24},{24,16},{1,9},{9,1},{17,25},{25,17},{2,10},{10... | collective-permute-start | bytes 1179656 | tf_op jit(solution)/shard_map/ppermute | solution.py:385
  64.8 13.7 %copy-start.5 = (bf16[1024,128]{1,0:T(8,128)(2,1)S(1)}, bf16[1024,128]{1,0:T(8,128)(2,1)}, u32[]{:S(2)}) copy-start(bf16[1024,128]{1,0:T(8,128)(2,1)} %w_proj.1) | copy-start | bytes 786436
  64.8 13.7 %copy-start.9 = (f32[1024]{0:T(1024)S(1)}, f32[1024]{0:T(1024)}, u32[]{:S(2)}) copy-start(f32[1024]{0:T(1024)} %param.20) | copy-start | bytes 12292
  71.2 21.9 %copy-start.10 = (s32[64]{0:T(128)S(1)}, s32[64]{0:T(128)}, u32[]{:S(2)}) copy-start(s32[64]{0:T(128)} %lengths.1) | copy-start | bytes 772
  71.3 7.2 %collective-permute-start.15 = (bf16[96,1024]{1,0:T(8,128)(2,1)S(1)}, bf16[96,1024]{1,0:T(8,128)(2,1)S(1)}, u32[]{:S(2)}, u32[]{:S(2)}) collective-permute-start(bf16[96,1024]{1,0:T(8,128)(2,1)S(1)} %add_convert_fusion), channel_id=1, source_target_pairs={{0,16},{8,24},{16,0},{24,8},{1,17},{9,25},{17,1},{25,9},{2,18},{10... | collective-permute-start | bytes 589832 | tf_op jit(solution)/shard_map/ppermute | solution.py:385
  79.7 13.4 %all-to-all-start.1 = ((bf16[8,96,128]{2,1,0:T(8,128)(2,1)}), bf16[8,96,128]{2,1,0:T(8,128)(2,1)S(1)}, u32[]{:S(2)}, u32[]{:S(2)}) async-start(bf16[8,96,128]{2,1,0:T(8,128)(2,1)} %project.1), calls=%async_computation.1 | async-start | bytes 393216 | tf_op jit(solution)/shard_map/all_to_all | solution.py:471
  86.1 3.8 %collective-permute-start.16 = (bf16[96,128]{1,0:T(8,128)(2,1)S(1)}, bf16[96,128]{1,0:T(8,128)(2,1)S(1)}, u32[]{:S(2)}, u32[]{:S(2)}) collective-permute-start(bf16[96,128]{1,0:T(8,128)(2,1)S(1)} %slice_bitcast_fusion.2), channel_id=1, source_target_pairs={{0,16},{8,24},{16,0},{24,8},{1,17},{9,25},{17,1},{25,9},{2,18},{10... | collective-permute-start | bytes 73736 | tf_op jit(solution)/shard_map/ppermute | solution.py:385
  89.9 23.3 %collective-permute-start.17 = (bf16[192,128]{1,0:T(8,128)(2,1)S(1)}, bf16[192,128]{1,0:T(8,128)(2,1)S(1)}, u32[]{:S(2)}, u32[]{:S(2)}) collective-permute-start(bf16[192,128]{1,0:T(8,128)(2,1)S(1)} %maximum_select_fusion.1), channel_id=1, source_target_pairs={{0,8},{8,0},{16,24},{24,16},{1,9},{9,1},{17,25},{25,17},{2,10},{10... | collective-permute-start | bytes 147464 | tf_op jit(solution)/shard_map/ppermute | solution.py:385
  93.1 2.2 %copy-start.1 = (bf16[64,256,128]{2,1,0:T(8,128)(2,1)S(1)}, bf16[64,256,128]{2,1,0:T(8,128)(2,1)}, u32[]{:S(2)}) copy-start(bf16[64,256,128]{2,1,0:T(8,128)(2,1)} %docs.1) | copy-start | bytes 12582916
  103.2 17.1 %all-to-all-start.2 = ((f32[32,1,24]{2,1,0:T(1,128)}), f32[32,1,24]{2,1,0:T(1,128)S(1)}, u32[]{:S(2)}, u32[]{:S(2)}) async-start(f32[32,1,24]{2,1,0:T(1,128)} %bitcast.16), calls=%async_computation.2 | async-start | bytes 32768 | tf_op jit(solution)/shard_map/all_to_all | solution.py:493

commit v2 on v1

--- a/solution.py
+++ b/solution.py
@@ -152,115 +152,177 @@
 
 LANES = 128
 MIB = 1 << 20
+PREP_UNROLL = 4
+ATT_UNROLL = 4
 
 
 def full_specs(count):
     return [pl.BlockSpec(memory_space=pltpu.VMEM)] * count
 
 
-def params():
-    return pltpu.CompilerParams(vmem_limit_bytes=48 * MIB)
-
-
-def attend_kernel(
-    krow, vrow, qkv, relq, relk, k_zero, k_one, k_two, k_three, v_zero, v_one, att, k_all, v_all
-):
-    width = att.shape[1]
+def params(mib):
+    return pltpu.CompilerParams(vmem_limit_bytes=mib * MIB)
+
+
+def by_head(values):
+    head_of = lax.broadcasted_iota(jnp.int32, values.shape, 1) // HD
+    heads = values.shape[1] // HD
+    zero = jnp.zeros_like(values)
+    return jnp.concatenate([jnp.where(head_of == h, values, zero) for h in range(heads)], axis=0)
+
+
+def times_rows(left, right):
+    return lax.dot_general(left, right, (((1,), (1,)), ((), ())), preferred_element_type=jnp.float32)
+
+
+def key_terms(keys, rel_q_heads, first):
+    key_rel = times_rows(keys, rel_q_heads)
+    slot = lax.broadcasted_iota(jnp.int32, (keys.shape[0], LANES), 1) // QLEN
+    turned = None
+    for h in range(rel_q_heads.shape[0] // LANES):
+        shift = (LANES - PLEN - QLEN + first + h * QLEN) % LANES
+        rolled = pltpu.roll(
+            key_rel[:, h * LANES : (h + 1) * LANES], shift, 1, stride=1, stride_axis=0
+        )
+        turned = rolled if turned is None else jnp.where(slot == h, rolled, turned)
+    return turned
+
+
+def prepare_kernel(tokens, weight, rel_rows, qkv, base, rel_q_heads):
+    width = weight.shape[1] // 3
     heads = width // HD
-    for place, piece in enumerate((k_zero, k_one, k_two, k_three)):
-        k_all[place * piece.shape[0] : (place + 1) * piece.shape[0], :] = piece[...]
-    for place, piece in enumerate((v_zero, v_one)):
-        v_all[place * piece.shape[0] : (place + 1) * piece.shape[0], :] = piece[...]
-    zero = jnp.bfloat16(0)
-    turn = (
-        lax.broadcasted_iota(jnp.int32, (LANES, LANES), 0)
-        + lax.broadcasted_iota(jnp.int32, (LANES, LANES), 1)
-        == LANES - 1
-    )
-    flip = jnp.where(turn, 1.0, 0.0).astype(jnp.bfloat16)
-    rel_k = jnp.dot(flip, relk[...], preferred_element_type=jnp.float32).astype(jnp.bfloat16)
-    rel_q = jnp.dot(flip, relq[...], preferred_element_type=jnp.float32).astype(jnp.bfloat16)
-    head_of = lax.broadcasted_iota(jnp.int32, (LANES, width), 1) // HD
-    rel_q_heads = jnp.concatenate([jnp.where(head_of == h, rel_q, zero) for h in range(heads)], axis=0)
-    small_head = lax.broadcasted_iota(jnp.int32, (QLEN, width), 1) // HD
-    slot = lax.broadcasted_iota(jnp.int32, (LANES, LANES), 1) // QLEN
+    qkv[...] = jnp.dot(tokens[...], weight[...], preferred_element_type=jnp.float32).astype(
+        jnp.bfloat16
+    )
+    rel = jnp.dot(
+        rel_rows[...], weight[:, : 2 * width], preferred_element_type=jnp.float32
+    ).astype(jnp.bfloat16)
+    count = rel_rows.shape[0]
+    both = lax.broadcasted_iota(jnp.int32, (LANES, count), 0) + lax.broadcasted_iota(
+        jnp.int32, (LANES, count), 1
+    )
+    flip_q = jnp.where(both == LANES, 1.0, 0.0).astype(jnp.bfloat16)
+    flip_k = jnp.where(both == LANES + PLEN - 1, 1.0, 0.0).astype(jnp.bfloat16)
+    rel_q = jnp.dot(flip_q, rel[:, :width], preferred_element_type=jnp.float32)
+    rel_k = jnp.dot(flip_k, rel[:, width:], preferred_element_type=jnp.float32)
+    rel_k = rel_k.astype(jnp.bfloat16)
+    rel_q_heads[...] = by_head(rel_q.astype(jnp.bfloat16))
     live = lax.broadcasted_iota(jnp.int32, (heads * QLEN, LANES), 1) < PLEN + QLEN
-    padding = jnp.zeros((LANES - PLEN - QLEN, width), jnp.bfloat16)
+    above = jnp.zeros((PLEN, width), jnp.bfloat16)
+    below = jnp.zeros((LANES - PLEN - QLEN, width), jnp.bfloat16)
+    above_terms = jnp.zeros((PLEN, LANES), jnp.float32)
+    below_terms = jnp.zeros((LANES - PLEN - QLEN, LANES), jnp.float32)
     scale = 1.0 / math.sqrt(3 * HD)
 
     def one_request(r, carry):
         rows = pl.ds(pl.multiple_of(r * QLEN, QLEN), QLEN)
-        q = qkv[rows, 0:width]
-        k_own = qkv[rows, width : 2 * width]
-        v_own = qkv[rows, 2 * width : 3 * width]
-        k_group = k_all[pl.ds(pl.multiple_of(krow[r], PLEN), PLEN), :]
-        v_group = v_all[pl.ds(pl.multiple_of(vrow[r], PLEN), PLEN), :]
-        keys = jnp.concatenate([k_group, k_own, padding], axis=0)
-        values = jnp.concatenate([v_group, v_own, padding], axis=0)
-        q_heads = jnp.concatenate([jnp.where(small_head == h, q, zero) for h in range(heads)], axis=0)
-        both = lax.dot_general(
-            q_heads,
-            jnp.concatenate([keys, rel_k], axis=0),
-            (((1,), (1,)), ((), ())),
-            preferred_element_type=jnp.float32,
-        )
-        content = both[:, :LANES]
-        query_rel = both[:, LANES:]
+        keys = qkv[rows, width : 2 * width]
+        right = jnp.concatenate([above, keys, below, rel_k], axis=0)
+        product = times_rows(by_head(qkv[rows, 0:width]), right)
+        query_rel = product[:, LANES:]
         c2p = jnp.concatenate(
             [
                 pltpu.roll(
-                    query_rel[h * QLEN : (h + 1) * QLEN], 97, 1, stride=1, stride_axis=0
+                    query_rel[h * QLEN : (h + 1) * QLEN],
+                    LANES - QLEN + 1,
+                    1,
+                    stride=1,
+                    stride_axis=0,
                 )
                 for h in range(heads)
             ],
             axis=0,
         )
-        key_rel = lax.dot_general(
-            keys, rel_q_heads, (((1,), (1,)), ((), ())), preferred_element_type=jnp.float32
-        )
-        turned = jnp.zeros((LANES, LANES), jnp.float32)
-        for h in range(heads):
-            rolled = pltpu.roll(
-                key_rel[:, h * LANES : (h + 1) * LANES],
-                (32 + h * QLEN) % LANES,
-                1,
-                stride=1,
-                stride_axis=0,
-            )
-            turned = jnp.where(slot == h, rolled, turned)
-        p2c = turned.T[: heads * QLEN]
-        logits = jnp.where(live, (content + c2p + p2c) * scale, -jnp.inf)
+        terms = key_terms(keys, rel_q_heads[...], PLEN)
+        p2c = jnp.concatenate([above_terms, terms, below_terms], axis=0).T[: heads * QLEN]
+        logits = (product[:, :LANES] + c2p + p2c) * scale
+        base[r] = jnp.where(live, logits, -jnp.inf)
+        return carry
+
+    lax.fori_loop(0, base.shape[0], one_request, 0, unroll=PREP_UNROLL)
+
+
+def prepare(tokens, weight, rel_rows):
+    rows = tokens.shape[0]
+    width = weight.shape[1] // 3
+    heads = width // HD
+    return pl.pallas_call(
+        prepare_kernel,
+        out_shape=[
+            jax.ShapeDtypeStruct((rows, 3 * width), jnp.bfloat16),
+            jax.ShapeDtypeStruct((rows // QLEN, heads * QLEN, LANES), jnp.float32),
+            jax.ShapeDtypeStruct((heads * LANES, width), jnp.bfloat16),
+        ],
+        in_specs=full_specs(3),
+        out_specs=full_specs(3),
+        compiler_params=params(12),
+        cost_estimate=pl.CostEstimate(flops=4000 * MIB, bytes_accessed=4 * MIB, transcendentals=0),
+        name="prepare",
+    )(tokens, weight, rel_rows)
+
+
+def attend_kernel(krow, qkv, base, rel_q_heads, *rest):
+    pieces, (att, cache, arrived) = rest[:-3], rest[-3:]
+    copies = [
+        pltpu.make_async_copy(piece, cache.at[at], arrived.at[at]) for at, piece in enumerate(pieces)
+    ]
+    for copy in copies:
+        copy.start()
+    for copy in copies:
+        copy.wait()
+    width = att.shape[1]
+    heads = width // HD
+    held = cache.shape[2]
+    padding = jnp.zeros((LANES - PLEN - QLEN, width), jnp.bfloat16)
+    below = jnp.zeros((LANES - PLEN, width), jnp.bfloat16)
+    below_terms = jnp.zeros((LANES - PLEN, LANES), jnp.float32)
+    small_head = lax.broadcasted_iota(jnp.int32, (QLEN, width), 1) // HD
+    scale = 1.0 / math.sqrt(3 * HD)
+
+    def one_request(r, carry):
+        rows = pl.ds(pl.multiple_of(r * QLEN, QLEN), QLEN)
+        piece = krow[r] // held
+        within = pl.ds(pl.multiple_of(krow[r] % held, PLEN), PLEN)
+        keys = cache[piece, 0, within, :]
+        content = times_rows(by_head(qkv[rows, 0:width]), jnp.concatenate([keys, below], axis=0))
+        terms = key_terms(keys, rel_q_heads[...], 0)
+        p2c = jnp.concatenate([terms, below_terms], axis=0).T[: heads * QLEN]
+        logits = base[r] + (content + p2c) * scale
         largest = jnp.max(logits, axis=1, keepdims=True)
         weights = jnp.exp(logits - largest)
         denominator = jnp.sum(weights, axis=1, keepdims=True)
+        values = jnp.concatenate(
+            [cache[piece, 1, within, :], qkv[rows, 2 * width : 3 * width], padding], axis=0
+        )
         summed = jnp.dot(weights.astype(jnp.bfloat16), values, preferred_element_type=jnp.float32)
-        summed = summed / denominator
+        summed = summed * (1.0 / denominator)
         out = summed[:QLEN]
         for h in range(1, heads):
             out = jnp.where(small_head == h, summed[h * QLEN : (h + 1) * QLEN], out)
         att[rows, :] = out.astype(jnp.bfloat16)
         return carry
 
-    lax.fori_loop(0, att.shape[0] // QLEN, one_request, 0, unroll=2)
-
-
-def attend(krow, vrow, qkv, relq, relk, k_pieces, v_pieces):
+    lax.fori_loop(0, base.shape[0], one_request, 0, unroll=ATT_UNROLL)
+
+
+def attend(krow, qkv, base, rel_q_heads, pieces):
     rows = qkv.shape[0]
     width = qkv.shape[1] // 3
-    cached = sum(piece.shape[0] for piece in v_pieces)
     return pl.pallas_call(
         attend_kernel,
         out_shape=jax.ShapeDtypeStruct((rows, width), jnp.bfloat16),
-        in_specs=[pl.BlockSpec(memory_space=pltpu.SMEM)] * 2 + full_specs(9),
+        in_specs=[pl.BlockSpec(memory_space=pltpu.SMEM)]
+        + full_specs(3)
+        + [pl.BlockSpec(memory_space=pl.ANY)] * len(pieces),
         out_specs=pl.BlockSpec(memory_space=pltpu.VMEM),
         scratch_shapes=[
-            pltpu.VMEM((cached, width), jnp.bfloat16),
-            pltpu.VMEM((cached, width), jnp.bfloat16),
+            pltpu.VMEM((len(pieces),) + pieces[0].shape, jnp.bfloat16),
+            pltpu.SemaphoreType.DMA((len(pieces),)),
         ],
-        compiler_params=params(),
-        cost_estimate=pl.CostEstimate(flops=400 * MIB, bytes_accessed=2 * MIB, transcendentals=0),
+        compiler_params=params(12),
+        cost_estimate=pl.CostEstimate(flops=2000 * MIB, bytes_accessed=2 * MIB, transcendentals=0),
         name="attend",
-    )(krow, vrow, qkv, relq, relk, *k_pieces, *v_pieces)
+    )(krow, qkv, base, rel_q_heads, *pieces)
 
 
 def norm_rows(values, gain):
@@ -294,10 +356,18 @@
 
 def feed_own_kernel(start, a0, a1, a2, a3, w0, w1, w2, w3, tokens, gain, w_up, w_down, out, own):
     pieces, weights = (a0, a1, a2, a3), (w0, w1, w2, w3)
-    _, total = feed_rows(start[0], out.shape[0], pieces, weights, tokens, gain, w_up, w_down)
-    out[...] = total
-    hidden, total = feed_rows(start[1], own.shape[0], pieces, weights, tokens, gain, w_up, w_down)
-    own[...] = hidden.astype(jnp.float32) + total
+    count = out.shape[0]
+    hidden, total = feed_rows(start[0], 2 * count, pieces, weights, tokens, gain, w_up, w_down)
+
+    @pl.when(start[1] == 0)
+    def first():
+        out[...] = total[count:]
+        own[...] = hidden[:count].astype(jnp.float32) + total[:count]
+
+    @pl.when(start[1] != 0)
+    def second():
+        out[...] = total[:count]
+        own[...] = hidden[count:].astype(jnp.float32) + total[count:]
 
 
 def feed(kernel, start, pieces, weights, tokens, gain, w_up, w_down, outs, name):
@@ -306,7 +376,7 @@
         out_shape=outs,
         in_specs=[pl.BlockSpec(memory_space=pltpu.SMEM)] + full_specs(12),
         out_specs=full_specs(len(outs)),
-        compiler_params=params(),
+        compiler_params=params(20),
         cost_estimate=pl.CostEstimate(flops=1600 * MIB, bytes_accessed=6 * MIB, transcendentals=0),
         name=name,
     )(start, *pieces, *weights, tokens, gain, w_up, w_down)
@@ -323,14 +393,10 @@
 
 
 def score_kernel(slots, count, lengths, queries, docs, out):
-    lanes = out.shape[1]
-    flat = (
-        lax.broadcasted_iota(jnp.int32, out.shape, 0) * lanes
-        + lax.broadcasted_iota(jnp.int32, out.shape, 1)
-    )
-    slots_doc = docs.shape[1]
-    position = lax.broadcasted_iota(jnp.int32, (QLEN, slots_doc), 1)
-    unroll = 4
+    shape = (8, LANES)
+    flat = lax.broadcasted_iota(jnp.int32, shape, 0) * LANES + lax.broadcasted_iota(jnp.int32, shape, 1)
+    position = lax.broadcasted_iota(jnp.int32, (QLEN, docs.shape[1]), 1)
+    unroll = 16
 
     def some(i, totals):
         for u in range(unroll):
@@ -348,9 +414,28 @@
             totals = jnp.where(flat == entry, total, totals)
         return totals
 
-    out[...] = lax.fori_loop(
-        0, (count[0] + unroll - 1) // unroll, some, jnp.zeros(out.shape, jnp.float32)
-    )
+    totals = lax.fori_loop(
+        0, (count[0] + unroll - 1) // unroll, some, jnp.zeros(shape, jnp.float32)
+    )
+    for o in range(out.shape[0]):
+        row = jnp.broadcast_to(totals[o : o + 1], shape)
+        for h in range(out.shape[1]):
+            out[o, h] = row
+
+
+def collect_kernel(place, tiles, out):
+    n_head = tiles.shape[1]
+    cols = out.shape[1]
+    reqs = out.shape[0] // n_head
+    for h in range(n_head):
+        total = tiles[0, h]
+        for o in range(1, tiles.shape[0]):
+            total = total + tiles[o, h]
+        total = pltpu.roll(total, LANES - place[0] * (reqs * cols), 1)
+        at = (h % 2 * 2 + h // 2) * reqs
+        for r in range(reqs):
+            row = total if r == 0 else pltpu.roll(total, LANES - r * cols, 1)
+            out[at + r : at + r + 1, :] = row[:1, :cols]
 
 
 def body(
@@ -384,29 +469,16 @@
     def over_head(x, k):
         return lax.ppermute(x, "head", [(i, i ^ k) for i in range(n_head)])
 
-    keys, values = prompt_cache[0], prompt_cache[1]
-    keys_two = jnp.concatenate([keys, over_doc(keys, 1)], axis=0)
-    values_four = jnp.concatenate([values] + [over_doc(values, k) for k in (2, 4, 6)], axis=0)
-    key_pieces = [keys_two] + [over_doc(keys_two, k) for k in (2, 4, 6)]
-    value_pieces = [values_four, over_doc(values_four, 1)]
-    groups_dev = keys.shape[0] // PLEN
+    along_z = [prompt_cache] + [over_doc(prompt_cache, k) for k in (2, 4, 6)]
+    pieces = along_z + [over_doc(piece, 1) for piece in along_z]
+    held = prompt_cache.shape[1]
+    groups_dev = held // PLEN
     relative = (group_ids // groups_dev) ^ me
-    within = group_ids % groups_dev * PLEN
-    krow = relative * keys.shape[0] + within
-    vrow = (relative // 2 + relative % 2 * (n_doc // 2)) * keys.shape[0] + within
+    krow = (relative // 2 + relative % 2 * (n_doc // 2)) * held + group_ids % groups_dev * PLEN
 
     weight = w_qkv.reshape(w_qkv.shape[0], 3 * width)
-    qkv = jnp.dot(tokens, weight, preferred_element_type=jnp.float32).astype(jnp.bfloat16)
-    low_q = RELS // 2 - PLEN - QLEN + 1
-    low_k = RELS // 2 - QLEN
-    relq = jnp.dot(
-        rel_table[low_q : low_q + LANES], weight[:, :width], preferred_element_type=jnp.float32
-    ).astype(jnp.bfloat16)
-    relk = jnp.dot(
-        rel_table[low_k : low_k + LANES],
-        weight[:, width : 2 * width],
-        preferred_element_type=jnp.float32,
-    ).astype(jnp.bfloat16)
+    low = RELS // 2 - PLEN - QLEN
+    qkv, base, rel_q_heads = prepare(tokens, weight, rel_table[low : low + 2 * (PLEN + QLEN)])
 
     reqs = candidates.shape[0] // n_head
     cols = candidates.shape[1]
@@ -430,7 +502,7 @@
     out_one = over_head(w_out, 2)
     out_pieces = [w_out, over_head(w_out, 1), out_one, over_head(out_one, 1)]
 
-    att = attend(krow, vrow, qkv, relq, relk, key_pieces, value_pieces)
+    att = attend(krow, qkv, base, rel_q_heads, pieces)
     att_y = over_head(att, 2)
     att_pieces = [att, over_head(att, 1), att_y, over_head(att_y, 1)]
 
@@ -445,9 +517,7 @@
         "feed_other",
     )[0]
     from_core = over_head(other, 1)
-    start_own = jnp.stack(
-        [own_c * half + (1 - own_y) * quarter, own_c * half + own_y * quarter]
-    ).astype(jnp.int32)
+    start_own = jnp.stack([own_c * half, own_y]).astype(jnp.int32)
     for_y, own = feed(
         feed_own_kernel,
         start_own,
@@ -465,7 +535,7 @@
         out_shape=jax.ShapeDtypeStruct((n_doc, quarter, emb), jnp.bfloat16),
         in_specs=full_specs(5),
         out_specs=full_specs(1)[0],
-        compiler_params=params(),
+        compiler_params=params(8),
         name="project",
     )(own, core_own, from_y, gain_two.reshape(1, -1), w_proj)
     queries = lax.all_to_all(vectors, "doc", 0, 0, tiled=True).reshape(n_doc * quarter, emb)
@@ -483,16 +553,22 @@
     smem = pl.BlockSpec(memory_space=pltpu.SMEM)
     rated = pl.pallas_call(
         score_kernel,
-        out_shape=jax.ShapeDtypeStruct((n_doc, LANES), jnp.float32),
+        out_shape=jax.ShapeDtypeStruct((n_doc, n_head, 8, LANES), jnp.float32),
         in_specs=[smem, smem, smem] + full_specs(2),
         out_specs=full_specs(1)[0],
-        compiler_params=params(),
+        compiler_params=params(8),
         name="rate",
     )(slots, count.reshape(1), doc_lengths, queries, doc_vectors)
-    tiles = rated[:, :block].reshape(n_doc * n_head, reqs * cols)
+    tiles = rated.reshape(n_doc * n_head * 8, LANES)
     back = lax.all_to_all(tiles, ("doc", "head"), 0, 0, tiled=True)
-    scores = jnp.sum(back.reshape(n_doc, n_head, reqs, cols), axis=0)
-    scores = scores.reshape(2, 2, reqs, cols).transpose(1, 0, 2, 3).reshape(n_head * reqs, cols)
+    scores = pl.pallas_call(
+        collect_kernel,
+        out_shape=jax.ShapeDtypeStruct(candidates.shape, jnp.float32),
+        in_specs=[smem] + full_specs(1),
+        out_specs=full_specs(1)[0],
+        compiler_params=params(4),
+        name="collect",
+    )(place.reshape(1), back.reshape(n_doc, n_head, 8, LANES))
     return (query_vectors, scores)
 
 

time: 124 us -> 109 us (0.88); the launches traced: 122 us -> 109 us
  starting transfers between devices: 40 us -> 30.7 us
  waiting for transfers between devices: 22.2 us -> 28.4 us
  matrix products: 5.54 us -> 0 us
  other arithmetic: 9.11 us -> 4.93 us
  Pallas kernels: 28.7 us -> 26.7 us
    all_to_all x1, starting transfers between devices: 9.92 us -> 2.57 us  [body(): back = lax.all_to_all(tiles, ('doc', 'head'), 0, 0, tiled=True)]
    pallas_call x2, Pallas kernels: 10.9 us -> 5.08 us  [feed(): pl.pallas_call(kernel, out_shape=outs, in_specs=[pl.BlockSpec(memory_spac...]
    dot_general x3 -> x0, matrix products: 5.54 us -> none  [the longest x1 1.96 us: body(): jnp.dot(rel_table[low_k:low_k + LANES], weight[:, width:2 * width], prefe...]
    pallas_call x1 -> x3, Pallas kernels: 7.26 us -> 12.7 us  [the longest x1 9.06 us: body(): pl.pallas_call(score_kernel, out_shape=jax.ShapeDtypeStruct((n_doc, n_hea...]
    unnamed x36 -> x43, local copies, waits for them, and re-layouts: 8.26 us -> 11.9 us
    ppermute x10, waiting for transfers between devices: 9.11 us -> 12 us  [over_head(): return lax.ppermute(x, 'head', [(i, i ^ k) for i in range(n_head)])]
    concatenate x2 -> x0, other arithmetic: 2.51 us -> none  [the longest x1 1.66 us: body(): jnp.concatenate([values] + [over_doc(values, k) for k in (2, 4, 6)], axis=0)]
    all_to_all x1, waiting for transfers between devices: 2.47 us -> 4.89 us  [body(): lax.all_to_all(vectors, 'doc', 0, 0, tiled=True)]
  transfers between devices with their start and end apart: 21 -> 20, of which waited for: 7 -> 9; matrix products, arithmetic and copies ran while one was open for 17% -> 12% of each run, Pallas kernels for 19% -> 21%
where the time goes in v2:
time: 109 us
  starting transfers between devices  30.7 us (28%)
  waiting for transfers between devices  28.4 us (26%)
  Pallas kernels  26.7 us (24%)
  local copies, waits for them, and re-layouts  17.1 us (16%)
  other arithmetic  4.93 us (5%)
    ppermute x10, waiting for transfers between devices, over_head(): return lax.ppermute(x, 'head', [(i, i ^ k) for i in range(n_head)])  12 us
    unnamed x43, local copies, waits for them, and re-layouts  11.9 us
    ppermute x7, starting transfers between devices, over_doc(): return lax.ppermute(x, 'doc', [(i, i ^ k) for i in range(n_doc)])  11.2 us
    pallas_call x1, Pallas kernels, body(): pl.pallas_call(score_kernel, out_shape=jax.ShapeDtypeStruct((n_doc, n_hea...  9.06 us
    pallas_call x1, Pallas kernels, attend(): pl.pallas_call(attend_kernel, out_shape=jax.ShapeDtypeStruct((rows, width...  7.76 us
    ppermute x10, starting transfers between devices, over_head(): return lax.ppermute(x, 'head', [(i, i ^ k) for i in range(n_head)])  7.33 us
    all_to_all x1, waiting for transfers between devices, body(): back = lax.all_to_all(tiles, ('doc', 'head'), 0, 0, tiled=True)  6.23 us
    all_to_all x1, starting transfers between devices, body(): lax.all_to_all(vectors, 'doc', 0, 0, tiled=True)  5.6 us
  transfers between devices with their start and end apart: 20, of which 9 were waited for; matrix products, arithmetic and copies ran while one was open for 12% of the time, Pallas kernels for 21%

profile of v2, /device:TPU:0, one launch (start us, length us, event | category | flops | bytes accessed | tf_op | source)
XLA Modules:
  0.0 108.9 jit_solution(5287722345687126537)
XLA Ops:
  0.6 3.1 %collective-permute-start = (bf16[2,128,256]{2,1,0:T(8,128)(2,1)}, bf16[2,128,256]{2,1,0:T(8,128)(2,1)}, u32[]{:S(2)}, u32[]{:S(2)}) collective-permute-start(bf16[2,128,256]{2,1,0:T(8,128)(2,1)} %rest_0_.1), channel_id=1, source_target_pairs={{0,2},{1,3},{2,0},{3,1},{4,6},{5,7},{6,4},{7,5},{8,10},{9,11},{10,... | collective-permute-start | bytes 393224 | tf_op jit(solution)/shard_map/ppermute | solution.py:467
  3.7 2.6 %collective-permute-start.1 = (bf16[2,128,256]{2,1,0:T(8,128)(2,1)}, bf16[2,128,256]{2,1,0:T(8,128)(2,1)}, u32[]{:S(2)}, u32[]{:S(2)}) collective-permute-start(bf16[2,128,256]{2,1,0:T(8,128)(2,1)} %rest_0_.1), channel_id=1, source_target_pairs={{0,4},{1,5},{2,6},{3,7},{4,0},{5,1},{6,2},{7,3},{8,12},{9,13},{10,... | collective-permute-start | bytes 393224 | tf_op jit(solution)/shard_map/ppermute | solution.py:467
  6.3 1.7 %collective-permute-start.3 = (bf16[2,128,256]{2,1,0:T(8,128)(2,1)}, bf16[2,128,256]{2,1,0:T(8,128)(2,1)}, u32[]{:S(2)}, u32[]{:S(2)}) collective-permute-start(bf16[2,128,256]{2,1,0:T(8,128)(2,1)} %rest_0_.1), channel_id=1, source_target_pairs={{0,1},{1,0},{2,3},{3,2},{4,5},{5,4},{6,7},{7,6},{8,9},{9,8},{10,11... | collective-permute-start | bytes 393224 | tf_op jit(solution)/shard_map/ppermute | solution.py:467
  8.0 1.5 %collective-permute-start.11 = (bf16[256,1024]{1,0:T(8,128)(2,1)}, bf16[256,1024]{1,0:T(8,128)(2,1)S(1)}, u32[]{:S(2)}, u32[]{:S(2)}) collective-permute-start(bf16[256,1024]{1,0:T(8,128)(2,1)} %w0.3), channel_id=1, source_target_pairs={{0,16},{8,24},{16,0},{24,8},{1,17},{9,25},{17,1},{25,9},{2,18},{10... | collective-permute-start | bytes 1572872 | tf_op jit(solution)/shard_map/ppermute | solution.py:470
  9.5 0.8 copy.32
  10.4 0.6 broadcast_in_dim.28
  11.0 4.0 %all-to-all-start = ((s32[32,1,24]{2,1,0:T(1,128)}), s32[32,1,24]{2,1,0:T(1,128)S(1)}, u32[]{:S(2)}, u32[]{:S(2)}) async-start(s32[32,1,24]{2,1,0:T(1,128)} %bitcast.10), calls=%async_computation | async-start | bytes 32768 | tf_op jit(solution)/shard_map/all_to_all | solution.py:487
  15.0 0.5 and_select_fusion
  15.5 0.6 iota_multiply_fusion
  16.1 2.6 %copy.30 = bf16[1024,3,256]{0,2,1:T(8,128)(2,1)} copy(bf16[1024,3,256]{2,0,1:T(8,128)(2,1)} %param.15) | data formatting | bytes 3145728 | tf_op args[1]
  18.7 1.8 %copy.31.weight = bf16[1024,768]{1,0:T(8,128)(2,1)S(1)} copy(bf16[1024,768]{0,1:T(8,128)(2,1)} %bitcast.25) | data formatting | bytes 3145728 | tf_op jit(solution)/shard_map/reshape | solution.py:479
  20.5 1.0 slice.13.rel_rows
  21.6 3.5 %prepare.1 = (bf16[384,768]{1,0:T(8,128)(2,1)S(1)}, f32[12,128,128]{2,1,0:T(8,128)S(1)}, bf16[512,256]{1,0:T(8,128)(2,1)S(1)}) custom-call(bf16[384,1024]{1,0:T(8,128)(2,1)S(1)} %copy-done.3, bf16[1024,768]{1,0:T(8,128)(2,1)S(1)} %copy.31.weight, bf16[192,1024]{1,0:T(8,128)(2,1)S(1)} %slice.13.rel_rows), custom_call_target="tpu_custom_call" | custom-call | flops 4194304000 | bytes 4194304 | tf_op jit(solution)/shard_map/prepare/pallas_call | solution.py:249
  25.1 0.9 copy-done.10
  26.0 0.8 copy-done.12
  26.9 0.7 copy-done.14
  27.9 1.8 %collective-permute-start.4 = (bf16[2,128,256]{2,1,0:T(8,128)(2,1)}, bf16[2,128,256]{2,1,0:T(8,128)(2,1)S(1)}, u32[]{:S(2)}, u32[]{:S(2)}) collective-permute-start(bf16[2,128,256]{2,1,0:T(8,128)(2,1)} %collective-permute-done.rest_1_), channel_id=1, source_target_pairs={{0,1},{1,0},{2,3},{3,2},{4,5},{5,4},{6,7},{7,6},{8,9},{9,8},{10,11... | collective-permute-start | bytes 393224 | tf_op jit(solution)/shard_map/ppermute | solution.py:467
  30.0 1.8 %collective-permute-start.6 = (bf16[2,128,256]{2,1,0:T(8,128)(2,1)}, bf16[2,128,256]{2,1,0:T(8,128)(2,1)S(1)}, u32[]{:S(2)}, u32[]{:S(2)}) collective-permute-start(bf16[2,128,256]{2,1,0:T(8,128)(2,1)} %collective-permute-done.2.rest_3_), channel_id=1, source_target_pairs={{0,1},{1,0},{2,3},{3,2},{4,5},{5,4},{6,7},{7,6},{8,9},{9,8},{10,11... | collective-permute-start | bytes 393224 | tf_op jit(solution)/shard_map/ppermute | solution.py:467
  31.8 0.5 broadcast.274
  32.3 0.7 reduce.8
  34.5 2.8 %collective-permute-done.5.rest_6_ = bf16[2,128,256]{2,1,0:T(8,128)(2,1)S(1)} collective-permute-done((bf16[2,128,256]{2,1,0:T(8,128)(2,1)}, bf16[2,128,256]{2,1,0:T(8,128)(2,1)S(1)}, u32[]{:S(2)}, u32[]{:S(2)}) %collective-permute-start.5) | collective-permute-done | bytes 131104 | tf_op jit(solution)/shard_map/ppermute | solution.py:467
  37.4 2.1 %collective-permute-done.6.rest_7_ = bf16[2,128,256]{2,1,0:T(8,128)(2,1)S(1)} collective-permute-done((bf16[2,128,256]{2,1,0:T(8,128)(2,1)}, bf16[2,128,256]{2,1,0:T(8,128)(2,1)S(1)}, u32[]{:S(2)}, u32[]{:S(2)}) %collective-permute-start.6) | collective-permute-done | bytes 131104 | tf_op jit(solution)/shard_map/ppermute | solution.py:467
  39.5 1.1 %copy-done.11 = f32[12,128,128]{2,1,0:T(8,128)S(1)} copy-done((f32[12,128,128]{2,1,0:T(8,128)S(1)}, f32[12,128,128]{2,1,0:T(8,128)}, u32[]{:S(2)}) %copy-start.11) | copy-done | bytes 786456
  40.6 1.1 copy-done.13
  41.7 0.9 copy-done.15
  42.7 7.8 %attend.1.a0 = bf16[384,256]{1,0:T(8,128)(2,1)S(1)} custom-call(s32[12]{0:T(128)S(1)} %fusion.18.krow, bf16[384,768]{1,0:T(8,128)(2,1)S(1)} %copy-done.13, f32[12,128,128]{2,1,0:T(8,128)S(1)} %copy-done.11, bf16[512,256]{1,0:T(8,128)(2,1)S(1)} %copy-done.15, bf16[2,128,256]{2,1,0:T(8,128)(2,1)S(1)} %copy-done.9, ...), custom_call_target="tpu_custom_call" | custom-call | flops 2097152000 | bytes 2097152 | tf_op jit(solution)/shard_map/attend/pallas_call | solution.py:311
  50.4 1.7 %collective-permute-start.8 = (bf16[384,256]{1,0:T(8,128)(2,1)S(1)}, bf16[384,256]{1,0:T(8,128)(2,1)S(1)}, u32[]{:S(2)}, u32[]{:S(2)}) collective-permute-start(bf16[384,256]{1,0:T(8,128)(2,1)S(1)} %attend.1.a0), channel_id=1, source_target_pairs={{0,16},{8,24},{16,0},{24,8},{1,17},{9,25},{17,1},{25,9},{2,18},{10... | collective-permute-start | bytes 589832 | tf_op jit(solution)/shard_map/ppermute | solution.py:470
  52.2 4.6 %collective-permute-done.8.a2 = bf16[384,256]{1,0:T(8,128)(2,1)S(1)} collective-permute-done((bf16[384,256]{1,0:T(8,128)(2,1)S(1)}, bf16[384,256]{1,0:T(8,128)(2,1)S(1)}, u32[]{:S(2)}, u32[]{:S(2)}) %collective-permute-start.8) | collective-permute-done | bytes 196640 | tf_op jit(solution)/shard_map/ppermute | solution.py:470
  56.8 1.4 %collective-permute-done.9.a3 = bf16[384,256]{1,0:T(8,128)(2,1)S(1)} collective-permute-done((bf16[384,256]{1,0:T(8,128)(2,1)S(1)}, bf16[384,256]{1,0:T(8,128)(2,1)S(1)}, u32[]{:S(2)}, u32[]{:S(2)}) %collective-permute-start.9) | collective-permute-done | bytes 196640 | tf_op jit(solution)/shard_map/ppermute | solution.py:470
  58.2 2.2 %feed_other.1 = bf16[192,1024]{1,0:T(8,128)(2,1)S(1)} custom-call(s32[1]{0:T(128)} %bitcast.4.start, bf16[384,256]{1,0:T(8,128)(2,1)S(1)} %attend.1.a0, bf16[384,256]{1,0:T(8,128)(2,1)S(1)} %collective-permute-done.7.a1, bf16[384,256]{1,0:T(8,128)(2,1)S(1)} %collective-permute-done.8.a2, bf16[384,256]{1,0:T(8,128)(2,1)S(1)} %collective-permute-done.9.a3, ...), custom_call_target="tpu_custom_call" | custom-call | flops 1677721600 | bytes 6291456 | tf_op jit(solution)/shard_map/feed_other/pallas_call | solution.py:374
  60.7 0.5 select_reduce_fusion
  61.2 2.8 %feed_own.1 = (f32[96,1024]{1,0:T(8,128)S(1)}, f32[96,1024]{1,0:T(8,128)S(1)}) custom-call(s32[2]{0:T(128)S(1)} %pad_add_fusion.start, bf16[384,256]{1,0:T(8,128)(2,1)S(1)} %attend.1.a0, bf16[384,256]{1,0:T(8,128)(2,1)S(1)} %collective-permute-done.7.a1, bf16[384,256]{1,0:T(8,128)(2,1)S(1)} %collective-permute-done.8.a2, ...), custom_call_target="tpu_custom_call" | custom-call | flops 1677721600 | bytes 6291456 | tf_op jit(solution)/shard_map/feed_own/pallas_call | solution.py:374
  64.1 1.6 %collective-permute-start.14 = (bf16[96,1024]{1,0:T(8,128)(2,1)S(1)}, bf16[96,1024]{1,0:T(8,128)(2,1)S(1)}, u32[]{:S(2)}, u32[]{:S(2)}) collective-permute-start(bf16[96,1024]{1,0:T(8,128)(2,1)S(1)} %add_convert_fusion), channel_id=1, source_target_pairs={{0,16},{8,24},{16,0},{24,8},{1,17},{9,25},{17,1},{25,9},{2,18},{10... | collective-permute-start | bytes 589832 | tf_op jit(solution)/shard_map/ppermute | solution.py:470
  65.8 0.6 convert_reduce_fusion
  66.4 4.9 %collective-permute-done.14.from_y = bf16[96,1024]{1,0:T(8,128)(2,1)S(1)} collective-permute-done((bf16[96,1024]{1,0:T(8,128)(2,1)S(1)}, bf16[96,1024]{1,0:T(8,128)(2,1)S(1)}, u32[]{:S(2)}, u32[]{:S(2)}) %collective-permute-start.14) | collective-permute-done | bytes 196640 | tf_op jit(solution)/shard_map/ppermute | solution.py:470
  71.4 1.2 %project.1 = bf16[8,96,128]{2,1,0:T(8,128)(2,1)} custom-call(f32[96,1024]{1,0:T(8,128)S(1)} %get-tuple-element.10.own, bf16[96,1024]{1,0:T(8,128)(2,1)S(1)} %constant_dynamic-slice_fusion.from_core, bf16[96,1024]{1,0:T(8,128)(2,1)S(1)} %collective-permute-done.14.from_y, f32[1,1024]{1,0:T(1,128)S(1)} %bitcast.24, bf16[1024,128]{1,0:T(8,128)(2,1)S(1)} %copy-done.5), custom_call_target="tpu_custom_call" | custom-call | tf_op jit(solution)/shard_map/project/pallas_call | solution.py:533
  72.6 5.6 %all-to-all-start.1 = ((bf16[8,96,128]{2,1,0:T(8,128)(2,1)}), bf16[8,96,128]{2,1,0:T(8,128)(2,1)S(1)}, u32[]{:S(2)}, u32[]{:S(2)}) async-start(bf16[8,96,128]{2,1,0:T(8,128)(2,1)} %project.1), calls=%async_computation.1 | async-start | bytes 393216 | tf_op jit(solution)/shard_map/all_to_all | solution.py:541
  78.2 0.7 slice_bitcast_fusion
  78.9 1.5 %collective-permute-start.15 = (bf16[96,128]{1,0:T(8,128)(2,1)S(1)}, bf16[96,128]{1,0:T(8,128)(2,1)S(1)}, u32[]{:S(2)}, u32[]{:S(2)}) collective-permute-start(bf16[96,128]{1,0:T(8,128)(2,1)S(1)} %slice_bitcast_fusion), channel_id=1, source_target_pairs={{0,16},{8,24},{16,0},{24,8},{1,17},{9,25},{17,1},{25,9},{2,18},{10... | collective-permute-start | bytes 73736 | tf_op jit(solution)/shard_map/ppermute | solution.py:470
  80.4 0.6 fusion.9.slots
  81.1 4.9 %all-to-all-done.1 = bf16[8,96,128]{2,1,0:T(8,128)(2,1)S(1)} async-done(((bf16[8,96,128]{2,1,0:T(8,128)(2,1)}), bf16[8,96,128]{2,1,0:T(8,128)(2,1)S(1)}, u32[]{:S(2)}, u32[]{:S(2)}) %all-to-all-start.1) | async-done | bytes 196640 | tf_op jit(solution)/shard_map/all_to_all | solution.py:541
  86.0 2.2 %copy-done.2 = bf16[64,256,128]{2,1,0:T(8,128)(2,1)S(1)} copy-done((bf16[64,256,128]{2,1,0:T(8,128)(2,1)S(1)}, bf16[64,256,128]{2,1,0:T(8,128)(2,1)}, u32[]{:S(2)}) %copy-start.2) | copy-done | bytes 4194328
  88.2 9.1 %rate.1 = f32[8,4,8,128]{3,2,1,0:T(8,128)} custom-call(s32[768]{0:T(1024)S(1)} %fusion.9.slots, s32[1]{0:T(128)} %bitcast.13.count, s32[64]{0:T(128)S(1)} %copy-done.8, bf16[768,128]{1,0:T(8,128)(2,1)S(1)} %bitcast.20, bf16[64,256,128]{2,1,0:T(8,128)(2,1)S(1)} %copy-done.2), custom_call_target="tpu_custom_call" | custom-call | tf_op jit(solution)/shard_map/rate/pallas_call | solution.py:554
  97.2 2.6 %all-to-all-start.2 = ((f32[32,8,128]{2,1,0:T(8,128)}), f32[32,8,128]{2,1,0:T(8,128)S(1)}, u32[]{:S(2)}, u32[]{:S(2)}) async-start(f32[32,8,128]{2,1,0:T(8,128)} %bitcast.15), calls=%async_computation.2 | async-start | bytes 262144 | tf_op jit(solution)/shard_map/all_to_all | solution.py:563
  100.0 1.1 %collective-permute-done.16 = bf16[192,128]{1,0:T(8,128)(2,1)S(1)} collective-permute-done((bf16[192,128]{1,0:T(8,128)(2,1)S(1)}, bf16[192,128]{1,0:T(8,128)(2,1)S(1)}, u32[]{:S(2)}, u32[]{:S(2)}) %collective-permute-start.16) | collective-permute-done | bytes 49184 | tf_op jit(solution)/shard_map/ppermute | solution.py:470
  101.1 0.7 maximum_select_fusion
  101.8 6.2 %all-to-all-done.2 = f32[32,8,128]{2,1,0:T(8,128)S(1)} async-done(((f32[32,8,128]{2,1,0:T(8,128)}), f32[32,8,128]{2,1,0:T(8,128)S(1)}, u32[]{:S(2)}, u32[]{:S(2)}) %all-to-all-start.2) | async-done | bytes 131104 | tf_op jit(solution)/shard_map/all_to_all | solution.py:563
  108.2 0.7 copy.34
  (73 shorter events, 3.0 us)
Async XLA Ops:
  0.6 27.3 %collective-permute-start = (bf16[2,128,256]{2,1,0:T(8,128)(2,1)}, bf16[2,128,256]{2,1,0:T(8,128)(2,1)}, u32[]{:S(2)}, u32[]{:S(2)}) collective-permute-start(bf16[2,128,256]{2,1,0:T(8,128)(2,1)} %rest_0_.1), channel_id=1, source_target_pairs={{0,2},{1,3},{2,0},{3,1},{4,6},{5,7},{6,4},{7,5},{8,10},{9,11},{10,... | collective-permute-start | bytes 393224 | tf_op jit(solution)/shard_map/ppermute | solution.py:467
  3.7 26.1 %collective-permute-start.1 = (bf16[2,128,256]{2,1,0:T(8,128)(2,1)}, bf16[2,128,256]{2,1,0:T(8,128)(2,1)}, u32[]{:S(2)}, u32[]{:S(2)}) collective-permute-start(bf16[2,128,256]{2,1,0:T(8,128)(2,1)} %rest_0_.1), channel_id=1, source_target_pairs={{0,4},{1,5},{2,6},{3,7},{4,0},{5,1},{6,2},{7,3},{8,12},{9,13},{10,... | collective-permute-start | bytes 393224 | tf_op jit(solution)/shard_map/ppermute | solution.py:467
  6.3 23.7 %collective-permute-start.2 = (bf16[2,128,256]{2,1,0:T(8,128)(2,1)}, bf16[2,128,256]{2,1,0:T(8,128)(2,1)}, u32[]{:S(2)}, u32[]{:S(2)}) collective-permute-start(bf16[2,128,256]{2,1,0:T(8,128)(2,1)} %rest_0_.1), channel_id=1, source_target_pairs={{0,6},{1,7},{2,4},{3,5},{4,2},{5,3},{6,0},{7,1},{8,14},{9,15},{10,... | collective-permute-start | bytes 393224 | tf_op jit(solution)/shard_map/ppermute | solution.py:467
  6.3 27.3 %collective-permute-start.3 = (bf16[2,128,256]{2,1,0:T(8,128)(2,1)}, bf16[2,128,256]{2,1,0:T(8,128)(2,1)}, u32[]{:S(2)}, u32[]{:S(2)}) collective-permute-start(bf16[2,128,256]{2,1,0:T(8,128)(2,1)} %rest_0_.1), channel_id=1, source_target_pairs={{0,1},{1,0},{2,3},{3,2},{4,5},{5,4},{6,7},{7,6},{8,9},{9,8},{10,11... | collective-permute-start | bytes 393224 | tf_op jit(solution)/shard_map/ppermute | solution.py:467
  8.0 25.7 %collective-permute-start.11 = (bf16[256,1024]{1,0:T(8,128)(2,1)}, bf16[256,1024]{1,0:T(8,128)(2,1)S(1)}, u32[]{:S(2)}, u32[]{:S(2)}) collective-permute-start(bf16[256,1024]{1,0:T(8,128)(2,1)} %w0.3), channel_id=1, source_target_pairs={{0,16},{8,24},{16,0},{24,8},{1,17},{9,25},{17,1},{25,9},{2,18},{10... | collective-permute-start | bytes 1572872 | tf_op jit(solution)/shard_map/ppermute | solution.py:470
  11.0 16.8 %all-to-all-start = ((s32[32,1,24]{2,1,0:T(1,128)}), s32[32,1,24]{2,1,0:T(1,128)S(1)}, u32[]{:S(2)}, u32[]{:S(2)}) async-start(s32[32,1,24]{2,1,0:T(1,128)} %bitcast.10), calls=%async_computation | async-start | bytes 32768 | tf_op jit(solution)/shard_map/all_to_all | solution.py:487
  18.7 2.8 %copy-start.3 = (bf16[384,1024]{1,0:T(8,128)(2,1)S(1)}, bf16[384,1024]{1,0:T(8,128)(2,1)}, u32[]{:S(2)}) copy-start(bf16[384,1024]{1,0:T(8,128)(2,1)} %tokens.5) | copy-start | bytes 2359300
  21.5 6.0 %copy-start.16 = (s32[96]{0:T(128)S(1)}, s32[96]{0:T(128)}, u32[]{:S(2)}) copy-start(s32[96]{0:T(128)} %and_select_fusion) | copy-start | bytes 1156
  21.6 6.0 %copy-start.17 = (s32[8]{0:T(128)S(1)}, s32[8]{0:T(128)}, u32[]{:S(2)}) copy-start(s32[8]{0:T(128)} %get-tuple-element.20) | copy-start | bytes 100
  21.6 6.0 %copy-start.18 = (s32[8]{0:T(128)S(1)}, s32[8]{0:T(128)}, u32[]{:S(2)}) copy-start(s32[8]{0:T(128)} %get-tuple-element.21) | copy-start | bytes 100
  21.6 6.1 %copy-start.19 = (s32[12]{0:T(128)S(1)}, s32[12]{0:T(128)}, u32[]{:S(2)}) copy-start(s32[12]{0:T(128)} %param.26) | copy-start | bytes 148
  21.6 12.0 %copy-start.4 = (bf16[256,1024]{1,0:T(8,128)(2,1)S(1)}, bf16[256,1024]{1,0:T(8,128)(2,1)}, u32[]{:S(2)}) copy-start(bf16[256,1024]{1,0:T(8,128)(2,1)} %w0.3) | copy-start | bytes 1572868
  21.6 17.9 %copy-start.9 = (bf16[2,128,256]{2,1,0:T(8,128)(2,1)S(1)}, bf16[2,128,256]{2,1,0:T(8,128)(2,1)}, u32[]{:S(2)}) copy-start(bf16[2,128,256]{2,1,0:T(8,128)(2,1)} %rest_0_.1) | copy-start | bytes 393220
  25.1 0.9 copy-start.10
  26.0 0.8 copy-start.12
  26.9 0.7 copy-start.14
  27.9 6.6 %collective-permute-start.4 = (bf16[2,128,256]{2,1,0:T(8,128)(2,1)}, bf16[2,128,256]{2,1,0:T(8,128)(2,1)S(1)}, u32[]{:S(2)}, u32[]{:S(2)}) collective-permute-start(bf16[2,128,256]{2,1,0:T(8,128)(2,1)} %collective-permute-done.rest_1_), channel_id=1, source_target_pairs={{0,1},{1,0},{2,3},{3,2},{4,5},{5,4},{6,7},{7,6},{8,9},{9,8},{10,11... | collective-permute-start | bytes 393224 | tf_op jit(solution)/shard_map/ppermute | solution.py:467
  29.8 7.6 %collective-permute-start.5 = (bf16[2,128,256]{2,1,0:T(8,128)(2,1)}, bf16[2,128,256]{2,1,0:T(8,128)(2,1)S(1)}, u32[]{:S(2)}, u32[]{:S(2)}) collective-permute-start(bf16[2,128,256]{2,1,0:T(8,128)(2,1)} %collective-permute-done.1.rest_2_), channel_id=1, source_target_pairs={{0,1},{1,0},{2,3},{3,2},{4,5},{5,4},{6,7},{7,6},{8,9},{9,8},{10,11... | collective-permute-start | bytes 393224 | tf_op jit(solution)/shard_map/ppermute | solution.py:467
  30.0 9.4 %collective-permute-start.6 = (bf16[2,128,256]{2,1,0:T(8,128)(2,1)}, bf16[2,128,256]{2,1,0:T(8,128)(2,1)S(1)}, u32[]{:S(2)}, u32[]{:S(2)}) collective-permute-start(bf16[2,128,256]{2,1,0:T(8,128)(2,1)} %collective-permute-done.2.rest_3_), channel_id=1, source_target_pairs={{0,1},{1,0},{2,3},{3,2},{4,5},{5,4},{6,7},{7,6},{8,9},{9,8},{10,11... | collective-permute-start | bytes 393224 | tf_op jit(solution)/shard_map/ppermute | solution.py:467
  33.6 23.2 %collective-permute-start.10 = (bf16[256,1024]{1,0:T(8,128)(2,1)S(1)}, bf16[256,1024]{1,0:T(8,128)(2,1)S(1)}, u32[]{:S(2)}, u32[]{:S(2)}) collective-permute-start(bf16[256,1024]{1,0:T(8,128)(2,1)S(1)} %copy-done.4), channel_id=1, source_target_pairs={{0,8},{8,0},{16,24},{24,16},{1,9},{9,1},{17,25},{25,17},{2,10},{10... | collective-permute-start | bytes 1572872 | tf_op jit(solution)/shard_map/ppermute | solution.py:470
  33.7 24.5 %collective-permute-start.12 = (bf16[256,1024]{1,0:T(8,128)(2,1)S(1)}, bf16[256,1024]{1,0:T(8,128)(2,1)S(1)}, u32[]{:S(2)}, u32[]{:S(2)}) collective-permute-start(bf16[256,1024]{1,0:T(8,128)(2,1)S(1)} %collective-permute-done.11.w2), channel_id=1, source_target_pairs={{0,8},{8,0},{16,24},{24,16},{1,9},{9,1},{17,25},{25,17},{2,10},{10... | collective-permute-start | bytes 1572872 | tf_op jit(solution)/shard_map/ppermute | solution.py:470
  39.5 1.1 %copy-start.11 = (f32[12,128,128]{2,1,0:T(8,128)S(1)}, f32[12,128,128]{2,1,0:T(8,128)}, u32[]{:S(2)}) copy-start(f32[12,128,128]{2,1,0:T(8,128)} %copy-done.10) | copy-start | bytes 2359300
  40.6 1.1 copy-start.13
  41.7 0.9 copy-start.15
  42.6 15.5 %copy-start = (bf16[1024,1024]{1,0:T(8,128)(2,1)S(1)}, bf16[1024,1024]{1,0:T(8,128)(2,1)}, u32[]{:S(2)}) copy-start(bf16[1024,1024]{1,0:T(8,128)(2,1)} %w_up.3) | copy-start | bytes 6291460
  42.6 15.5 %copy-start.1 = (bf16[1024,1024]{1,0:T(8,128)(2,1)S(1)}, bf16[1024,1024]{1,0:T(8,128)(2,1)}, u32[]{:S(2)}) copy-start(bf16[1024,1024]{1,0:T(8,128)(2,1)} %w_down.3) | copy-start | bytes 6291460
  42.6 15.5 %copy-start.6 = (f32[1024]{0:T(1024)S(1)}, f32[1024]{0:T(1024)}, u32[]{:S(2)}) copy-start(f32[1024]{0:T(1024)} %param.19) | copy-start | bytes 12292
  50.4 6.3 %collective-permute-start.8 = (bf16[384,256]{1,0:T(8,128)(2,1)S(1)}, bf16[384,256]{1,0:T(8,128)(2,1)S(1)}, u32[]{:S(2)}, u32[]{:S(2)}) collective-permute-start(bf16[384,256]{1,0:T(8,128)(2,1)S(1)} %attend.1.a0), channel_id=1, source_target_pairs={{0,16},{8,24},{16,0},{24,8},{1,17},{9,25},{17,1},{25,9},{2,18},{10... | collective-permute-start | bytes 589832 | tf_op jit(solution)/shard_map/ppermute | solution.py:470
  52.2 4.6 %collective-permute-start.7 = (bf16[384,256]{1,0:T(8,128)(2,1)S(1)}, bf16[384,256]{1,0:T(8,128)(2,1)S(1)}, u32[]{:S(2)}, u32[]{:S(2)}) collective-permute-start(bf16[384,256]{1,0:T(8,128)(2,1)S(1)} %attend.1.a0), channel_id=1, source_target_pairs={{0,8},{8,0},{16,24},{24,16},{1,9},{9,1},{17,25},{25,17},{2,10},{10... | collective-permute-start | bytes 589832 | tf_op jit(solution)/shard_map/ppermute | solution.py:470
  56.7 1.4 %collective-permute-start.9 = (bf16[384,256]{1,0:T(8,128)(2,1)S(1)}, bf16[384,256]{1,0:T(8,128)(2,1)S(1)}, u32[]{:S(2)}, u32[]{:S(2)}) collective-permute-start(bf16[384,256]{1,0:T(8,128)(2,1)S(1)} %collective-permute-done.8.a2), channel_id=1, source_target_pairs={{0,8},{8,0},{16,24},{24,16},{1,9},{9,1},{17,25},{25,17},{2,10},{10... | collective-permute-start | bytes 589832 | tf_op jit(solution)/shard_map/ppermute | solution.py:470
  60.4 3.6 %collective-permute-start.13 = (bf16[192,1024]{1,0:T(8,128)(2,1)S(1)}, bf16[192,1024]{1,0:T(8,128)(2,1)S(1)}, u32[]{:S(2)}, u32[]{:S(2)}) collective-permute-start(bf16[192,1024]{1,0:T(8,128)(2,1)S(1)} %feed_other.1), channel_id=1, source_target_pairs={{0,8},{8,0},{16,24},{24,16},{1,9},{9,1},{17,25},{25,17},{2,10},{10... | collective-permute-start | bytes 1179656 | tf_op jit(solution)/shard_map/ppermute | solution.py:470
  61.2 10.2 %copy-start.5 = (bf16[1024,128]{1,0:T(8,128)(2,1)S(1)}, bf16[1024,128]{1,0:T(8,128)(2,1)}, u32[]{:S(2)}) copy-start(bf16[1024,128]{1,0:T(8,128)(2,1)} %w_proj.1) | copy-start | bytes 786436
  61.2 10.2 %copy-start.7 = (f32[1024]{0:T(1024)S(1)}, f32[1024]{0:T(1024)}, u32[]{:S(2)}) copy-start(f32[1024]{0:T(1024)} %param.20) | copy-start | bytes 12292
  64.1 21.9 %copy-start.8 = (s32[64]{0:T(128)S(1)}, s32[64]{0:T(128)}, u32[]{:S(2)}) copy-start(s32[64]{0:T(128)} %lengths.1) | copy-start | bytes 772
  64.1 7.2 %collective-permute-start.14 = (bf16[96,1024]{1,0:T(8,128)(2,1)S(1)}, bf16[96,1024]{1,0:T(8,128)(2,1)S(1)}, u32[]{:S(2)}, u32[]{:S(2)}) collective-permute-start(bf16[96,1024]{1,0:T(8,128)(2,1)S(1)} %add_convert_fusion), channel_id=1, source_target_pairs={{0,16},{8,24},{16,0},{24,8},{1,17},{9,25},{17,1},{25,9},{2,18},{10... | collective-permute-start | bytes 589832 | tf_op jit(solution)/shard_map/ppermute | solution.py:470
  72.6 13.4 %all-to-all-start.1 = ((bf16[8,96,128]{2,1,0:T(8,128)(2,1)}), bf16[8,96,128]{2,1,0:T(8,128)(2,1)S(1)}, u32[]{:S(2)}, u32[]{:S(2)}) async-start(bf16[8,96,128]{2,1,0:T(8,128)(2,1)} %project.1), calls=%async_computation.1 | async-start | bytes 393216 | tf_op jit(solution)/shard_map/all_to_all | solution.py:541
  78.9 20.9 %collective-permute-start.15 = (bf16[96,128]{1,0:T(8,128)(2,1)S(1)}, bf16[96,128]{1,0:T(8,128)(2,1)S(1)}, u32[]{:S(2)}, u32[]{:S(2)}) collective-permute-start(bf16[96,128]{1,0:T(8,128)(2,1)S(1)} %slice_bitcast_fusion), channel_id=1, source_target_pairs={{0,16},{8,24},{16,0},{24,8},{1,17},{9,25},{17,1},{25,9},{2,18},{10... | collective-permute-start | bytes 73736 | tf_op jit(solution)/shard_map/ppermute | solution.py:470
  86.0 2.2 %copy-start.2 = (bf16[64,256,128]{2,1,0:T(8,128)(2,1)S(1)}, bf16[64,256,128]{2,1,0:T(8,128)(2,1)}, u32[]{:S(2)}) copy-start(bf16[64,256,128]{2,1,0:T(8,128)(2,1)} %docs.1) | copy-start | bytes 12582916
  97.2 10.8 %all-to-all-start.2 = ((f32[32,8,128]{2,1,0:T(8,128)}), f32[32,8,128]{2,1,0:T(8,128)S(1)}, u32[]{:S(2)}, u32[]{:S(2)}) async-start(f32[32,8,128]{2,1,0:T(8,128)} %bitcast.15), calls=%async_computation.2 | async-start | bytes 262144 | tf_op jit(solution)/shard_map/all_to_all | solution.py:563
  99.8 1.3 %collective-permute-start.16 = (bf16[192,128]{1,0:T(8,128)(2,1)S(1)}, bf16[192,128]{1,0:T(8,128)(2,1)S(1)}, u32[]{:S(2)}, u32[]{:S(2)}) collective-permute-start(bf16[192,128]{1,0:T(8,128)(2,1)S(1)} %maximum_select_fusion.1), channel_id=1, source_target_pairs={{0,8},{8,0},{16,24},{24,16},{1,9},{9,1},{17,25},{25,17},{2,10},{10... | collective-permute-start | bytes 147464 | tf_op jit(solution)/shard_map/ppermute | solution.py:470

commit v3 on v2

v3 whole, which is shorter than its diff:
```python
import functools
import math

import jax
import jax.numpy as jnp
from jax import lax
from jax.experimental import pallas as pl
from jax.experimental.pallas import tpu as pltpu
from jax.sharding import PartitionSpec as P

HD = 64
RELS = 512
QLEN = 32
PLEN = 64
DOC_DEV = 64


def layer_norm(values, gain):
    centre = values - jnp.mean(values, axis=-1, keepdims=True)
    spread = jnp.mean(centre * centre, axis=-1, keepdims=True)
    return centre * lax.rsqrt(spread + 1e-07) * gain


def slot_order(holders):
    count = holders.shape[0]
    same = holders[:, None] == holders[None, :]
    earlier = jnp.arange(count)[:, None] > jnp.arange(count)[None, :]
    return jnp.sum(same & earlier, axis=1)


def rate_slots(slot_query, slot_doc, doc_vectors, doc_lengths):
    shape = slot_doc.shape
    flat_doc = slot_doc.reshape(-1)
    flat_query = slot_query.reshape((flat_doc.shape[0],) + slot_query.shape[-2:])
    safe_doc = jnp.maximum(flat_doc, 0)
    documents = doc_vectors[safe_doc]
    lengths = doc_lengths[safe_doc]
    sims = jnp.einsum("sqe,sje->sqj", flat_query, documents, preferred_element_type=jnp.float32)
    live = jnp.arange(documents.shape[1], dtype=jnp.int32)[None, None, :] < lengths[:, None, None]
    best = jnp.max(jnp.where(live, sims, -jnp.inf), axis=2)
    totals = jnp.where(flat_doc >= 0, jnp.sum(best, axis=1), 0.0)
    return totals.reshape(shape)


def body_any(
    tokens,
    w_qkv,
    w_out,
    w_up,
    w_down,
    gain_one,
    gain_two,
    rel_table,
    prompt_cache,
    w_proj,
    doc_vectors,
    doc_lengths,
    group_ids,
    candidates,
):
    rows_dev = tokens.shape[0]
    req_dev = rows_dev // QLEN
    width = w_qkv.shape[2]
    heads_loc = width // HD
    half = RELS // 2
    scale_root = math.sqrt(3 * HD)
    gathered = lax.all_gather(prompt_cache, "doc", axis=1, tiled=True)
    weights_split = w_qkv.reshape(w_qkv.shape[0], 3, heads_loc, HD)
    projected_all = jnp.einsum(
        "td,dchf->chtf", tokens, weights_split, preferred_element_type=jnp.float32
    ).astype(jnp.bfloat16)
    rel_both = jnp.einsum(
        "rd,dchf->chrf", rel_table, weights_split[:, :2], preferred_element_type=jnp.float32
    ).astype(jnp.bfloat16)
    head_shape = (heads_loc, req_dev, QLEN, HD)
    query_four = projected_all[0].reshape(head_shape)
    keys_four = projected_all[1].reshape(head_shape)
    values_four = projected_all[2].reshape(head_shape)
    groups_all = gathered.shape[1] // PLEN
    cache_all = gathered.reshape(2, groups_all, PLEN, heads_loc, HD)
    picked = jnp.transpose(cache_all[:, group_ids], (0, 3, 1, 2, 4))
    keys = jnp.concatenate([keys_four, picked[0]], axis=2)
    values = jnp.concatenate([values_four, picked[1]], axis=2)
    pos_query = PLEN + jnp.arange(QLEN, dtype=jnp.int32)
    pos_key = jnp.concatenate([pos_query, jnp.arange(PLEN, dtype=jnp.int32)])
    index_one = pos_query[:, None] - pos_key[None, :] + half
    index_two = pos_key[:, None] - pos_query[None, :] + half
    rel_k_rows = rel_both[1][:, index_one]
    rel_q_rows = rel_both[0][:, index_two]
    c2p = jnp.einsum("hrqd,hqkd->hrqk", query_four, rel_k_rows, preferred_element_type=jnp.float32)
    p2c = jnp.einsum("hrkd,hkqd->hrqk", keys, rel_q_rows, preferred_element_type=jnp.float32)
    content = jnp.einsum("hrqd,hrkd->hrqk", query_four, keys, preferred_element_type=jnp.float32)
    logits = (content + c2p + p2c) / scale_root
    largest = jnp.max(logits, axis=-1, keepdims=True)
    weights = jnp.exp(logits - largest)
    denominator = jnp.sum(weights, axis=-1)
    summed = jnp.einsum(
        "hrqk,hrkd->hrqd", weights.astype(jnp.bfloat16), values, preferred_element_type=jnp.float32
    )
    attended = (summed / denominator[..., None]).astype(jnp.bfloat16)
    out_split = w_out.reshape(heads_loc, HD, w_out.shape[1])
    attn_part = jnp.einsum(
        "hrqd,hde->rqe", attended, out_split, preferred_element_type=jnp.float32
    ).reshape(rows_dev, w_out.shape[1])
    attn_total = lax.psum(attn_part.astype(jnp.bfloat16), "head").astype(jnp.float32)
    hidden_one = layer_norm(tokens.astype(jnp.float32) + attn_total, gain_one).astype(jnp.bfloat16)
    inner = jax.nn.gelu(
        jnp.dot(hidden_one, w_up, preferred_element_type=jnp.float32), approximate=False
    ).astype(jnp.bfloat16)
    ffn_total = lax.psum(
        jnp.dot(inner, w_down, preferred_element_type=jnp.float32).astype(jnp.bfloat16), "head"
    ).astype(jnp.float32)
    hidden_two = layer_norm(hidden_one.astype(jnp.float32) + ffn_total, gain_two).astype(
        jnp.bfloat16
    )
    projected = jnp.dot(hidden_two, w_proj, preferred_element_type=jnp.float32)
    query_vectors = (
        projected * lax.rsqrt(jnp.sum(projected * projected, axis=-1, keepdims=True) + 1e-06)
    ).astype(jnp.bfloat16)
    shards = lax.axis_size("doc")
    cand_dev = candidates.shape[1]
    pairs = req_dev * cand_dev
    capacity = max(2, 2 * pairs // shards)
    flat_cand = candidates.reshape(-1)
    holders = flat_cand // DOC_DEV
    request_of = jnp.arange(pairs, dtype=jnp.int32) // cand_dev
    slot_rank = slot_order(holders)
    copies, cand_copies = (
        lax.all_gather(query_vectors, "doc", axis=0, tiled=True),
        lax.all_gather(candidates, "doc", axis=0, tiled=True),
    )
    all_query = copies.reshape(shards, req_dev, QLEN, copies.shape[1])
    all_cand = cand_copies.reshape(shards, pairs)
    holder_all = all_cand // DOC_DEV
    local_all = all_cand % DOC_DEV
    rank_all = jax.vmap(slot_order)(holder_all)
    own_index = lax.axis_index("doc")
    chosen = (holder_all[:, None, :] == own_index) & (
        rank_all[:, None, :] == jnp.arange(capacity, dtype=jnp.int32)[None, :, None]
    )
    filled = jnp.any(chosen, axis=2)
    slot_request = jnp.sum(jnp.where(chosen, request_of[None, None, :], 0), axis=2)
    slot_doc = jnp.where(
        filled, jnp.sum(jnp.where(chosen, local_all[:, None, :], 0), axis=2), -1
    ).astype(jnp.int32)
    slot_query = all_query[jnp.arange(shards)[:, None], slot_request]
    slot_scores = rate_slots(slot_query, slot_doc, doc_vectors, doc_lengths)
    returned = lax.all_to_all(slot_scores, "doc", split_axis=0, concat_axis=0, tiled=True)
    scores = returned.reshape(-1)[holders * capacity + slot_rank].reshape(candidates.shape)
    return (query_vectors, scores)


LANES = 128
MIB = 1 << 20
EXTRA = 16
PREP_UNROLL = 6
ATT_UNROLL = 6
SCORE_UNROLL = 16


def full_specs(count):
    return [pl.BlockSpec(memory_space=pltpu.VMEM)] * count


def params(mib):
    return pltpu.CompilerParams(vmem_limit_bytes=mib * MIB)


def by_head(values):
    head_of = lax.broadcasted_iota(jnp.int32, values.shape, 1) // HD
    heads = values.shape[1] // HD
    zero = jnp.zeros_like(values)
    return jnp.concatenate([jnp.where(head_of == h, values, zero) for h in range(heads)], axis=0)


def times_rows(left, right):
    return lax.dot_general(left, right, (((1,), (1,)), ((), ())), preferred_element_type=jnp.float32)


def key_terms(key_rel, first):
    slot = lax.broadcasted_iota(jnp.int32, (key_rel.shape[0], LANES), 1) // QLEN
    turned = None
    for h in range(key_rel.shape[1] // LANES):
        shift = (LANES - PLEN - QLEN + first + h * QLEN) % LANES
        rolled = pltpu.roll(
            key_rel[:, h * LANES : (h + 1) * LANES], shift, 1, stride=1, stride_axis=0
        )
        turned = rolled if turned is None else jnp.where(slot == h, rolled, turned)
    return turned


def prepare_kernel(tokens, weight, rel_table, qkv, base, rel_q_heads, q_heads, query_rel, key_rel):
    width = weight.shape[2]
    heads = width // HD
    for i in range(3):
        qkv[:, i * width : (i + 1) * width] = jnp.dot(
            tokens[...], weight[i], preferred_element_type=jnp.float32
        ).astype(jnp.bfloat16)
    count = 2 * (PLEN + QLEN)
    low = RELS // 2 - PLEN - QLEN
    rel = [
        jnp.dot(
            rel_table[low : low + count, :], weight[i], preferred_element_type=jnp.float32
        ).astype(jnp.bfloat16)
        for i in range(2)
    ]
    both = lax.broadcasted_iota(jnp.int32, (LANES, count), 0) + lax.broadcasted_iota(
        jnp.int32, (LANES, count), 1
    )
    flip_q = jnp.where(both == LANES, 1.0, 0.0).astype(jnp.bfloat16)
    flip_k = jnp.where(both == LANES + PLEN - 1, 1.0, 0.0).astype(jnp.bfloat16)
    rel_q = jnp.dot(flip_q, rel[0], preferred_element_type=jnp.float32)
    rel_k = jnp.dot(flip_k, rel[1], preferred_element_type=jnp.float32)
    rel_q_heads[...] = by_head(rel_q.astype(jnp.bfloat16))
    requests, many, _ = base.shape
    for r in range(requests):
        q_heads[r * many : (r + 1) * many, :] = by_head(qkv[r * QLEN : (r + 1) * QLEN, :width])
    query_rel[...] = times_rows(q_heads[...], rel_k.astype(jnp.bfloat16))
    key_rel[...] = times_rows(qkv[:, width : 2 * width], rel_q_heads[...])
    live = lax.broadcasted_iota(jnp.int32, (many, LANES), 1) < PLEN + QLEN
    above = jnp.zeros((PLEN, LANES), jnp.float32)
    below = jnp.zeros((LANES - PLEN - QLEN, LANES), jnp.float32)
    scale = 1.0 / math.sqrt(3 * HD)

    def one_request(r, carry):
        rows = pl.ds(pl.multiple_of(r * QLEN, QLEN), QLEN)
        spread = pl.ds(pl.multiple_of(r * many, many), many)
        turned = times_rows(qkv[rows, width : 2 * width], q_heads[spread, :])
        turned = turned + key_terms(key_rel[rows, :], PLEN)
        own = jnp.concatenate([above, turned, below], axis=0).T[:many]
        spread_rel = query_rel[spread, :]
        c2p = jnp.concatenate(
            [
                pltpu.roll(
                    spread_rel[h * QLEN : (h + 1) * QLEN],
                    LANES - QLEN + 1,
                    1,
                    stride=1,
                    stride_axis=0,
                )
                for h in range(heads)
            ],
            axis=0,
        )
        base[r] = jnp.where(live, (own + c2p) * scale, -jnp.inf)
        return carry

    lax.fori_loop(0, requests, one_request, 0, unroll=PREP_UNROLL)


def prepare(tokens, weight, rel_table):
    rows = tokens.shape[0]
    width = weight.shape[2]
    heads = width // HD
    return pl.pallas_call(
        prepare_kernel,
        out_shape=[
            jax.ShapeDtypeStruct((rows, 3 * width), jnp.bfloat16),
            jax.ShapeDtypeStruct((rows // QLEN, heads * QLEN, LANES), jnp.float32),
            jax.ShapeDtypeStruct((heads * LANES, width), jnp.bfloat16),
        ],
        in_specs=full_specs(3),
        out_specs=full_specs(3),
        scratch_shapes=[
            pltpu.VMEM((rows * heads, width), jnp.bfloat16),
            pltpu.VMEM((rows * heads, LANES), jnp.float32),
            pltpu.VMEM((rows, heads * LANES), jnp.float32),
        ],
        compiler_params=params(12),
        cost_estimate=pl.CostEstimate(flops=4000 * MIB, bytes_accessed=4 * MIB, transcendentals=0),
        name="prepare",
    )(tokens, weight, rel_table)


def attend_kernel(group_ids, qkv, base, rel_q_heads, columns, *rest):
    pieces, (att, cache, picked, key_rel, arrived) = rest[:-5], rest[-5:]
    copies = [
        [
            pltpu.make_async_copy(piece.at[kind], cache.at[kind, at], arrived.at[kind, at])
            for at, piece in enumerate(pieces)
        ]
        for kind in range(2)
    ]
    for copy in copies[0] + copies[1]:
        copy.start()
    requests, _, _ = base.shape
    tokens = requests * QLEN
    ids = columns[...].T
    spare = jnp.zeros((1, LANES - columns.shape[0] * columns.shape[1]), jnp.int32)
    line = jnp.concatenate([ids[r : r + 1, :] for r in range(ids.shape[0])] + [spare], axis=1)
    line = jnp.concatenate([line // DOC_DEV, line % DOC_DEV], axis=1)
    extra = jnp.broadcast_to(line.astype(jnp.float32), (EXTRA, line.shape[1]))
    att[tokens:, :] = extra.astype(att.dtype)
    width = att.shape[1]
    heads = width // HD
    groups_dev = cache.shape[2] // PLEN
    me = lax.axis_index("doc")
    padding = jnp.zeros((LANES - PLEN - QLEN, width), jnp.bfloat16)
    below_terms = jnp.zeros((LANES - PLEN, LANES), jnp.float32)
    small_head = lax.broadcasted_iota(jnp.int32, (QLEN, width), 1) // HD
    scale = 1.0 / math.sqrt(3 * HD)

    def place_of(r):
        owner = group_ids[r] // groups_dev
        within = pl.multiple_of((group_ids[r] - owner * groups_dev) * PLEN, PLEN)
        return owner ^ me, pl.ds(within, PLEN)

    for copy in copies[0]:
        copy.wait()
    for r in range(requests):
        piece, within = place_of(r)
        picked[r * PLEN : (r + 1) * PLEN, :] = cache[0, piece, within, :]
    key_rel[...] = times_rows(picked[...], rel_q_heads[...])
    for copy in copies[1]:
        copy.wait()

    def one_request(r, carry):
        rows = pl.ds(pl.multiple_of(r * QLEN, QLEN), QLEN)
        cached = pl.ds(pl.multiple_of(r * PLEN, PLEN), PLEN)
        turned = times_rows(picked[cached, :], by_head(qkv[rows, 0:width]))
        turned = (turned + key_terms(key_rel[cached, :], 0)) * scale
        logits = base[r] + jnp.concatenate([turned, below_terms], axis=0).T[: heads * QLEN]
        largest = jnp.max(logits, axis=1, keepdims=True)
        weights = jnp.exp(logits - largest)
        weights = weights * (1.0 / jnp.sum(weights, axis=1, keepdims=True))
        piece, within = place_of(r)
        values = jnp.concatenate(
            [cache[1, piece, within, :], qkv[rows, 2 * width : 3 * width], padding], axis=0
        )
        summed = jnp.dot(weights.astype(jnp.bfloat16), values, preferred_element_type=jnp.float32)
        out = summed[:QLEN]
        for h in range(1, heads):
            out = jnp.where(small_head == h, summed[h * QLEN : (h + 1) * QLEN], out)
        att[rows, :] = out.astype(jnp.bfloat16)
        return carry

    lax.fori_loop(0, requests, one_request, 0, unroll=ATT_UNROLL)


def attend(group_ids, qkv, base, rel_q_heads, columns, pieces):
    rows = qkv.shape[0]
    width = qkv.shape[1] // 3
    cached = rows // QLEN * PLEN
    return pl.pallas_call(
        attend_kernel,
        out_shape=jax.ShapeDtypeStruct((rows + EXTRA, width), jnp.bfloat16),
        in_specs=[pl.BlockSpec(memory_space=pltpu.SMEM)]
        + full_specs(4)
        + [pl.BlockSpec(memory_space=pl.ANY)] * len(pieces),
        out_specs=pl.BlockSpec(memory_space=pltpu.VMEM),
        scratch_shapes=[
            pltpu.VMEM((2, len(pieces)) + pieces[0].shape[1:], jnp.bfloat16),
            pltpu.VMEM((cached, width), jnp.bfloat16),
            pltpu.VMEM((cached, rel_q_heads.shape[0]), jnp.float32),
            pltpu.SemaphoreType.DMA((2, len(pieces))),
        ],
        compiler_params=params(12),
        cost_estimate=pl.CostEstimate(flops=2000 * MIB, bytes_accessed=2 * MIB, transcendentals=0),
        name="attend",
    )(group_ids, qkv, base, rel_q_heads, columns, *pieces)


def norm_rows(values, gain):
    centre = values - jnp.mean(values, axis=-1, keepdims=True)
    spread = jnp.mean(centre * centre, axis=-1, keepdims=True)
    return centre * lax.rsqrt(spread + 1e-07) * gain


def feed_rows(start, count, a, w, tokens, gain, w_up, w_down):
    rows = pl.ds(pl.multiple_of(start, 32), count)
    mixed = tokens[rows, :].astype(jnp.float32)
    for piece, weight in zip(a, w):
        mixed = mixed + jnp.dot(piece[rows, :], weight[...], preferred_element_type=jnp.float32)
    hidden = norm_rows(mixed, gain[...]).astype(jnp.bfloat16)
    total = None
    step = 256
    for at in range(0, w_up.shape[1], step):
        up = jnp.dot(hidden, w_up[:, at : at + step], preferred_element_type=jnp.float32)
        inner = (0.5 * up * (1.0 + lax.erf(up * math.sqrt(0.5)))).astype(jnp.bfloat16)
        part = jnp.dot(inner, w_down[at : at + step, :], preferred_element_type=jnp.float32)
        total = part if total is None else total + part
    return hidden, total


def feed_other_kernel(a0, a1, a2, a3, w0, w1, w2, w3, tokens, gain, w_up, w_down, out):
    core = lax.axis_index("head") % 2
    _, total = feed_rows(
        (1 - core) * out.shape[0], out.shape[0], (a0, a1, a2, a3), (w0, w1, w2, w3), tokens, gain, w_up, w_down
    )
    out[...] = total.astype(out.dtype)


def feed_own_kernel(a0, a1, a2, a3, w0, w1, w2, w3, tokens, gain, w_up, w_down, out, own):
    pieces, weights = (a0, a1, a2, a3), (w0, w1, w2, w3)
    count = out.shape[0]
    place = lax.axis_index("head")
    start = place % 2 * (2 * count)
    hidden, total = feed_rows(start, 2 * count, pieces, weights, tokens, gain, w_up, w_down)

    @pl.when(place // 2 == 0)
    def first():
        out[...] = total[count:]
        own[...] = hidden[:count].astype(jnp.float32) + total[:count]

    @pl.when(place // 2 != 0)
    def second():
        out[...] = total[:count]
        own[...] = hidden[count:].astype(jnp.float32) + total[count:]


def feed(kernel, pieces, weights, tokens, gain, w_up, w_down, outs, name):
    return pl.pallas_call(
        kernel,
        out_shape=outs,
        in_specs=full_specs(12),
        out_specs=full_specs(len(outs)),
        compiler_params=params(20),
        cost_estimate=pl.CostEstimate(flops=1600 * MIB, bytes_accessed=6 * MIB, transcendentals=0),
        name=name,
    )(*pieces, *weights, tokens, gain, w_up, w_down)


def fold_kernel(for_y, from_core, out):
    count = out.shape[0]
    other = 1 - lax.axis_index("head") // 2
    rows = pl.ds(pl.multiple_of(other * count, 32), count)
    out[...] = (for_y[...] + from_core[rows, :].astype(jnp.float32)).astype(out.dtype)


def block_of(head):
    return head % 2 * 2 + head // 2


def project_kernel(own, from_core, from_y, gain, w_proj, a0, a1, a2, a3, out, single):
    count = own.shape[0]
    place = lax.axis_index("head")
    rows = pl.ds(pl.multiple_of(place // 2 * count, 32), count)
    after = own[...] + from_core[rows, :].astype(jnp.float32) + from_y[...].astype(jnp.float32)
    hidden = norm_rows(after, gain[...]).astype(jnp.bfloat16)
    projected = jnp.dot(hidden, w_proj[...], preferred_element_type=jnp.float32)
    length = jnp.sum(projected * projected, axis=-1, keepdims=True)
    vectors = (projected * lax.rsqrt(length + 1e-06)).astype(jnp.bfloat16)
    single[...] = vectors
    pieces = (a0, a1, a2, a3)
    part = LANES // len(pieces) * 3 // 4
    lane = lax.broadcasted_iota(jnp.int32, (EXTRA, LANES), 1)
    lines = []
    for kind in range(2):
        line = jnp.zeros((EXTRA, LANES), jnp.float32)
        for x, piece in enumerate(pieces):
            from_head = place ^ x
            values = piece[piece.shape[0] - EXTRA :, kind * LANES : (kind + 1) * LANES]
            shift = lax.rem((from_head - block_of(place)) * part + LANES, LANES)
            rolled = pltpu.roll(values.astype(jnp.float32), shift, 1)
            line = jnp.where(lane // part == from_head, rolled, line)
        lines.append(line)
    which = lax.broadcasted_iota(jnp.int32, (EXTRA, LANES), 0)
    tail = jnp.where(which == 0, lines[0], lines[1]).astype(out.dtype)
    for o in range(out.shape[0]):
        out[o, :count] = vectors
        out[o, count:] = tail


def make_slots(queries, n_doc):
    rows = queries.shape[0] // n_doc
    part = (rows - EXTRA) // QLEN * 8
    me = lax.axis_index("doc")
    shape = (n_doc, LANES)
    lane = lax.broadcasted_iota(jnp.int32, shape, 1)
    row = lax.broadcasted_iota(jnp.int32, shape, 0)
    tails = [
        queries[o * rows + rows - EXTRA : (o + 1) * rows, :].astype(jnp.float32) for o in range(n_doc)
    ]
    holder = jnp.concatenate([tail[:1] for tail in tails], axis=0).astype(jnp.int32)
    doc = jnp.concatenate([tail[1:2] for tail in tails], axis=0).astype(jnp.int32)
    mine = (lane < 4 * part) & (holder == me)
    entry = row * LANES + lane
    group = (row * rows + lane % part // 8 * QLEN) // 16
    packed = entry | (group << 12) | (doc << 20)
    ones = jnp.where(mine, 1.0, 0.0)
    earlier = lax.broadcasted_iota(jnp.int32, (LANES, LANES), 0) < lax.broadcasted_iota(
        jnp.int32, (LANES, LANES), 1
    )
    before = jnp.where(earlier, 1.0, 0.0).astype(jnp.bfloat16)
    rank = jnp.dot(ones.astype(jnp.bfloat16), before, preferred_element_type=jnp.float32)
    in_row = jnp.sum(ones, axis=1, keepdims=True)
    above = jnp.zeros((1, 1), jnp.float32)
    starts = []
    for o in range(n_doc):
        starts.append(above)
        above = above + in_row[o : o + 1]
    rank = (rank + jnp.concatenate(starts, axis=0)).astype(jnp.int32)
    rank = jnp.where(mine, rank, -1)
    pad = jnp.zeros((LANES - n_doc, LANES), jnp.int32)
    rank_columns = jnp.concatenate([rank, pad], axis=0).T
    packed_columns = jnp.concatenate([packed, pad], axis=0).T
    square_lane = lax.broadcasted_iota(jnp.int32, (LANES, LANES), 1)
    lines = []
    for block in range(n_doc * 4 * part // LANES):
        total = jnp.zeros((LANES, LANES), jnp.int32)
        for o in range(n_doc):
            hit = rank_columns[:, o : o + 1] == square_lane + block * LANES
            total = total + jnp.where(hit, packed_columns[:, o : o + 1], 0)
        lines.append(jnp.sum(total, axis=0, keepdims=True))
    count = jnp.broadcast_to(above.astype(jnp.int32), (8 - len(lines), LANES))
    return jnp.concatenate(lines + [count], axis=0)


def score_kernel(lengths, queries, docs, out, held, listed, slots, arrived, ready):
    chunks = arrived.shape[0]
    per = docs.shape[0] // chunks
    copies = [
        pltpu.make_async_copy(
            docs.at[pl.ds(c * per, per)], held.at[pl.ds(c * per, per)], arrived.at[c]
        )
        for c in range(chunks)
    ]
    for copy in copies:
        copy.start()
    listed[...] = make_slots(queries, out.shape[0])
    to_scalars = pltpu.make_async_copy(listed, slots, ready)
    to_scalars.start()
    to_scalars.wait()
    for copy in copies:
        copy.wait()

    shape = (8, LANES)
    flat = lax.broadcasted_iota(jnp.int32, shape, 0) * LANES + lax.broadcasted_iota(jnp.int32, shape, 1)
    position = lax.broadcasted_iota(jnp.int32, (QLEN, docs.shape[1]), 1)
    unroll = SCORE_UNROLL
    count = slots[slots.shape[0] - 1, 0]

    def packed_of(s):
        return slots[s // LANES, s % LANES]

    def some(i, totals):
        for u in range(unroll):
            packed = packed_of(i * unroll + u)
            entry = jnp.where(i * unroll + u < count, packed & 4095, shape[0] * LANES)
            group = (packed >> 12) & 255
            doc = packed >> 20
            query = queries[pl.ds(pl.multiple_of(group * 16, 16), QLEN), :]
            sims = times_rows(query, held[doc])
            sims = jnp.where(position < lengths[doc], sims, -jnp.inf)
            best = jnp.max(sims, axis=1, keepdims=True)
            total = jnp.sum(best, axis=0, keepdims=True)
            totals = jnp.where(flat == entry, total, totals)
        return totals

    totals = lax.fori_loop(
        0, (count + unroll - 1) // unroll, some, jnp.zeros(shape, jnp.float32)
    )
    for o in range(out.shape[0]):
        row = jnp.broadcast_to(totals[o : o + 1], shape)
        for h in range(out.shape[1]):
            out[o, h] = row


def collect_kernel(tiles, out):
    n_head = tiles.shape[1]
    cols, reqs_all = out.shape
    reqs = reqs_all // n_head
    place = lax.axis_index("head")
    lines = []
    for h in range(n_head):
        total = tiles[0, h]
        for o in range(1, tiles.shape[0]):
            total = total + tiles[o, h]
        total = pltpu.roll(total, LANES - place * (reqs * cols), 1)
        lines.append(total[:1, : reqs * cols])
    order = sorted(range(n_head), key=block_of)
    rows = [lines[h][:, r * cols : (r + 1) * cols] for h in order for r in range(reqs)]
    out[...] = jnp.concatenate(rows, axis=0).T


def body(
    tokens,
    w_qkv,
    w_out,
    w_up,
    w_down,
    gain_one,
    gain_two,
    rel_table,
    prompt_cache,
    w_proj,
    doc_vectors,
    doc_lengths,
    group_ids,
    candidates,
):
    rows, depth = tokens.shape
    n_doc = lax.axis_size("doc")
    n_head = lax.axis_size("head")
    half, quarter = rows // 2, rows // n_head
    cand_rows, cols = candidates.shape
    reqs = cand_rows // n_head
    smem = pl.BlockSpec(memory_space=pltpu.SMEM)

    def over_doc(x, k):
        return lax.ppermute(x, "doc", [(i, i ^ k) for i in range(n_doc)])

    def over_head(x, k):
        return lax.ppermute(x, "head", [(i, i ^ k) for i in range(n_head)])

    tile = (8, LANES)
    pieces = {k: over_doc(prompt_cache, k) for k in (4, 6, 2, 1, 3)}
    pieces[0] = prompt_cache
    pieces[4], pieces[6], rel_table = lax.optimization_barrier((pieces[4], pieces[6], rel_table))
    pieces[5], pieces[7] = over_doc(pieces[4], 1), over_doc(pieces[6], 1)
    pieces = [pieces[k] for k in range(n_doc)]
    weight = jnp.transpose(w_qkv, (1, 0, 2))
    qkv, base, rel_q_heads = prepare(tokens, weight, rel_table)

    out_one = over_head(w_out, 2)
    out_pieces = [w_out, over_head(w_out, 1), out_one, over_head(out_one, 1)]

    att = attend(group_ids, qkv, base, rel_q_heads, candidates.T, pieces)
    att_y = over_head(att, 2)
    att_pieces = [att, over_head(att, 1), att_y, over_head(att_y, 1)]

    common = (att_pieces, out_pieces, tokens, gain_one.reshape(1, -1), w_up, w_down)
    other = feed(
        feed_other_kernel,
        *common,
        [jax.ShapeDtypeStruct((half, depth), jnp.bfloat16)],
        "feed_other",
    )[0]
    from_core = over_head(other, 1)
    for_y, own = feed(
        feed_own_kernel,
        *common,
        [jax.ShapeDtypeStruct((quarter, depth), jnp.float32)] * 2,
        "feed_own",
    )
    folded = pl.pallas_call(
        fold_kernel,
        out_shape=jax.ShapeDtypeStruct((quarter, depth), jnp.bfloat16),
        in_specs=full_specs(2),
        out_specs=full_specs(1)[0],
        compiler_params=params(4),
        name="fold",
    )(for_y, from_core)
    from_y = over_head(folded, 2)

    emb = w_proj.shape[1]
    vectors, single = pl.pallas_call(
        project_kernel,
        out_shape=[
            jax.ShapeDtypeStruct((n_doc, quarter + EXTRA, emb), jnp.bfloat16),
            jax.ShapeDtypeStruct((quarter, emb), jnp.bfloat16),
        ],
        in_specs=full_specs(9),
        out_specs=full_specs(2),
        compiler_params=params(8),
        name="project",
    )(own, from_core, from_y, gain_two.reshape(1, -1), w_proj, *att_pieces)
    queries = lax.all_to_all(vectors, "doc", 0, 0, tiled=True).reshape(-1, emb)

    rated = pl.pallas_call(
        score_kernel,
        out_shape=jax.ShapeDtypeStruct((n_doc, n_head) + tile, jnp.float32),
        in_specs=[smem] + full_specs(1) + [pl.BlockSpec(memory_space=pltpu.HBM)],
        out_specs=full_specs(1)[0],
        scratch_shapes=[
            pltpu.VMEM(doc_vectors.shape, jnp.bfloat16),
            pltpu.VMEM(tile, jnp.int32),
            pltpu.SMEM(tile, jnp.int32),
            pltpu.SemaphoreType.DMA((8,)),
            pltpu.SemaphoreType.DMA,
        ],
        compiler_params=params(56),
        name="rate",
    )(doc_lengths, queries, doc_vectors)
    back = lax.all_to_all(rated.reshape(-1, LANES), ("doc", "head"), 0, 0, tiled=True)

    place = lax.axis_index("head")
    own_y, own_c = place // 2, place % 2
    y_rows = over_head(single, 2)
    pair = jnp.where(
        own_y == 0, jnp.concatenate([single, y_rows]), jnp.concatenate([y_rows, single])
    )
    core_pair = over_head(pair, 1)
    query_vectors = jnp.where(
        own_c == 0, jnp.concatenate([pair, core_pair]), jnp.concatenate([core_pair, pair])
    )

    scores = pl.pallas_call(
        collect_kernel,
        out_shape=jax.ShapeDtypeStruct((cols, cand_rows), jnp.float32),
        in_specs=full_specs(1),
        out_specs=full_specs(1)[0],
        compiler_params=params(4),
        name="collect",
    )(back.reshape((n_doc, n_head) + tile))
    return (query_vectors, scores.T)


def solution(mesh):
    placed = (
        P("doc", None),
        P(None, None, "head"),
        P("head", None),
        P(None, "head"),
        P("head", None),
        P(),
        P(),
        P(),
        P(None, "doc", "head"),
        P(),
        P("doc", None, None),
        P("doc"),
        P("doc"),
        P("doc", "head"),
    )
    fits = mesh.shape["head"] == 4 and mesh.shape["doc"] == 8
    return jax.shard_map(
        body if fits else body_any,
        mesh=mesh,
        in_specs=placed,
        out_specs=(P("doc", None), P("doc", "head")),
        check_vma=False,
    )
```

time: 109 us -> 88.7 us (0.81)
  local copies, waits for them, and re-layouts: 17.1 us -> 4.5 us
  waiting for transfers between devices: 28.4 us -> 33.7 us
  Pallas kernels: 26.7 us -> 21.5 us
  other arithmetic: 4.93 us -> 0.68 us
  starting transfers between devices: 30.7 us -> 27.2 us
    unnamed x43 -> x28, local copies, waits for them, and re-layouts: 11.9 us -> 4.5 us
    pallas_call x5 -> x6, Pallas kernels: 14.2 us -> 12 us  [the longest x1 5.46 us: attend(): pl.pallas_call(attend_kernel, out_shape=jax.ShapeDtypeStruct((rows + EXTR...]
    ppermute x10, waiting for transfers between devices: 12 us -> 14.1 us  [over_head(): return lax.ppermute(x, 'head', [(i, i ^ k) for i in range(n_head)])]
    pallas_call x1, Pallas kernels: 9.06 us -> 6.96 us  [body(): pl.pallas_call(score_kernel, out_shape=jax.ShapeDtypeStruct((n_doc, n_hea...]
    reshape x4 -> x0, local copies, waits for them, and re-layouts: 2.02 us -> none  [the longest x1 1.78 us: body(): weight = w_qkv.reshape(w_qkv.shape[0], 3 * width)]
    all_to_all x3 -> x2, waiting for transfers between devices: 11.1 us -> 12.9 us  [the longest x1 6.62 us: body(): queries = lax.all_to_all(vectors, 'doc', 0, 0, tiled=True).reshape(-1, emb)]
    all_to_all x3 -> x2, starting transfers between devices: 12.1 us -> 10.7 us  [the longest x1 5.37 us: body(): lax.all_to_all(rated.reshape(-1, LANES), ('doc', 'head'), 0, 0, tiled=True)]
    ppermute x7, waiting for transfers between devices: 5.29 us -> 6.67 us  [over_doc(): return lax.ppermute(x, 'doc', [(i, i ^ k) for i in range(n_doc)])]
  transfers between devices with their start and end apart: 20 -> 19, of which waited for: 9 -> 8; matrix products, arithmetic and copies ran while one was open for 12% -> 1% of each run, Pallas kernels for 21% -> 20%
where the time goes in v3:
time: 88.7 us; the launch traced here: 88.4 us
  waiting for transfers between devices  33.7 us (38%)
  starting transfers between devices  27.2 us (31%)
  Pallas kernels  21.5 us (24%)
  local copies, waits for them, and re-layouts  4.5 us (5%)
    ppermute x10, waiting for transfers between devices, over_head(): return lax.ppermute(x, 'head', [(i, i ^ k) for i in range(n_head)])  14.1 us
    ppermute x7, starting transfers between devices, over_doc(): return lax.ppermute(x, 'doc', [(i, i ^ k) for i in range(n_doc)])  10.2 us
    pallas_call x1, Pallas kernels, body(): pl.pallas_call(score_kernel, out_shape=jax.ShapeDtypeStruct((n_doc, n_hea...  6.96 us
    ppermute x7, waiting for transfers between devices, over_doc(): return lax.ppermute(x, 'doc', [(i, i ^ k) for i in range(n_doc)])  6.67 us
    all_to_all x1, waiting for transfers between devices, body(): queries = lax.all_to_all(vectors, 'doc', 0, 0, tiled=True).reshape(-1, emb)  6.62 us
    ppermute x10, starting transfers between devices, over_head(): return lax.ppermute(x, 'head', [(i, i ^ k) for i in range(n_head)])  6.27 us
    all_to_all x1, waiting for transfers between devices, body(): lax.all_to_all(rated.reshape(-1, LANES), ('doc', 'head'), 0, 0, tiled=True)  6.23 us
    pallas_call x1, Pallas kernels, attend(): pl.pallas_call(attend_kernel, out_shape=jax.ShapeDtypeStruct((rows + EXTR...  5.46 us
  transfers between devices with their start and end apart: 19, of which 8 were waited for; matrix products, arithmetic and copies ran while one was open for 1% of the time, Pallas kernels for 20%

profile of v3, /device:TPU:0, one launch (start us, length us, event | category | flops | bytes accessed | tf_op | source)
XLA Modules:
  0.0 88.4 jit_solution(5724155240432208518)
XLA Ops:
  0.6 4.1 %collective-permute-start = (bf16[2,128,256]{2,1,0:T(8,128)(2,1)}, bf16[2,128,256]{2,1,0:T(8,128)(2,1)S(1)}, u32[]{:S(2)}, u32[]{:S(2)}) collective-permute-start(bf16[2,128,256]{2,1,0:T(8,128)(2,1)} %rest_0_.1), channel_id=1, source_target_pairs={{0,4},{1,5},{2,6},{3,7},{4,0},{5,1},{6,2},{7,3},{8,12},{9,13},{10,... | collective-permute-start | bytes 393224 | tf_op jit(solution)/shard_map/ppermute | solution.py:601
  4.7 1.3 %collective-permute-start.1 = (bf16[2,128,256]{2,1,0:T(8,128)(2,1)}, bf16[2,128,256]{2,1,0:T(8,128)(2,1)S(1)}, u32[]{:S(2)}, u32[]{:S(2)}) collective-permute-start(bf16[2,128,256]{2,1,0:T(8,128)(2,1)} %rest_0_.1), channel_id=1, source_target_pairs={{0,6},{1,7},{2,4},{3,5},{4,2},{5,3},{6,0},{7,1},{8,14},{9,15},{10,... | collective-permute-start | bytes 393224 | tf_op jit(solution)/shard_map/ppermute | solution.py:601
  6.1 1.5 %collective-permute-start.2 = (bf16[2,128,256]{2,1,0:T(8,128)(2,1)}, bf16[2,128,256]{2,1,0:T(8,128)(2,1)S(1)}, u32[]{:S(2)}, u32[]{:S(2)}) collective-permute-start(bf16[2,128,256]{2,1,0:T(8,128)(2,1)} %rest_0_.1), channel_id=1, source_target_pairs={{0,1},{1,0},{2,3},{3,2},{4,5},{5,4},{6,7},{7,6},{8,9},{9,8},{10,11... | collective-permute-start | bytes 393224 | tf_op jit(solution)/shard_map/ppermute | solution.py:601
  7.6 1.5 %collective-permute-start.11 = (bf16[256,1024]{1,0:T(8,128)(2,1)}, bf16[256,1024]{1,0:T(8,128)(2,1)S(1)}, u32[]{:S(2)}, u32[]{:S(2)}) collective-permute-start(bf16[256,1024]{1,0:T(8,128)(2,1)} %w0.3), channel_id=1, source_target_pairs={{0,16},{8,24},{16,0},{24,8},{1,17},{9,25},{17,1},{25,9},{2,18},{10... | collective-permute-start | bytes 1572872 | tf_op jit(solution)/shard_map/ppermute | solution.py:604
  9.1 0.2 collective-permute-start.3
  9.3 5.6 %collective-permute-done.rest_4_ = bf16[2,128,256]{2,1,0:T(8,128)(2,1)S(1)} collective-permute-done((bf16[2,128,256]{2,1,0:T(8,128)(2,1)}, bf16[2,128,256]{2,1,0:T(8,128)(2,1)S(1)}, u32[]{:S(2)}, u32[]{:S(2)}) %collective-permute-start) | collective-permute-done | bytes 131104 | tf_op jit(solution)/shard_map/ppermute | solution.py:601
  14.9 1.0 %collective-permute-start.4 = (bf16[2,128,256]{2,1,0:T(8,128)(2,1)}, bf16[2,128,256]{2,1,0:T(8,128)(2,1)S(1)}, u32[]{:S(2)}, u32[]{:S(2)}) collective-permute-start(bf16[2,128,256]{2,1,0:T(8,128)(2,1)} %rest_0_.1), channel_id=1, source_target_pairs={{0,3},{1,2},{2,1},{3,0},{4,7},{5,6},{6,5},{7,4},{8,11},{9,10},{10,... | collective-permute-start | bytes 393224 | tf_op jit(solution)/shard_map/ppermute | solution.py:601
  15.9 0.0 collective-permute-done.1.rest_6_
  16.0 0.8 collective-permute-start.5
  16.8 0.0 collective-permute-done.2.rest_1_
  16.8 1.2 %collective-permute-start.6 = (bf16[2,128,256]{2,1,0:T(8,128)(2,1)S(1)}, bf16[2,128,256]{2,1,0:T(8,128)(2,1)S(1)}, u32[]{:S(2)}, u32[]{:S(2)}) collective-permute-start(bf16[2,128,256]{2,1,0:T(8,128)(2,1)S(1)} %collective-permute-done.1.rest_6_), channel_id=1, source_target_pairs={{0,1},{1,0},{2,3},{3,2},{4,5},{5,4},{6,7},{7,6},{8,9},{9,8},{10,11... | collective-permute-start | bytes 393224 | tf_op jit(solution)/shard_map/ppermute | solution.py:601
  18.0 1.1 %copy-done.2 = bf16[384,1024]{1,0:T(8,128)(2,1)S(1)} copy-done((bf16[384,1024]{1,0:T(8,128)(2,1)S(1)}, bf16[384,1024]{1,0:T(8,128)(2,1)}, u32[]{:S(2)}) %copy-start.2) | copy-done | bytes 786456
  19.1 1.4 %copy-done.8 = bf16[1024,3,256]{2,0,1:T(8,128)(2,1)S(1)} copy-done((bf16[1024,3,256]{2,0,1:T(8,128)(2,1)S(1)}, bf16[1024,3,256]{2,0,1:T(8,128)(2,1)}, u32[]{:S(2)}) %copy-start.8) | copy-done | bytes 1572888
  20.5 1.2 %copy-done.9 = bf16[512,1024]{1,0:T(8,128)(2,1)S(1)} copy-done((bf16[512,1024]{1,0:T(8,128)(2,1)S(1)}, bf16[512,1024]{1,0:T(8,128)(2,1)}, u32[]{:S(2)}) %copy-start.9) | copy-done | bytes 1048600
  21.8 2.6 %prepare.1 = (bf16[384,768]{1,0:T(8,128)(2,1)S(1)}, f32[12,128,128]{2,1,0:T(8,128)S(1)}, bf16[512,256]{1,0:T(8,128)(2,1)S(1)}) custom-call(bf16[384,1024]{1,0:T(8,128)(2,1)S(1)} %copy-done.2, bf16[3,1024,256]{2,1,0:T(8,128)(2,1)S(1)} %bitcast.12, bf16[512,1024]{1,0:T(8,128)(2,1)S(1)} %copy-done.9), custom_call_target="tpu_custom_call" | custom-call | flops 4194304000 | bytes 4194304 | tf_op jit(solution)/shard_map/prepare/pallas_call | solution.py:255
  24.3 0.1 collective-permute-start.10
  24.4 0.5 collective-permute-start.12
  24.9 0.0 collective-permute-done.4.rest_3_
  24.9 0.0 collective-permute-done.5.rest_5_
  24.9 1.1 %collective-permute-done.6.rest_7_ = bf16[2,128,256]{2,1,0:T(8,128)(2,1)S(1)} collective-permute-done((bf16[2,128,256]{2,1,0:T(8,128)(2,1)S(1)}, bf16[2,128,256]{2,1,0:T(8,128)(2,1)S(1)}, u32[]{:S(2)}, u32[]{:S(2)}) %collective-permute-start.6) | collective-permute-done | bytes 131104 | tf_op jit(solution)/shard_map/ppermute | solution.py:601
  26.0 0.0 copy-start
  26.0 0.0 copy-start.1
  26.0 0.0 copy-start.3
  26.0 0.0 copy-start.6
  26.0 5.5 %attend.1.a0 = bf16[400,256]{1,0:T(8,128)(2,1)S(1)} custom-call(s32[12]{0:T(128)S(1)} %copy-done.12, bf16[384,768]{1,0:T(8,128)(2,1)S(1)} %get-tuple-element.13.qkv, f32[12,128,128]{2,1,0:T(8,128)S(1)} %get-tuple-element.14.base, bf16[512,256]{1,0:T(8,128)(2,1)S(1)} %get-tuple-element.15.rel_q_heads, s32[8,12]{1,0:T(8,128)S(1)} %bitcast.13, ...), custom_call_target="tpu_custom_call" | custom-call | flops 2097152000 | bytes 2097152 | tf_op jit(solution)/shard_map/attend/pallas_call | solution.py:344
  31.5 1.0 %collective-permute-start.8 = (bf16[400,256]{1,0:T(8,128)(2,1)S(1)}, bf16[400,256]{1,0:T(8,128)(2,1)S(1)}, u32[]{:S(2)}, u32[]{:S(2)}) collective-permute-start(bf16[400,256]{1,0:T(8,128)(2,1)S(1)} %attend.1.a0), channel_id=1, source_target_pairs={{0,16},{8,24},{16,0},{24,8},{1,17},{9,25},{17,1},{25,9},{2,18},{10... | collective-permute-start | bytes 614408 | tf_op jit(solution)/shard_map/ppermute | solution.py:604
  32.5 5.6 %collective-permute-done.8.a2 = bf16[400,256]{1,0:T(8,128)(2,1)S(1)} collective-permute-done((bf16[400,256]{1,0:T(8,128)(2,1)S(1)}, bf16[400,256]{1,0:T(8,128)(2,1)S(1)}, u32[]{:S(2)}, u32[]{:S(2)}) %collective-permute-start.8) | collective-permute-done | bytes 204832 | tf_op jit(solution)/shard_map/ppermute | solution.py:604
  38.1 1.4 %collective-permute-done.9.a3 = bf16[400,256]{1,0:T(8,128)(2,1)S(1)} collective-permute-done((bf16[400,256]{1,0:T(8,128)(2,1)S(1)}, bf16[400,256]{1,0:T(8,128)(2,1)S(1)}, u32[]{:S(2)}, u32[]{:S(2)}) %collective-permute-start.9) | collective-permute-done | bytes 204832 | tf_op jit(solution)/shard_map/ppermute | solution.py:604
  39.6 2.2 %feed_other.1 = bf16[192,1024]{1,0:T(8,128)(2,1)S(1)} custom-call(bf16[400,256]{1,0:T(8,128)(2,1)S(1)} %attend.1.a0, bf16[400,256]{1,0:T(8,128)(2,1)S(1)} %collective-permute-done.7.a1, bf16[400,256]{1,0:T(8,128)(2,1)S(1)} %collective-permute-done.8.a2, bf16[400,256]{1,0:T(8,128)(2,1)S(1)} %collective-permute-done.9.a3, bf16[256,1024]{1,0:T(8,128)(2,1)S(1)} %copy-done.4, ...), custom_call_target="tpu_custom_call" | custom-call | flops 1677721600 | bytes 6291456 | tf_op jit(solution)/shard_map/feed_other/pallas_call | solution.py:412
  41.8 0.0 copy-start.5
  41.8 0.0 copy-start.7
  41.8 0.2 collective-permute-start.13
  42.0 2.3 %feed_own.1 = (f32[96,1024]{1,0:T(8,128)S(1)}, f32[96,1024]{1,0:T(8,128)S(1)}) custom-call(bf16[400,256]{1,0:T(8,128)(2,1)S(1)} %attend.1.a0, bf16[400,256]{1,0:T(8,128)(2,1)S(1)} %collective-permute-done.7.a1, bf16[400,256]{1,0:T(8,128)(2,1)S(1)} %collective-permute-done.8.a2, bf16[400,256]{1,0:T(8,128)(2,1)S(1)} %collective-permute-done.9.a3, ...), custom_call_target="tpu_custom_call" | custom-call | flops 1677721600 | bytes 6291456 | tf_op jit(solution)/shard_map/feed_own/pallas_call | solution.py:412
  44.3 0.1 fold.1
  44.4 1.2 %collective-permute-start.14 = (bf16[96,1024]{1,0:T(8,128)(2,1)S(1)}, bf16[96,1024]{1,0:T(8,128)(2,1)S(1)}, u32[]{:S(2)}, u32[]{:S(2)}) collective-permute-start(bf16[96,1024]{1,0:T(8,128)(2,1)S(1)} %fold.1), channel_id=1, source_target_pairs={{0,16},{8,24},{16,0},{24,8},{1,17},{9,25},{17,1},{25,9},{2,18},{10... | collective-permute-start | bytes 589832 | tf_op jit(solution)/shard_map/ppermute | solution.py:604
  45.5 6.1 %collective-permute-done.14.from_y = bf16[96,1024]{1,0:T(8,128)(2,1)S(1)} collective-permute-done((bf16[96,1024]{1,0:T(8,128)(2,1)S(1)}, bf16[96,1024]{1,0:T(8,128)(2,1)S(1)}, u32[]{:S(2)}, u32[]{:S(2)}) %collective-permute-start.14) | collective-permute-done | bytes 196640 | tf_op jit(solution)/shard_map/ppermute | solution.py:604
  51.6 1.2 %project.1 = (bf16[8,112,128]{2,1,0:T(8,128)(2,1)}, bf16[96,128]{1,0:T(8,128)(2,1)S(1)}) custom-call(f32[96,1024]{1,0:T(8,128)S(1)} %get-tuple-element.18.own, bf16[192,1024]{1,0:T(8,128)(2,1)S(1)} %collective-permute-done.13.from_core, bf16[96,1024]{1,0:T(8,128)(2,1)S(1)} %collective-permute-done.14.from_y, f32[1,1024]{1,0:T(1,128)S(1)} %bitcast.11, ...), custom_call_target="tpu_custom_call" | custom-call | tf_op jit(solution)/shard_map/project/pallas_call | solution.py:647
  52.8 5.3 %all-to-all-start = ((bf16[8,112,128]{2,1,0:T(8,128)(2,1)}), bf16[8,112,128]{2,1,0:T(8,128)(2,1)S(1)}, u32[]{:S(2)}, u32[]{:S(2)}) async-start(bf16[8,112,128]{2,1,0:T(8,128)(2,1)} %get-tuple-element.21), calls=%async_computation | async-start | bytes 458752 | tf_op jit(solution)/shard_map/all_to_all | solution.py:658
  58.2 1.5 %collective-permute-start.15 = (bf16[96,128]{1,0:T(8,128)(2,1)S(1)}, bf16[96,128]{1,0:T(8,128)(2,1)S(1)}, u32[]{:S(2)}, u32[]{:S(2)}) collective-permute-start(bf16[96,128]{1,0:T(8,128)(2,1)S(1)} %get-tuple-element.20), channel_id=1, source_target_pairs={{0,16},{8,24},{16,0},{24,8},{1,17},{9,25},{17,1},{25,9},{2,18},{10... | collective-permute-start | bytes 73736 | tf_op jit(solution)/shard_map/ppermute | solution.py:604
  59.7 6.6 %all-to-all-done = bf16[8,112,128]{2,1,0:T(8,128)(2,1)S(1)} async-done(((bf16[8,112,128]{2,1,0:T(8,128)(2,1)}), bf16[8,112,128]{2,1,0:T(8,128)(2,1)S(1)}, u32[]{:S(2)}, u32[]{:S(2)}) %all-to-all-start) | async-done | bytes 229408 | tf_op jit(solution)/shard_map/all_to_all | solution.py:658
  66.3 0.7 copy-done.13
  67.0 7.0 %rate.1 = f32[8,4,8,128]{3,2,1,0:T(8,128)} custom-call(s32[64]{0:T(128)} %lengths.1, bf16[896,128]{1,0:T(8,128)(2,1)} %bitcast.14, bf16[64,256,128]{2,1,0:T(8,128)(2,1)} %docs.1), custom_call_target="tpu_custom_call" | custom-call | tf_op jit(solution)/shard_map/rate/pallas_call | solution.py:660
  74.0 5.4 %all-to-all-start.1 = ((f32[32,8,128]{2,1,0:T(8,128)}), f32[32,8,128]{2,1,0:T(8,128)S(1)}, u32[]{:S(2)}, u32[]{:S(2)}) async-start(f32[32,8,128]{2,1,0:T(8,128)} %bitcast.15), calls=%async_computation.1 | async-start | bytes 262144 | tf_op jit(solution)/shard_map/all_to_all | solution.py:675
  79.4 0.3 collective-permute-start.16
  79.7 1.0 %collective-permute-done.16 = bf16[192,128]{1,0:T(8,128)(2,1)S(1)} collective-permute-done((bf16[192,128]{1,0:T(8,128)(2,1)S(1)}, bf16[192,128]{1,0:T(8,128)(2,1)S(1)}, u32[]{:S(2)}, u32[]{:S(2)}) %collective-permute-start.16) | collective-permute-done | bytes 49184 | tf_op jit(solution)/shard_map/ppermute | solution.py:604
  80.7 0.7 maximum_select_fusion
  81.3 6.2 %all-to-all-done.1 = f32[32,8,128]{2,1,0:T(8,128)S(1)} async-done(((f32[32,8,128]{2,1,0:T(8,128)}), f32[32,8,128]{2,1,0:T(8,128)S(1)}, u32[]{:S(2)}, u32[]{:S(2)}) %all-to-all-start.1) | async-done | bytes 131104 | tf_op jit(solution)/shard_map/all_to_all | solution.py:675
  87.6 0.8 collect.1
  (28 shorter events, 0.1 us)
Async XLA Ops:
  0.6 14.3 %collective-permute-start = (bf16[2,128,256]{2,1,0:T(8,128)(2,1)}, bf16[2,128,256]{2,1,0:T(8,128)(2,1)S(1)}, u32[]{:S(2)}, u32[]{:S(2)}) collective-permute-start(bf16[2,128,256]{2,1,0:T(8,128)(2,1)} %rest_0_.1), channel_id=1, source_target_pairs={{0,4},{1,5},{2,6},{3,7},{4,0},{5,1},{6,2},{7,3},{8,12},{9,13},{10,... | collective-permute-start | bytes 393224 | tf_op jit(solution)/shard_map/ppermute | solution.py:601
  4.7 11.2 %collective-permute-start.1 = (bf16[2,128,256]{2,1,0:T(8,128)(2,1)}, bf16[2,128,256]{2,1,0:T(8,128)(2,1)S(1)}, u32[]{:S(2)}, u32[]{:S(2)}) collective-permute-start(bf16[2,128,256]{2,1,0:T(8,128)(2,1)} %rest_0_.1), channel_id=1, source_target_pairs={{0,6},{1,7},{2,4},{3,5},{4,2},{5,3},{6,0},{7,1},{8,14},{9,15},{10,... | collective-permute-start | bytes 393224 | tf_op jit(solution)/shard_map/ppermute | solution.py:601
  6.1 10.7 %collective-permute-start.2 = (bf16[2,128,256]{2,1,0:T(8,128)(2,1)}, bf16[2,128,256]{2,1,0:T(8,128)(2,1)S(1)}, u32[]{:S(2)}, u32[]{:S(2)}) collective-permute-start(bf16[2,128,256]{2,1,0:T(8,128)(2,1)} %rest_0_.1), channel_id=1, source_target_pairs={{0,1},{1,0},{2,3},{3,2},{4,5},{5,4},{6,7},{7,6},{8,9},{9,8},{10,11... | collective-permute-start | bytes 393224 | tf_op jit(solution)/shard_map/ppermute | solution.py:601
  7.6 16.8 %collective-permute-start.11 = (bf16[256,1024]{1,0:T(8,128)(2,1)}, bf16[256,1024]{1,0:T(8,128)(2,1)S(1)}, u32[]{:S(2)}, u32[]{:S(2)}) collective-permute-start(bf16[256,1024]{1,0:T(8,128)(2,1)} %w0.3), channel_id=1, source_target_pairs={{0,16},{8,24},{16,0},{24,8},{1,17},{9,25},{17,1},{25,9},{2,18},{10... | collective-permute-start | bytes 1572872 | tf_op jit(solution)/shard_map/ppermute | solution.py:604
  9.1 15.2 %collective-permute-start.3 = (bf16[2,128,256]{2,1,0:T(8,128)(2,1)}, bf16[2,128,256]{2,1,0:T(8,128)(2,1)S(1)}, u32[]{:S(2)}, u32[]{:S(2)}) collective-permute-start(bf16[2,128,256]{2,1,0:T(8,128)(2,1)} %rest_0_.1), channel_id=1, source_target_pairs={{0,2},{1,3},{2,0},{3,1},{4,6},{5,7},{6,4},{7,5},{8,10},{9,11},{10,... | collective-permute-start | bytes 393224 | tf_op jit(solution)/shard_map/ppermute | solution.py:601
  14.9 10.0 %collective-permute-start.4 = (bf16[2,128,256]{2,1,0:T(8,128)(2,1)}, bf16[2,128,256]{2,1,0:T(8,128)(2,1)S(1)}, u32[]{:S(2)}, u32[]{:S(2)}) collective-permute-start(bf16[2,128,256]{2,1,0:T(8,128)(2,1)} %rest_0_.1), channel_id=1, source_target_pairs={{0,3},{1,2},{2,1},{3,0},{4,7},{5,6},{6,5},{7,4},{8,11},{9,10},{10,... | collective-permute-start | bytes 393224 | tf_op jit(solution)/shard_map/ppermute | solution.py:601
  16.0 9.0 %collective-permute-start.5 = (bf16[2,128,256]{2,1,0:T(8,128)(2,1)S(1)}, bf16[2,128,256]{2,1,0:T(8,128)(2,1)S(1)}, u32[]{:S(2)}, u32[]{:S(2)}) collective-permute-start(bf16[2,128,256]{2,1,0:T(8,128)(2,1)S(1)} %collective-permute-done.rest_4_), channel_id=1, source_target_pairs={{0,1},{1,0},{2,3},{3,2},{4,5},{5,4},{6,7},{7,6},{8,9},{9,8},{10,11... | collective-permute-start | bytes 393224 | tf_op jit(solution)/shard_map/ppermute | solution.py:601
  16.8 9.2 %collective-permute-start.6 = (bf16[2,128,256]{2,1,0:T(8,128)(2,1)S(1)}, bf16[2,128,256]{2,1,0:T(8,128)(2,1)S(1)}, u32[]{:S(2)}, u32[]{:S(2)}) collective-permute-start(bf16[2,128,256]{2,1,0:T(8,128)(2,1)S(1)} %collective-permute-done.1.rest_6_), channel_id=1, source_target_pairs={{0,1},{1,0},{2,3},{3,2},{4,5},{5,4},{6,7},{7,6},{8,9},{9,8},{10,11... | collective-permute-start | bytes 393224 | tf_op jit(solution)/shard_map/ppermute | solution.py:601
  18.0 1.1 %copy-start.2 = (bf16[384,1024]{1,0:T(8,128)(2,1)S(1)}, bf16[384,1024]{1,0:T(8,128)(2,1)}, u32[]{:S(2)}) copy-start(bf16[384,1024]{1,0:T(8,128)(2,1)} %tokens.5) | copy-start | bytes 2359300
  19.1 1.4 %copy-start.8 = (bf16[1024,3,256]{2,0,1:T(8,128)(2,1)S(1)}, bf16[1024,3,256]{2,0,1:T(8,128)(2,1)}, u32[]{:S(2)}) copy-start(bf16[1024,3,256]{2,0,1:T(8,128)(2,1)} %param.15) | copy-start | bytes 4718596
  20.5 1.2 %copy-start.9 = (bf16[512,1024]{1,0:T(8,128)(2,1)S(1)}, bf16[512,1024]{1,0:T(8,128)(2,1)}, u32[]{:S(2)}) copy-start(bf16[512,1024]{1,0:T(8,128)(2,1)} %rel_table) | copy-start | bytes 3145732
  21.8 2.6 %copy-start.4 = (bf16[256,1024]{1,0:T(8,128)(2,1)S(1)}, bf16[256,1024]{1,0:T(8,128)(2,1)}, u32[]{:S(2)}) copy-start(bf16[256,1024]{1,0:T(8,128)(2,1)} %w0.3) | copy-start | bytes 1572868
  21.8 4.2 %copy-start.10 = (bf16[2,128,256]{2,1,0:T(8,128)(2,1)S(1)}, bf16[2,128,256]{2,1,0:T(8,128)(2,1)}, u32[]{:S(2)}) copy-start(bf16[2,128,256]{2,1,0:T(8,128)(2,1)} %rest_0_.1) | copy-start | bytes 393220
  21.8 4.2 %copy-start.11 = (s32[12,8]{0,1:T(8,128)S(1)}, s32[12,8]{0,1:T(8,128)}, u32[]{:S(2)}) copy-start(s32[12,8]{0,1:T(8,128)} %param.27) | copy-start | bytes 1156
  21.8 4.2 %copy-start.12 = (s32[12]{0:T(128)S(1)}, s32[12]{0:T(128)}, u32[]{:S(2)}) copy-start(s32[12]{0:T(128)} %group_ids.1) | copy-start | bytes 148
  24.3 13.7 %collective-permute-start.10 = (bf16[256,1024]{1,0:T(8,128)(2,1)S(1)}, bf16[256,1024]{1,0:T(8,128)(2,1)S(1)}, u32[]{:S(2)}, u32[]{:S(2)}) collective-permute-start(bf16[256,1024]{1,0:T(8,128)(2,1)S(1)} %copy-done.4), channel_id=1, source_target_pairs={{0,8},{8,0},{16,24},{24,16},{1,9},{9,1},{17,25},{25,17},{2,10},{10... | collective-permute-start | bytes 1572872 | tf_op jit(solution)/shard_map/ppermute | solution.py:604
  24.4 15.1 %collective-permute-start.12 = (bf16[256,1024]{1,0:T(8,128)(2,1)S(1)}, bf16[256,1024]{1,0:T(8,128)(2,1)S(1)}, u32[]{:S(2)}, u32[]{:S(2)}) collective-permute-start(bf16[256,1024]{1,0:T(8,128)(2,1)S(1)} %collective-permute-done.11.w2), channel_id=1, source_target_pairs={{0,8},{8,0},{16,24},{24,16},{1,9},{9,1},{17,25},{25,17},{2,10},{10... | collective-permute-start | bytes 1572872 | tf_op jit(solution)/shard_map/ppermute | solution.py:604
  26.0 13.5 %copy-start = (bf16[1024,1024]{1,0:T(8,128)(2,1)S(1)}, bf16[1024,1024]{1,0:T(8,128)(2,1)}, u32[]{:S(2)}) copy-start(bf16[1024,1024]{1,0:T(8,128)(2,1)} %w_up.3) | copy-start | bytes 6291460
  26.0 13.5 %copy-start.1 = (bf16[1024,1024]{1,0:T(8,128)(2,1)S(1)}, bf16[1024,1024]{1,0:T(8,128)(2,1)}, u32[]{:S(2)}) copy-start(bf16[1024,1024]{1,0:T(8,128)(2,1)} %w_down.3) | copy-start | bytes 6291460
  26.0 13.5 %copy-start.3 = (bf16[384,1024]{1,0:T(8,128)(2,1)S(1)}, bf16[384,1024]{1,0:T(8,128)(2,1)}, u32[]{:S(2)}) copy-start(bf16[384,1024]{1,0:T(8,128)(2,1)} %tokens.5) | copy-start | bytes 2359300
  26.0 13.5 %copy-start.6 = (f32[1024]{0:T(1024)S(1)}, f32[1024]{0:T(1024)}, u32[]{:S(2)}) copy-start(f32[1024]{0:T(1024)} %param.19) | copy-start | bytes 12292
  31.5 6.6 %collective-permute-start.8 = (bf16[400,256]{1,0:T(8,128)(2,1)S(1)}, bf16[400,256]{1,0:T(8,128)(2,1)S(1)}, u32[]{:S(2)}, u32[]{:S(2)}) collective-permute-start(bf16[400,256]{1,0:T(8,128)(2,1)S(1)} %attend.1.a0), channel_id=1, source_target_pairs={{0,16},{8,24},{16,0},{24,8},{1,17},{9,25},{17,1},{25,9},{2,18},{10... | collective-permute-start | bytes 614408 | tf_op jit(solution)/shard_map/ppermute | solution.py:604
  32.5 5.6 %collective-permute-start.7 = (bf16[400,256]{1,0:T(8,128)(2,1)S(1)}, bf16[400,256]{1,0:T(8,128)(2,1)S(1)}, u32[]{:S(2)}, u32[]{:S(2)}) collective-permute-start(bf16[400,256]{1,0:T(8,128)(2,1)S(1)} %attend.1.a0), channel_id=1, source_target_pairs={{0,8},{8,0},{16,24},{24,16},{1,9},{9,1},{17,25},{25,17},{2,10},{10... | collective-permute-start | bytes 614408 | tf_op jit(solution)/shard_map/ppermute | solution.py:604
  38.1 1.5 %collective-permute-start.9 = (bf16[400,256]{1,0:T(8,128)(2,1)S(1)}, bf16[400,256]{1,0:T(8,128)(2,1)S(1)}, u32[]{:S(2)}, u32[]{:S(2)}) collective-permute-start(bf16[400,256]{1,0:T(8,128)(2,1)S(1)} %collective-permute-done.8.a2), channel_id=1, source_target_pairs={{0,8},{8,0},{16,24},{24,16},{1,9},{9,1},{17,25},{25,17},{2,10},{10... | collective-permute-start | bytes 614408 | tf_op jit(solution)/shard_map/ppermute | solution.py:604
  41.8 9.8 %copy-start.5 = (bf16[1024,128]{1,0:T(8,128)(2,1)S(1)}, bf16[1024,128]{1,0:T(8,128)(2,1)}, u32[]{:S(2)}) copy-start(bf16[1024,128]{1,0:T(8,128)(2,1)} %w_proj.1) | copy-start | bytes 786436
  41.8 9.8 %copy-start.7 = (f32[1024]{0:T(1024)S(1)}, f32[1024]{0:T(1024)}, u32[]{:S(2)}) copy-start(f32[1024]{0:T(1024)} %param.20) | copy-start | bytes 12292
  41.8 2.5 %collective-permute-start.13 = (bf16[192,1024]{1,0:T(8,128)(2,1)S(1)}, bf16[192,1024]{1,0:T(8,128)(2,1)S(1)}, u32[]{:S(2)}, u32[]{:S(2)}) collective-permute-start(bf16[192,1024]{1,0:T(8,128)(2,1)S(1)} %feed_other.1), channel_id=1, source_target_pairs={{0,8},{8,0},{16,24},{24,16},{1,9},{9,1},{17,25},{25,17},{2,10},{10... | collective-permute-start | bytes 1179656 | tf_op jit(solution)/shard_map/ppermute | solution.py:604
  44.4 7.3 %collective-permute-start.14 = (bf16[96,1024]{1,0:T(8,128)(2,1)S(1)}, bf16[96,1024]{1,0:T(8,128)(2,1)S(1)}, u32[]{:S(2)}, u32[]{:S(2)}) collective-permute-start(bf16[96,1024]{1,0:T(8,128)(2,1)S(1)} %fold.1), channel_id=1, source_target_pairs={{0,16},{8,24},{16,0},{24,8},{1,17},{9,25},{17,1},{25,9},{2,18},{10... | collective-permute-start | bytes 589832 | tf_op jit(solution)/shard_map/ppermute | solution.py:604
  52.8 13.5 %all-to-all-start = ((bf16[8,112,128]{2,1,0:T(8,128)(2,1)}), bf16[8,112,128]{2,1,0:T(8,128)(2,1)S(1)}, u32[]{:S(2)}, u32[]{:S(2)}) async-start(bf16[8,112,128]{2,1,0:T(8,128)(2,1)} %get-tuple-element.21), calls=%async_computation | async-start | bytes 458752 | tf_op jit(solution)/shard_map/all_to_all | solution.py:658
  58.2 21.2 %collective-permute-start.15 = (bf16[96,128]{1,0:T(8,128)(2,1)S(1)}, bf16[96,128]{1,0:T(8,128)(2,1)S(1)}, u32[]{:S(2)}, u32[]{:S(2)}) collective-permute-start(bf16[96,128]{1,0:T(8,128)(2,1)S(1)} %get-tuple-element.20), channel_id=1, source_target_pairs={{0,16},{8,24},{16,0},{24,8},{1,17},{9,25},{17,1},{25,9},{2,18},{10... | collective-permute-start | bytes 73736 | tf_op jit(solution)/shard_map/ppermute | solution.py:604
  66.3 0.7 copy-start.13
  74.0 13.6 %all-to-all-start.1 = ((f32[32,8,128]{2,1,0:T(8,128)}), f32[32,8,128]{2,1,0:T(8,128)S(1)}, u32[]{:S(2)}, u32[]{:S(2)}) async-start(f32[32,8,128]{2,1,0:T(8,128)} %bitcast.15), calls=%async_computation.1 | async-start | bytes 262144 | tf_op jit(solution)/shard_map/all_to_all | solution.py:675
  79.4 1.3 %collective-permute-start.16 = (bf16[192,128]{1,0:T(8,128)(2,1)S(1)}, bf16[192,128]{1,0:T(8,128)(2,1)S(1)}, u32[]{:S(2)}, u32[]{:S(2)}) collective-permute-start(bf16[192,128]{1,0:T(8,128)(2,1)S(1)} %maximum_select_fusion.1), channel_id=1, source_target_pairs={{0,8},{8,0},{16,24},{24,16},{1,9},{9,1},{17,25},{25,17},{2,10},{10... | collective-permute-start | bytes 147464 | tf_op jit(solution)/shard_map/ppermute | solution.py:604

commit v4 on v3

--- a/solution.py
+++ b/solution.py
@@ -155,7 +155,7 @@
 EXTRA = 16
 PREP_UNROLL = 6
 ATT_UNROLL = 6
-SCORE_UNROLL = 16
+SCORE_UNROLL = 32
 
 
 def full_specs(count):
@@ -461,7 +461,7 @@
         out[o, count:] = tail
 
 
-def make_slots(queries, n_doc):
+def list_slots(queries, n_doc, listed):
     rows = queries.shape[0] // n_doc
     part = (rows - EXTRA) // QLEN * 8
     me = lax.axis_index("doc")
@@ -474,36 +474,36 @@
     holder = jnp.concatenate([tail[:1] for tail in tails], axis=0).astype(jnp.int32)
     doc = jnp.concatenate([tail[1:2] for tail in tails], axis=0).astype(jnp.int32)
     mine = (lane < 4 * part) & (holder == me)
-    entry = row * LANES + lane
     group = (row * rows + lane % part // 8 * QLEN) // 16
-    packed = entry | (group << 12) | (doc << 20)
+    listed[n_doc : 2 * n_doc, :] = group | (doc << 8)
     ones = jnp.where(mine, 1.0, 0.0)
-    earlier = lax.broadcasted_iota(jnp.int32, (LANES, LANES), 0) < lax.broadcasted_iota(
+    until = lax.broadcasted_iota(jnp.int32, (LANES, LANES), 0) <= lax.broadcasted_iota(
         jnp.int32, (LANES, LANES), 1
     )
-    before = jnp.where(earlier, 1.0, 0.0).astype(jnp.bfloat16)
-    rank = jnp.dot(ones.astype(jnp.bfloat16), before, preferred_element_type=jnp.float32)
+    until = jnp.where(until, 1.0, 0.0).astype(jnp.bfloat16)
+    reached = jnp.dot(ones.astype(jnp.bfloat16), until, preferred_element_type=jnp.float32)
     in_row = jnp.sum(ones, axis=1, keepdims=True)
     above = jnp.zeros((1, 1), jnp.float32)
     starts = []
     for o in range(n_doc):
         starts.append(above)
         above = above + in_row[o : o + 1]
-    rank = (rank + jnp.concatenate(starts, axis=0)).astype(jnp.int32)
-    rank = jnp.where(mine, rank, -1)
+    reached = (reached + jnp.concatenate(starts, axis=0)).astype(jnp.int32)
     pad = jnp.zeros((LANES - n_doc, LANES), jnp.int32)
-    rank_columns = jnp.concatenate([rank, pad], axis=0).T
-    packed_columns = jnp.concatenate([packed, pad], axis=0).T
+    columns = jnp.concatenate([reached, pad], axis=0).T
     square_lane = lax.broadcasted_iota(jnp.int32, (LANES, LANES), 1)
-    lines = []
-    for block in range(n_doc * 4 * part // LANES):
+    blocks = (jnp.sum(ones).astype(jnp.int32) + LANES - 1) // LANES
+
+    def one_block(block, carry):
         total = jnp.zeros((LANES, LANES), jnp.int32)
         for o in range(n_doc):
-            hit = rank_columns[:, o : o + 1] == square_lane + block * LANES
-            total = total + jnp.where(hit, packed_columns[:, o : o + 1], 0)
-        lines.append(jnp.sum(total, axis=0, keepdims=True))
-    count = jnp.broadcast_to(above.astype(jnp.int32), (8 - len(lines), LANES))
-    return jnp.concatenate(lines + [count], axis=0)
+            passed = columns[:, o : o + 1] <= square_lane + block * LANES
+            total = total + jnp.where(passed, 1, 0)
+        listed[pl.ds(block, 1), :] = jnp.sum(total, axis=0, keepdims=True)
+        return carry
+
+    lax.fori_loop(0, blocks, one_block, 0)
+    listed[n_doc - 1 : n_doc, :] = jnp.broadcast_to(above.astype(jnp.int32), (1, LANES))
 
 
 def score_kernel(lengths, queries, docs, out, held, listed, slots, arrived, ready):
@@ -517,7 +517,7 @@
     ]
     for copy in copies:
         copy.start()
-    listed[...] = make_slots(queries, out.shape[0])
+    list_slots(queries, out.shape[0], listed)
     to_scalars = pltpu.make_async_copy(listed, slots, ready)
     to_scalars.start()
     to_scalars.wait()
@@ -526,25 +526,33 @@
 
     shape = (8, LANES)
     flat = lax.broadcasted_iota(jnp.int32, shape, 0) * LANES + lax.broadcasted_iota(jnp.int32, shape, 1)
-    position = lax.broadcasted_iota(jnp.int32, (QLEN, docs.shape[1]), 1)
     unroll = SCORE_UNROLL
-    count = slots[slots.shape[0] - 1, 0]
-
-    def packed_of(s):
-        return slots[s // LANES, s % LANES]
+    zero = jnp.zeros((QLEN, docs.shape[2]), jnp.bfloat16)
+    position = lax.broadcasted_iota(jnp.int32, (docs.shape[1], 2 * QLEN), 0)
+    side = lax.broadcasted_iota(jnp.int32, (1, 2 * QLEN), 1) < QLEN
+    tables = out.shape[0]
+    count = slots[tables - 1, 0]
 
     def some(i, totals):
-        for u in range(unroll):
-            packed = packed_of(i * unroll + u)
-            entry = jnp.where(i * unroll + u < count, packed & 4095, shape[0] * LANES)
-            group = (packed >> 12) & 255
-            doc = packed >> 20
-            query = queries[pl.ds(pl.multiple_of(group * 16, 16), QLEN), :]
-            sims = times_rows(query, held[doc])
-            sims = jnp.where(position < lengths[doc], sims, -jnp.inf)
-            best = jnp.max(sims, axis=1, keepdims=True)
-            total = jnp.sum(best, axis=0, keepdims=True)
-            totals = jnp.where(flat == entry, total, totals)
+        for u in range(0, unroll, 2):
+            left, right, marks, limits = [], [], [], []
+            for v in range(2):
+                s = i * unroll + u + v
+                used = s < count
+                entry = jnp.where(used, slots[s >> 7, s & 127], 0)
+                found = slots[tables + (entry >> 7), entry & 127]
+                query = queries[pl.ds(pl.multiple_of((found & 255) * 16, 16), QLEN), :]
+                doc = found >> 8
+                left.append(jnp.concatenate([query, zero] if v == 0 else [zero, query], axis=1))
+                right.append(held[doc])
+                marks.append(jnp.where(used, entry, -1))
+                limits.append(lengths[doc])
+            sims = times_rows(jnp.concatenate(right, axis=1), jnp.concatenate(left, axis=0))
+            limit = jnp.where(side, limits[0], limits[1])
+            best = jnp.max(jnp.where(position < limit, sims, -jnp.inf), axis=0, keepdims=True)
+            for v in range(2):
+                total = jnp.sum(jnp.where(side if v == 0 else ~side, best, 0.0), axis=1, keepdims=True)
+                totals = jnp.where(flat == marks[v], total, totals)
         return totals
 
     totals = lax.fori_loop(
@@ -554,6 +562,14 @@
         row = jnp.broadcast_to(totals[o : o + 1], shape)
         for h in range(out.shape[1]):
             out[o, h] = row
+
+
+def arrange_kernel(*refs):
+    shares, out = refs[:-1], refs[-1]
+    place = lax.axis_index("head")
+    for k, share in enumerate(shares):
+        count = share.shape[0]
+        out[pl.ds(pl.multiple_of(block_of(place ^ k) * count, 32), count), :] = share[...]
 
 
 def collect_kernel(tiles, out):
@@ -604,7 +620,9 @@
         return lax.ppermute(x, "head", [(i, i ^ k) for i in range(n_head)])
 
     tile = (8, LANES)
-    pieces = {k: over_doc(prompt_cache, k) for k in (4, 6, 2, 1, 3)}
+    pieces = {k: over_doc(prompt_cache, k) for k in (4, 1, 2, 3)}
+    pieces[1], again = lax.optimization_barrier((pieces[1], prompt_cache))
+    pieces[6] = over_doc(again, 6)
     pieces[0] = prompt_cache
     pieces[4], pieces[6], rel_table = lax.optimization_barrier((pieces[4], pieces[6], rel_table))
     pieces[5], pieces[7] = over_doc(pieces[4], 1), over_doc(pieces[6], 1)
@@ -664,8 +682,8 @@
         out_specs=full_specs(1)[0],
         scratch_shapes=[
             pltpu.VMEM(doc_vectors.shape, jnp.bfloat16),
-            pltpu.VMEM(tile, jnp.int32),
-            pltpu.SMEM(tile, jnp.int32),
+            pltpu.VMEM((2 * n_doc, LANES), jnp.int32),
+            pltpu.SMEM((2 * n_doc, LANES), jnp.int32),
             pltpu.SemaphoreType.DMA((8,)),
             pltpu.SemaphoreType.DMA,
         ],
@@ -674,16 +692,16 @@
     )(doc_lengths, queries, doc_vectors)
     back = lax.all_to_all(rated.reshape(-1, LANES), ("doc", "head"), 0, 0, tiled=True)
 
-    place = lax.axis_index("head")
-    own_y, own_c = place // 2, place % 2
-    y_rows = over_head(single, 2)
-    pair = jnp.where(
-        own_y == 0, jnp.concatenate([single, y_rows]), jnp.concatenate([y_rows, single])
-    )
-    core_pair = over_head(pair, 1)
-    query_vectors = jnp.where(
-        own_c == 0, jnp.concatenate([pair, core_pair]), jnp.concatenate([core_pair, pair])
-    )
+    single, _ = lax.optimization_barrier((single, rated))
+    shares = [single] + [over_head(single, k) for k in range(1, n_head)]
+    query_vectors = pl.pallas_call(
+        arrange_kernel,
+        out_shape=jax.ShapeDtypeStruct((rows, emb), jnp.bfloat16),
+        in_specs=full_specs(n_head),
+        out_specs=full_specs(1)[0],
+        compiler_params=params(4),
+        name="arrange",
+    )(*shares)
 
     scores = pl.pallas_call(
         collect_kernel,

time: 88.7 us -> 86.5 us (0.975)
  blocking collectives: 0 us -> 13.6 us
  waiting for transfers between devices: 33.7 us -> 20.2 us
    all_to_all x0 -> x1, blocking collectives: none -> 13.6 us  [body(): queries = lax.all_to_all(vectors, 'doc', 0, 0, tiled=True).reshape(-1, emb)]
    all_to_all x1 -> x0, waiting for transfers between devices: 6.62 us -> none  [body(): queries = lax.all_to_all(vectors, 'doc', 0, 0, tiled=True).reshape(-1, emb)]
    all_to_all x1 -> x0, starting transfers between devices: 5.34 us -> none  [body(): queries = lax.all_to_all(vectors, 'doc', 0, 0, tiled=True).reshape(-1, emb)]
    ppermute x7, waiting for transfers between devices: 6.67 us -> 1.96 us  [over_doc(): return lax.ppermute(x, 'doc', [(i, i ^ k) for i in range(n_doc)])]
    ppermute x7, starting transfers between devices: 10.2 us -> 14.4 us  [over_doc(): return lax.ppermute(x, 'doc', [(i, i ^ k) for i in range(n_doc)])]
    all_to_all x1, waiting for transfers between devices: 6.23 us -> 2.2 us  [body(): lax.all_to_all(rated.reshape(-1, LANES), ('doc', 'head'), 0, 0, tiled=True)]
    ppermute x10 -> x11, waiting for transfers between devices: 14.1 us -> 16 us  [over_head(): return lax.ppermute(x, 'head', [(i, i ^ k) for i in range(n_head)])]
    ppermute x10 -> x11, starting transfers between devices: 6.27 us -> 7.48 us  [over_head(): return lax.ppermute(x, 'head', [(i, i ^ k) for i in range(n_head)])]
  transfers between devices with their start and end apart: 19 -> 19, of which waited for: 8 -> 8; matrix products, arithmetic and copies ran while one was open for 1% -> 0% of each run, Pallas kernels for 20% -> 13%
where the time goes in v4:
time: 86.5 us; the launch traced here: 86.6 us
  starting transfers between devices  27.3 us (32%)
  Pallas kernels  20.8 us (24%)
  waiting for transfers between devices  20.2 us (23%)
  blocking collectives  13.6 us (16%)
  local copies, waits for them, and re-layouts  3.82 us (4%)
    ppermute x11, waiting for transfers between devices, over_head(): return lax.ppermute(x, 'head', [(i, i ^ k) for i in range(n_head)])  16 us
    ppermute x7, starting transfers between devices, over_doc(): return lax.ppermute(x, 'doc', [(i, i ^ k) for i in range(n_doc)])  14.4 us
    all_to_all x1, blocking collectives, body(): queries = lax.all_to_all(vectors, 'doc', 0, 0, tiled=True).reshape(-1, emb)  13.6 us
    ppermute x11, starting transfers between devices, over_head(): return lax.ppermute(x, 'head', [(i, i ^ k) for i in range(n_head)])  7.48 us
    pallas_call x1, Pallas kernels, body(): pl.pallas_call(score_kernel, out_shape=jax.ShapeDtypeStruct((n_doc, n_hea...  6.25 us
    pallas_call x1, Pallas kernels, attend(): pl.pallas_call(attend_kernel, out_shape=jax.ShapeDtypeStruct((rows + EXTR...  5.46 us
    all_to_all x1, starting transfers between devices, body(): lax.all_to_all(rated.reshape(-1, LANES), ('doc', 'head'), 0, 0, tiled=True)  5.4 us
    pallas_call x2, Pallas kernels, feed(): pl.pallas_call(kernel, out_shape=outs, in_specs=full_specs(12), out_specs...  4.51 us
  transfers between devices with their start and end apart: 19, of which 8 were waited for; matrix products, arithmetic and copies ran while one was open for 0% of the time, Pallas kernels for 13%

profile of v4, /device:TPU:0, one launch (start us, length us, event | category | flops | bytes accessed | tf_op | source)
XLA Modules:
  0.0 86.6 jit_solution(17022220365134232465)
XLA Ops:
  0.6 3.0 %collective-permute-start.1 = (bf16[2,128,256]{2,1,0:T(8,128)(2,1)}, bf16[2,128,256]{2,1,0:T(8,128)(2,1)S(1)}, u32[]{:S(2)}, u32[]{:S(2)}) collective-permute-start(bf16[2,128,256]{2,1,0:T(8,128)(2,1)} %rest_0_.1), channel_id=1, source_target_pairs={{0,1},{1,0},{2,3},{3,2},{4,5},{5,4},{6,7},{7,6},{8,9},{9,8},{10,11... | collective-permute-start | bytes 393224 | tf_op jit(solution)/shard_map/ppermute | solution.py:617
  3.6 2.6 %collective-permute-start = (bf16[2,128,256]{2,1,0:T(8,128)(2,1)}, bf16[2,128,256]{2,1,0:T(8,128)(2,1)S(1)}, u32[]{:S(2)}, u32[]{:S(2)}) collective-permute-start(bf16[2,128,256]{2,1,0:T(8,128)(2,1)} %rest_0_.1), channel_id=1, source_target_pairs={{0,4},{1,5},{2,6},{3,7},{4,0},{5,1},{6,2},{7,3},{8,12},{9,13},{10,... | collective-permute-start | bytes 393224 | tf_op jit(solution)/shard_map/ppermute | solution.py:617
  6.2 1.1 %collective-permute-done.1.rest_1_ = bf16[2,128,256]{2,1,0:T(8,128)(2,1)S(1)} collective-permute-done((bf16[2,128,256]{2,1,0:T(8,128)(2,1)}, bf16[2,128,256]{2,1,0:T(8,128)(2,1)S(1)}, u32[]{:S(2)}, u32[]{:S(2)}) %collective-permute-start.1) | collective-permute-done | bytes 131104 | tf_op jit(solution)/shard_map/ppermute | solution.py:617
  7.3 3.9 %collective-permute-start.2 = (bf16[2,128,256]{2,1,0:T(8,128)(2,1)}, bf16[2,128,256]{2,1,0:T(8,128)(2,1)S(1)}, u32[]{:S(2)}, u32[]{:S(2)}) collective-permute-start(bf16[2,128,256]{2,1,0:T(8,128)(2,1)} %rest_0_.1), channel_id=1, source_target_pairs={{0,6},{1,7},{2,4},{3,5},{4,2},{5,3},{6,0},{7,1},{8,14},{9,15},{10,... | collective-permute-start | bytes 393224 | tf_op jit(solution)/shard_map/ppermute | solution.py:617
  11.2 1.5 %collective-permute-start.11 = (bf16[256,1024]{1,0:T(8,128)(2,1)}, bf16[256,1024]{1,0:T(8,128)(2,1)S(1)}, u32[]{:S(2)}, u32[]{:S(2)}) collective-permute-start(bf16[256,1024]{1,0:T(8,128)(2,1)} %w0.3), channel_id=1, source_target_pairs={{0,16},{8,24},{16,0},{24,8},{1,17},{9,25},{17,1},{25,9},{2,18},{10... | collective-permute-start | bytes 1572872 | tf_op jit(solution)/shard_map/ppermute | solution.py:620
  12.7 3.0 %collective-permute-start.4 = (bf16[2,128,256]{2,1,0:T(8,128)(2,1)}, bf16[2,128,256]{2,1,0:T(8,128)(2,1)S(1)}, u32[]{:S(2)}, u32[]{:S(2)}) collective-permute-start(bf16[2,128,256]{2,1,0:T(8,128)(2,1)} %rest_0_.1), channel_id=1, source_target_pairs={{0,3},{1,2},{2,1},{3,0},{4,7},{5,6},{6,5},{7,4},{8,11},{9,10},{10,... | collective-permute-start | bytes 393224 | tf_op jit(solution)/shard_map/ppermute | solution.py:617
  15.7 0.8 collective-permute-done.rest_4_
  16.5 0.0 collective-permute-done.2.rest_6_
  16.5 0.9 %collective-permute-start.5 = (bf16[2,128,256]{2,1,0:T(8,128)(2,1)S(1)}, bf16[2,128,256]{2,1,0:T(8,128)(2,1)S(1)}, u32[]{:S(2)}, u32[]{:S(2)}) collective-permute-start(bf16[2,128,256]{2,1,0:T(8,128)(2,1)S(1)} %collective-permute-done.rest_4_), channel_id=1, source_target_pairs={{0,1},{1,0},{2,3},{3,2},{4,5},{5,4},{6,7},{7,6},{8,9},{9,8},{10,11... | collective-permute-start | bytes 393224 | tf_op jit(solution)/shard_map/ppermute | solution.py:617
  17.4 1.2 %collective-permute-start.6 = (bf16[2,128,256]{2,1,0:T(8,128)(2,1)S(1)}, bf16[2,128,256]{2,1,0:T(8,128)(2,1)S(1)}, u32[]{:S(2)}, u32[]{:S(2)}) collective-permute-start(bf16[2,128,256]{2,1,0:T(8,128)(2,1)S(1)} %collective-permute-done.2.rest_6_), channel_id=1, source_target_pairs={{0,1},{1,0},{2,3},{3,2},{4,5},{5,4},{6,7},{7,6},{8,9},{9,8},{10,11... | collective-permute-start | bytes 393224 | tf_op jit(solution)/shard_map/ppermute | solution.py:617
  18.5 1.1 %copy-done.2 = bf16[384,1024]{1,0:T(8,128)(2,1)S(1)} copy-done((bf16[384,1024]{1,0:T(8,128)(2,1)S(1)}, bf16[384,1024]{1,0:T(8,128)(2,1)}, u32[]{:S(2)}) %copy-start.2) | copy-done | bytes 786456
  19.7 1.4 %copy-done.8 = bf16[1024,3,256]{2,0,1:T(8,128)(2,1)S(1)} copy-done((bf16[1024,3,256]{2,0,1:T(8,128)(2,1)S(1)}, bf16[1024,3,256]{2,0,1:T(8,128)(2,1)}, u32[]{:S(2)}) %copy-start.8) | copy-done | bytes 1572888
  21.1 1.2 %copy-done.9 = bf16[512,1024]{1,0:T(8,128)(2,1)S(1)} copy-done((bf16[512,1024]{1,0:T(8,128)(2,1)S(1)}, bf16[512,1024]{1,0:T(8,128)(2,1)}, u32[]{:S(2)}) %copy-start.9) | copy-done | bytes 1048600
  22.3 2.5 %prepare.1 = (bf16[384,768]{1,0:T(8,128)(2,1)S(1)}, f32[12,128,128]{2,1,0:T(8,128)S(1)}, bf16[512,256]{1,0:T(8,128)(2,1)S(1)}) custom-call(bf16[384,1024]{1,0:T(8,128)(2,1)S(1)} %copy-done.2, bf16[3,1024,256]{2,1,0:T(8,128)(2,1)S(1)} %bitcast.12, bf16[512,1024]{1,0:T(8,128)(2,1)S(1)} %copy-done.9), custom_call_target="tpu_custom_call" | custom-call | flops 4194304000 | bytes 4194304 | tf_op jit(solution)/shard_map/prepare/pallas_call | solution.py:255
  24.9 0.0 collective-permute-done.3.rest_2_
  24.9 0.1 collective-permute-start.10
  25.0 0.0 collective-permute-done.11.w2
  25.0 0.5 collective-permute-start.12
  25.5 0.0 collective-permute-done.5.rest_5_
  25.5 0.0 collective-permute-done.6.rest_7_
  25.5 0.0 copy-start
  25.5 0.0 copy-start.1
  25.5 0.0 copy-start.3
  25.5 0.0 copy-start.6
  25.6 5.5 %attend.1.a0 = bf16[400,256]{1,0:T(8,128)(2,1)S(1)} custom-call(s32[12]{0:T(128)S(1)} %copy-done.12, bf16[384,768]{1,0:T(8,128)(2,1)S(1)} %get-tuple-element.17.qkv, f32[12,128,128]{2,1,0:T(8,128)S(1)} %get-tuple-element.18.base, bf16[512,256]{1,0:T(8,128)(2,1)S(1)} %get-tuple-element.19.rel_q_heads, s32[8,12]{1,0:T(8,128)S(1)} %bitcast.13, ...), custom_call_target="tpu_custom_call" | custom-call | flops 2097152000 | bytes 2097152 | tf_op jit(solution)/shard_map/attend/pallas_call | solution.py:344
  31.0 1.6 %collective-permute-start.8 = (bf16[400,256]{1,0:T(8,128)(2,1)S(1)}, bf16[400,256]{1,0:T(8,128)(2,1)S(1)}, u32[]{:S(2)}, u32[]{:S(2)}) collective-permute-start(bf16[400,256]{1,0:T(8,128)(2,1)S(1)} %attend.1.a0), channel_id=1, source_target_pairs={{0,16},{8,24},{16,0},{24,8},{1,17},{9,25},{17,1},{25,9},{2,18},{10... | collective-permute-start | bytes 614408 | tf_op jit(solution)/shard_map/ppermute | solution.py:620
  32.6 0.0 collective-permute-start.7
  32.6 5.5 %collective-permute-done.8.a2 = bf16[400,256]{1,0:T(8,128)(2,1)S(1)} collective-permute-done((bf16[400,256]{1,0:T(8,128)(2,1)S(1)}, bf16[400,256]{1,0:T(8,128)(2,1)S(1)}, u32[]{:S(2)}, u32[]{:S(2)}) %collective-permute-start.8) | collective-permute-done | bytes 204832 | tf_op jit(solution)/shard_map/ppermute | solution.py:620
  38.2 1.4 %collective-permute-done.9.a3 = bf16[400,256]{1,0:T(8,128)(2,1)S(1)} collective-permute-done((bf16[400,256]{1,0:T(8,128)(2,1)S(1)}, bf16[400,256]{1,0:T(8,128)(2,1)S(1)}, u32[]{:S(2)}, u32[]{:S(2)}) %collective-permute-start.9) | collective-permute-done | bytes 204832 | tf_op jit(solution)/shard_map/ppermute | solution.py:620
  39.6 2.2 %feed_other.1 = bf16[192,1024]{1,0:T(8,128)(2,1)S(1)} custom-call(bf16[400,256]{1,0:T(8,128)(2,1)S(1)} %attend.1.a0, bf16[400,256]{1,0:T(8,128)(2,1)S(1)} %collective-permute-done.7.a1, bf16[400,256]{1,0:T(8,128)(2,1)S(1)} %collective-permute-done.8.a2, bf16[400,256]{1,0:T(8,128)(2,1)S(1)} %collective-permute-done.9.a3, bf16[256,1024]{1,0:T(8,128)(2,1)S(1)} %copy-done.4, ...), custom_call_target="tpu_custom_call" | custom-call | flops 1677721600 | bytes 6291456 | tf_op jit(solution)/shard_map/feed_other/pallas_call | solution.py:412
  41.9 0.0 copy-start.5
  41.9 0.0 copy-start.7
  41.9 0.2 collective-permute-start.13
  42.1 2.3 %feed_own.1 = (f32[96,1024]{1,0:T(8,128)S(1)}, f32[96,1024]{1,0:T(8,128)S(1)}) custom-call(bf16[400,256]{1,0:T(8,128)(2,1)S(1)} %attend.1.a0, bf16[400,256]{1,0:T(8,128)(2,1)S(1)} %collective-permute-done.7.a1, bf16[400,256]{1,0:T(8,128)(2,1)S(1)} %collective-permute-done.8.a2, bf16[400,256]{1,0:T(8,128)(2,1)S(1)} %collective-permute-done.9.a3, ...), custom_call_target="tpu_custom_call" | custom-call | flops 1677721600 | bytes 6291456 | tf_op jit(solution)/shard_map/feed_own/pallas_call | solution.py:412
  44.4 0.1 fold.1
  44.5 1.6 %collective-permute-start.14 = (bf16[96,1024]{1,0:T(8,128)(2,1)S(1)}, bf16[96,1024]{1,0:T(8,128)(2,1)S(1)}, u32[]{:S(2)}, u32[]{:S(2)}) collective-permute-start(bf16[96,1024]{1,0:T(8,128)(2,1)S(1)} %fold.1), channel_id=1, source_target_pairs={{0,16},{8,24},{16,0},{24,8},{1,17},{9,25},{17,1},{25,9},{2,18},{10... | collective-permute-start | bytes 589832 | tf_op jit(solution)/shard_map/ppermute | solution.py:620
  46.1 5.6 %collective-permute-done.14.from_y = bf16[96,1024]{1,0:T(8,128)(2,1)S(1)} collective-permute-done((bf16[96,1024]{1,0:T(8,128)(2,1)S(1)}, bf16[96,1024]{1,0:T(8,128)(2,1)S(1)}, u32[]{:S(2)}, u32[]{:S(2)}) %collective-permute-start.14) | collective-permute-done | bytes 196640 | tf_op jit(solution)/shard_map/ppermute | solution.py:620
  51.7 0.5 project.1
  52.2 13.6 %all_to_all.14 = bf16[8,112,128]{2,1,0:T(8,128)(2,1)} all-to-all(bf16[8,112,128]{2,1,0:T(8,128)(2,1)S(1)} %get-tuple-element.26), channel_id=1, replica_groups=mesh['head'=4,'doc'=8] {'doc'}, dimensions={0} | all-to-all | bytes 458752 | tf_op jit(solution)/shard_map/all_to_all | solution.py:676
  65.9 6.2 %rate.1 = f32[8,4,8,128]{3,2,1,0:T(8,128)} custom-call(s32[64]{0:T(128)} %lengths.1, bf16[896,128]{1,0:T(8,128)(2,1)} %bitcast.14, bf16[64,256,128]{2,1,0:T(8,128)(2,1)} %docs.1), custom_call_target="tpu_custom_call" | custom-call | tf_op jit(solution)/shard_map/rate/pallas_call | solution.py:678
  72.1 5.4 %all-to-all-start.1 = ((f32[32,8,128]{2,1,0:T(8,128)}), f32[32,8,128]{2,1,0:T(8,128)S(1)}, u32[]{:S(2)}, u32[]{:S(2)}) async-start(f32[32,8,128]{2,1,0:T(8,128)} %bitcast.15), calls=%async_computation.1 | async-start | bytes 262144 | tf_op jit(solution)/shard_map/all_to_all | solution.py:693
  77.5 0.3 collective-permute-start.15
  77.8 1.7 %collective-permute-start.16 = (bf16[96,128]{1,0:T(8,128)(2,1)S(1)}, bf16[96,128]{1,0:T(8,128)(2,1)S(1)}, u32[]{:S(2)}, u32[]{:S(2)}) collective-permute-start(bf16[96,128]{1,0:T(8,128)(2,1)S(1)} %get-tuple-element.27.refs_0_), channel_id=1, source_target_pairs={{0,16},{8,24},{16,0},{24,8},{1,17},{9,25},{17,1},{25,9},{2,18},{10... | collective-permute-start | bytes 73736 | tf_op jit(solution)/shard_map/ppermute | solution.py:620
  79.5 2.2 %collective-permute-done.16.refs_2_ = bf16[96,128]{1,0:T(8,128)(2,1)S(1)} collective-permute-done((bf16[96,128]{1,0:T(8,128)(2,1)S(1)}, bf16[96,128]{1,0:T(8,128)(2,1)S(1)}, u32[]{:S(2)}, u32[]{:S(2)}) %collective-permute-start.16) | collective-permute-done | bytes 24608 | tf_op jit(solution)/shard_map/ppermute | solution.py:620
  81.8 1.1 %collective-permute-done.17.refs_3_ = bf16[96,128]{1,0:T(8,128)(2,1)S(1)} collective-permute-done((bf16[96,128]{1,0:T(8,128)(2,1)S(1)}, bf16[96,128]{1,0:T(8,128)(2,1)S(1)}, u32[]{:S(2)}, u32[]{:S(2)}) %collective-permute-start.17) | collective-permute-done | bytes 24608 | tf_op jit(solution)/shard_map/ppermute | solution.py:620
  82.9 0.7 arrange.1
  83.5 2.2 %all-to-all-done.1 = f32[32,8,128]{2,1,0:T(8,128)S(1)} async-done(((f32[32,8,128]{2,1,0:T(8,128)}), f32[32,8,128]{2,1,0:T(8,128)S(1)}, u32[]{:S(2)}, u32[]{:S(2)}) %all-to-all-start.1) | async-done | bytes 131104 | tf_op jit(solution)/shard_map/all_to_all | solution.py:693
  85.8 0.8 collect.1
  (26 shorter events, 0.1 us)
Async XLA Ops:
  0.6 6.7 %collective-permute-start.1 = (bf16[2,128,256]{2,1,0:T(8,128)(2,1)}, bf16[2,128,256]{2,1,0:T(8,128)(2,1)S(1)}, u32[]{:S(2)}, u32[]{:S(2)}) collective-permute-start(bf16[2,128,256]{2,1,0:T(8,128)(2,1)} %rest_0_.1), channel_id=1, source_target_pairs={{0,1},{1,0},{2,3},{3,2},{4,5},{5,4},{6,7},{7,6},{8,9},{9,8},{10,11... | collective-permute-start | bytes 393224 | tf_op jit(solution)/shard_map/ppermute | solution.py:617
  3.6 12.9 %collective-permute-start = (bf16[2,128,256]{2,1,0:T(8,128)(2,1)}, bf16[2,128,256]{2,1,0:T(8,128)(2,1)S(1)}, u32[]{:S(2)}, u32[]{:S(2)}) collective-permute-start(bf16[2,128,256]{2,1,0:T(8,128)(2,1)} %rest_0_.1), channel_id=1, source_target_pairs={{0,4},{1,5},{2,6},{3,7},{4,0},{5,1},{6,2},{7,3},{8,12},{9,13},{10,... | collective-permute-start | bytes 393224 | tf_op jit(solution)/shard_map/ppermute | solution.py:617
  7.3 9.2 %collective-permute-start.2 = (bf16[2,128,256]{2,1,0:T(8,128)(2,1)}, bf16[2,128,256]{2,1,0:T(8,128)(2,1)S(1)}, u32[]{:S(2)}, u32[]{:S(2)}) collective-permute-start(bf16[2,128,256]{2,1,0:T(8,128)(2,1)} %rest_0_.1), channel_id=1, source_target_pairs={{0,6},{1,7},{2,4},{3,5},{4,2},{5,3},{6,0},{7,1},{8,14},{9,15},{10,... | collective-permute-start | bytes 393224 | tf_op jit(solution)/shard_map/ppermute | solution.py:617
  11.2 13.8 %collective-permute-start.11 = (bf16[256,1024]{1,0:T(8,128)(2,1)}, bf16[256,1024]{1,0:T(8,128)(2,1)S(1)}, u32[]{:S(2)}, u32[]{:S(2)}) collective-permute-start(bf16[256,1024]{1,0:T(8,128)(2,1)} %w0.3), channel_id=1, source_target_pairs={{0,16},{8,24},{16,0},{24,8},{1,17},{9,25},{17,1},{25,9},{2,18},{10... | collective-permute-start | bytes 1572872 | tf_op jit(solution)/shard_map/ppermute | solution.py:620
  12.7 12.2 %collective-permute-start.3 = (bf16[2,128,256]{2,1,0:T(8,128)(2,1)}, bf16[2,128,256]{2,1,0:T(8,128)(2,1)S(1)}, u32[]{:S(2)}, u32[]{:S(2)}) collective-permute-start(bf16[2,128,256]{2,1,0:T(8,128)(2,1)} %rest_0_.1), channel_id=1, source_target_pairs={{0,2},{1,3},{2,0},{3,1},{4,6},{5,7},{6,4},{7,5},{8,10},{9,11},{10,... | collective-permute-start | bytes 393224 | tf_op jit(solution)/shard_map/ppermute | solution.py:617
  12.7 12.8 %collective-permute-start.4 = (bf16[2,128,256]{2,1,0:T(8,128)(2,1)}, bf16[2,128,256]{2,1,0:T(8,128)(2,1)S(1)}, u32[]{:S(2)}, u32[]{:S(2)}) collective-permute-start(bf16[2,128,256]{2,1,0:T(8,128)(2,1)} %rest_0_.1), channel_id=1, source_target_pairs={{0,3},{1,2},{2,1},{3,0},{4,7},{5,6},{6,5},{7,4},{8,11},{9,10},{10,... | collective-permute-start | bytes 393224 | tf_op jit(solution)/shard_map/ppermute | solution.py:617
  16.5 9.0 %collective-permute-start.5 = (bf16[2,128,256]{2,1,0:T(8,128)(2,1)S(1)}, bf16[2,128,256]{2,1,0:T(8,128)(2,1)S(1)}, u32[]{:S(2)}, u32[]{:S(2)}) collective-permute-start(bf16[2,128,256]{2,1,0:T(8,128)(2,1)S(1)} %collective-permute-done.rest_4_), channel_id=1, source_target_pairs={{0,1},{1,0},{2,3},{3,2},{4,5},{5,4},{6,7},{7,6},{8,9},{9,8},{10,11... | collective-permute-start | bytes 393224 | tf_op jit(solution)/shard_map/ppermute | solution.py:617
  17.4 8.1 %collective-permute-start.6 = (bf16[2,128,256]{2,1,0:T(8,128)(2,1)S(1)}, bf16[2,128,256]{2,1,0:T(8,128)(2,1)S(1)}, u32[]{:S(2)}, u32[]{:S(2)}) collective-permute-start(bf16[2,128,256]{2,1,0:T(8,128)(2,1)S(1)} %collective-permute-done.2.rest_6_), channel_id=1, source_target_pairs={{0,1},{1,0},{2,3},{3,2},{4,5},{5,4},{6,7},{7,6},{8,9},{9,8},{10,11... | collective-permute-start | bytes 393224 | tf_op jit(solution)/shard_map/ppermute | solution.py:617
  18.5 1.1 %copy-start.2 = (bf16[384,1024]{1,0:T(8,128)(2,1)S(1)}, bf16[384,1024]{1,0:T(8,128)(2,1)}, u32[]{:S(2)}) copy-start(bf16[384,1024]{1,0:T(8,128)(2,1)} %tokens.5) | copy-start | bytes 2359300
  19.7 1.4 %copy-start.8 = (bf16[1024,3,256]{2,0,1:T(8,128)(2,1)S(1)}, bf16[1024,3,256]{2,0,1:T(8,128)(2,1)}, u32[]{:S(2)}) copy-start(bf16[1024,3,256]{2,0,1:T(8,128)(2,1)} %param.15) | copy-start | bytes 4718596
  21.1 1.2 %copy-start.9 = (bf16[512,1024]{1,0:T(8,128)(2,1)S(1)}, bf16[512,1024]{1,0:T(8,128)(2,1)}, u32[]{:S(2)}) copy-start(bf16[512,1024]{1,0:T(8,128)(2,1)} %rel_table) | copy-start | bytes 3145732
  22.3 2.6 %copy-start.4 = (bf16[256,1024]{1,0:T(8,128)(2,1)S(1)}, bf16[256,1024]{1,0:T(8,128)(2,1)}, u32[]{:S(2)}) copy-start(bf16[256,1024]{1,0:T(8,128)(2,1)} %w0.3) | copy-start | bytes 1572868
  22.3 3.2 %copy-start.10 = (bf16[2,128,256]{2,1,0:T(8,128)(2,1)S(1)}, bf16[2,128,256]{2,1,0:T(8,128)(2,1)}, u32[]{:S(2)}) copy-start(bf16[2,128,256]{2,1,0:T(8,128)(2,1)} %rest_0_.1) | copy-start | bytes 393220
  22.3 3.2 %copy-start.11 = (s32[12,8]{0,1:T(8,128)S(1)}, s32[12,8]{0,1:T(8,128)}, u32[]{:S(2)}) copy-start(s32[12,8]{0,1:T(8,128)} %param.27) | copy-start | bytes 1156
  22.3 3.2 %copy-start.12 = (s32[12]{0:T(128)S(1)}, s32[12]{0:T(128)}, u32[]{:S(2)}) copy-start(s32[12]{0:T(128)} %group_ids.1) | copy-start | bytes 148
  24.9 13.3 %collective-permute-start.10 = (bf16[256,1024]{1,0:T(8,128)(2,1)S(1)}, bf16[256,1024]{1,0:T(8,128)(2,1)S(1)}, u32[]{:S(2)}, u32[]{:S(2)}) collective-permute-start(bf16[256,1024]{1,0:T(8,128)(2,1)S(1)} %copy-done.4), channel_id=1, source_target_pairs={{0,8},{8,0},{16,24},{24,16},{1,9},{9,1},{17,25},{25,17},{2,10},{10... | collective-permute-start | bytes 1572872 | tf_op jit(solution)/shard_map/ppermute | solution.py:620
  25.0 14.6 %collective-permute-start.12 = (bf16[256,1024]{1,0:T(8,128)(2,1)S(1)}, bf16[256,1024]{1,0:T(8,128)(2,1)S(1)}, u32[]{:S(2)}, u32[]{:S(2)}) collective-permute-start(bf16[256,1024]{1,0:T(8,128)(2,1)S(1)} %collective-permute-done.11.w2), channel_id=1, source_target_pairs={{0,8},{8,0},{16,24},{24,16},{1,9},{9,1},{17,25},{25,17},{2,10},{10... | collective-permute-start | bytes 1572872 | tf_op jit(solution)/shard_map/ppermute | solution.py:620
  25.5 14.1 %copy-start = (bf16[1024,1024]{1,0:T(8,128)(2,1)S(1)}, bf16[1024,1024]{1,0:T(8,128)(2,1)}, u32[]{:S(2)}) copy-start(bf16[1024,1024]{1,0:T(8,128)(2,1)} %w_up.3) | copy-start | bytes 6291460
  25.5 14.1 %copy-start.1 = (bf16[1024,1024]{1,0:T(8,128)(2,1)S(1)}, bf16[1024,1024]{1,0:T(8,128)(2,1)}, u32[]{:S(2)}) copy-start(bf16[1024,1024]{1,0:T(8,128)(2,1)} %w_down.3) | copy-start | bytes 6291460
  25.5 14.1 %copy-start.3 = (bf16[384,1024]{1,0:T(8,128)(2,1)S(1)}, bf16[384,1024]{1,0:T(8,128)(2,1)}, u32[]{:S(2)}) copy-start(bf16[384,1024]{1,0:T(8,128)(2,1)} %tokens.5) | copy-start | bytes 2359300
  25.5 14.1 %copy-start.6 = (f32[1024]{0:T(1024)S(1)}, f32[1024]{0:T(1024)}, u32[]{:S(2)}) copy-start(f32[1024]{0:T(1024)} %param.19) | copy-start | bytes 12292
  31.0 7.1 %collective-permute-start.8 = (bf16[400,256]{1,0:T(8,128)(2,1)S(1)}, bf16[400,256]{1,0:T(8,128)(2,1)S(1)}, u32[]{:S(2)}, u32[]{:S(2)}) collective-permute-start(bf16[400,256]{1,0:T(8,128)(2,1)S(1)} %attend.1.a0), channel_id=1, source_target_pairs={{0,16},{8,24},{16,0},{24,8},{1,17},{9,25},{17,1},{25,9},{2,18},{10... | collective-permute-start | bytes 614408 | tf_op jit(solution)/shard_map/ppermute | solution.py:620
  32.6 5.6 %collective-permute-start.7 = (bf16[400,256]{1,0:T(8,128)(2,1)S(1)}, bf16[400,256]{1,0:T(8,128)(2,1)S(1)}, u32[]{:S(2)}, u32[]{:S(2)}) collective-permute-start(bf16[400,256]{1,0:T(8,128)(2,1)S(1)} %attend.1.a0), channel_id=1, source_target_pairs={{0,8},{8,0},{16,24},{24,16},{1,9},{9,1},{17,25},{25,17},{2,10},{10... | collective-permute-start | bytes 614408 | tf_op jit(solution)/shard_map/ppermute | solution.py:620
  38.2 1.5 %collective-permute-start.9 = (bf16[400,256]{1,0:T(8,128)(2,1)S(1)}, bf16[400,256]{1,0:T(8,128)(2,1)S(1)}, u32[]{:S(2)}, u32[]{:S(2)}) collective-permute-start(bf16[400,256]{1,0:T(8,128)(2,1)S(1)} %collective-permute-done.8.a2), channel_id=1, source_target_pairs={{0,8},{8,0},{16,24},{24,16},{1,9},{9,1},{17,25},{25,17},{2,10},{10... | collective-permute-start | bytes 614408 | tf_op jit(solution)/shard_map/ppermute | solution.py:620
  41.9 9.8 %copy-start.5 = (bf16[1024,128]{1,0:T(8,128)(2,1)S(1)}, bf16[1024,128]{1,0:T(8,128)(2,1)}, u32[]{:S(2)}) copy-start(bf16[1024,128]{1,0:T(8,128)(2,1)} %w_proj.1) | copy-start | bytes 786436
  41.9 9.8 %copy-start.7 = (f32[1024]{0:T(1024)S(1)}, f32[1024]{0:T(1024)}, u32[]{:S(2)}) copy-start(f32[1024]{0:T(1024)} %param.20) | copy-start | bytes 12292
  41.9 2.5 %collective-permute-start.13 = (bf16[192,1024]{1,0:T(8,128)(2,1)S(1)}, bf16[192,1024]{1,0:T(8,128)(2,1)S(1)}, u32[]{:S(2)}, u32[]{:S(2)}) collective-permute-start(bf16[192,1024]{1,0:T(8,128)(2,1)S(1)} %feed_other.1), channel_id=1, source_target_pairs={{0,8},{8,0},{16,24},{24,16},{1,9},{9,1},{17,25},{25,17},{2,10},{10... | collective-permute-start | bytes 1179656 | tf_op jit(solution)/shard_map/ppermute | solution.py:620
  44.5 7.3 %collective-permute-start.14 = (bf16[96,1024]{1,0:T(8,128)(2,1)S(1)}, bf16[96,1024]{1,0:T(8,128)(2,1)S(1)}, u32[]{:S(2)}, u32[]{:S(2)}) collective-permute-start(bf16[96,1024]{1,0:T(8,128)(2,1)S(1)} %fold.1), channel_id=1, source_target_pairs={{0,16},{8,24},{16,0},{24,8},{1,17},{9,25},{17,1},{25,9},{2,18},{10... | collective-permute-start | bytes 589832 | tf_op jit(solution)/shard_map/ppermute | solution.py:620
  72.1 13.6 %all-to-all-start.1 = ((f32[32,8,128]{2,1,0:T(8,128)}), f32[32,8,128]{2,1,0:T(8,128)S(1)}, u32[]{:S(2)}, u32[]{:S(2)}) async-start(f32[32,8,128]{2,1,0:T(8,128)} %bitcast.15), calls=%async_computation.1 | async-start | bytes 262144 | tf_op jit(solution)/shard_map/all_to_all | solution.py:693
  77.5 2.0 %collective-permute-start.15 = (bf16[96,128]{1,0:T(8,128)(2,1)S(1)}, bf16[96,128]{1,0:T(8,128)(2,1)S(1)}, u32[]{:S(2)}, u32[]{:S(2)}) collective-permute-start(bf16[96,128]{1,0:T(8,128)(2,1)S(1)} %get-tuple-element.27.refs_0_), channel_id=1, source_target_pairs={{0,8},{8,0},{16,24},{24,16},{1,9},{9,1},{17,25},{25,17},{2,10},{10... | collective-permute-start | bytes 73736 | tf_op jit(solution)/shard_map/ppermute | solution.py:620
  77.8 3.9 %collective-permute-start.16 = (bf16[96,128]{1,0:T(8,128)(2,1)S(1)}, bf16[96,128]{1,0:T(8,128)(2,1)S(1)}, u32[]{:S(2)}, u32[]{:S(2)}) collective-permute-start(bf16[96,128]{1,0:T(8,128)(2,1)S(1)} %get-tuple-element.27.refs_0_), channel_id=1, source_target_pairs={{0,16},{8,24},{16,0},{24,8},{1,17},{9,25},{17,1},{25,9},{2,18},{10... | collective-permute-start | bytes 73736 | tf_op jit(solution)/shard_map/ppermute | solution.py:620
  79.5 3.4 %collective-permute-start.17 = (bf16[96,128]{1,0:T(8,128)(2,1)S(1)}, bf16[96,128]{1,0:T(8,128)(2,1)S(1)}, u32[]{:S(2)}, u32[]{:S(2)}) collective-permute-start(bf16[96,128]{1,0:T(8,128)(2,1)S(1)} %get-tuple-element.27.refs_0_), channel_id=1, source_target_pairs={{0,24},{8,16},{16,8},{24,0},{1,25},{9,17},{17,9},{25,1},{2,26},{10... | collective-permute-start | bytes 73736 | tf_op jit(solution)/shard_map/ppermute | solution.py:620

commit v5 on v4

--- a/solution.py
+++ b/solution.py
@@ -162,6 +162,10 @@
     return [pl.BlockSpec(memory_space=pltpu.VMEM)] * count
 
 
+def far(x):
+    return pltpu.with_memory_space_constraint(x, pltpu.HBM)
+
+
 def params(mib):
     return pltpu.CompilerParams(vmem_limit_bytes=mib * MIB)
 
@@ -189,19 +193,28 @@
     return turned
 
 
-def prepare_kernel(tokens, weight, rel_table, qkv, base, rel_q_heads, q_heads, query_rel, key_rel):
+def prepare_kernel(
+    tokens_far, weight_far, rel_table, qkv, base, rel_q_heads, q_heads, query_rel, key_rel, *scratch
+):
+    tokens, weight, rel_rows, arrived = scratch
+    rel_far = rel_table.at[pl.ds(RELS // 2 - PLEN - QLEN, rel_rows.shape[0])]
+    copies = [pltpu.make_async_copy(tokens_far, tokens, arrived.at[0])]
+    copies += [pltpu.make_async_copy(weight_far.at[i], weight.at[i], arrived.at[1 + i]) for i in range(3)]
+    copies += [pltpu.make_async_copy(rel_far, rel_rows, arrived.at[4])]
+    for copy in copies:
+        copy.start()
+    copies[0].wait()
     width = weight.shape[2]
     heads = width // HD
     for i in range(3):
+        copies[1 + i].wait()
         qkv[:, i * width : (i + 1) * width] = jnp.dot(
             tokens[...], weight[i], preferred_element_type=jnp.float32
         ).astype(jnp.bfloat16)
-    count = 2 * (PLEN + QLEN)
-    low = RELS // 2 - PLEN - QLEN
+    count = rel_rows.shape[0]
+    copies[4].wait()
     rel = [
-        jnp.dot(
-            rel_table[low : low + count, :], weight[i], preferred_element_type=jnp.float32
-        ).astype(jnp.bfloat16)
+        jnp.dot(rel_rows[...], weight[i], preferred_element_type=jnp.float32).astype(jnp.bfloat16)
         for i in range(2)
     ]
     both = lax.broadcasted_iota(jnp.int32, (LANES, count), 0) + lax.broadcasted_iota(
@@ -259,17 +272,21 @@
             jax.ShapeDtypeStruct((rows // QLEN, heads * QLEN, LANES), jnp.float32),
             jax.ShapeDtypeStruct((heads * LANES, width), jnp.bfloat16),
         ],
-        in_specs=full_specs(3),
+        in_specs=[pl.BlockSpec(memory_space=pltpu.HBM)] * 3,
         out_specs=full_specs(3),
         scratch_shapes=[
             pltpu.VMEM((rows * heads, width), jnp.bfloat16),
             pltpu.VMEM((rows * heads, LANES), jnp.float32),
             pltpu.VMEM((rows, heads * LANES), jnp.float32),
+            pltpu.VMEM(tokens.shape, jnp.bfloat16),
+            pltpu.VMEM(weight.shape, jnp.bfloat16),
+            pltpu.VMEM((2 * (PLEN + QLEN), rel_table.shape[1]), jnp.bfloat16),
+            pltpu.SemaphoreType.DMA((5,)),
         ],
-        compiler_params=params(12),
+        compiler_params=params(16),
         cost_estimate=pl.CostEstimate(flops=4000 * MIB, bytes_accessed=4 * MIB, transcendentals=0),
         name="prepare",
-    )(tokens, weight, rel_table)
+    )(far(tokens), far(weight), far(rel_table))
 
 
 def attend_kernel(group_ids, qkv, base, rel_q_heads, columns, *rest):
@@ -620,12 +637,10 @@
         return lax.ppermute(x, "head", [(i, i ^ k) for i in range(n_head)])
 
     tile = (8, LANES)
-    pieces = {k: over_doc(prompt_cache, k) for k in (4, 1, 2, 3)}
-    pieces[1], again = lax.optimization_barrier((pieces[1], prompt_cache))
-    pieces[6] = over_doc(again, 6)
+    pieces = {k: over_doc(prompt_cache, k) for k in (6, 5, 4, 3, 1, 2)}
     pieces[0] = prompt_cache
-    pieces[4], pieces[6], rel_table = lax.optimization_barrier((pieces[4], pieces[6], rel_table))
-    pieces[5], pieces[7] = over_doc(pieces[4], 1), over_doc(pieces[6], 1)
+    pieces[6], rel_table = lax.optimization_barrier((pieces[6], rel_table))
+    pieces[7] = over_doc(pieces[6], 1)
     pieces = [pieces[k] for k in range(n_doc)]
     weight = jnp.transpose(w_qkv, (1, 0, 2))
     qkv, base, rel_q_heads = prepare(tokens, weight, rel_table)
@@ -687,9 +702,9 @@
             pltpu.SemaphoreType.DMA((8,)),
             pltpu.SemaphoreType.DMA,
         ],
-        compiler_params=params(56),
+        compiler_params=params(16),
         name="rate",
-    )(doc_lengths, queries, doc_vectors)
+    )(doc_lengths, queries, far(doc_vectors))
     back = lax.all_to_all(rated.reshape(-1, LANES), ("doc", "head"), 0, 0, tiled=True)
 
     single, _ = lax.optimization_barrier((single, rated))

time: 86.5 us -> 82.9 us (0.958)
  local copies, waits for them, and re-layouts: 3.82 us -> 0.06 us
  starting transfers between devices: 27.3 us -> 23.8 us
  waiting for transfers between devices: 20.2 us -> 22.8 us
  Pallas kernels: 20.8 us -> 23 us
  blocking collectives: 13.6 us -> 12.5 us
    unnamed x26 -> x22, local copies, waits for them, and re-layouts: 3.82 us -> 0.06 us
    ppermute x7, waiting for transfers between devices: 1.96 us -> 4.71 us  [over_doc(): return lax.ppermute(x, 'doc', [(i, i ^ k) for i in range(n_doc)])]
    pallas_call x1, Pallas kernels: 2.55 us -> 5.15 us  [prepare(): pl.pallas_call(prepare_kernel, out_shape=[jax.ShapeDtypeStruct((rows, 3 *...]
    ppermute x7, starting transfers between devices: 14.4 us -> 12.5 us  [over_doc(): return lax.ppermute(x, 'doc', [(i, i ^ k) for i in range(n_doc)])]
    ppermute x11, starting transfers between devices: 7.48 us -> 6.27 us  [over_head(): return lax.ppermute(x, 'head', [(i, i ^ k) for i in range(n_head)])]
    all_to_all x1, blocking collectives: 13.6 us -> 12.5 us  [body(): queries = lax.all_to_all(vectors, 'doc', 0, 0, tiled=True).reshape(-1, emb)]
  transfers between devices with their start and end apart: 19 -> 19, of which waited for: 8 -> 9; matrix products, arithmetic and copies ran while one was open for 0% -> 0% of each run, Pallas kernels for 13% -> 16%
where the time goes in v5:
time: 82.9 us; the launch traced here: 83.1 us
  starting transfers between devices  23.8 us (29%)
  Pallas kernels  23 us (28%)
  waiting for transfers between devices  22.8 us (28%)
  blocking collectives  12.5 us (15%)
  between operations  0.84 us (1%)
    ppermute x11, waiting for transfers between devices, over_head(): return lax.ppermute(x, 'head', [(i, i ^ k) for i in range(n_head)])  15.9 us
    all_to_all x1, blocking collectives, body(): queries = lax.all_to_all(vectors, 'doc', 0, 0, tiled=True).reshape(-1, emb)  12.5 us
    ppermute x7, starting transfers between devices, over_doc(): return lax.ppermute(x, 'doc', [(i, i ^ k) for i in range(n_doc)])  12.5 us
    ppermute x11, starting transfers between devices, over_head(): return lax.ppermute(x, 'head', [(i, i ^ k) for i in range(n_head)])  6.27 us
    pallas_call x1, Pallas kernels, body(): pl.pallas_call(score_kernel, out_shape=jax.ShapeDtypeStruct((n_doc, n_hea...  5.83 us
    pallas_call x1, Pallas kernels, attend(): pl.pallas_call(attend_kernel, out_shape=jax.ShapeDtypeStruct((rows + EXTR...  5.46 us
    pallas_call x1, Pallas kernels, prepare(): pl.pallas_call(prepare_kernel, out_shape=[jax.ShapeDtypeStruct((rows, 3 *...  5.15 us
    all_to_all x1, starting transfers between devices, body(): lax.all_to_all(rated.reshape(-1, LANES), ('doc', 'head'), 0, 0, tiled=True)  5.08 us
  transfers between devices with their start and end apart: 19, of which 9 were waited for; matrix products, arithmetic and copies ran while one was open for 0% of the time, Pallas kernels for 16%

profile of v5, /device:TPU:0, one launch (start us, length us, event | category | flops | bytes accessed | tf_op | source)
XLA Modules:
  0.0 83.1 jit_solution(4454795785250703110)
XLA Ops:
  0.6 5.1 %collective-permute-start = (bf16[2,128,256]{2,1,0:T(8,128)(2,1)}, bf16[2,128,256]{2,1,0:T(8,128)(2,1)S(1)}, u32[]{:S(2)}, u32[]{:S(2)}) collective-permute-start(bf16[2,128,256]{2,1,0:T(8,128)(2,1)} %rest_0_.1), channel_id=1, source_target_pairs={{0,6},{1,7},{2,4},{3,5},{4,2},{5,3},{6,0},{7,1},{8,14},{9,15},{10,... | collective-permute-start | bytes 393224 | tf_op jit(solution)/shard_map/ppermute | solution.py:634
  5.7 1.5 %collective-permute-start.1 = (bf16[2,128,256]{2,1,0:T(8,128)(2,1)}, bf16[2,128,256]{2,1,0:T(8,128)(2,1)S(1)}, u32[]{:S(2)}, u32[]{:S(2)}) collective-permute-start(bf16[2,128,256]{2,1,0:T(8,128)(2,1)} %rest_0_.1), channel_id=1, source_target_pairs={{0,1},{1,0},{2,3},{3,2},{4,5},{5,4},{6,7},{7,6},{8,9},{9,8},{10,11... | collective-permute-start | bytes 393224 | tf_op jit(solution)/shard_map/ppermute | solution.py:634
  7.2 0.0 collective-permute-start.2
  7.2 1.5 %collective-permute-start.11 = (bf16[256,1024]{1,0:T(8,128)(2,1)}, bf16[256,1024]{1,0:T(8,128)(2,1)S(1)}, u32[]{:S(2)}, u32[]{:S(2)}) collective-permute-start(bf16[256,1024]{1,0:T(8,128)(2,1)} %w0.3), channel_id=1, source_target_pairs={{0,16},{8,24},{16,0},{24,8},{1,17},{9,25},{17,1},{25,9},{2,18},{10... | collective-permute-start | bytes 1572872 | tf_op jit(solution)/shard_map/ppermute | solution.py:637
  8.8 2.0 %collective-permute-start.3 = (bf16[2,128,256]{2,1,0:T(8,128)(2,1)}, bf16[2,128,256]{2,1,0:T(8,128)(2,1)S(1)}, u32[]{:S(2)}, u32[]{:S(2)}) collective-permute-start(bf16[2,128,256]{2,1,0:T(8,128)(2,1)} %rest_0_.1), channel_id=1, source_target_pairs={{0,3},{1,2},{2,1},{3,0},{4,7},{5,6},{6,5},{7,4},{8,11},{9,10},{10,... | collective-permute-start | bytes 393224 | tf_op jit(solution)/shard_map/ppermute | solution.py:634
  10.8 2.0 %collective-permute-start.4 = (bf16[2,128,256]{2,1,0:T(8,128)(2,1)}, bf16[2,128,256]{2,1,0:T(8,128)(2,1)S(1)}, u32[]{:S(2)}, u32[]{:S(2)}) collective-permute-start(bf16[2,128,256]{2,1,0:T(8,128)(2,1)} %rest_0_.1), channel_id=1, source_target_pairs={{0,4},{1,5},{2,6},{3,7},{4,0},{5,1},{6,2},{7,3},{8,12},{9,13},{10,... | collective-permute-start | bytes 393224 | tf_op jit(solution)/shard_map/ppermute | solution.py:634
  12.7 1.9 %collective-permute-start.5 = (bf16[2,128,256]{2,1,0:T(8,128)(2,1)}, bf16[2,128,256]{2,1,0:T(8,128)(2,1)S(1)}, u32[]{:S(2)}, u32[]{:S(2)}) collective-permute-start(bf16[2,128,256]{2,1,0:T(8,128)(2,1)} %rest_0_.1), channel_id=1, source_target_pairs={{0,5},{1,4},{2,7},{3,6},{4,1},{5,0},{6,3},{7,2},{8,13},{9,12},{10,... | collective-permute-start | bytes 393224 | tf_op jit(solution)/shard_map/ppermute | solution.py:634
  14.6 1.5 %collective-permute-done.2.rest_2_ = bf16[2,128,256]{2,1,0:T(8,128)(2,1)S(1)} collective-permute-done((bf16[2,128,256]{2,1,0:T(8,128)(2,1)}, bf16[2,128,256]{2,1,0:T(8,128)(2,1)S(1)}, u32[]{:S(2)}, u32[]{:S(2)}) %collective-permute-start.2) | collective-permute-done | bytes 131104 | tf_op jit(solution)/shard_map/ppermute | solution.py:634
  16.2 0.0 collective-permute-start.6
  16.2 5.1 %prepare.1 = (bf16[384,768]{1,0:T(8,128)(2,1)S(1)}, f32[12,128,128]{2,1,0:T(8,128)S(1)}, bf16[512,256]{1,0:T(8,128)(2,1)S(1)}) custom-call(bf16[384,1024]{1,0:T(8,128)(2,1)} %tokens.3, bf16[3,1024,256]{2,1,0:T(8,128)(2,1)} %bitcast.15, bf16[512,1024]{1,0:T(8,128)(2,1)} %rel_table), custom_call_target="tpu_custom_call" | custom-call | flops 4194304000 | bytes 4194304 | tf_op jit(solution)/shard_map/prepare/pallas_call | solution.py:268
  21.4 0.1 collective-permute-start.10
  21.4 0.0 collective-permute-done.11.w2
  21.5 0.5 collective-permute-start.12
  21.9 0.8 %collective-permute-done.4.rest_4_ = bf16[2,128,256]{2,1,0:T(8,128)(2,1)S(1)} collective-permute-done((bf16[2,128,256]{2,1,0:T(8,128)(2,1)}, bf16[2,128,256]{2,1,0:T(8,128)(2,1)S(1)}, u32[]{:S(2)}, u32[]{:S(2)}) %collective-permute-start.4) | collective-permute-done | bytes 131104 | tf_op jit(solution)/shard_map/ppermute | solution.py:634
  22.8 2.3 %collective-permute-done.5.rest_5_ = bf16[2,128,256]{2,1,0:T(8,128)(2,1)S(1)} collective-permute-done((bf16[2,128,256]{2,1,0:T(8,128)(2,1)}, bf16[2,128,256]{2,1,0:T(8,128)(2,1)S(1)}, u32[]{:S(2)}, u32[]{:S(2)}) %collective-permute-start.5) | collective-permute-done | bytes 131104 | tf_op jit(solution)/shard_map/ppermute | solution.py:634
  25.1 0.0 collective-permute-done.6.rest_7_
  25.1 0.0 copy-start
  25.1 0.0 copy-start.1
  25.2 0.0 copy-start.2
  25.2 0.0 copy-start.5
  25.2 5.5 %attend.1.a0 = bf16[400,256]{1,0:T(8,128)(2,1)S(1)} custom-call(s32[12]{0:T(128)S(1)} %copy-done.10, bf16[384,768]{1,0:T(8,128)(2,1)S(1)} %get-tuple-element.13.qkv, f32[12,128,128]{2,1,0:T(8,128)S(1)} %get-tuple-element.14.base, bf16[512,256]{1,0:T(8,128)(2,1)S(1)} %get-tuple-element.15.rel_q_heads, s32[8,12]{1,0:T(8,128)S(1)} %bitcast.13, ...), custom_call_target="tpu_custom_call" | custom-call | flops 2097152000 | bytes 2097152 | tf_op jit(solution)/shard_map/attend/pallas_call | solution.py:361
  30.6 1.0 %collective-permute-start.8 = (bf16[400,256]{1,0:T(8,128)(2,1)S(1)}, bf16[400,256]{1,0:T(8,128)(2,1)S(1)}, u32[]{:S(2)}, u32[]{:S(2)}) collective-permute-start(bf16[400,256]{1,0:T(8,128)(2,1)S(1)} %attend.1.a0), channel_id=1, source_target_pairs={{0,16},{8,24},{16,0},{24,8},{1,17},{9,25},{17,1},{25,9},{2,18},{10... | collective-permute-start | bytes 614408 | tf_op jit(solution)/shard_map/ppermute | solution.py:637
  31.6 4.9 %collective-permute-done.8.a2 = bf16[400,256]{1,0:T(8,128)(2,1)S(1)} collective-permute-done((bf16[400,256]{1,0:T(8,128)(2,1)S(1)}, bf16[400,256]{1,0:T(8,128)(2,1)S(1)}, u32[]{:S(2)}, u32[]{:S(2)}) %collective-permute-start.8) | collective-permute-done | bytes 204832 | tf_op jit(solution)/shard_map/ppermute | solution.py:637
  36.5 0.0 collective-permute-start.9
  36.5 0.0 collective-permute-done.7.a1
  36.5 0.0 collective-permute-done.10.w1
  36.5 1.4 %collective-permute-done.9.a3 = bf16[400,256]{1,0:T(8,128)(2,1)S(1)} collective-permute-done((bf16[400,256]{1,0:T(8,128)(2,1)S(1)}, bf16[400,256]{1,0:T(8,128)(2,1)S(1)}, u32[]{:S(2)}, u32[]{:S(2)}) %collective-permute-start.9) | collective-permute-done | bytes 204832 | tf_op jit(solution)/shard_map/ppermute | solution.py:637
  38.0 2.2 %feed_other.1 = bf16[192,1024]{1,0:T(8,128)(2,1)S(1)} custom-call(bf16[400,256]{1,0:T(8,128)(2,1)S(1)} %attend.1.a0, bf16[400,256]{1,0:T(8,128)(2,1)S(1)} %collective-permute-done.7.a1, bf16[400,256]{1,0:T(8,128)(2,1)S(1)} %collective-permute-done.8.a2, bf16[400,256]{1,0:T(8,128)(2,1)S(1)} %collective-permute-done.9.a3, bf16[256,1024]{1,0:T(8,128)(2,1)S(1)} %copy-done.3, ...), custom_call_target="tpu_custom_call" | custom-call | flops 1677721600 | bytes 6291456 | tf_op jit(solution)/shard_map/feed_other/pallas_call | solution.py:429
  40.2 0.0 copy-start.4
  40.2 0.0 copy-start.6
  40.2 0.2 collective-permute-start.13
  40.4 2.3 %feed_own.1 = (f32[96,1024]{1,0:T(8,128)S(1)}, f32[96,1024]{1,0:T(8,128)S(1)}) custom-call(bf16[400,256]{1,0:T(8,128)(2,1)S(1)} %attend.1.a0, bf16[400,256]{1,0:T(8,128)(2,1)S(1)} %collective-permute-done.7.a1, bf16[400,256]{1,0:T(8,128)(2,1)S(1)} %collective-permute-done.8.a2, bf16[400,256]{1,0:T(8,128)(2,1)S(1)} %collective-permute-done.9.a3, ...), custom_call_target="tpu_custom_call" | custom-call | flops 1677721600 | bytes 6291456 | tf_op jit(solution)/shard_map/feed_own/pallas_call | solution.py:429
  42.7 0.0 copy-start.7
  42.8 0.0 collective-permute-done.13.from_core
  42.8 0.1 fold.1
  42.8 1.0 %collective-permute-start.14 = (bf16[96,1024]{1,0:T(8,128)(2,1)S(1)}, bf16[96,1024]{1,0:T(8,128)(2,1)S(1)}, u32[]{:S(2)}, u32[]{:S(2)}) collective-permute-start(bf16[96,1024]{1,0:T(8,128)(2,1)S(1)} %fold.1), channel_id=1, source_target_pairs={{0,16},{8,24},{16,0},{24,8},{1,17},{9,25},{17,1},{25,9},{2,18},{10... | collective-permute-start | bytes 589832 | tf_op jit(solution)/shard_map/ppermute | solution.py:637
  43.9 6.2 %collective-permute-done.14.from_y = bf16[96,1024]{1,0:T(8,128)(2,1)S(1)} collective-permute-done((bf16[96,1024]{1,0:T(8,128)(2,1)S(1)}, bf16[96,1024]{1,0:T(8,128)(2,1)S(1)}, u32[]{:S(2)}, u32[]{:S(2)}) %collective-permute-start.14) | collective-permute-done | bytes 196640 | tf_op jit(solution)/shard_map/ppermute | solution.py:637
  50.1 0.5 project.1
  50.6 12.5 %all_to_all.14 = bf16[8,112,128]{2,1,0:T(8,128)(2,1)S(1)} all-to-all(bf16[8,112,128]{2,1,0:T(8,128)(2,1)S(1)} %get-tuple-element.20), channel_id=1, replica_groups=mesh['head'=4,'doc'=8] {'doc'}, dimensions={0} | all-to-all | bytes 458752 | tf_op jit(solution)/shard_map/all_to_all | solution.py:691
  63.1 5.8 %rate.1 = f32[8,4,8,128]{3,2,1,0:T(8,128)} custom-call(s32[64]{0:T(128)S(1)} %copy-done.7, bf16[896,128]{1,0:T(8,128)(2,1)S(1)} %bitcast.8, bf16[64,256,128]{2,1,0:T(8,128)(2,1)} %docs.1), custom_call_target="tpu_custom_call" | custom-call | tf_op jit(solution)/shard_map/rate/pallas_call | solution.py:693
  69.0 5.1 %all-to-all-start.1 = ((f32[32,8,128]{2,1,0:T(8,128)}), f32[32,8,128]{2,1,0:T(8,128)S(1)}, u32[]{:S(2)}, u32[]{:S(2)}) async-start(f32[32,8,128]{2,1,0:T(8,128)} %bitcast.5), calls=%async_computation.1 | async-start | bytes 262144 | tf_op jit(solution)/shard_map/all_to_all | solution.py:708
  74.1 0.3 collective-permute-start.15
  74.4 1.7 %collective-permute-start.16 = (bf16[96,128]{1,0:T(8,128)(2,1)S(1)}, bf16[96,128]{1,0:T(8,128)(2,1)S(1)}, u32[]{:S(2)}, u32[]{:S(2)}) collective-permute-start(bf16[96,128]{1,0:T(8,128)(2,1)S(1)} %get-tuple-element.21.refs_0_), channel_id=1, source_target_pairs={{0,16},{8,24},{16,0},{24,8},{1,17},{9,25},{17,1},{25,9},{2,18},{10... | collective-permute-start | bytes 73736 | tf_op jit(solution)/shard_map/ppermute | solution.py:637
  76.1 2.2 %collective-permute-done.16.refs_2_ = bf16[96,128]{1,0:T(8,128)(2,1)S(1)} collective-permute-done((bf16[96,128]{1,0:T(8,128)(2,1)S(1)}, bf16[96,128]{1,0:T(8,128)(2,1)S(1)}, u32[]{:S(2)}, u32[]{:S(2)}) %collective-permute-start.16) | collective-permute-done | bytes 24608 | tf_op jit(solution)/shard_map/ppermute | solution.py:637
  78.3 1.1 %collective-permute-done.17.refs_3_ = bf16[96,128]{1,0:T(8,128)(2,1)S(1)} collective-permute-done((bf16[96,128]{1,0:T(8,128)(2,1)S(1)}, bf16[96,128]{1,0:T(8,128)(2,1)S(1)}, u32[]{:S(2)}, u32[]{:S(2)}) %collective-permute-start.17) | collective-permute-done | bytes 24608 | tf_op jit(solution)/shard_map/ppermute | solution.py:637
  79.4 0.7 arrange.1
  80.1 2.2 %all-to-all-done.1 = f32[32,8,128]{2,1,0:T(8,128)S(1)} async-done(((f32[32,8,128]{2,1,0:T(8,128)}), f32[32,8,128]{2,1,0:T(8,128)S(1)}, u32[]{:S(2)}, u32[]{:S(2)}) %all-to-all-start.1) | async-done | bytes 131104 | tf_op jit(solution)/shard_map/all_to_all | solution.py:708
  82.3 0.8 collect.1
  (22 shorter events, 0.0 us)
Async XLA Ops:
  0.6 10.1 %collective-permute-start = (bf16[2,128,256]{2,1,0:T(8,128)(2,1)}, bf16[2,128,256]{2,1,0:T(8,128)(2,1)S(1)}, u32[]{:S(2)}, u32[]{:S(2)}) collective-permute-start(bf16[2,128,256]{2,1,0:T(8,128)(2,1)} %rest_0_.1), channel_id=1, source_target_pairs={{0,6},{1,7},{2,4},{3,5},{4,2},{5,3},{6,0},{7,1},{8,14},{9,15},{10,... | collective-permute-start | bytes 393224 | tf_op jit(solution)/shard_map/ppermute | solution.py:634
  5.7 7.0 %collective-permute-start.1 = (bf16[2,128,256]{2,1,0:T(8,128)(2,1)}, bf16[2,128,256]{2,1,0:T(8,128)(2,1)S(1)}, u32[]{:S(2)}, u32[]{:S(2)}) collective-permute-start(bf16[2,128,256]{2,1,0:T(8,128)(2,1)} %rest_0_.1), channel_id=1, source_target_pairs={{0,1},{1,0},{2,3},{3,2},{4,5},{5,4},{6,7},{7,6},{8,9},{9,8},{10,11... | collective-permute-start | bytes 393224 | tf_op jit(solution)/shard_map/ppermute | solution.py:634
  7.2 8.9 %collective-permute-start.2 = (bf16[2,128,256]{2,1,0:T(8,128)(2,1)}, bf16[2,128,256]{2,1,0:T(8,128)(2,1)S(1)}, u32[]{:S(2)}, u32[]{:S(2)}) collective-permute-start(bf16[2,128,256]{2,1,0:T(8,128)(2,1)} %rest_0_.1), channel_id=1, source_target_pairs={{0,2},{1,3},{2,0},{3,1},{4,6},{5,7},{6,4},{7,5},{8,10},{9,11},{10,... | collective-permute-start | bytes 393224 | tf_op jit(solution)/shard_map/ppermute | solution.py:634
  7.2 14.2 %collective-permute-start.11 = (bf16[256,1024]{1,0:T(8,128)(2,1)}, bf16[256,1024]{1,0:T(8,128)(2,1)S(1)}, u32[]{:S(2)}, u32[]{:S(2)}) collective-permute-start(bf16[256,1024]{1,0:T(8,128)(2,1)} %w0.3), channel_id=1, source_target_pairs={{0,16},{8,24},{16,0},{24,8},{1,17},{9,25},{17,1},{25,9},{2,18},{10... | collective-permute-start | bytes 1572872 | tf_op jit(solution)/shard_map/ppermute | solution.py:637
  8.8 12.6 %collective-permute-start.3 = (bf16[2,128,256]{2,1,0:T(8,128)(2,1)}, bf16[2,128,256]{2,1,0:T(8,128)(2,1)S(1)}, u32[]{:S(2)}, u32[]{:S(2)}) collective-permute-start(bf16[2,128,256]{2,1,0:T(8,128)(2,1)} %rest_0_.1), channel_id=1, source_target_pairs={{0,3},{1,2},{2,1},{3,0},{4,7},{5,6},{6,5},{7,4},{8,11},{9,10},{10,... | collective-permute-start | bytes 393224 | tf_op jit(solution)/shard_map/ppermute | solution.py:634
  10.8 12.0 %collective-permute-start.4 = (bf16[2,128,256]{2,1,0:T(8,128)(2,1)}, bf16[2,128,256]{2,1,0:T(8,128)(2,1)S(1)}, u32[]{:S(2)}, u32[]{:S(2)}) collective-permute-start(bf16[2,128,256]{2,1,0:T(8,128)(2,1)} %rest_0_.1), channel_id=1, source_target_pairs={{0,4},{1,5},{2,6},{3,7},{4,0},{5,1},{6,2},{7,3},{8,12},{9,13},{10,... | collective-permute-start | bytes 393224 | tf_op jit(solution)/shard_map/ppermute | solution.py:634
  12.7 12.4 %collective-permute-start.5 = (bf16[2,128,256]{2,1,0:T(8,128)(2,1)}, bf16[2,128,256]{2,1,0:T(8,128)(2,1)S(1)}, u32[]{:S(2)}, u32[]{:S(2)}) collective-permute-start(bf16[2,128,256]{2,1,0:T(8,128)(2,1)} %rest_0_.1), channel_id=1, source_target_pairs={{0,5},{1,4},{2,7},{3,6},{4,1},{5,0},{6,3},{7,2},{8,13},{9,12},{10,... | collective-permute-start | bytes 393224 | tf_op jit(solution)/shard_map/ppermute | solution.py:634
  16.2 9.0 %collective-permute-start.6 = (bf16[2,128,256]{2,1,0:T(8,128)(2,1)S(1)}, bf16[2,128,256]{2,1,0:T(8,128)(2,1)S(1)}, u32[]{:S(2)}, u32[]{:S(2)}) collective-permute-start(bf16[2,128,256]{2,1,0:T(8,128)(2,1)S(1)} %collective-permute-done.rest_6_), channel_id=1, source_target_pairs={{0,1},{1,0},{2,3},{3,2},{4,5},{5,4},{6,7},{7,6},{8,9},{9,8},{10,11... | collective-permute-start | bytes 393224 | tf_op jit(solution)/shard_map/ppermute | solution.py:634
  16.2 5.2 %copy-start.3 = (bf16[256,1024]{1,0:T(8,128)(2,1)S(1)}, bf16[256,1024]{1,0:T(8,128)(2,1)}, u32[]{:S(2)}) copy-start(bf16[256,1024]{1,0:T(8,128)(2,1)} %w0.3) | copy-start | bytes 1572868
  16.2 8.9 %copy-start.8 = (bf16[2,128,256]{2,1,0:T(8,128)(2,1)S(1)}, bf16[2,128,256]{2,1,0:T(8,128)(2,1)}, u32[]{:S(2)}) copy-start(bf16[2,128,256]{2,1,0:T(8,128)(2,1)} %rest_0_.1) | copy-start | bytes 393220
  16.2 8.9 %copy-start.9 = (s32[12,8]{0,1:T(8,128)S(1)}, s32[12,8]{0,1:T(8,128)}, u32[]{:S(2)}) copy-start(s32[12,8]{0,1:T(8,128)} %param.27) | copy-start | bytes 1156
  16.2 8.9 %copy-start.10 = (s32[12]{0:T(128)S(1)}, s32[12]{0:T(128)}, u32[]{:S(2)}) copy-start(s32[12]{0:T(128)} %group_ids.1) | copy-start | bytes 148
  21.4 15.1 %collective-permute-start.10 = (bf16[256,1024]{1,0:T(8,128)(2,1)S(1)}, bf16[256,1024]{1,0:T(8,128)(2,1)S(1)}, u32[]{:S(2)}, u32[]{:S(2)}) collective-permute-start(bf16[256,1024]{1,0:T(8,128)(2,1)S(1)} %copy-done.3), channel_id=1, source_target_pairs={{0,8},{8,0},{16,24},{24,16},{1,9},{9,1},{17,25},{25,17},{2,10},{10... | collective-permute-start | bytes 1572872 | tf_op jit(solution)/shard_map/ppermute | solution.py:637
  21.5 16.5 %collective-permute-start.12 = (bf16[256,1024]{1,0:T(8,128)(2,1)S(1)}, bf16[256,1024]{1,0:T(8,128)(2,1)S(1)}, u32[]{:S(2)}, u32[]{:S(2)}) collective-permute-start(bf16[256,1024]{1,0:T(8,128)(2,1)S(1)} %collective-permute-done.11.w2), channel_id=1, source_target_pairs={{0,8},{8,0},{16,24},{24,16},{1,9},{9,1},{17,25},{25,17},{2,10},{10... | collective-permute-start | bytes 1572872 | tf_op jit(solution)/shard_map/ppermute | solution.py:637
  25.1 12.8 %copy-start = (bf16[1024,1024]{1,0:T(8,128)(2,1)S(1)}, bf16[1024,1024]{1,0:T(8,128)(2,1)}, u32[]{:S(2)}) copy-start(bf16[1024,1024]{1,0:T(8,128)(2,1)} %w_up.3) | copy-start | bytes 6291460
  25.1 12.8 %copy-start.1 = (bf16[1024,1024]{1,0:T(8,128)(2,1)S(1)}, bf16[1024,1024]{1,0:T(8,128)(2,1)}, u32[]{:S(2)}) copy-start(bf16[1024,1024]{1,0:T(8,128)(2,1)} %w_down.3) | copy-start | bytes 6291460
  25.2 12.8 %copy-start.2 = (bf16[384,1024]{1,0:T(8,128)(2,1)S(1)}, bf16[384,1024]{1,0:T(8,128)(2,1)}, u32[]{:S(2)}) copy-start(bf16[384,1024]{1,0:T(8,128)(2,1)} %tokens.3) | copy-start | bytes 2359300
  25.2 12.8 %copy-start.5 = (f32[1024]{0:T(1024)S(1)}, f32[1024]{0:T(1024)}, u32[]{:S(2)}) copy-start(f32[1024]{0:T(1024)} %param.19) | copy-start | bytes 12292
  30.6 5.8 %collective-permute-start.8 = (bf16[400,256]{1,0:T(8,128)(2,1)S(1)}, bf16[400,256]{1,0:T(8,128)(2,1)S(1)}, u32[]{:S(2)}, u32[]{:S(2)}) collective-permute-start(bf16[400,256]{1,0:T(8,128)(2,1)S(1)} %attend.1.a0), channel_id=1, source_target_pairs={{0,16},{8,24},{16,0},{24,8},{1,17},{9,25},{17,1},{25,9},{2,18},{10... | collective-permute-start | bytes 614408 | tf_op jit(solution)/shard_map/ppermute | solution.py:637
  31.6 4.9 %collective-permute-start.7 = (bf16[400,256]{1,0:T(8,128)(2,1)S(1)}, bf16[400,256]{1,0:T(8,128)(2,1)S(1)}, u32[]{:S(2)}, u32[]{:S(2)}) collective-permute-start(bf16[400,256]{1,0:T(8,128)(2,1)S(1)} %attend.1.a0), channel_id=1, source_target_pairs={{0,8},{8,0},{16,24},{24,16},{1,9},{9,1},{17,25},{25,17},{2,10},{10... | collective-permute-start | bytes 614408 | tf_op jit(solution)/shard_map/ppermute | solution.py:637
  36.5 1.5 %collective-permute-start.9 = (bf16[400,256]{1,0:T(8,128)(2,1)S(1)}, bf16[400,256]{1,0:T(8,128)(2,1)S(1)}, u32[]{:S(2)}, u32[]{:S(2)}) collective-permute-start(bf16[400,256]{1,0:T(8,128)(2,1)S(1)} %collective-permute-done.8.a2), channel_id=1, source_target_pairs={{0,8},{8,0},{16,24},{24,16},{1,9},{9,1},{17,25},{25,17},{2,10},{10... | collective-permute-start | bytes 614408 | tf_op jit(solution)/shard_map/ppermute | solution.py:637
  40.2 9.9 %copy-start.4 = (bf16[1024,128]{1,0:T(8,128)(2,1)S(1)}, bf16[1024,128]{1,0:T(8,128)(2,1)}, u32[]{:S(2)}) copy-start(bf16[1024,128]{1,0:T(8,128)(2,1)} %w_proj.1) | copy-start | bytes 786436
  40.2 9.9 %copy-start.6 = (f32[1024]{0:T(1024)S(1)}, f32[1024]{0:T(1024)}, u32[]{:S(2)}) copy-start(f32[1024]{0:T(1024)} %param.20) | copy-start | bytes 12292
  40.2 2.5 %collective-permute-start.13 = (bf16[192,1024]{1,0:T(8,128)(2,1)S(1)}, bf16[192,1024]{1,0:T(8,128)(2,1)S(1)}, u32[]{:S(2)}, u32[]{:S(2)}) collective-permute-start(bf16[192,1024]{1,0:T(8,128)(2,1)S(1)} %feed_other.1), channel_id=1, source_target_pairs={{0,8},{8,0},{16,24},{24,16},{1,9},{9,1},{17,25},{25,17},{2,10},{10... | collective-permute-start | bytes 1179656 | tf_op jit(solution)/shard_map/ppermute | solution.py:637
  42.7 20.4 %copy-start.7 = (s32[64]{0:T(128)S(1)}, s32[64]{0:T(128)}, u32[]{:S(2)}) copy-start(s32[64]{0:T(128)} %lengths.1) | copy-start | bytes 772
  42.8 7.3 %collective-permute-start.14 = (bf16[96,1024]{1,0:T(8,128)(2,1)S(1)}, bf16[96,1024]{1,0:T(8,128)(2,1)S(1)}, u32[]{:S(2)}, u32[]{:S(2)}) collective-permute-start(bf16[96,1024]{1,0:T(8,128)(2,1)S(1)} %fold.1), channel_id=1, source_target_pairs={{0,16},{8,24},{16,0},{24,8},{1,17},{9,25},{17,1},{25,9},{2,18},{10... | collective-permute-start | bytes 589832 | tf_op jit(solution)/shard_map/ppermute | solution.py:637
  69.0 13.3 %all-to-all-start.1 = ((f32[32,8,128]{2,1,0:T(8,128)}), f32[32,8,128]{2,1,0:T(8,128)S(1)}, u32[]{:S(2)}, u32[]{:S(2)}) async-start(f32[32,8,128]{2,1,0:T(8,128)} %bitcast.5), calls=%async_computation.1 | async-start | bytes 262144 | tf_op jit(solution)/shard_map/all_to_all | solution.py:708
  74.1 2.0 %collective-permute-start.15 = (bf16[96,128]{1,0:T(8,128)(2,1)S(1)}, bf16[96,128]{1,0:T(8,128)(2,1)S(1)}, u32[]{:S(2)}, u32[]{:S(2)}) collective-permute-start(bf16[96,128]{1,0:T(8,128)(2,1)S(1)} %get-tuple-element.21.refs_0_), channel_id=1, source_target_pairs={{0,8},{8,0},{16,24},{24,16},{1,9},{9,1},{17,25},{25,17},{2,10},{10... | collective-permute-start | bytes 73736 | tf_op jit(solution)/shard_map/ppermute | solution.py:637
  74.4 3.9 %collective-permute-start.16 = (bf16[96,128]{1,0:T(8,128)(2,1)S(1)}, bf16[96,128]{1,0:T(8,128)(2,1)S(1)}, u32[]{:S(2)}, u32[]{:S(2)}) collective-permute-start(bf16[96,128]{1,0:T(8,128)(2,1)S(1)} %get-tuple-element.21.refs_0_), channel_id=1, source_target_pairs={{0,16},{8,24},{16,0},{24,8},{1,17},{9,25},{17,1},{25,9},{2,18},{10... | collective-permute-start | bytes 73736 | tf_op jit(solution)/shard_map/ppermute | solution.py:637
  76.1 3.4 %collective-permute-start.17 = (bf16[96,128]{1,0:T(8,128)(2,1)S(1)}, bf16[96,128]{1,0:T(8,128)(2,1)S(1)}, u32[]{:S(2)}, u32[]{:S(2)}) collective-permute-start(bf16[96,128]{1,0:T(8,128)(2,1)S(1)} %get-tuple-element.21.refs_0_), channel_id=1, source_target_pairs={{0,24},{8,16},{16,8},{24,0},{1,25},{9,17},{17,9},{25,1},{2,26},{10... | collective-permute-start | bytes 73736 | tf_op jit(solution)/shard_map/ppermute | solution.py:637

commit v6 on v5

--- a/solution.py
+++ b/solution.py
@@ -154,7 +154,7 @@
 MIB = 1 << 20
 EXTRA = 16
 PREP_UNROLL = 6
-ATT_UNROLL = 6
+ATT_UNROLL = 12
 SCORE_UNROLL = 32
 
 
@@ -225,14 +225,11 @@
     rel_q = jnp.dot(flip_q, rel[0], preferred_element_type=jnp.float32)
     rel_k = jnp.dot(flip_k, rel[1], preferred_element_type=jnp.float32)
     rel_q_heads[...] = by_head(rel_q.astype(jnp.bfloat16))
-    requests, many, _ = base.shape
+    requests, _, many = base.shape
     for r in range(requests):
         q_heads[r * many : (r + 1) * many, :] = by_head(qkv[r * QLEN : (r + 1) * QLEN, :width])
     query_rel[...] = times_rows(q_heads[...], rel_k.astype(jnp.bfloat16))
     key_rel[...] = times_rows(qkv[:, width : 2 * width], rel_q_heads[...])
-    live = lax.broadcasted_iota(jnp.int32, (many, LANES), 1) < PLEN + QLEN
-    above = jnp.zeros((PLEN, LANES), jnp.float32)
-    below = jnp.zeros((LANES - PLEN - QLEN, LANES), jnp.float32)
     scale = 1.0 / math.sqrt(3 * HD)
 
     def one_request(r, carry):
@@ -240,7 +237,6 @@
         spread = pl.ds(pl.multiple_of(r * many, many), many)
         turned = times_rows(qkv[rows, width : 2 * width], q_heads[spread, :])
         turned = turned + key_terms(key_rel[rows, :], PLEN)
-        own = jnp.concatenate([above, turned, below], axis=0).T[:many]
         spread_rel = query_rel[spread, :]
         c2p = jnp.concatenate(
             [
@@ -255,7 +251,9 @@
             ],
             axis=0,
         )
-        base[r] = jnp.where(live, (own + c2p) * scale, -jnp.inf)
+        c2p = c2p.T
+        base[r, :PLEN] = c2p[:PLEN] * scale
+        base[r, PLEN:] = (c2p[PLEN : PLEN + QLEN] + turned) * scale
         return carry
 
     lax.fori_loop(0, requests, one_request, 0, unroll=PREP_UNROLL)
@@ -269,7 +267,7 @@
         prepare_kernel,
         out_shape=[
             jax.ShapeDtypeStruct((rows, 3 * width), jnp.bfloat16),
-            jax.ShapeDtypeStruct((rows // QLEN, heads * QLEN, LANES), jnp.float32),
+            jax.ShapeDtypeStruct((rows // QLEN, PLEN + QLEN, heads * QLEN), jnp.float32),
             jax.ShapeDtypeStruct((heads * LANES, width), jnp.bfloat16),
         ],
         in_specs=[pl.BlockSpec(memory_space=pltpu.HBM)] * 3,
@@ -290,7 +288,7 @@
 
 
 def attend_kernel(group_ids, qkv, base, rel_q_heads, columns, *rest):
-    pieces, (att, cache, picked, key_rel, arrived) = rest[:-5], rest[-5:]
+    pieces, (att, cache, picked, key_rel, shares, arrived) = rest[:-6], rest[-6:]
     copies = [
         [
             pltpu.make_async_copy(piece.at[kind], cache.at[kind, at], arrived.at[kind, at])
@@ -312,8 +310,6 @@
     heads = width // HD
     groups_dev = cache.shape[2] // PLEN
     me = lax.axis_index("doc")
-    padding = jnp.zeros((LANES - PLEN - QLEN, width), jnp.bfloat16)
-    below_terms = jnp.zeros((LANES - PLEN, LANES), jnp.float32)
     small_head = lax.broadcasted_iota(jnp.int32, (QLEN, width), 1) // HD
     scale = 1.0 / math.sqrt(3 * HD)
 
@@ -328,30 +324,41 @@
         piece, within = place_of(r)
         picked[r * PLEN : (r + 1) * PLEN, :] = cache[0, piece, within, :]
     key_rel[...] = times_rows(picked[...], rel_q_heads[...])
-    for copy in copies[1]:
-        copy.wait()
-
-    def one_request(r, carry):
+
+    def one_softmax(r, carry):
         rows = pl.ds(pl.multiple_of(r * QLEN, QLEN), QLEN)
         cached = pl.ds(pl.multiple_of(r * PLEN, PLEN), PLEN)
         turned = times_rows(picked[cached, :], by_head(qkv[rows, 0:width]))
         turned = (turned + key_terms(key_rel[cached, :], 0)) * scale
-        logits = base[r] + jnp.concatenate([turned, below_terms], axis=0).T[: heads * QLEN]
-        largest = jnp.max(logits, axis=1, keepdims=True)
-        weights = jnp.exp(logits - largest)
-        weights = weights * (1.0 / jnp.sum(weights, axis=1, keepdims=True))
+        logits = jnp.concatenate([base[r, :PLEN] + turned, base[r, PLEN:]], axis=0)
+        weights = jnp.exp(logits - jnp.max(logits, axis=0, keepdims=True))
+        weights = weights * (1.0 / jnp.sum(weights, axis=0, keepdims=True))
+        shares[r] = weights.astype(shares.dtype)
+        return carry
+
+    lax.fori_loop(0, requests, one_softmax, 0, unroll=ATT_UNROLL)
+    for copy in copies[1]:
+        copy.wait()
+
+    def one_sum(r, carry):
+        rows = pl.ds(pl.multiple_of(r * QLEN, QLEN), QLEN)
         piece, within = place_of(r)
         values = jnp.concatenate(
-            [cache[1, piece, within, :], qkv[rows, 2 * width : 3 * width], padding], axis=0
+            [cache[1, piece, within, :], qkv[rows, 2 * width : 3 * width]], axis=0
         )
-        summed = jnp.dot(weights.astype(jnp.bfloat16), values, preferred_element_type=jnp.float32)
+        summed = lax.dot_general(
+            shares[r],
+            values,
+            (((0,), (0,)), ((), ())),
+            preferred_element_type=jnp.float32,
+        )
         out = summed[:QLEN]
         for h in range(1, heads):
             out = jnp.where(small_head == h, summed[h * QLEN : (h + 1) * QLEN], out)
         att[rows, :] = out.astype(jnp.bfloat16)
         return carry
 
-    lax.fori_loop(0, requests, one_request, 0, unroll=ATT_UNROLL)
+    lax.fori_loop(0, requests, one_sum, 0, unroll=ATT_UNROLL)
 
 
 def attend(group_ids, qkv, base, rel_q_heads, columns, pieces):
@@ -369,6 +376,7 @@
             pltpu.VMEM((2, len(pieces)) + pieces[0].shape[1:], jnp.bfloat16),
             pltpu.VMEM((cached, width), jnp.bfloat16),
             pltpu.VMEM((cached, rel_q_heads.shape[0]), jnp.float32),
+            pltpu.VMEM(base.shape, jnp.bfloat16),
             pltpu.SemaphoreType.DMA((2, len(pieces))),
         ],
         compiler_params=params(12),

time: 82.9 us -> 81 us (0.977)
  starting transfers between devices: 23.8 us -> 21.6 us
    all_to_all x1, starting transfers between devices: 5.08 us -> 2.7 us  [body(): lax.all_to_all(rated.reshape(-1, LANES), ('doc', 'head'), 0, 0, tiled=True)]
    pallas_call x1, Pallas kernels: 5.83 us -> 8.2 us  [body(): pl.pallas_call(score_kernel, out_shape=jax.ShapeDtypeStruct((n_doc, n_hea...]
    pallas_call x1, Pallas kernels: 5.46 us -> 3.42 us  [attend(): pl.pallas_call(attend_kernel, out_shape=jax.ShapeDtypeStruct((rows + EXTR...]
  transfers between devices with their start and end apart: 19 -> 19, of which waited for: 9 -> 9; matrix products, arithmetic and copies ran while one was open for 0% -> 0% of each run, Pallas kernels for 16% -> 14%
where the time goes in v6:
time: 81 us; the launch traced here: 81.1 us
  Pallas kernels  23.3 us (29%)
  waiting for transfers between devices  22.7 us (28%)
  starting transfers between devices  21.6 us (27%)
  blocking collectives  12.5 us (15%)
  between operations  0.84 us (1%)
    ppermute x11, waiting for transfers between devices, over_head(): return lax.ppermute(x, 'head', [(i, i ^ k) for i in range(n_head)])  15.9 us
    all_to_all x1, blocking collectives, body(): queries = lax.all_to_all(vectors, 'doc', 0, 0, tiled=True).reshape(-1, emb)  12.5 us
    ppermute x7, starting transfers between devices, over_doc(): return lax.ppermute(x, 'doc', [(i, i ^ k) for i in range(n_doc)])  12.5 us
    pallas_call x1, Pallas kernels, body(): pl.pallas_call(score_kernel, out_shape=jax.ShapeDtypeStruct((n_doc, n_hea...  8.2 us
    ppermute x11, starting transfers between devices, over_head(): return lax.ppermute(x, 'head', [(i, i ^ k) for i in range(n_head)])  6.42 us
    pallas_call x1, Pallas kernels, prepare(): pl.pallas_call(prepare_kernel, out_shape=[jax.ShapeDtypeStruct((rows, 3 *...  5.08 us
    ppermute x7, waiting for transfers between devices, over_doc(): return lax.ppermute(x, 'doc', [(i, i ^ k) for i in range(n_doc)])  4.78 us
    pallas_call x2, Pallas kernels, feed(): pl.pallas_call(kernel, out_shape=outs, in_specs=full_specs(12), out_specs...  4.56 us
  transfers between devices with their start and end apart: 19, of which 9 were waited for; matrix products, arithmetic and copies ran while one was open for 0% of the time, Pallas kernels for 14%

profile of v6, /device:TPU:0, one launch (start us, length us, event | category | flops | bytes accessed | tf_op | source)
XLA Modules:
  0.0 81.1 jit_solution(1006643742529195539)
XLA Ops:
  0.6 5.1 %collective-permute-start = (bf16[2,128,256]{2,1,0:T(8,128)(2,1)}, bf16[2,128,256]{2,1,0:T(8,128)(2,1)S(1)}, u32[]{:S(2)}, u32[]{:S(2)}) collective-permute-start(bf16[2,128,256]{2,1,0:T(8,128)(2,1)} %rest_0_.1), channel_id=1, source_target_pairs={{0,6},{1,7},{2,4},{3,5},{4,2},{5,3},{6,0},{7,1},{8,14},{9,15},{10,... | collective-permute-start | bytes 393224 | tf_op jit(solution)/shard_map/ppermute | solution.py:642
  5.7 1.5 %collective-permute-start.1 = (bf16[2,128,256]{2,1,0:T(8,128)(2,1)}, bf16[2,128,256]{2,1,0:T(8,128)(2,1)S(1)}, u32[]{:S(2)}, u32[]{:S(2)}) collective-permute-start(bf16[2,128,256]{2,1,0:T(8,128)(2,1)} %rest_0_.1), channel_id=1, source_target_pairs={{0,1},{1,0},{2,3},{3,2},{4,5},{5,4},{6,7},{7,6},{8,9},{9,8},{10,11... | collective-permute-start | bytes 393224 | tf_op jit(solution)/shard_map/ppermute | solution.py:642
  7.2 0.0 collective-permute-start.2
  7.2 1.5 %collective-permute-start.11 = (bf16[256,1024]{1,0:T(8,128)(2,1)}, bf16[256,1024]{1,0:T(8,128)(2,1)S(1)}, u32[]{:S(2)}, u32[]{:S(2)}) collective-permute-start(bf16[256,1024]{1,0:T(8,128)(2,1)} %w0.3), channel_id=1, source_target_pairs={{0,16},{8,24},{16,0},{24,8},{1,17},{9,25},{17,1},{25,9},{2,18},{10... | collective-permute-start | bytes 1572872 | tf_op jit(solution)/shard_map/ppermute | solution.py:645
  8.8 2.0 %collective-permute-start.3 = (bf16[2,128,256]{2,1,0:T(8,128)(2,1)}, bf16[2,128,256]{2,1,0:T(8,128)(2,1)S(1)}, u32[]{:S(2)}, u32[]{:S(2)}) collective-permute-start(bf16[2,128,256]{2,1,0:T(8,128)(2,1)} %rest_0_.1), channel_id=1, source_target_pairs={{0,3},{1,2},{2,1},{3,0},{4,7},{5,6},{6,5},{7,4},{8,11},{9,10},{10,... | collective-permute-start | bytes 393224 | tf_op jit(solution)/shard_map/ppermute | solution.py:642
  10.8 2.0 %collective-permute-start.4 = (bf16[2,128,256]{2,1,0:T(8,128)(2,1)}, bf16[2,128,256]{2,1,0:T(8,128)(2,1)S(1)}, u32[]{:S(2)}, u32[]{:S(2)}) collective-permute-start(bf16[2,128,256]{2,1,0:T(8,128)(2,1)} %rest_0_.1), channel_id=1, source_target_pairs={{0,4},{1,5},{2,6},{3,7},{4,0},{5,1},{6,2},{7,3},{8,12},{9,13},{10,... | collective-permute-start | bytes 393224 | tf_op jit(solution)/shard_map/ppermute | solution.py:642
  12.7 1.9 %collective-permute-start.5 = (bf16[2,128,256]{2,1,0:T(8,128)(2,1)}, bf16[2,128,256]{2,1,0:T(8,128)(2,1)S(1)}, u32[]{:S(2)}, u32[]{:S(2)}) collective-permute-start(bf16[2,128,256]{2,1,0:T(8,128)(2,1)} %rest_0_.1), channel_id=1, source_target_pairs={{0,5},{1,4},{2,7},{3,6},{4,1},{5,0},{6,3},{7,2},{8,13},{9,12},{10,... | collective-permute-start | bytes 393224 | tf_op jit(solution)/shard_map/ppermute | solution.py:642
  14.6 1.5 %collective-permute-done.2.rest_2_ = bf16[2,128,256]{2,1,0:T(8,128)(2,1)S(1)} collective-permute-done((bf16[2,128,256]{2,1,0:T(8,128)(2,1)}, bf16[2,128,256]{2,1,0:T(8,128)(2,1)S(1)}, u32[]{:S(2)}, u32[]{:S(2)}) %collective-permute-start.2) | collective-permute-done | bytes 131104 | tf_op jit(solution)/shard_map/ppermute | solution.py:642
  16.2 0.0 collective-permute-start.6
  16.2 5.1 %prepare.1 = (bf16[384,768]{1,0:T(8,128)(2,1)S(1)}, f32[12,96,128]{2,1,0:T(8,128)S(1)}, bf16[512,256]{1,0:T(8,128)(2,1)S(1)}) custom-call(bf16[384,1024]{1,0:T(8,128)(2,1)} %tokens.3, bf16[3,1024,256]{2,1,0:T(8,128)(2,1)} %bitcast.15, bf16[512,1024]{1,0:T(8,128)(2,1)} %rel_table), custom_call_target="tpu_custom_call" | custom-call | flops 4194304000 | bytes 4194304 | tf_op jit(solution)/shard_map/prepare/pallas_call | solution.py:266
  21.3 0.1 collective-permute-start.10
  21.4 0.0 collective-permute-done.11.w2
  21.4 0.5 collective-permute-start.12
  21.9 0.9 %collective-permute-done.4.rest_4_ = bf16[2,128,256]{2,1,0:T(8,128)(2,1)S(1)} collective-permute-done((bf16[2,128,256]{2,1,0:T(8,128)(2,1)}, bf16[2,128,256]{2,1,0:T(8,128)(2,1)S(1)}, u32[]{:S(2)}, u32[]{:S(2)}) %collective-permute-start.4) | collective-permute-done | bytes 131104 | tf_op jit(solution)/shard_map/ppermute | solution.py:642
  22.8 2.3 %collective-permute-done.5.rest_5_ = bf16[2,128,256]{2,1,0:T(8,128)(2,1)S(1)} collective-permute-done((bf16[2,128,256]{2,1,0:T(8,128)(2,1)}, bf16[2,128,256]{2,1,0:T(8,128)(2,1)S(1)}, u32[]{:S(2)}, u32[]{:S(2)}) %collective-permute-start.5) | collective-permute-done | bytes 131104 | tf_op jit(solution)/shard_map/ppermute | solution.py:642
  25.1 0.0 collective-permute-done.6.rest_7_
  25.1 0.0 copy-start
  25.1 0.0 copy-start.1
  25.2 0.0 copy-start.2
  25.2 0.0 copy-start.5
  25.2 3.4 %attend.1.a0 = bf16[400,256]{1,0:T(8,128)(2,1)S(1)} custom-call(s32[12]{0:T(128)S(1)} %copy-done.10, bf16[384,768]{1,0:T(8,128)(2,1)S(1)} %get-tuple-element.13.qkv, f32[12,96,128]{2,1,0:T(8,128)S(1)} %get-tuple-element.14.base, bf16[512,256]{1,0:T(8,128)(2,1)S(1)} %get-tuple-element.15.rel_q_heads, s32[8,12]{1,0:T(8,128)S(1)} %bitcast.13, ...), custom_call_target="tpu_custom_call" | custom-call | flops 2097152000 | bytes 2097152 | tf_op jit(solution)/shard_map/attend/pallas_call | solution.py:368
  28.6 1.0 %collective-permute-start.8 = (bf16[400,256]{1,0:T(8,128)(2,1)S(1)}, bf16[400,256]{1,0:T(8,128)(2,1)S(1)}, u32[]{:S(2)}, u32[]{:S(2)}) collective-permute-start(bf16[400,256]{1,0:T(8,128)(2,1)S(1)} %attend.1.a0), channel_id=1, source_target_pairs={{0,16},{8,24},{16,0},{24,8},{1,17},{9,25},{17,1},{25,9},{2,18},{10... | collective-permute-start | bytes 614408 | tf_op jit(solution)/shard_map/ppermute | solution.py:645
  29.6 0.0 collective-permute-start.7
  29.6 4.8 %collective-permute-done.8.a2 = bf16[400,256]{1,0:T(8,128)(2,1)S(1)} collective-permute-done((bf16[400,256]{1,0:T(8,128)(2,1)S(1)}, bf16[400,256]{1,0:T(8,128)(2,1)S(1)}, u32[]{:S(2)}, u32[]{:S(2)}) %collective-permute-start.8) | collective-permute-done | bytes 204832 | tf_op jit(solution)/shard_map/ppermute | solution.py:645
  34.4 0.0 collective-permute-start.9
  34.4 0.0 collective-permute-done.7.a1
  34.4 1.4 %collective-permute-done.9.a3 = bf16[400,256]{1,0:T(8,128)(2,1)S(1)} collective-permute-done((bf16[400,256]{1,0:T(8,128)(2,1)S(1)}, bf16[400,256]{1,0:T(8,128)(2,1)S(1)}, u32[]{:S(2)}, u32[]{:S(2)}) %collective-permute-start.9) | collective-permute-done | bytes 204832 | tf_op jit(solution)/shard_map/ppermute | solution.py:645
  35.9 2.3 %feed_other.1 = bf16[192,1024]{1,0:T(8,128)(2,1)S(1)} custom-call(bf16[400,256]{1,0:T(8,128)(2,1)S(1)} %attend.1.a0, bf16[400,256]{1,0:T(8,128)(2,1)S(1)} %collective-permute-done.7.a1, bf16[400,256]{1,0:T(8,128)(2,1)S(1)} %collective-permute-done.8.a2, bf16[400,256]{1,0:T(8,128)(2,1)S(1)} %collective-permute-done.9.a3, bf16[256,1024]{1,0:T(8,128)(2,1)S(1)} %copy-done.3, ...), custom_call_target="tpu_custom_call" | custom-call | flops 1677721600 | bytes 6291456 | tf_op jit(solution)/shard_map/feed_other/pallas_call | solution.py:437
  38.2 0.0 copy-start.4
  38.2 0.0 copy-start.6
  38.2 0.2 collective-permute-start.13
  38.4 2.3 %feed_own.1 = (f32[96,1024]{1,0:T(8,128)S(1)}, f32[96,1024]{1,0:T(8,128)S(1)}) custom-call(bf16[400,256]{1,0:T(8,128)(2,1)S(1)} %attend.1.a0, bf16[400,256]{1,0:T(8,128)(2,1)S(1)} %collective-permute-done.7.a1, bf16[400,256]{1,0:T(8,128)(2,1)S(1)} %collective-permute-done.8.a2, bf16[400,256]{1,0:T(8,128)(2,1)S(1)} %collective-permute-done.9.a3, ...), custom_call_target="tpu_custom_call" | custom-call | flops 1677721600 | bytes 6291456 | tf_op jit(solution)/shard_map/feed_own/pallas_call | solution.py:437
  40.7 0.0 copy-start.7
  40.7 0.1 fold.1
  40.8 1.0 %collective-permute-start.14 = (bf16[96,1024]{1,0:T(8,128)(2,1)S(1)}, bf16[96,1024]{1,0:T(8,128)(2,1)S(1)}, u32[]{:S(2)}, u32[]{:S(2)}) collective-permute-start(bf16[96,1024]{1,0:T(8,128)(2,1)S(1)} %fold.1), channel_id=1, source_target_pairs={{0,16},{8,24},{16,0},{24,8},{1,17},{9,25},{17,1},{25,9},{2,18},{10... | collective-permute-start | bytes 589832 | tf_op jit(solution)/shard_map/ppermute | solution.py:645
  41.8 6.3 %collective-permute-done.14.from_y = bf16[96,1024]{1,0:T(8,128)(2,1)S(1)} collective-permute-done((bf16[96,1024]{1,0:T(8,128)(2,1)S(1)}, bf16[96,1024]{1,0:T(8,128)(2,1)S(1)}, u32[]{:S(2)}, u32[]{:S(2)}) %collective-permute-start.14) | collective-permute-done | bytes 196640 | tf_op jit(solution)/shard_map/ppermute | solution.py:645
  48.1 0.5 project.1
  48.6 12.5 %all_to_all.14 = bf16[8,112,128]{2,1,0:T(8,128)(2,1)S(1)} all-to-all(bf16[8,112,128]{2,1,0:T(8,128)(2,1)S(1)} %get-tuple-element.20), channel_id=1, replica_groups=mesh['head'=4,'doc'=8] {'doc'}, dimensions={0} | all-to-all | bytes 458752 | tf_op jit(solution)/shard_map/all_to_all | solution.py:699
  61.1 8.2 %rate.1 = f32[8,4,8,128]{3,2,1,0:T(8,128)} custom-call(s32[64]{0:T(128)S(1)} %copy-done.7, bf16[896,128]{1,0:T(8,128)(2,1)S(1)} %bitcast.8, bf16[64,256,128]{2,1,0:T(8,128)(2,1)} %docs.1), custom_call_target="tpu_custom_call" | custom-call | tf_op jit(solution)/shard_map/rate/pallas_call | solution.py:701
  69.3 2.7 %all-to-all-start.1 = ((f32[32,8,128]{2,1,0:T(8,128)}), f32[32,8,128]{2,1,0:T(8,128)S(1)}, u32[]{:S(2)}, u32[]{:S(2)}) async-start(f32[32,8,128]{2,1,0:T(8,128)} %bitcast.5), calls=%async_computation.1 | async-start | bytes 262144 | tf_op jit(solution)/shard_map/all_to_all | solution.py:716
  72.0 0.3 collective-permute-start.15
  72.3 1.8 %collective-permute-start.16 = (bf16[96,128]{1,0:T(8,128)(2,1)S(1)}, bf16[96,128]{1,0:T(8,128)(2,1)S(1)}, u32[]{:S(2)}, u32[]{:S(2)}) collective-permute-start(bf16[96,128]{1,0:T(8,128)(2,1)S(1)} %get-tuple-element.21.refs_0_), channel_id=1, source_target_pairs={{0,16},{8,24},{16,0},{24,8},{1,17},{9,25},{17,1},{25,9},{2,18},{10... | collective-permute-start | bytes 73736 | tf_op jit(solution)/shard_map/ppermute | solution.py:645
  74.1 0.1 collective-permute-start.17
  74.2 2.1 %collective-permute-done.16.refs_2_ = bf16[96,128]{1,0:T(8,128)(2,1)S(1)} collective-permute-done((bf16[96,128]{1,0:T(8,128)(2,1)S(1)}, bf16[96,128]{1,0:T(8,128)(2,1)S(1)}, u32[]{:S(2)}, u32[]{:S(2)}) %collective-permute-start.16) | collective-permute-done | bytes 24608 | tf_op jit(solution)/shard_map/ppermute | solution.py:645
  76.3 1.3 %collective-permute-done.17.refs_3_ = bf16[96,128]{1,0:T(8,128)(2,1)S(1)} collective-permute-done((bf16[96,128]{1,0:T(8,128)(2,1)S(1)}, bf16[96,128]{1,0:T(8,128)(2,1)S(1)}, u32[]{:S(2)}, u32[]{:S(2)}) %collective-permute-start.17) | collective-permute-done | bytes 24608 | tf_op jit(solution)/shard_map/ppermute | solution.py:645
  77.5 0.7 arrange.1
  78.2 2.1 %all-to-all-done.1 = f32[32,8,128]{2,1,0:T(8,128)S(1)} async-done(((f32[32,8,128]{2,1,0:T(8,128)}), f32[32,8,128]{2,1,0:T(8,128)S(1)}, u32[]{:S(2)}, u32[]{:S(2)}) %all-to-all-start.1) | async-done | bytes 131104 | tf_op jit(solution)/shard_map/all_to_all | solution.py:716
  80.2 0.8 %collect.1 = f32[8,12]{1,0:T(8,128)} custom-call(f32[8,4,8,128]{3,2,1,0:T(8,128)S(1)} %bitcast.9), custom_call_target="tpu_custom_call" | custom-call | tf_op jit(solution)/shard_map/collect/pallas_call | solution.py:729
  (22 shorter events, 0.0 us)
Async XLA Ops:
  0.6 10.1 %collective-permute-start = (bf16[2,128,256]{2,1,0:T(8,128)(2,1)}, bf16[2,128,256]{2,1,0:T(8,128)(2,1)S(1)}, u32[]{:S(2)}, u32[]{:S(2)}) collective-permute-start(bf16[2,128,256]{2,1,0:T(8,128)(2,1)} %rest_0_.1), channel_id=1, source_target_pairs={{0,6},{1,7},{2,4},{3,5},{4,2},{5,3},{6,0},{7,1},{8,14},{9,15},{10,... | collective-permute-start | bytes 393224 | tf_op jit(solution)/shard_map/ppermute | solution.py:642
  5.7 7.0 %collective-permute-start.1 = (bf16[2,128,256]{2,1,0:T(8,128)(2,1)}, bf16[2,128,256]{2,1,0:T(8,128)(2,1)S(1)}, u32[]{:S(2)}, u32[]{:S(2)}) collective-permute-start(bf16[2,128,256]{2,1,0:T(8,128)(2,1)} %rest_0_.1), channel_id=1, source_target_pairs={{0,1},{1,0},{2,3},{3,2},{4,5},{5,4},{6,7},{7,6},{8,9},{9,8},{10,11... | collective-permute-start | bytes 393224 | tf_op jit(solution)/shard_map/ppermute | solution.py:642
  7.2 8.9 %collective-permute-start.2 = (bf16[2,128,256]{2,1,0:T(8,128)(2,1)}, bf16[2,128,256]{2,1,0:T(8,128)(2,1)S(1)}, u32[]{:S(2)}, u32[]{:S(2)}) collective-permute-start(bf16[2,128,256]{2,1,0:T(8,128)(2,1)} %rest_0_.1), channel_id=1, source_target_pairs={{0,2},{1,3},{2,0},{3,1},{4,6},{5,7},{6,4},{7,5},{8,10},{9,11},{10,... | collective-permute-start | bytes 393224 | tf_op jit(solution)/shard_map/ppermute | solution.py:642
  7.2 14.1 %collective-permute-start.11 = (bf16[256,1024]{1,0:T(8,128)(2,1)}, bf16[256,1024]{1,0:T(8,128)(2,1)S(1)}, u32[]{:S(2)}, u32[]{:S(2)}) collective-permute-start(bf16[256,1024]{1,0:T(8,128)(2,1)} %w0.3), channel_id=1, source_target_pairs={{0,16},{8,24},{16,0},{24,8},{1,17},{9,25},{17,1},{25,9},{2,18},{10... | collective-permute-start | bytes 1572872 | tf_op jit(solution)/shard_map/ppermute | solution.py:645
  8.8 12.5 %collective-permute-start.3 = (bf16[2,128,256]{2,1,0:T(8,128)(2,1)}, bf16[2,128,256]{2,1,0:T(8,128)(2,1)S(1)}, u32[]{:S(2)}, u32[]{:S(2)}) collective-permute-start(bf16[2,128,256]{2,1,0:T(8,128)(2,1)} %rest_0_.1), channel_id=1, source_target_pairs={{0,3},{1,2},{2,1},{3,0},{4,7},{5,6},{6,5},{7,4},{8,11},{9,10},{10,... | collective-permute-start | bytes 393224 | tf_op jit(solution)/shard_map/ppermute | solution.py:642
  10.8 12.0 %collective-permute-start.4 = (bf16[2,128,256]{2,1,0:T(8,128)(2,1)}, bf16[2,128,256]{2,1,0:T(8,128)(2,1)S(1)}, u32[]{:S(2)}, u32[]{:S(2)}) collective-permute-start(bf16[2,128,256]{2,1,0:T(8,128)(2,1)} %rest_0_.1), channel_id=1, source_target_pairs={{0,4},{1,5},{2,6},{3,7},{4,0},{5,1},{6,2},{7,3},{8,12},{9,13},{10,... | collective-permute-start | bytes 393224 | tf_op jit(solution)/shard_map/ppermute | solution.py:642
  12.7 12.4 %collective-permute-start.5 = (bf16[2,128,256]{2,1,0:T(8,128)(2,1)}, bf16[2,128,256]{2,1,0:T(8,128)(2,1)S(1)}, u32[]{:S(2)}, u32[]{:S(2)}) collective-permute-start(bf16[2,128,256]{2,1,0:T(8,128)(2,1)} %rest_0_.1), channel_id=1, source_target_pairs={{0,5},{1,4},{2,7},{3,6},{4,1},{5,0},{6,3},{7,2},{8,13},{9,12},{10,... | collective-permute-start | bytes 393224 | tf_op jit(solution)/shard_map/ppermute | solution.py:642
  16.2 9.0 %collective-permute-start.6 = (bf16[2,128,256]{2,1,0:T(8,128)(2,1)S(1)}, bf16[2,128,256]{2,1,0:T(8,128)(2,1)S(1)}, u32[]{:S(2)}, u32[]{:S(2)}) collective-permute-start(bf16[2,128,256]{2,1,0:T(8,128)(2,1)S(1)} %collective-permute-done.rest_6_), channel_id=1, source_target_pairs={{0,1},{1,0},{2,3},{3,2},{4,5},{5,4},{6,7},{7,6},{8,9},{9,8},{10,11... | collective-permute-start | bytes 393224 | tf_op jit(solution)/shard_map/ppermute | solution.py:642
  16.2 5.1 %copy-start.3 = (bf16[256,1024]{1,0:T(8,128)(2,1)S(1)}, bf16[256,1024]{1,0:T(8,128)(2,1)}, u32[]{:S(2)}) copy-start(bf16[256,1024]{1,0:T(8,128)(2,1)} %w0.3) | copy-start | bytes 1572868
  16.2 8.9 %copy-start.8 = (bf16[2,128,256]{2,1,0:T(8,128)(2,1)S(1)}, bf16[2,128,256]{2,1,0:T(8,128)(2,1)}, u32[]{:S(2)}) copy-start(bf16[2,128,256]{2,1,0:T(8,128)(2,1)} %rest_0_.1) | copy-start | bytes 393220
  16.2 8.9 %copy-start.9 = (s32[12,8]{0,1:T(8,128)S(1)}, s32[12,8]{0,1:T(8,128)}, u32[]{:S(2)}) copy-start(s32[12,8]{0,1:T(8,128)} %param.27) | copy-start | bytes 1156
  16.2 8.9 %copy-start.10 = (s32[12]{0:T(128)S(1)}, s32[12]{0:T(128)}, u32[]{:S(2)}) copy-start(s32[12]{0:T(128)} %group_ids.1) | copy-start | bytes 148
  21.3 13.1 %collective-permute-start.10 = (bf16[256,1024]{1,0:T(8,128)(2,1)S(1)}, bf16[256,1024]{1,0:T(8,128)(2,1)S(1)}, u32[]{:S(2)}, u32[]{:S(2)}) collective-permute-start(bf16[256,1024]{1,0:T(8,128)(2,1)S(1)} %copy-done.3), channel_id=1, source_target_pairs={{0,8},{8,0},{16,24},{24,16},{1,9},{9,1},{17,25},{25,17},{2,10},{10... | collective-permute-start | bytes 1572872 | tf_op jit(solution)/shard_map/ppermute | solution.py:645
  21.4 14.5 %collective-permute-start.12 = (bf16[256,1024]{1,0:T(8,128)(2,1)S(1)}, bf16[256,1024]{1,0:T(8,128)(2,1)S(1)}, u32[]{:S(2)}, u32[]{:S(2)}) collective-permute-start(bf16[256,1024]{1,0:T(8,128)(2,1)S(1)} %collective-permute-done.11.w2), channel_id=1, source_target_pairs={{0,8},{8,0},{16,24},{24,16},{1,9},{9,1},{17,25},{25,17},{2,10},{10... | collective-permute-start | bytes 1572872 | tf_op jit(solution)/shard_map/ppermute | solution.py:645
  25.1 10.8 %copy-start = (bf16[1024,1024]{1,0:T(8,128)(2,1)S(1)}, bf16[1024,1024]{1,0:T(8,128)(2,1)}, u32[]{:S(2)}) copy-start(bf16[1024,1024]{1,0:T(8,128)(2,1)} %w_up.3) | copy-start | bytes 6291460
  25.1 10.8 %copy-start.1 = (bf16[1024,1024]{1,0:T(8,128)(2,1)S(1)}, bf16[1024,1024]{1,0:T(8,128)(2,1)}, u32[]{:S(2)}) copy-start(bf16[1024,1024]{1,0:T(8,128)(2,1)} %w_down.3) | copy-start | bytes 6291460
  25.2 10.7 %copy-start.2 = (bf16[384,1024]{1,0:T(8,128)(2,1)S(1)}, bf16[384,1024]{1,0:T(8,128)(2,1)}, u32[]{:S(2)}) copy-start(bf16[384,1024]{1,0:T(8,128)(2,1)} %tokens.3) | copy-start | bytes 2359300
  25.2 10.7 %copy-start.5 = (f32[1024]{0:T(1024)S(1)}, f32[1024]{0:T(1024)}, u32[]{:S(2)}) copy-start(f32[1024]{0:T(1024)} %param.19) | copy-start | bytes 12292
  28.6 5.8 %collective-permute-start.8 = (bf16[400,256]{1,0:T(8,128)(2,1)S(1)}, bf16[400,256]{1,0:T(8,128)(2,1)S(1)}, u32[]{:S(2)}, u32[]{:S(2)}) collective-permute-start(bf16[400,256]{1,0:T(8,128)(2,1)S(1)} %attend.1.a0), channel_id=1, source_target_pairs={{0,16},{8,24},{16,0},{24,8},{1,17},{9,25},{17,1},{25,9},{2,18},{10... | collective-permute-start | bytes 614408 | tf_op jit(solution)/shard_map/ppermute | solution.py:645
  29.6 4.9 %collective-permute-start.7 = (bf16[400,256]{1,0:T(8,128)(2,1)S(1)}, bf16[400,256]{1,0:T(8,128)(2,1)S(1)}, u32[]{:S(2)}, u32[]{:S(2)}) collective-permute-start(bf16[400,256]{1,0:T(8,128)(2,1)S(1)} %attend.1.a0), channel_id=1, source_target_pairs={{0,8},{8,0},{16,24},{24,16},{1,9},{9,1},{17,25},{25,17},{2,10},{10... | collective-permute-start | bytes 614408 | tf_op jit(solution)/shard_map/ppermute | solution.py:645
  34.4 1.5 %collective-permute-start.9 = (bf16[400,256]{1,0:T(8,128)(2,1)S(1)}, bf16[400,256]{1,0:T(8,128)(2,1)S(1)}, u32[]{:S(2)}, u32[]{:S(2)}) collective-permute-start(bf16[400,256]{1,0:T(8,128)(2,1)S(1)} %collective-permute-done.8.a2), channel_id=1, source_target_pairs={{0,8},{8,0},{16,24},{24,16},{1,9},{9,1},{17,25},{25,17},{2,10},{10... | collective-permute-start | bytes 614408 | tf_op jit(solution)/shard_map/ppermute | solution.py:645
  38.2 9.9 %copy-start.4 = (bf16[1024,128]{1,0:T(8,128)(2,1)S(1)}, bf16[1024,128]{1,0:T(8,128)(2,1)}, u32[]{:S(2)}) copy-start(bf16[1024,128]{1,0:T(8,128)(2,1)} %w_proj.1) | copy-start | bytes 786436
  38.2 9.9 %copy-start.6 = (f32[1024]{0:T(1024)S(1)}, f32[1024]{0:T(1024)}, u32[]{:S(2)}) copy-start(f32[1024]{0:T(1024)} %param.20) | copy-start | bytes 12292
  38.2 2.5 %collective-permute-start.13 = (bf16[192,1024]{1,0:T(8,128)(2,1)S(1)}, bf16[192,1024]{1,0:T(8,128)(2,1)S(1)}, u32[]{:S(2)}, u32[]{:S(2)}) collective-permute-start(bf16[192,1024]{1,0:T(8,128)(2,1)S(1)} %feed_other.1), channel_id=1, source_target_pairs={{0,8},{8,0},{16,24},{24,16},{1,9},{9,1},{17,25},{25,17},{2,10},{10... | collective-permute-start | bytes 1179656 | tf_op jit(solution)/shard_map/ppermute | solution.py:645
  40.7 20.4 %copy-start.7 = (s32[64]{0:T(128)S(1)}, s32[64]{0:T(128)}, u32[]{:S(2)}) copy-start(s32[64]{0:T(128)} %lengths.1) | copy-start | bytes 772
  40.8 7.3 %collective-permute-start.14 = (bf16[96,1024]{1,0:T(8,128)(2,1)S(1)}, bf16[96,1024]{1,0:T(8,128)(2,1)S(1)}, u32[]{:S(2)}, u32[]{:S(2)}) collective-permute-start(bf16[96,1024]{1,0:T(8,128)(2,1)S(1)} %fold.1), channel_id=1, source_target_pairs={{0,16},{8,24},{16,0},{24,8},{1,17},{9,25},{17,1},{25,9},{2,18},{10... | collective-permute-start | bytes 589832 | tf_op jit(solution)/shard_map/ppermute | solution.py:645
  69.3 10.9 %all-to-all-start.1 = ((f32[32,8,128]{2,1,0:T(8,128)}), f32[32,8,128]{2,1,0:T(8,128)S(1)}, u32[]{:S(2)}, u32[]{:S(2)}) async-start(f32[32,8,128]{2,1,0:T(8,128)} %bitcast.5), calls=%async_computation.1 | async-start | bytes 262144 | tf_op jit(solution)/shard_map/all_to_all | solution.py:716
  72.0 2.2 %collective-permute-start.15 = (bf16[96,128]{1,0:T(8,128)(2,1)S(1)}, bf16[96,128]{1,0:T(8,128)(2,1)S(1)}, u32[]{:S(2)}, u32[]{:S(2)}) collective-permute-start(bf16[96,128]{1,0:T(8,128)(2,1)S(1)} %get-tuple-element.21.refs_0_), channel_id=1, source_target_pairs={{0,8},{8,0},{16,24},{24,16},{1,9},{9,1},{17,25},{25,17},{2,10},{10... | collective-permute-start | bytes 73736 | tf_op jit(solution)/shard_map/ppermute | solution.py:645
  72.3 3.9 %collective-permute-start.16 = (bf16[96,128]{1,0:T(8,128)(2,1)S(1)}, bf16[96,128]{1,0:T(8,128)(2,1)S(1)}, u32[]{:S(2)}, u32[]{:S(2)}) collective-permute-start(bf16[96,128]{1,0:T(8,128)(2,1)S(1)} %get-tuple-element.21.refs_0_), channel_id=1, source_target_pairs={{0,16},{8,24},{16,0},{24,8},{1,17},{9,25},{17,1},{25,9},{2,18},{10... | collective-permute-start | bytes 73736 | tf_op jit(solution)/shard_map/ppermute | solution.py:645
  74.1 3.4 %collective-permute-start.17 = (bf16[96,128]{1,0:T(8,128)(2,1)S(1)}, bf16[96,128]{1,0:T(8,128)(2,1)S(1)}, u32[]{:S(2)}, u32[]{:S(2)}) collective-permute-start(bf16[96,128]{1,0:T(8,128)(2,1)S(1)} %get-tuple-element.21.refs_0_), channel_id=1, source_target_pairs={{0,24},{8,16},{16,8},{24,0},{1,25},{9,17},{17,9},{25,1},{2,26},{10... | collective-permute-start | bytes 73736 | tf_op jit(solution)/shard_map/ppermute | solution.py:645

commit v7 on v6

--- a/solution.py
+++ b/solution.py
@@ -153,7 +153,7 @@
 LANES = 128
 MIB = 1 << 20
 EXTRA = 16
-PREP_UNROLL = 6
+PREP_UNROLL = 12
 ATT_UNROLL = 12
 SCORE_UNROLL = 32
 
@@ -397,13 +397,9 @@
     for piece, weight in zip(a, w):
         mixed = mixed + jnp.dot(piece[rows, :], weight[...], preferred_element_type=jnp.float32)
     hidden = norm_rows(mixed, gain[...]).astype(jnp.bfloat16)
-    total = None
-    step = 256
-    for at in range(0, w_up.shape[1], step):
-        up = jnp.dot(hidden, w_up[:, at : at + step], preferred_element_type=jnp.float32)
-        inner = (0.5 * up * (1.0 + lax.erf(up * math.sqrt(0.5)))).astype(jnp.bfloat16)
-        part = jnp.dot(inner, w_down[at : at + step, :], preferred_element_type=jnp.float32)
-        total = part if total is None else total + part
+    up = jnp.dot(hidden, w_up[...], preferred_element_type=jnp.float32)
+    inner = (0.5 * up * (1.0 + lax.erf(up * math.sqrt(0.5)))).astype(jnp.bfloat16)
+    total = jnp.dot(inner, w_down[...], preferred_element_type=jnp.float32)
     return hidden, total
 
 

time: 81 us -> 79.7 us (0.984)
  Pallas kernels: 23.3 us -> 19.5 us
  starting transfers between devices: 21.6 us -> 23.4 us
    pallas_call x1, Pallas kernels: 8.2 us -> 5.83 us  [body(): pl.pallas_call(score_kernel, out_shape=jax.ShapeDtypeStruct((n_doc, n_hea...]
    all_to_all x1, starting transfers between devices: 2.7 us -> 4.62 us  [body(): lax.all_to_all(rated.reshape(-1, LANES), ('doc', 'head'), 0, 0, tiled=True)]
    pallas_call x2, Pallas kernels: 4.56 us -> 3.6 us  [feed(): pl.pallas_call(kernel, out_shape=outs, in_specs=full_specs(12), out_specs...]
  transfers between devices with their start and end apart: 19 -> 19, of which waited for: 9 -> 9; matrix products, arithmetic and copies ran while one was open for 0% -> 0% of each run, Pallas kernels for 14% -> 13%
where the time goes in v7:
time: 79.7 us; the launch traced here: 79.6 us
  starting transfers between devices  23.4 us (29%)
  waiting for transfers between devices  23.4 us (29%)
  Pallas kernels  19.5 us (24%)
  blocking collectives  12.5 us (16%)
  between operations  0.84 us (1%)
    ppermute x11, waiting for transfers between devices, over_head(): return lax.ppermute(x, 'head', [(i, i ^ k) for i in range(n_head)])  15.9 us
    all_to_all x1, blocking collectives, body(): queries = lax.all_to_all(vectors, 'doc', 0, 0, tiled=True).reshape(-1, emb)  12.5 us
    ppermute x7, starting transfers between devices, over_doc(): return lax.ppermute(x, 'doc', [(i, i ^ k) for i in range(n_doc)])  12.5 us
    ppermute x11, starting transfers between devices, over_head(): return lax.ppermute(x, 'head', [(i, i ^ k) for i in range(n_head)])  6.26 us
    pallas_call x1, Pallas kernels, body(): pl.pallas_call(score_kernel, out_shape=jax.ShapeDtypeStruct((n_doc, n_hea...  5.83 us
    ppermute x7, waiting for transfers between devices, over_doc(): return lax.ppermute(x, 'doc', [(i, i ^ k) for i in range(n_doc)])  5.22 us
    pallas_call x1, Pallas kernels, prepare(): pl.pallas_call(prepare_kernel, out_shape=[jax.ShapeDtypeStruct((rows, 3 *...  4.63 us
    all_to_all x1, starting transfers between devices, body(): lax.all_to_all(rated.reshape(-1, LANES), ('doc', 'head'), 0, 0, tiled=True)  4.62 us
  transfers between devices with their start and end apart: 19, of which 9 were waited for; matrix products, arithmetic and copies ran while one was open for 0% of the time, Pallas kernels for 13%

profile of v7, /device:TPU:0, one launch (start us, length us, event | category | flops | bytes accessed | tf_op | source)
XLA Modules:
  0.0 79.6 jit_solution(11584277155951949458)
XLA Ops:
  0.6 5.1 %collective-permute-start = (bf16[2,128,256]{2,1,0:T(8,128)(2,1)}, bf16[2,128,256]{2,1,0:T(8,128)(2,1)S(1)}, u32[]{:S(2)}, u32[]{:S(2)}) collective-permute-start(bf16[2,128,256]{2,1,0:T(8,128)(2,1)} %rest_0_.1), channel_id=1, source_target_pairs={{0,6},{1,7},{2,4},{3,5},{4,2},{5,3},{6,0},{7,1},{8,14},{9,15},{10,... | collective-permute-start | bytes 393224 | tf_op jit(solution)/shard_map/ppermute | solution.py:638
  5.7 1.5 %collective-permute-start.1 = (bf16[2,128,256]{2,1,0:T(8,128)(2,1)}, bf16[2,128,256]{2,1,0:T(8,128)(2,1)S(1)}, u32[]{:S(2)}, u32[]{:S(2)}) collective-permute-start(bf16[2,128,256]{2,1,0:T(8,128)(2,1)} %rest_0_.1), channel_id=1, source_target_pairs={{0,1},{1,0},{2,3},{3,2},{4,5},{5,4},{6,7},{7,6},{8,9},{9,8},{10,11... | collective-permute-start | bytes 393224 | tf_op jit(solution)/shard_map/ppermute | solution.py:638
  7.2 0.0 collective-permute-start.2
  7.2 1.5 %collective-permute-start.11 = (bf16[256,1024]{1,0:T(8,128)(2,1)}, bf16[256,1024]{1,0:T(8,128)(2,1)S(1)}, u32[]{:S(2)}, u32[]{:S(2)}) collective-permute-start(bf16[256,1024]{1,0:T(8,128)(2,1)} %w0.3), channel_id=1, source_target_pairs={{0,16},{8,24},{16,0},{24,8},{1,17},{9,25},{17,1},{25,9},{2,18},{10... | collective-permute-start | bytes 1572872 | tf_op jit(solution)/shard_map/ppermute | solution.py:641
  8.8 2.0 %collective-permute-start.3 = (bf16[2,128,256]{2,1,0:T(8,128)(2,1)}, bf16[2,128,256]{2,1,0:T(8,128)(2,1)S(1)}, u32[]{:S(2)}, u32[]{:S(2)}) collective-permute-start(bf16[2,128,256]{2,1,0:T(8,128)(2,1)} %rest_0_.1), channel_id=1, source_target_pairs={{0,3},{1,2},{2,1},{3,0},{4,7},{5,6},{6,5},{7,4},{8,11},{9,10},{10,... | collective-permute-start | bytes 393224 | tf_op jit(solution)/shard_map/ppermute | solution.py:638
  10.8 2.0 %collective-permute-start.4 = (bf16[2,128,256]{2,1,0:T(8,128)(2,1)}, bf16[2,128,256]{2,1,0:T(8,128)(2,1)S(1)}, u32[]{:S(2)}, u32[]{:S(2)}) collective-permute-start(bf16[2,128,256]{2,1,0:T(8,128)(2,1)} %rest_0_.1), channel_id=1, source_target_pairs={{0,4},{1,5},{2,6},{3,7},{4,0},{5,1},{6,2},{7,3},{8,12},{9,13},{10,... | collective-permute-start | bytes 393224 | tf_op jit(solution)/shard_map/ppermute | solution.py:638
  12.7 1.9 %collective-permute-start.5 = (bf16[2,128,256]{2,1,0:T(8,128)(2,1)}, bf16[2,128,256]{2,1,0:T(8,128)(2,1)S(1)}, u32[]{:S(2)}, u32[]{:S(2)}) collective-permute-start(bf16[2,128,256]{2,1,0:T(8,128)(2,1)} %rest_0_.1), channel_id=1, source_target_pairs={{0,5},{1,4},{2,7},{3,6},{4,1},{5,0},{6,3},{7,2},{8,13},{9,12},{10,... | collective-permute-start | bytes 393224 | tf_op jit(solution)/shard_map/ppermute | solution.py:638
  14.6 1.5 %collective-permute-done.2.rest_2_ = bf16[2,128,256]{2,1,0:T(8,128)(2,1)S(1)} collective-permute-done((bf16[2,128,256]{2,1,0:T(8,128)(2,1)}, bf16[2,128,256]{2,1,0:T(8,128)(2,1)S(1)}, u32[]{:S(2)}, u32[]{:S(2)}) %collective-permute-start.2) | collective-permute-done | bytes 131104 | tf_op jit(solution)/shard_map/ppermute | solution.py:638
  16.2 0.0 collective-permute-start.6
  16.2 4.6 %prepare.1 = (bf16[384,768]{1,0:T(8,128)(2,1)S(1)}, f32[12,96,128]{2,1,0:T(8,128)S(1)}, bf16[512,256]{1,0:T(8,128)(2,1)S(1)}) custom-call(bf16[384,1024]{1,0:T(8,128)(2,1)} %tokens.3, bf16[3,1024,256]{2,1,0:T(8,128)(2,1)} %bitcast.15, bf16[512,1024]{1,0:T(8,128)(2,1)} %rel_table), custom_call_target="tpu_custom_call" | custom-call | flops 4194304000 | bytes 4194304 | tf_op jit(solution)/shard_map/prepare/pallas_call | solution.py:266
  20.8 0.0 collective-permute-done.3.rest_3_
  20.8 0.1 collective-permute-start.10
  20.9 0.0 collective-permute-done.11.w2
  20.9 0.5 collective-permute-start.12
  21.4 1.3 %collective-permute-done.4.rest_4_ = bf16[2,128,256]{2,1,0:T(8,128)(2,1)S(1)} collective-permute-done((bf16[2,128,256]{2,1,0:T(8,128)(2,1)}, bf16[2,128,256]{2,1,0:T(8,128)(2,1)S(1)}, u32[]{:S(2)}, u32[]{:S(2)}) %collective-permute-start.4) | collective-permute-done | bytes 131104 | tf_op jit(solution)/shard_map/ppermute | solution.py:638
  22.8 2.3 %collective-permute-done.5.rest_5_ = bf16[2,128,256]{2,1,0:T(8,128)(2,1)S(1)} collective-permute-done((bf16[2,128,256]{2,1,0:T(8,128)(2,1)}, bf16[2,128,256]{2,1,0:T(8,128)(2,1)S(1)}, u32[]{:S(2)}, u32[]{:S(2)}) %collective-permute-start.5) | collective-permute-done | bytes 131104 | tf_op jit(solution)/shard_map/ppermute | solution.py:638
  25.1 0.0 collective-permute-done.6.rest_7_
  25.1 0.0 copy-start
  25.1 0.0 copy-start.1
  25.2 0.0 copy-start.2
  25.2 0.0 copy-start.5
  25.2 3.4 %attend.1.a0 = bf16[400,256]{1,0:T(8,128)(2,1)S(1)} custom-call(s32[12]{0:T(128)S(1)} %copy-done.10, bf16[384,768]{1,0:T(8,128)(2,1)S(1)} %get-tuple-element.13.qkv, f32[12,96,128]{2,1,0:T(8,128)S(1)} %get-tuple-element.14.base, bf16[512,256]{1,0:T(8,128)(2,1)S(1)} %get-tuple-element.15.rel_q_heads, s32[8,12]{1,0:T(8,128)S(1)} %bitcast.13, ...), custom_call_target="tpu_custom_call" | custom-call | flops 2097152000 | bytes 2097152 | tf_op jit(solution)/shard_map/attend/pallas_call | solution.py:368
  28.6 1.0 %collective-permute-start.8 = (bf16[400,256]{1,0:T(8,128)(2,1)S(1)}, bf16[400,256]{1,0:T(8,128)(2,1)S(1)}, u32[]{:S(2)}, u32[]{:S(2)}) collective-permute-start(bf16[400,256]{1,0:T(8,128)(2,1)S(1)} %attend.1.a0), channel_id=1, source_target_pairs={{0,16},{8,24},{16,0},{24,8},{1,17},{9,25},{17,1},{25,9},{2,18},{10... | collective-permute-start | bytes 614408 | tf_op jit(solution)/shard_map/ppermute | solution.py:641
  29.6 0.0 collective-permute-start.7
  29.6 4.8 %collective-permute-done.8.a2 = bf16[400,256]{1,0:T(8,128)(2,1)S(1)} collective-permute-done((bf16[400,256]{1,0:T(8,128)(2,1)S(1)}, bf16[400,256]{1,0:T(8,128)(2,1)S(1)}, u32[]{:S(2)}, u32[]{:S(2)}) %collective-permute-start.8) | collective-permute-done | bytes 204832 | tf_op jit(solution)/shard_map/ppermute | solution.py:641
  34.4 0.0 collective-permute-start.9
  34.4 0.0 collective-permute-done.7.a1
  34.4 1.4 %collective-permute-done.9.a3 = bf16[400,256]{1,0:T(8,128)(2,1)S(1)} collective-permute-done((bf16[400,256]{1,0:T(8,128)(2,1)S(1)}, bf16[400,256]{1,0:T(8,128)(2,1)S(1)}, u32[]{:S(2)}, u32[]{:S(2)}) %collective-permute-start.9) | collective-permute-done | bytes 204832 | tf_op jit(solution)/shard_map/ppermute | solution.py:641
  35.9 1.8 %feed_other.1 = bf16[192,1024]{1,0:T(8,128)(2,1)S(1)} custom-call(bf16[400,256]{1,0:T(8,128)(2,1)S(1)} %attend.1.a0, bf16[400,256]{1,0:T(8,128)(2,1)S(1)} %collective-permute-done.7.a1, bf16[400,256]{1,0:T(8,128)(2,1)S(1)} %collective-permute-done.8.a2, bf16[400,256]{1,0:T(8,128)(2,1)S(1)} %collective-permute-done.9.a3, bf16[256,1024]{1,0:T(8,128)(2,1)S(1)} %copy-done.3, ...), custom_call_target="tpu_custom_call" | custom-call | flops 1677721600 | bytes 6291456 | tf_op jit(solution)/shard_map/feed_other/pallas_call | solution.py:433
  37.7 0.0 copy-start.4
  37.7 0.0 copy-start.6
  37.7 0.2 collective-permute-start.13
  37.9 1.8 %feed_own.1 = (f32[96,1024]{1,0:T(8,128)S(1)}, f32[96,1024]{1,0:T(8,128)S(1)}) custom-call(bf16[400,256]{1,0:T(8,128)(2,1)S(1)} %attend.1.a0, bf16[400,256]{1,0:T(8,128)(2,1)S(1)} %collective-permute-done.7.a1, bf16[400,256]{1,0:T(8,128)(2,1)S(1)} %collective-permute-done.8.a2, bf16[400,256]{1,0:T(8,128)(2,1)S(1)} %collective-permute-done.9.a3, ...), custom_call_target="tpu_custom_call" | custom-call | flops 1677721600 | bytes 6291456 | tf_op jit(solution)/shard_map/feed_own/pallas_call | solution.py:433
  39.8 0.0 copy-start.7
  39.8 0.1 fold.1
  39.8 1.0 %collective-permute-start.14 = (bf16[96,1024]{1,0:T(8,128)(2,1)S(1)}, bf16[96,1024]{1,0:T(8,128)(2,1)S(1)}, u32[]{:S(2)}, u32[]{:S(2)}) collective-permute-start(bf16[96,1024]{1,0:T(8,128)(2,1)S(1)} %fold.1), channel_id=1, source_target_pairs={{0,16},{8,24},{16,0},{24,8},{1,17},{9,25},{17,1},{25,9},{2,18},{10... | collective-permute-start | bytes 589832 | tf_op jit(solution)/shard_map/ppermute | solution.py:641
  40.8 6.3 %collective-permute-done.14.from_y = bf16[96,1024]{1,0:T(8,128)(2,1)S(1)} collective-permute-done((bf16[96,1024]{1,0:T(8,128)(2,1)S(1)}, bf16[96,1024]{1,0:T(8,128)(2,1)S(1)}, u32[]{:S(2)}, u32[]{:S(2)}) %collective-permute-start.14) | collective-permute-done | bytes 196640 | tf_op jit(solution)/shard_map/ppermute | solution.py:641
  47.1 0.5 project.1
  47.6 12.5 %all_to_all.14 = bf16[8,112,128]{2,1,0:T(8,128)(2,1)S(1)} all-to-all(bf16[8,112,128]{2,1,0:T(8,128)(2,1)S(1)} %get-tuple-element.20), channel_id=1, replica_groups=mesh['head'=4,'doc'=8] {'doc'}, dimensions={0} | all-to-all | bytes 458752 | tf_op jit(solution)/shard_map/all_to_all | solution.py:695
  60.1 5.8 %rate.1 = f32[8,4,8,128]{3,2,1,0:T(8,128)} custom-call(s32[64]{0:T(128)S(1)} %copy-done.7, bf16[896,128]{1,0:T(8,128)(2,1)S(1)} %bitcast.8, bf16[64,256,128]{2,1,0:T(8,128)(2,1)} %docs.1), custom_call_target="tpu_custom_call" | custom-call | tf_op jit(solution)/shard_map/rate/pallas_call | solution.py:697
  66.0 4.6 %all-to-all-start.1 = ((f32[32,8,128]{2,1,0:T(8,128)}), f32[32,8,128]{2,1,0:T(8,128)S(1)}, u32[]{:S(2)}, u32[]{:S(2)}) async-start(f32[32,8,128]{2,1,0:T(8,128)} %bitcast.5), calls=%async_computation.1 | async-start | bytes 262144 | tf_op jit(solution)/shard_map/all_to_all | solution.py:712
  70.6 0.3 collective-permute-start.15
  70.9 1.7 %collective-permute-start.16 = (bf16[96,128]{1,0:T(8,128)(2,1)S(1)}, bf16[96,128]{1,0:T(8,128)(2,1)S(1)}, u32[]{:S(2)}, u32[]{:S(2)}) collective-permute-start(bf16[96,128]{1,0:T(8,128)(2,1)S(1)} %get-tuple-element.21.refs_0_), channel_id=1, source_target_pairs={{0,16},{8,24},{16,0},{24,8},{1,17},{9,25},{17,1},{25,9},{2,18},{10... | collective-permute-start | bytes 73736 | tf_op jit(solution)/shard_map/ppermute | solution.py:641
  72.6 2.2 %collective-permute-done.16.refs_2_ = bf16[96,128]{1,0:T(8,128)(2,1)S(1)} collective-permute-done((bf16[96,128]{1,0:T(8,128)(2,1)S(1)}, bf16[96,128]{1,0:T(8,128)(2,1)S(1)}, u32[]{:S(2)}, u32[]{:S(2)}) %collective-permute-start.16) | collective-permute-done | bytes 24608 | tf_op jit(solution)/shard_map/ppermute | solution.py:641
  74.9 1.1 %collective-permute-done.17.refs_3_ = bf16[96,128]{1,0:T(8,128)(2,1)S(1)} collective-permute-done((bf16[96,128]{1,0:T(8,128)(2,1)S(1)}, bf16[96,128]{1,0:T(8,128)(2,1)S(1)}, u32[]{:S(2)}, u32[]{:S(2)}) %collective-permute-start.17) | collective-permute-done | bytes 24608 | tf_op jit(solution)/shard_map/ppermute | solution.py:641
  76.0 0.7 arrange.1
  76.6 2.2 %all-to-all-done.1 = f32[32,8,128]{2,1,0:T(8,128)S(1)} async-done(((f32[32,8,128]{2,1,0:T(8,128)}), f32[32,8,128]{2,1,0:T(8,128)S(1)}, u32[]{:S(2)}, u32[]{:S(2)}) %all-to-all-start.1) | async-done | bytes 131104 | tf_op jit(solution)/shard_map/all_to_all | solution.py:712
  78.8 0.8 %collect.1 = f32[8,12]{1,0:T(8,128)} custom-call(f32[8,4,8,128]{3,2,1,0:T(8,128)S(1)} %bitcast.9), custom_call_target="tpu_custom_call" | custom-call | tf_op jit(solution)/shard_map/collect/pallas_call | solution.py:725
  (22 shorter events, 0.0 us)
Async XLA Ops:
  0.6 10.1 %collective-permute-start = (bf16[2,128,256]{2,1,0:T(8,128)(2,1)}, bf16[2,128,256]{2,1,0:T(8,128)(2,1)S(1)}, u32[]{:S(2)}, u32[]{:S(2)}) collective-permute-start(bf16[2,128,256]{2,1,0:T(8,128)(2,1)} %rest_0_.1), channel_id=1, source_target_pairs={{0,6},{1,7},{2,4},{3,5},{4,2},{5,3},{6,0},{7,1},{8,14},{9,15},{10,... | collective-permute-start | bytes 393224 | tf_op jit(solution)/shard_map/ppermute | solution.py:638
  5.7 7.0 %collective-permute-start.1 = (bf16[2,128,256]{2,1,0:T(8,128)(2,1)}, bf16[2,128,256]{2,1,0:T(8,128)(2,1)S(1)}, u32[]{:S(2)}, u32[]{:S(2)}) collective-permute-start(bf16[2,128,256]{2,1,0:T(8,128)(2,1)} %rest_0_.1), channel_id=1, source_target_pairs={{0,1},{1,0},{2,3},{3,2},{4,5},{5,4},{6,7},{7,6},{8,9},{9,8},{10,11... | collective-permute-start | bytes 393224 | tf_op jit(solution)/shard_map/ppermute | solution.py:638
  7.2 8.9 %collective-permute-start.2 = (bf16[2,128,256]{2,1,0:T(8,128)(2,1)}, bf16[2,128,256]{2,1,0:T(8,128)(2,1)S(1)}, u32[]{:S(2)}, u32[]{:S(2)}) collective-permute-start(bf16[2,128,256]{2,1,0:T(8,128)(2,1)} %rest_0_.1), channel_id=1, source_target_pairs={{0,2},{1,3},{2,0},{3,1},{4,6},{5,7},{6,4},{7,5},{8,10},{9,11},{10,... | collective-permute-start | bytes 393224 | tf_op jit(solution)/shard_map/ppermute | solution.py:638
  7.2 13.7 %collective-permute-start.11 = (bf16[256,1024]{1,0:T(8,128)(2,1)}, bf16[256,1024]{1,0:T(8,128)(2,1)S(1)}, u32[]{:S(2)}, u32[]{:S(2)}) collective-permute-start(bf16[256,1024]{1,0:T(8,128)(2,1)} %w0.3), channel_id=1, source_target_pairs={{0,16},{8,24},{16,0},{24,8},{1,17},{9,25},{17,1},{25,9},{2,18},{10... | collective-permute-start | bytes 1572872 | tf_op jit(solution)/shard_map/ppermute | solution.py:641
  8.8 12.1 %collective-permute-start.3 = (bf16[2,128,256]{2,1,0:T(8,128)(2,1)}, bf16[2,128,256]{2,1,0:T(8,128)(2,1)S(1)}, u32[]{:S(2)}, u32[]{:S(2)}) collective-permute-start(bf16[2,128,256]{2,1,0:T(8,128)(2,1)} %rest_0_.1), channel_id=1, source_target_pairs={{0,3},{1,2},{2,1},{3,0},{4,7},{5,6},{6,5},{7,4},{8,11},{9,10},{10,... | collective-permute-start | bytes 393224 | tf_op jit(solution)/shard_map/ppermute | solution.py:638
  10.8 12.0 %collective-permute-start.4 = (bf16[2,128,256]{2,1,0:T(8,128)(2,1)}, bf16[2,128,256]{2,1,0:T(8,128)(2,1)S(1)}, u32[]{:S(2)}, u32[]{:S(2)}) collective-permute-start(bf16[2,128,256]{2,1,0:T(8,128)(2,1)} %rest_0_.1), channel_id=1, source_target_pairs={{0,4},{1,5},{2,6},{3,7},{4,0},{5,1},{6,2},{7,3},{8,12},{9,13},{10,... | collective-permute-start | bytes 393224 | tf_op jit(solution)/shard_map/ppermute | solution.py:638
  12.7 12.4 %collective-permute-start.5 = (bf16[2,128,256]{2,1,0:T(8,128)(2,1)}, bf16[2,128,256]{2,1,0:T(8,128)(2,1)S(1)}, u32[]{:S(2)}, u32[]{:S(2)}) collective-permute-start(bf16[2,128,256]{2,1,0:T(8,128)(2,1)} %rest_0_.1), channel_id=1, source_target_pairs={{0,5},{1,4},{2,7},{3,6},{4,1},{5,0},{6,3},{7,2},{8,13},{9,12},{10,... | collective-permute-start | bytes 393224 | tf_op jit(solution)/shard_map/ppermute | solution.py:638
  16.2 9.0 %collective-permute-start.6 = (bf16[2,128,256]{2,1,0:T(8,128)(2,1)S(1)}, bf16[2,128,256]{2,1,0:T(8,128)(2,1)S(1)}, u32[]{:S(2)}, u32[]{:S(2)}) collective-permute-start(bf16[2,128,256]{2,1,0:T(8,128)(2,1)S(1)} %collective-permute-done.rest_6_), channel_id=1, source_target_pairs={{0,1},{1,0},{2,3},{3,2},{4,5},{5,4},{6,7},{7,6},{8,9},{9,8},{10,11... | collective-permute-start | bytes 393224 | tf_op jit(solution)/shard_map/ppermute | solution.py:638
  16.2 4.7 %copy-start.3 = (bf16[256,1024]{1,0:T(8,128)(2,1)S(1)}, bf16[256,1024]{1,0:T(8,128)(2,1)}, u32[]{:S(2)}) copy-start(bf16[256,1024]{1,0:T(8,128)(2,1)} %w0.3) | copy-start | bytes 1572868
  16.2 8.9 %copy-start.8 = (bf16[2,128,256]{2,1,0:T(8,128)(2,1)S(1)}, bf16[2,128,256]{2,1,0:T(8,128)(2,1)}, u32[]{:S(2)}) copy-start(bf16[2,128,256]{2,1,0:T(8,128)(2,1)} %rest_0_.1) | copy-start | bytes 393220
  16.2 8.9 %copy-start.9 = (s32[12,8]{0,1:T(8,128)S(1)}, s32[12,8]{0,1:T(8,128)}, u32[]{:S(2)}) copy-start(s32[12,8]{0,1:T(8,128)} %param.27) | copy-start | bytes 1156
  16.2 8.9 %copy-start.10 = (s32[12]{0:T(128)S(1)}, s32[12]{0:T(128)}, u32[]{:S(2)}) copy-start(s32[12]{0:T(128)} %group_ids.1) | copy-start | bytes 148
  20.8 13.6 %collective-permute-start.10 = (bf16[256,1024]{1,0:T(8,128)(2,1)S(1)}, bf16[256,1024]{1,0:T(8,128)(2,1)S(1)}, u32[]{:S(2)}, u32[]{:S(2)}) collective-permute-start(bf16[256,1024]{1,0:T(8,128)(2,1)S(1)} %copy-done.3), channel_id=1, source_target_pairs={{0,8},{8,0},{16,24},{24,16},{1,9},{9,1},{17,25},{25,17},{2,10},{10... | collective-permute-start | bytes 1572872 | tf_op jit(solution)/shard_map/ppermute | solution.py:641
  20.9 15.0 %collective-permute-start.12 = (bf16[256,1024]{1,0:T(8,128)(2,1)S(1)}, bf16[256,1024]{1,0:T(8,128)(2,1)S(1)}, u32[]{:S(2)}, u32[]{:S(2)}) collective-permute-start(bf16[256,1024]{1,0:T(8,128)(2,1)S(1)} %collective-permute-done.11.w2), channel_id=1, source_target_pairs={{0,8},{8,0},{16,24},{24,16},{1,9},{9,1},{17,25},{25,17},{2,10},{10... | collective-permute-start | bytes 1572872 | tf_op jit(solution)/shard_map/ppermute | solution.py:641
  25.1 10.8 %copy-start = (bf16[1024,1024]{1,0:T(8,128)(2,1)S(1)}, bf16[1024,1024]{1,0:T(8,128)(2,1)}, u32[]{:S(2)}) copy-start(bf16[1024,1024]{1,0:T(8,128)(2,1)} %w_up.3) | copy-start | bytes 6291460
  25.1 10.8 %copy-start.1 = (bf16[1024,1024]{1,0:T(8,128)(2,1)S(1)}, bf16[1024,1024]{1,0:T(8,128)(2,1)}, u32[]{:S(2)}) copy-start(bf16[1024,1024]{1,0:T(8,128)(2,1)} %w_down.3) | copy-start | bytes 6291460
  25.2 10.7 %copy-start.2 = (bf16[384,1024]{1,0:T(8,128)(2,1)S(1)}, bf16[384,1024]{1,0:T(8,128)(2,1)}, u32[]{:S(2)}) copy-start(bf16[384,1024]{1,0:T(8,128)(2,1)} %tokens.3) | copy-start | bytes 2359300
  25.2 10.7 %copy-start.5 = (f32[1024]{0:T(1024)S(1)}, f32[1024]{0:T(1024)}, u32[]{:S(2)}) copy-start(f32[1024]{0:T(1024)} %param.19) | copy-start | bytes 12292
  28.6 5.8 %collective-permute-start.8 = (bf16[400,256]{1,0:T(8,128)(2,1)S(1)}, bf16[400,256]{1,0:T(8,128)(2,1)S(1)}, u32[]{:S(2)}, u32[]{:S(2)}) collective-permute-start(bf16[400,256]{1,0:T(8,128)(2,1)S(1)} %attend.1.a0), channel_id=1, source_target_pairs={{0,16},{8,24},{16,0},{24,8},{1,17},{9,25},{17,1},{25,9},{2,18},{10... | collective-permute-start | bytes 614408 | tf_op jit(solution)/shard_map/ppermute | solution.py:641
  29.6 4.9 %collective-permute-start.7 = (bf16[400,256]{1,0:T(8,128)(2,1)S(1)}, bf16[400,256]{1,0:T(8,128)(2,1)S(1)}, u32[]{:S(2)}, u32[]{:S(2)}) collective-permute-start(bf16[400,256]{1,0:T(8,128)(2,1)S(1)} %attend.1.a0), channel_id=1, source_target_pairs={{0,8},{8,0},{16,24},{24,16},{1,9},{9,1},{17,25},{25,17},{2,10},{10... | collective-permute-start | bytes 614408 | tf_op jit(solution)/shard_map/ppermute | solution.py:641
  34.4 1.5 %collective-permute-start.9 = (bf16[400,256]{1,0:T(8,128)(2,1)S(1)}, bf16[400,256]{1,0:T(8,128)(2,1)S(1)}, u32[]{:S(2)}, u32[]{:S(2)}) collective-permute-start(bf16[400,256]{1,0:T(8,128)(2,1)S(1)} %collective-permute-done.8.a2), channel_id=1, source_target_pairs={{0,8},{8,0},{16,24},{24,16},{1,9},{9,1},{17,25},{25,17},{2,10},{10... | collective-permute-start | bytes 614408 | tf_op jit(solution)/shard_map/ppermute | solution.py:641
  37.7 9.4 %copy-start.4 = (bf16[1024,128]{1,0:T(8,128)(2,1)S(1)}, bf16[1024,128]{1,0:T(8,128)(2,1)}, u32[]{:S(2)}) copy-start(bf16[1024,128]{1,0:T(8,128)(2,1)} %w_proj.1) | copy-start | bytes 786436
  37.7 9.4 %copy-start.6 = (f32[1024]{0:T(1024)S(1)}, f32[1024]{0:T(1024)}, u32[]{:S(2)}) copy-start(f32[1024]{0:T(1024)} %param.20) | copy-start | bytes 12292
  37.7 2.0 %collective-permute-start.13 = (bf16[192,1024]{1,0:T(8,128)(2,1)S(1)}, bf16[192,1024]{1,0:T(8,128)(2,1)S(1)}, u32[]{:S(2)}, u32[]{:S(2)}) collective-permute-start(bf16[192,1024]{1,0:T(8,128)(2,1)S(1)} %feed_other.1), channel_id=1, source_target_pairs={{0,8},{8,0},{16,24},{24,16},{1,9},{9,1},{17,25},{25,17},{2,10},{10... | collective-permute-start | bytes 1179656 | tf_op jit(solution)/shard_map/ppermute | solution.py:641
  39.8 20.4 %copy-start.7 = (s32[64]{0:T(128)S(1)}, s32[64]{0:T(128)}, u32[]{:S(2)}) copy-start(s32[64]{0:T(128)} %lengths.1) | copy-start | bytes 772
  39.8 7.3 %collective-permute-start.14 = (bf16[96,1024]{1,0:T(8,128)(2,1)S(1)}, bf16[96,1024]{1,0:T(8,128)(2,1)S(1)}, u32[]{:S(2)}, u32[]{:S(2)}) collective-permute-start(bf16[96,1024]{1,0:T(8,128)(2,1)S(1)} %fold.1), channel_id=1, source_target_pairs={{0,16},{8,24},{16,0},{24,8},{1,17},{9,25},{17,1},{25,9},{2,18},{10... | collective-permute-start | bytes 589832 | tf_op jit(solution)/shard_map/ppermute | solution.py:641
  66.0 12.9 %all-to-all-start.1 = ((f32[32,8,128]{2,1,0:T(8,128)}), f32[32,8,128]{2,1,0:T(8,128)S(1)}, u32[]{:S(2)}, u32[]{:S(2)}) async-start(f32[32,8,128]{2,1,0:T(8,128)} %bitcast.5), calls=%async_computation.1 | async-start | bytes 262144 | tf_op jit(solution)/shard_map/all_to_all | solution.py:712
  70.6 2.0 %collective-permute-start.15 = (bf16[96,128]{1,0:T(8,128)(2,1)S(1)}, bf16[96,128]{1,0:T(8,128)(2,1)S(1)}, u32[]{:S(2)}, u32[]{:S(2)}) collective-permute-start(bf16[96,128]{1,0:T(8,128)(2,1)S(1)} %get-tuple-element.21.refs_0_), channel_id=1, source_target_pairs={{0,8},{8,0},{16,24},{24,16},{1,9},{9,1},{17,25},{25,17},{2,10},{10... | collective-permute-start | bytes 73736 | tf_op jit(solution)/shard_map/ppermute | solution.py:641
  70.9 3.9 %collective-permute-start.16 = (bf16[96,128]{1,0:T(8,128)(2,1)S(1)}, bf16[96,128]{1,0:T(8,128)(2,1)S(1)}, u32[]{:S(2)}, u32[]{:S(2)}) collective-permute-start(bf16[96,128]{1,0:T(8,128)(2,1)S(1)} %get-tuple-element.21.refs_0_), channel_id=1, source_target_pairs={{0,16},{8,24},{16,0},{24,8},{1,17},{9,25},{17,1},{25,9},{2,18},{10... | collective-permute-start | bytes 73736 | tf_op jit(solution)/shard_map/ppermute | solution.py:641
  72.6 3.4 %collective-permute-start.17 = (bf16[96,128]{1,0:T(8,128)(2,1)S(1)}, bf16[96,128]{1,0:T(8,128)(2,1)S(1)}, u32[]{:S(2)}, u32[]{:S(2)}) collective-permute-start(bf16[96,128]{1,0:T(8,128)(2,1)S(1)} %get-tuple-element.21.refs_0_), channel_id=1, source_target_pairs={{0,24},{8,16},{16,8},{24,0},{1,25},{9,17},{17,9},{25,1},{2,26},{10... | collective-permute-start | bytes 73736 | tf_op jit(solution)/shard_map/ppermute | solution.py:641

commit v8 on v7

--- a/solution.py
+++ b/solution.py
@@ -643,6 +643,7 @@
     tile = (8, LANES)
     pieces = {k: over_doc(prompt_cache, k) for k in (6, 5, 4, 3, 1, 2)}
     pieces[0] = prompt_cache
+    pieces[1], w_out = lax.optimization_barrier((pieces[1], w_out))
     pieces[6], rel_table = lax.optimization_barrier((pieces[6], rel_table))
     pieces[7] = over_doc(pieces[6], 1)
     pieces = [pieces[k] for k in range(n_doc)]

time: 79.7 us -> 79.8 us (level)
  starting transfers between devices: 23.4 us -> 24.6 us
  waiting for transfers between devices: 23.4 us -> 22.2 us
    ppermute x11, starting transfers between devices: 6.26 us -> 7.61 us  [over_head(): return lax.ppermute(x, 'head', [(i, i ^ k) for i in range(n_head)])]
    ppermute x11, waiting for transfers between devices: 15.9 us -> 15 us  [over_head(): return lax.ppermute(x, 'head', [(i, i ^ k) for i in range(n_head)])]
  transfers between devices with their start and end apart: 19 -> 19, of which waited for: 9 -> 10; matrix products, arithmetic and copies ran while one was open for 0% -> 0% of each run, Pallas kernels for 13% -> 13%
where the time goes in v8:
time: 79.8 us; the launch traced here: 79.6 us
  starting transfers between devices  24.6 us (31%)
  waiting for transfers between devices  22.2 us (28%)
  Pallas kernels  19.5 us (24%)
  blocking collectives  12.4 us (16%)
  between operations  0.84 us (1%)
    ppermute x11, waiting for transfers between devices, over_head(): return lax.ppermute(x, 'head', [(i, i ^ k) for i in range(n_head)])  15 us
    ppermute x7, starting transfers between devices, over_doc(): return lax.ppermute(x, 'doc', [(i, i ^ k) for i in range(n_doc)])  12.4 us
    all_to_all x1, blocking collectives, body(): queries = lax.all_to_all(vectors, 'doc', 0, 0, tiled=True).reshape(-1, emb)  12.4 us
    ppermute x11, starting transfers between devices, over_head(): return lax.ppermute(x, 'head', [(i, i ^ k) for i in range(n_head)])  7.61 us
    pallas_call x1, Pallas kernels, body(): pl.pallas_call(score_kernel, out_shape=jax.ShapeDtypeStruct((n_doc, n_hea...  5.83 us
    ppermute x7, waiting for transfers between devices, over_doc(): return lax.ppermute(x, 'doc', [(i, i ^ k) for i in range(n_doc)])  5.01 us
    pallas_call x1, Pallas kernels, prepare(): pl.pallas_call(prepare_kernel, out_shape=[jax.ShapeDtypeStruct((rows, 3 *...  4.64 us
    all_to_all x1, starting transfers between devices, body(): lax.all_to_all(rated.reshape(-1, LANES), ('doc', 'head'), 0, 0, tiled=True)  4.56 us
  transfers between devices with their start and end apart: 19, of which 10 were waited for; matrix products, arithmetic and copies ran while one was open for 0% of the time, Pallas kernels for 13%

profile of v8, /device:TPU:0, one launch (start us, length us, event | category | flops | bytes accessed | tf_op | source)
XLA Modules:
  0.0 79.6 jit_solution(13445547411161479713)
XLA Ops:
  0.6 3.0 %collective-permute-start.1 = (bf16[2,128,256]{2,1,0:T(8,128)(2,1)}, bf16[2,128,256]{2,1,0:T(8,128)(2,1)S(1)}, u32[]{:S(2)}, u32[]{:S(2)}) collective-permute-start(bf16[2,128,256]{2,1,0:T(8,128)(2,1)} %rest_0_.1), channel_id=1, source_target_pairs={{0,1},{1,0},{2,3},{3,2},{4,5},{5,4},{6,7},{7,6},{8,9},{9,8},{10,11... | collective-permute-start | bytes 393224 | tf_op jit(solution)/shard_map/ppermute | solution.py:638
  3.6 3.6 %collective-permute-start = (bf16[2,128,256]{2,1,0:T(8,128)(2,1)}, bf16[2,128,256]{2,1,0:T(8,128)(2,1)S(1)}, u32[]{:S(2)}, u32[]{:S(2)}) collective-permute-start(bf16[2,128,256]{2,1,0:T(8,128)(2,1)} %rest_0_.1), channel_id=1, source_target_pairs={{0,6},{1,7},{2,4},{3,5},{4,2},{5,3},{6,0},{7,1},{8,14},{9,15},{10,... | collective-permute-start | bytes 393224 | tf_op jit(solution)/shard_map/ppermute | solution.py:638
  7.2 0.0 collective-permute-start.2
  7.2 0.1 collective-permute-done.1.rest_1_
  7.3 1.8 %collective-permute-start.11 = (bf16[256,1024]{1,0:T(8,128)(2,1)}, bf16[256,1024]{1,0:T(8,128)(2,1)S(1)}, u32[]{:S(2)}, u32[]{:S(2)}) collective-permute-start(bf16[256,1024]{1,0:T(8,128)(2,1)} %w0.1), channel_id=1, source_target_pairs={{0,16},{8,24},{16,0},{24,8},{1,17},{9,25},{17,1},{25,9},{2,18},{10... | collective-permute-start | bytes 1572872 | tf_op jit(solution)/shard_map/ppermute | solution.py:641
  9.1 2.5 %collective-permute-start.3 = (bf16[2,128,256]{2,1,0:T(8,128)(2,1)}, bf16[2,128,256]{2,1,0:T(8,128)(2,1)S(1)}, u32[]{:S(2)}, u32[]{:S(2)}) collective-permute-start(bf16[2,128,256]{2,1,0:T(8,128)(2,1)} %rest_0_.1), channel_id=1, source_target_pairs={{0,3},{1,2},{2,1},{3,0},{4,7},{5,6},{6,5},{7,4},{8,11},{9,10},{10,... | collective-permute-start | bytes 393224 | tf_op jit(solution)/shard_map/ppermute | solution.py:638
  11.6 2.6 %collective-permute-start.4 = (bf16[2,128,256]{2,1,0:T(8,128)(2,1)}, bf16[2,128,256]{2,1,0:T(8,128)(2,1)S(1)}, u32[]{:S(2)}, u32[]{:S(2)}) collective-permute-start(bf16[2,128,256]{2,1,0:T(8,128)(2,1)} %rest_0_.1), channel_id=1, source_target_pairs={{0,4},{1,5},{2,6},{3,7},{4,0},{5,1},{6,2},{7,3},{8,12},{9,13},{10,... | collective-permute-start | bytes 393224 | tf_op jit(solution)/shard_map/ppermute | solution.py:638
  14.2 0.4 collective-permute-start.5
  14.6 1.1 %collective-permute-done.2.rest_2_ = bf16[2,128,256]{2,1,0:T(8,128)(2,1)S(1)} collective-permute-done((bf16[2,128,256]{2,1,0:T(8,128)(2,1)}, bf16[2,128,256]{2,1,0:T(8,128)(2,1)S(1)}, u32[]{:S(2)}, u32[]{:S(2)}) %collective-permute-start.2) | collective-permute-done | bytes 131104 | tf_op jit(solution)/shard_map/ppermute | solution.py:638
  15.7 0.3 collective-permute-start.6
  16.0 4.6 %prepare.1 = (bf16[384,768]{1,0:T(8,128)(2,1)S(1)}, f32[12,96,128]{2,1,0:T(8,128)S(1)}, bf16[512,256]{1,0:T(8,128)(2,1)S(1)}) custom-call(bf16[384,1024]{1,0:T(8,128)(2,1)} %tokens.3, bf16[3,1024,256]{2,1,0:T(8,128)(2,1)} %bitcast.15, bf16[512,1024]{1,0:T(8,128)(2,1)} %rel_table), custom_call_target="tpu_custom_call" | custom-call | flops 4194304000 | bytes 4194304 | tf_op jit(solution)/shard_map/prepare/pallas_call | solution.py:266
  20.7 0.0 collective-permute-done.3.rest_3_
  20.7 0.1 collective-permute-start.10
  20.8 0.0 collective-permute-done.11.w2
  20.8 0.5 collective-permute-start.12
  21.3 2.4 %collective-permute-done.4.rest_4_ = bf16[2,128,256]{2,1,0:T(8,128)(2,1)S(1)} collective-permute-done((bf16[2,128,256]{2,1,0:T(8,128)(2,1)}, bf16[2,128,256]{2,1,0:T(8,128)(2,1)S(1)}, u32[]{:S(2)}, u32[]{:S(2)}) %collective-permute-start.4) | collective-permute-done | bytes 131104 | tf_op jit(solution)/shard_map/ppermute | solution.py:638
  23.6 1.5 %collective-permute-done.5.rest_5_ = bf16[2,128,256]{2,1,0:T(8,128)(2,1)S(1)} collective-permute-done((bf16[2,128,256]{2,1,0:T(8,128)(2,1)}, bf16[2,128,256]{2,1,0:T(8,128)(2,1)S(1)}, u32[]{:S(2)}, u32[]{:S(2)}) %collective-permute-start.5) | collective-permute-done | bytes 131104 | tf_op jit(solution)/shard_map/ppermute | solution.py:638
  25.1 0.0 copy-start
  25.1 0.0 copy-start.1
  25.2 0.0 copy-start.2
  25.2 0.0 copy-start.5
  25.2 3.4 %attend.1.a0 = bf16[400,256]{1,0:T(8,128)(2,1)S(1)} custom-call(s32[12]{0:T(128)S(1)} %copy-done.10, bf16[384,768]{1,0:T(8,128)(2,1)S(1)} %get-tuple-element.15.qkv, f32[12,96,128]{2,1,0:T(8,128)S(1)} %get-tuple-element.16.base, bf16[512,256]{1,0:T(8,128)(2,1)S(1)} %get-tuple-element.17.rel_q_heads, s32[8,12]{1,0:T(8,128)S(1)} %bitcast.13, ...), custom_call_target="tpu_custom_call" | custom-call | flops 2097152000 | bytes 2097152 | tf_op jit(solution)/shard_map/attend/pallas_call | solution.py:368
  28.6 1.5 %collective-permute-start.8 = (bf16[400,256]{1,0:T(8,128)(2,1)S(1)}, bf16[400,256]{1,0:T(8,128)(2,1)S(1)}, u32[]{:S(2)}, u32[]{:S(2)}) collective-permute-start(bf16[400,256]{1,0:T(8,128)(2,1)S(1)} %attend.1.a0), channel_id=1, source_target_pairs={{0,16},{8,24},{16,0},{24,8},{1,17},{9,25},{17,1},{25,9},{2,18},{10... | collective-permute-start | bytes 614408 | tf_op jit(solution)/shard_map/ppermute | solution.py:641
  30.1 0.0 collective-permute-start.7
  30.1 4.5 %collective-permute-done.8.a2 = bf16[400,256]{1,0:T(8,128)(2,1)S(1)} collective-permute-done((bf16[400,256]{1,0:T(8,128)(2,1)S(1)}, bf16[400,256]{1,0:T(8,128)(2,1)S(1)}, u32[]{:S(2)}, u32[]{:S(2)}) %collective-permute-start.8) | collective-permute-done | bytes 204832 | tf_op jit(solution)/shard_map/ppermute | solution.py:641
  34.6 0.0 collective-permute-start.9
  34.6 0.0 collective-permute-done.7.a1
  34.6 1.4 %collective-permute-done.9.a3 = bf16[400,256]{1,0:T(8,128)(2,1)S(1)} collective-permute-done((bf16[400,256]{1,0:T(8,128)(2,1)S(1)}, bf16[400,256]{1,0:T(8,128)(2,1)S(1)}, u32[]{:S(2)}, u32[]{:S(2)}) %collective-permute-start.9) | collective-permute-done | bytes 204832 | tf_op jit(solution)/shard_map/ppermute | solution.py:641
  36.1 1.8 %feed_other.1 = bf16[192,1024]{1,0:T(8,128)(2,1)S(1)} custom-call(bf16[400,256]{1,0:T(8,128)(2,1)S(1)} %attend.1.a0, bf16[400,256]{1,0:T(8,128)(2,1)S(1)} %collective-permute-done.7.a1, bf16[400,256]{1,0:T(8,128)(2,1)S(1)} %collective-permute-done.8.a2, bf16[400,256]{1,0:T(8,128)(2,1)S(1)} %collective-permute-done.9.a3, bf16[256,1024]{1,0:T(8,128)(2,1)S(1)} %copy-done.3, ...), custom_call_target="tpu_custom_call" | custom-call | flops 1677721600 | bytes 6291456 | tf_op jit(solution)/shard_map/feed_other/pallas_call | solution.py:433
  37.8 0.0 copy-start.4
  37.8 0.0 copy-start.6
  37.9 0.2 collective-permute-start.13
  38.1 1.8 %feed_own.1 = (f32[96,1024]{1,0:T(8,128)S(1)}, f32[96,1024]{1,0:T(8,128)S(1)}) custom-call(bf16[400,256]{1,0:T(8,128)(2,1)S(1)} %attend.1.a0, bf16[400,256]{1,0:T(8,128)(2,1)S(1)} %collective-permute-done.7.a1, bf16[400,256]{1,0:T(8,128)(2,1)S(1)} %collective-permute-done.8.a2, bf16[400,256]{1,0:T(8,128)(2,1)S(1)} %collective-permute-done.9.a3, ...), custom_call_target="tpu_custom_call" | custom-call | flops 1677721600 | bytes 6291456 | tf_op jit(solution)/shard_map/feed_own/pallas_call | solution.py:433
  39.9 0.0 copy-start.7
  39.9 0.1 fold.1
  40.0 1.6 %collective-permute-start.14 = (bf16[96,1024]{1,0:T(8,128)(2,1)S(1)}, bf16[96,1024]{1,0:T(8,128)(2,1)S(1)}, u32[]{:S(2)}, u32[]{:S(2)}) collective-permute-start(bf16[96,1024]{1,0:T(8,128)(2,1)S(1)} %fold.1), channel_id=1, source_target_pairs={{0,16},{8,24},{16,0},{24,8},{1,17},{9,25},{17,1},{25,9},{2,18},{10... | collective-permute-start | bytes 589832 | tf_op jit(solution)/shard_map/ppermute | solution.py:641
  41.6 5.7 %collective-permute-done.14.from_y = bf16[96,1024]{1,0:T(8,128)(2,1)S(1)} collective-permute-done((bf16[96,1024]{1,0:T(8,128)(2,1)S(1)}, bf16[96,1024]{1,0:T(8,128)(2,1)S(1)}, u32[]{:S(2)}, u32[]{:S(2)}) %collective-permute-start.14) | collective-permute-done | bytes 196640 | tf_op jit(solution)/shard_map/ppermute | solution.py:641
  47.2 0.5 project.1
  47.8 12.4 %all_to_all.14 = bf16[8,112,128]{2,1,0:T(8,128)(2,1)S(1)} all-to-all(bf16[8,112,128]{2,1,0:T(8,128)(2,1)S(1)} %get-tuple-element.24), channel_id=1, replica_groups=mesh['head'=4,'doc'=8] {'doc'}, dimensions={0} | all-to-all | bytes 458752 | tf_op jit(solution)/shard_map/all_to_all | solution.py:696
  60.1 5.8 %rate.1 = f32[8,4,8,128]{3,2,1,0:T(8,128)} custom-call(s32[64]{0:T(128)S(1)} %copy-done.7, bf16[896,128]{1,0:T(8,128)(2,1)S(1)} %bitcast.8, bf16[64,256,128]{2,1,0:T(8,128)(2,1)} %docs.1), custom_call_target="tpu_custom_call" | custom-call | tf_op jit(solution)/shard_map/rate/pallas_call | solution.py:698
  66.0 4.6 %all-to-all-start.1 = ((f32[32,8,128]{2,1,0:T(8,128)}), f32[32,8,128]{2,1,0:T(8,128)S(1)}, u32[]{:S(2)}, u32[]{:S(2)}) async-start(f32[32,8,128]{2,1,0:T(8,128)} %bitcast.5), calls=%async_computation.1 | async-start | bytes 262144 | tf_op jit(solution)/shard_map/all_to_all | solution.py:713
  70.5 0.3 collective-permute-start.15
  70.9 1.7 %collective-permute-start.16 = (bf16[96,128]{1,0:T(8,128)(2,1)S(1)}, bf16[96,128]{1,0:T(8,128)(2,1)S(1)}, u32[]{:S(2)}, u32[]{:S(2)}) collective-permute-start(bf16[96,128]{1,0:T(8,128)(2,1)S(1)} %get-tuple-element.25.refs_0_), channel_id=1, source_target_pairs={{0,16},{8,24},{16,0},{24,8},{1,17},{9,25},{17,1},{25,9},{2,18},{10... | collective-permute-start | bytes 73736 | tf_op jit(solution)/shard_map/ppermute | solution.py:641
  72.6 2.2 %collective-permute-done.16.refs_2_ = bf16[96,128]{1,0:T(8,128)(2,1)S(1)} collective-permute-done((bf16[96,128]{1,0:T(8,128)(2,1)S(1)}, bf16[96,128]{1,0:T(8,128)(2,1)S(1)}, u32[]{:S(2)}, u32[]{:S(2)}) %collective-permute-start.16) | collective-permute-done | bytes 24608 | tf_op jit(solution)/shard_map/ppermute | solution.py:641
  74.8 1.1 %collective-permute-done.17.refs_3_ = bf16[96,128]{1,0:T(8,128)(2,1)S(1)} collective-permute-done((bf16[96,128]{1,0:T(8,128)(2,1)S(1)}, bf16[96,128]{1,0:T(8,128)(2,1)S(1)}, u32[]{:S(2)}, u32[]{:S(2)}) %collective-permute-start.17) | collective-permute-done | bytes 24608 | tf_op jit(solution)/shard_map/ppermute | solution.py:641
  75.9 0.7 arrange.1
  76.6 2.2 %all-to-all-done.1 = f32[32,8,128]{2,1,0:T(8,128)S(1)} async-done(((f32[32,8,128]{2,1,0:T(8,128)}), f32[32,8,128]{2,1,0:T(8,128)S(1)}, u32[]{:S(2)}, u32[]{:S(2)}) %all-to-all-start.1) | async-done | bytes 131104 | tf_op jit(solution)/shard_map/all_to_all | solution.py:713
  78.8 0.8 %collect.1 = f32[8,12]{1,0:T(8,128)} custom-call(f32[8,4,8,128]{3,2,1,0:T(8,128)S(1)} %bitcast.9), custom_call_target="tpu_custom_call" | custom-call | tf_op jit(solution)/shard_map/collect/pallas_call | solution.py:726
  (22 shorter events, 0.0 us)
Async XLA Ops:
  0.6 6.7 %collective-permute-start.1 = (bf16[2,128,256]{2,1,0:T(8,128)(2,1)}, bf16[2,128,256]{2,1,0:T(8,128)(2,1)S(1)}, u32[]{:S(2)}, u32[]{:S(2)}) collective-permute-start(bf16[2,128,256]{2,1,0:T(8,128)(2,1)} %rest_0_.1), channel_id=1, source_target_pairs={{0,1},{1,0},{2,3},{3,2},{4,5},{5,4},{6,7},{7,6},{8,9},{9,8},{10,11... | collective-permute-start | bytes 393224 | tf_op jit(solution)/shard_map/ppermute | solution.py:638
  3.6 10.6 %collective-permute-start = (bf16[2,128,256]{2,1,0:T(8,128)(2,1)}, bf16[2,128,256]{2,1,0:T(8,128)(2,1)S(1)}, u32[]{:S(2)}, u32[]{:S(2)}) collective-permute-start(bf16[2,128,256]{2,1,0:T(8,128)(2,1)} %rest_0_.1), channel_id=1, source_target_pairs={{0,6},{1,7},{2,4},{3,5},{4,2},{5,3},{6,0},{7,1},{8,14},{9,15},{10,... | collective-permute-start | bytes 393224 | tf_op jit(solution)/shard_map/ppermute | solution.py:638
  7.2 8.4 %collective-permute-start.2 = (bf16[2,128,256]{2,1,0:T(8,128)(2,1)}, bf16[2,128,256]{2,1,0:T(8,128)(2,1)S(1)}, u32[]{:S(2)}, u32[]{:S(2)}) collective-permute-start(bf16[2,128,256]{2,1,0:T(8,128)(2,1)} %rest_0_.1), channel_id=1, source_target_pairs={{0,2},{1,3},{2,0},{3,1},{4,6},{5,7},{6,4},{7,5},{8,10},{9,11},{10,... | collective-permute-start | bytes 393224 | tf_op jit(solution)/shard_map/ppermute | solution.py:638
  7.3 13.4 %collective-permute-start.11 = (bf16[256,1024]{1,0:T(8,128)(2,1)}, bf16[256,1024]{1,0:T(8,128)(2,1)S(1)}, u32[]{:S(2)}, u32[]{:S(2)}) collective-permute-start(bf16[256,1024]{1,0:T(8,128)(2,1)} %w0.1), channel_id=1, source_target_pairs={{0,16},{8,24},{16,0},{24,8},{1,17},{9,25},{17,1},{25,9},{2,18},{10... | collective-permute-start | bytes 1572872 | tf_op jit(solution)/shard_map/ppermute | solution.py:641
  9.1 11.6 %collective-permute-start.3 = (bf16[2,128,256]{2,1,0:T(8,128)(2,1)}, bf16[2,128,256]{2,1,0:T(8,128)(2,1)S(1)}, u32[]{:S(2)}, u32[]{:S(2)}) collective-permute-start(bf16[2,128,256]{2,1,0:T(8,128)(2,1)} %rest_0_.1), channel_id=1, source_target_pairs={{0,3},{1,2},{2,1},{3,0},{4,7},{5,6},{6,5},{7,4},{8,11},{9,10},{10,... | collective-permute-start | bytes 393224 | tf_op jit(solution)/shard_map/ppermute | solution.py:638
  11.6 12.0 %collective-permute-start.4 = (bf16[2,128,256]{2,1,0:T(8,128)(2,1)}, bf16[2,128,256]{2,1,0:T(8,128)(2,1)S(1)}, u32[]{:S(2)}, u32[]{:S(2)}) collective-permute-start(bf16[2,128,256]{2,1,0:T(8,128)(2,1)} %rest_0_.1), channel_id=1, source_target_pairs={{0,4},{1,5},{2,6},{3,7},{4,0},{5,1},{6,2},{7,3},{8,12},{9,13},{10,... | collective-permute-start | bytes 393224 | tf_op jit(solution)/shard_map/ppermute | solution.py:638
  14.2 10.9 %collective-permute-start.5 = (bf16[2,128,256]{2,1,0:T(8,128)(2,1)}, bf16[2,128,256]{2,1,0:T(8,128)(2,1)S(1)}, u32[]{:S(2)}, u32[]{:S(2)}) collective-permute-start(bf16[2,128,256]{2,1,0:T(8,128)(2,1)} %rest_0_.1), channel_id=1, source_target_pairs={{0,5},{1,4},{2,7},{3,6},{4,1},{5,0},{6,3},{7,2},{8,13},{9,12},{10,... | collective-permute-start | bytes 393224 | tf_op jit(solution)/shard_map/ppermute | solution.py:638
  15.7 9.4 %collective-permute-start.6 = (bf16[2,128,256]{2,1,0:T(8,128)(2,1)S(1)}, bf16[2,128,256]{2,1,0:T(8,128)(2,1)S(1)}, u32[]{:S(2)}, u32[]{:S(2)}) collective-permute-start(bf16[2,128,256]{2,1,0:T(8,128)(2,1)S(1)} %collective-permute-done.rest_6_), channel_id=1, source_target_pairs={{0,1},{1,0},{2,3},{3,2},{4,5},{5,4},{6,7},{7,6},{8,9},{9,8},{10,11... | collective-permute-start | bytes 393224 | tf_op jit(solution)/shard_map/ppermute | solution.py:638
  16.0 4.7 %copy-start.3 = (bf16[256,1024]{1,0:T(8,128)(2,1)S(1)}, bf16[256,1024]{1,0:T(8,128)(2,1)}, u32[]{:S(2)}) copy-start(bf16[256,1024]{1,0:T(8,128)(2,1)} %w0.1) | copy-start | bytes 1572868
  16.0 9.1 %copy-start.8 = (bf16[2,128,256]{2,1,0:T(8,128)(2,1)S(1)}, bf16[2,128,256]{2,1,0:T(8,128)(2,1)}, u32[]{:S(2)}) copy-start(bf16[2,128,256]{2,1,0:T(8,128)(2,1)} %rest_0_.1) | copy-start | bytes 393220
  16.0 9.1 %copy-start.9 = (s32[12,8]{0,1:T(8,128)S(1)}, s32[12,8]{0,1:T(8,128)}, u32[]{:S(2)}) copy-start(s32[12,8]{0,1:T(8,128)} %param.27) | copy-start | bytes 1156
  16.0 9.1 %copy-start.10 = (s32[12]{0:T(128)S(1)}, s32[12]{0:T(128)}, u32[]{:S(2)}) copy-start(s32[12]{0:T(128)} %group_ids.1) | copy-start | bytes 148
  20.7 13.9 %collective-permute-start.10 = (bf16[256,1024]{1,0:T(8,128)(2,1)S(1)}, bf16[256,1024]{1,0:T(8,128)(2,1)S(1)}, u32[]{:S(2)}, u32[]{:S(2)}) collective-permute-start(bf16[256,1024]{1,0:T(8,128)(2,1)S(1)} %copy-done.3), channel_id=1, source_target_pairs={{0,8},{8,0},{16,24},{24,16},{1,9},{9,1},{17,25},{25,17},{2,10},{10... | collective-permute-start | bytes 1572872 | tf_op jit(solution)/shard_map/ppermute | solution.py:641
  20.8 15.2 %collective-permute-start.12 = (bf16[256,1024]{1,0:T(8,128)(2,1)S(1)}, bf16[256,1024]{1,0:T(8,128)(2,1)S(1)}, u32[]{:S(2)}, u32[]{:S(2)}) collective-permute-start(bf16[256,1024]{1,0:T(8,128)(2,1)S(1)} %collective-permute-done.11.w2), channel_id=1, source_target_pairs={{0,8},{8,0},{16,24},{24,16},{1,9},{9,1},{17,25},{25,17},{2,10},{10... | collective-permute-start | bytes 1572872 | tf_op jit(solution)/shard_map/ppermute | solution.py:641
  25.1 10.9 %copy-start = (bf16[1024,1024]{1,0:T(8,128)(2,1)S(1)}, bf16[1024,1024]{1,0:T(8,128)(2,1)}, u32[]{:S(2)}) copy-start(bf16[1024,1024]{1,0:T(8,128)(2,1)} %w_up.3) | copy-start | bytes 6291460
  25.1 10.9 %copy-start.1 = (bf16[1024,1024]{1,0:T(8,128)(2,1)S(1)}, bf16[1024,1024]{1,0:T(8,128)(2,1)}, u32[]{:S(2)}) copy-start(bf16[1024,1024]{1,0:T(8,128)(2,1)} %w_down.3) | copy-start | bytes 6291460
  25.2 10.9 %copy-start.2 = (bf16[384,1024]{1,0:T(8,128)(2,1)S(1)}, bf16[384,1024]{1,0:T(8,128)(2,1)}, u32[]{:S(2)}) copy-start(bf16[384,1024]{1,0:T(8,128)(2,1)} %tokens.3) | copy-start | bytes 2359300
  25.2 10.9 %copy-start.5 = (f32[1024]{0:T(1024)S(1)}, f32[1024]{0:T(1024)}, u32[]{:S(2)}) copy-start(f32[1024]{0:T(1024)} %param.19) | copy-start | bytes 12292
  28.6 6.0 %collective-permute-start.8 = (bf16[400,256]{1,0:T(8,128)(2,1)S(1)}, bf16[400,256]{1,0:T(8,128)(2,1)S(1)}, u32[]{:S(2)}, u32[]{:S(2)}) collective-permute-start(bf16[400,256]{1,0:T(8,128)(2,1)S(1)} %attend.1.a0), channel_id=1, source_target_pairs={{0,16},{8,24},{16,0},{24,8},{1,17},{9,25},{17,1},{25,9},{2,18},{10... | collective-permute-start | bytes 614408 | tf_op jit(solution)/shard_map/ppermute | solution.py:641
  30.1 4.5 %collective-permute-start.7 = (bf16[400,256]{1,0:T(8,128)(2,1)S(1)}, bf16[400,256]{1,0:T(8,128)(2,1)S(1)}, u32[]{:S(2)}, u32[]{:S(2)}) collective-permute-start(bf16[400,256]{1,0:T(8,128)(2,1)S(1)} %attend.1.a0), channel_id=1, source_target_pairs={{0,8},{8,0},{16,24},{24,16},{1,9},{9,1},{17,25},{25,17},{2,10},{10... | collective-permute-start | bytes 614408 | tf_op jit(solution)/shard_map/ppermute | solution.py:641
  34.6 1.5 %collective-permute-start.9 = (bf16[400,256]{1,0:T(8,128)(2,1)S(1)}, bf16[400,256]{1,0:T(8,128)(2,1)S(1)}, u32[]{:S(2)}, u32[]{:S(2)}) collective-permute-start(bf16[400,256]{1,0:T(8,128)(2,1)S(1)} %collective-permute-done.8.a2), channel_id=1, source_target_pairs={{0,8},{8,0},{16,24},{24,16},{1,9},{9,1},{17,25},{25,17},{2,10},{10... | collective-permute-start | bytes 614408 | tf_op jit(solution)/shard_map/ppermute | solution.py:641
  37.8 9.4 %copy-start.4 = (bf16[1024,128]{1,0:T(8,128)(2,1)S(1)}, bf16[1024,128]{1,0:T(8,128)(2,1)}, u32[]{:S(2)}) copy-start(bf16[1024,128]{1,0:T(8,128)(2,1)} %w_proj.1) | copy-start | bytes 786436
  37.8 9.4 %copy-start.6 = (f32[1024]{0:T(1024)S(1)}, f32[1024]{0:T(1024)}, u32[]{:S(2)}) copy-start(f32[1024]{0:T(1024)} %param.20) | copy-start | bytes 12292
  37.9 2.0 %collective-permute-start.13 = (bf16[192,1024]{1,0:T(8,128)(2,1)S(1)}, bf16[192,1024]{1,0:T(8,128)(2,1)S(1)}, u32[]{:S(2)}, u32[]{:S(2)}) collective-permute-start(bf16[192,1024]{1,0:T(8,128)(2,1)S(1)} %feed_other.1), channel_id=1, source_target_pairs={{0,8},{8,0},{16,24},{24,16},{1,9},{9,1},{17,25},{25,17},{2,10},{10... | collective-permute-start | bytes 1179656 | tf_op jit(solution)/shard_map/ppermute | solution.py:641
  39.9 20.3 %copy-start.7 = (s32[64]{0:T(128)S(1)}, s32[64]{0:T(128)}, u32[]{:S(2)}) copy-start(s32[64]{0:T(128)} %lengths.1) | copy-start | bytes 772
  40.0 7.3 %collective-permute-start.14 = (bf16[96,1024]{1,0:T(8,128)(2,1)S(1)}, bf16[96,1024]{1,0:T(8,128)(2,1)S(1)}, u32[]{:S(2)}, u32[]{:S(2)}) collective-permute-start(bf16[96,1024]{1,0:T(8,128)(2,1)S(1)} %fold.1), channel_id=1, source_target_pairs={{0,16},{8,24},{16,0},{24,8},{1,17},{9,25},{17,1},{25,9},{2,18},{10... | collective-permute-start | bytes 589832 | tf_op jit(solution)/shard_map/ppermute | solution.py:641
  66.0 12.8 %all-to-all-start.1 = ((f32[32,8,128]{2,1,0:T(8,128)}), f32[32,8,128]{2,1,0:T(8,128)S(1)}, u32[]{:S(2)}, u32[]{:S(2)}) async-start(f32[32,8,128]{2,1,0:T(8,128)} %bitcast.5), calls=%async_computation.1 | async-start | bytes 262144 | tf_op jit(solution)/shard_map/all_to_all | solution.py:713
  70.5 2.0 %collective-permute-start.15 = (bf16[96,128]{1,0:T(8,128)(2,1)S(1)}, bf16[96,128]{1,0:T(8,128)(2,1)S(1)}, u32[]{:S(2)}, u32[]{:S(2)}) collective-permute-start(bf16[96,128]{1,0:T(8,128)(2,1)S(1)} %get-tuple-element.25.refs_0_), channel_id=1, source_target_pairs={{0,8},{8,0},{16,24},{24,16},{1,9},{9,1},{17,25},{25,17},{2,10},{10... | collective-permute-start | bytes 73736 | tf_op jit(solution)/shard_map/ppermute | solution.py:641
  70.9 3.9 %collective-permute-start.16 = (bf16[96,128]{1,0:T(8,128)(2,1)S(1)}, bf16[96,128]{1,0:T(8,128)(2,1)S(1)}, u32[]{:S(2)}, u32[]{:S(2)}) collective-permute-start(bf16[96,128]{1,0:T(8,128)(2,1)S(1)} %get-tuple-element.25.refs_0_), channel_id=1, source_target_pairs={{0,16},{8,24},{16,0},{24,8},{1,17},{9,25},{17,1},{25,9},{2,18},{10... | collective-permute-start | bytes 73736 | tf_op jit(solution)/shard_map/ppermute | solution.py:641
  72.5 3.4 %collective-permute-start.17 = (bf16[96,128]{1,0:T(8,128)(2,1)S(1)}, bf16[96,128]{1,0:T(8,128)(2,1)S(1)}, u32[]{:S(2)}, u32[]{:S(2)}) collective-permute-start(bf16[96,128]{1,0:T(8,128)(2,1)S(1)} %get-tuple-element.25.refs_0_), channel_id=1, source_target_pairs={{0,24},{8,16},{16,8},{24,0},{1,25},{9,17},{17,9},{25,1},{2,26},{10... | collective-permute-start | bytes 73736 | tf_op jit(solution)/shard_map/ppermute | solution.py:641

commit v9 on v7

--- a/solution.py
+++ b/solution.py
@@ -643,6 +643,7 @@
     tile = (8, LANES)
     pieces = {k: over_doc(prompt_cache, k) for k in (6, 5, 4, 3, 1, 2)}
     pieces[0] = prompt_cache
+    pieces[2], w_out = lax.optimization_barrier((pieces[2], w_out))
     pieces[6], rel_table = lax.optimization_barrier((pieces[6], rel_table))
     pieces[7] = over_doc(pieces[6], 1)
     pieces = [pieces[k] for k in range(n_doc)]

time: 79.7 us -> 80.4 us (level)
  starting transfers between devices: 23.4 us -> 26.9 us
  waiting for transfers between devices: 23.4 us -> 20.1 us
    ppermute x7, starting transfers between devices: 12.5 us -> 15.6 us  [over_doc(): return lax.ppermute(x, 'doc', [(i, i ^ k) for i in range(n_doc)])]
    ppermute x7, waiting for transfers between devices: 5.22 us -> 2.2 us  [over_doc(): return lax.ppermute(x, 'doc', [(i, i ^ k) for i in range(n_doc)])]
  transfers between devices with their start and end apart: 19 -> 19, of which waited for: 9 -> 8; matrix products, arithmetic and copies ran while one was open for 0% -> 0% of each run, Pallas kernels for 13% -> 13%
where the time goes in v9:
time: 80.4 us; the launch traced here: 79.8 us
  starting transfers between devices  26.9 us (33%)
  waiting for transfers between devices  20.1 us (25%)
  Pallas kernels  19.5 us (24%)
  blocking collectives  12.4 us (15%)
  between operations  0.84 us (1%)
    ppermute x11, waiting for transfers between devices, over_head(): return lax.ppermute(x, 'head', [(i, i ^ k) for i in range(n_head)])  15.7 us
    ppermute x7, starting transfers between devices, over_doc(): return lax.ppermute(x, 'doc', [(i, i ^ k) for i in range(n_doc)])  15.6 us
    all_to_all x1, blocking collectives, body(): queries = lax.all_to_all(vectors, 'doc', 0, 0, tiled=True).reshape(-1, emb)  12.4 us
    ppermute x11, starting transfers between devices, over_head(): return lax.ppermute(x, 'head', [(i, i ^ k) for i in range(n_head)])  6.48 us
    pallas_call x1, Pallas kernels, body(): pl.pallas_call(score_kernel, out_shape=jax.ShapeDtypeStruct((n_doc, n_hea...  5.84 us
    all_to_all x1, starting transfers between devices, body(): lax.all_to_all(rated.reshape(-1, LANES), ('doc', 'head'), 0, 0, tiled=True)  4.73 us
    pallas_call x1, Pallas kernels, prepare(): pl.pallas_call(prepare_kernel, out_shape=[jax.ShapeDtypeStruct((rows, 3 *...  4.63 us
    pallas_call x2, Pallas kernels, feed(): pl.pallas_call(kernel, out_shape=outs, in_specs=full_specs(12), out_specs...  3.59 us
  transfers between devices with their start and end apart: 19, of which 8 were waited for; matrix products, arithmetic and copies ran while one was open for 0% of the time, Pallas kernels for 13%

profile of v9, /device:TPU:0, one launch (start us, length us, event | category | flops | bytes accessed | tf_op | source)
XLA Modules:
  0.0 79.8 jit_solution(14585598258658884825)
XLA Ops:
  0.6 3.1 %collective-permute-start.2 = (bf16[2,128,256]{2,1,0:T(8,128)(2,1)}, bf16[2,128,256]{2,1,0:T(8,128)(2,1)S(1)}, u32[]{:S(2)}, u32[]{:S(2)}) collective-permute-start(bf16[2,128,256]{2,1,0:T(8,128)(2,1)} %rest_0_.1), channel_id=1, source_target_pairs={{0,2},{1,3},{2,0},{3,1},{4,6},{5,7},{6,4},{7,5},{8,10},{9,11},{10,... | collective-permute-start | bytes 393224 | tf_op jit(solution)/shard_map/ppermute | solution.py:638
  3.7 2.5 %collective-permute-start = (bf16[2,128,256]{2,1,0:T(8,128)(2,1)}, bf16[2,128,256]{2,1,0:T(8,128)(2,1)S(1)}, u32[]{:S(2)}, u32[]{:S(2)}) collective-permute-start(bf16[2,128,256]{2,1,0:T(8,128)(2,1)} %rest_0_.1), channel_id=1, source_target_pairs={{0,6},{1,7},{2,4},{3,5},{4,2},{5,3},{6,0},{7,1},{8,14},{9,15},{10,... | collective-permute-start | bytes 393224 | tf_op jit(solution)/shard_map/ppermute | solution.py:638
  6.2 1.5 %collective-permute-start.1 = (bf16[2,128,256]{2,1,0:T(8,128)(2,1)}, bf16[2,128,256]{2,1,0:T(8,128)(2,1)S(1)}, u32[]{:S(2)}, u32[]{:S(2)}) collective-permute-start(bf16[2,128,256]{2,1,0:T(8,128)(2,1)} %rest_0_.1), channel_id=1, source_target_pairs={{0,1},{1,0},{2,3},{3,2},{4,5},{5,4},{6,7},{7,6},{8,9},{9,8},{10,11... | collective-permute-start | bytes 393224 | tf_op jit(solution)/shard_map/ppermute | solution.py:638
  7.7 0.0 collective-permute-done.2.rest_2_
  7.7 1.5 %collective-permute-start.11 = (bf16[256,1024]{1,0:T(8,128)(2,1)}, bf16[256,1024]{1,0:T(8,128)(2,1)S(1)}, u32[]{:S(2)}, u32[]{:S(2)}) collective-permute-start(bf16[256,1024]{1,0:T(8,128)(2,1)} %w0.1), channel_id=1, source_target_pairs={{0,16},{8,24},{16,0},{24,8},{1,17},{9,25},{17,1},{25,9},{2,18},{10... | collective-permute-start | bytes 1572872 | tf_op jit(solution)/shard_map/ppermute | solution.py:641
  9.2 3.0 %collective-permute-start.3 = (bf16[2,128,256]{2,1,0:T(8,128)(2,1)}, bf16[2,128,256]{2,1,0:T(8,128)(2,1)S(1)}, u32[]{:S(2)}, u32[]{:S(2)}) collective-permute-start(bf16[2,128,256]{2,1,0:T(8,128)(2,1)} %rest_0_.1), channel_id=1, source_target_pairs={{0,3},{1,2},{2,1},{3,0},{4,7},{5,6},{6,5},{7,4},{8,11},{9,10},{10,... | collective-permute-start | bytes 393224 | tf_op jit(solution)/shard_map/ppermute | solution.py:638
  12.2 4.1 %collective-permute-start.4 = (bf16[2,128,256]{2,1,0:T(8,128)(2,1)}, bf16[2,128,256]{2,1,0:T(8,128)(2,1)S(1)}, u32[]{:S(2)}, u32[]{:S(2)}) collective-permute-start(bf16[2,128,256]{2,1,0:T(8,128)(2,1)} %rest_0_.1), channel_id=1, source_target_pairs={{0,4},{1,5},{2,6},{3,7},{4,0},{5,1},{6,2},{7,3},{8,12},{9,13},{10,... | collective-permute-start | bytes 393224 | tf_op jit(solution)/shard_map/ppermute | solution.py:638
  16.3 0.0 collective-permute-done.rest_6_
  16.3 0.7 collective-permute-start.5
  17.0 0.0 collective-permute-done.1.rest_1_
  17.0 0.8 %collective-permute-start.6 = (bf16[2,128,256]{2,1,0:T(8,128)(2,1)S(1)}, bf16[2,128,256]{2,1,0:T(8,128)(2,1)S(1)}, u32[]{:S(2)}, u32[]{:S(2)}) collective-permute-start(bf16[2,128,256]{2,1,0:T(8,128)(2,1)S(1)} %collective-permute-done.rest_6_), channel_id=1, source_target_pairs={{0,1},{1,0},{2,3},{3,2},{4,5},{5,4},{6,7},{7,6},{8,9},{9,8},{10,11... | collective-permute-start | bytes 393224 | tf_op jit(solution)/shard_map/ppermute | solution.py:638
  17.8 4.6 %prepare.1 = (bf16[384,768]{1,0:T(8,128)(2,1)S(1)}, f32[12,96,128]{2,1,0:T(8,128)S(1)}, bf16[512,256]{1,0:T(8,128)(2,1)S(1)}) custom-call(bf16[384,1024]{1,0:T(8,128)(2,1)} %tokens.3, bf16[3,1024,256]{2,1,0:T(8,128)(2,1)} %bitcast.15, bf16[512,1024]{1,0:T(8,128)(2,1)} %rel_table), custom_call_target="tpu_custom_call" | custom-call | flops 4194304000 | bytes 4194304 | tf_op jit(solution)/shard_map/prepare/pallas_call | solution.py:266
  22.5 0.0 collective-permute-done.3.rest_3_
  22.5 0.1 collective-permute-start.10
  22.6 0.5 collective-permute-start.12
  23.1 0.6 collective-permute-done.4.rest_4_
  23.6 1.6 %collective-permute-done.5.rest_5_ = bf16[2,128,256]{2,1,0:T(8,128)(2,1)S(1)} collective-permute-done((bf16[2,128,256]{2,1,0:T(8,128)(2,1)}, bf16[2,128,256]{2,1,0:T(8,128)(2,1)S(1)}, u32[]{:S(2)}, u32[]{:S(2)}) %collective-permute-start.5) | collective-permute-done | bytes 131104 | tf_op jit(solution)/shard_map/ppermute | solution.py:638
  25.3 0.0 copy-start
  25.3 0.0 copy-start.1
  25.3 0.0 copy-start.2
  25.3 0.0 copy-start.5
  25.3 3.4 %attend.1.a0 = bf16[400,256]{1,0:T(8,128)(2,1)S(1)} custom-call(s32[12]{0:T(128)S(1)} %copy-done.10, bf16[384,768]{1,0:T(8,128)(2,1)S(1)} %get-tuple-element.15.qkv, f32[12,96,128]{2,1,0:T(8,128)S(1)} %get-tuple-element.16.base, bf16[512,256]{1,0:T(8,128)(2,1)S(1)} %get-tuple-element.17.rel_q_heads, s32[8,12]{1,0:T(8,128)S(1)} %bitcast.13, ...), custom_call_target="tpu_custom_call" | custom-call | flops 2097152000 | bytes 2097152 | tf_op jit(solution)/shard_map/attend/pallas_call | solution.py:368
  28.8 1.1 %collective-permute-start.8 = (bf16[400,256]{1,0:T(8,128)(2,1)S(1)}, bf16[400,256]{1,0:T(8,128)(2,1)S(1)}, u32[]{:S(2)}, u32[]{:S(2)}) collective-permute-start(bf16[400,256]{1,0:T(8,128)(2,1)S(1)} %attend.1.a0), channel_id=1, source_target_pairs={{0,16},{8,24},{16,0},{24,8},{1,17},{9,25},{17,1},{25,9},{2,18},{10... | collective-permute-start | bytes 614408 | tf_op jit(solution)/shard_map/ppermute | solution.py:641
  29.8 4.7 %collective-permute-done.8.a2 = bf16[400,256]{1,0:T(8,128)(2,1)S(1)} collective-permute-done((bf16[400,256]{1,0:T(8,128)(2,1)S(1)}, bf16[400,256]{1,0:T(8,128)(2,1)S(1)}, u32[]{:S(2)}, u32[]{:S(2)}) %collective-permute-start.8) | collective-permute-done | bytes 204832 | tf_op jit(solution)/shard_map/ppermute | solution.py:641
  34.6 0.0 collective-permute-start.9
  34.6 0.0 collective-permute-done.7.a1
  34.6 1.4 %collective-permute-done.9.a3 = bf16[400,256]{1,0:T(8,128)(2,1)S(1)} collective-permute-done((bf16[400,256]{1,0:T(8,128)(2,1)S(1)}, bf16[400,256]{1,0:T(8,128)(2,1)S(1)}, u32[]{:S(2)}, u32[]{:S(2)}) %collective-permute-start.9) | collective-permute-done | bytes 204832 | tf_op jit(solution)/shard_map/ppermute | solution.py:641
  36.1 1.8 %feed_other.1 = bf16[192,1024]{1,0:T(8,128)(2,1)S(1)} custom-call(bf16[400,256]{1,0:T(8,128)(2,1)S(1)} %attend.1.a0, bf16[400,256]{1,0:T(8,128)(2,1)S(1)} %collective-permute-done.7.a1, bf16[400,256]{1,0:T(8,128)(2,1)S(1)} %collective-permute-done.8.a2, bf16[400,256]{1,0:T(8,128)(2,1)S(1)} %collective-permute-done.9.a3, bf16[256,1024]{1,0:T(8,128)(2,1)S(1)} %copy-done.3, ...), custom_call_target="tpu_custom_call" | custom-call | flops 1677721600 | bytes 6291456 | tf_op jit(solution)/shard_map/feed_other/pallas_call | solution.py:433
  37.8 0.0 copy-start.4
  37.8 0.0 copy-start.6
  37.9 0.2 collective-permute-start.13
  38.1 1.8 %feed_own.1 = (f32[96,1024]{1,0:T(8,128)S(1)}, f32[96,1024]{1,0:T(8,128)S(1)}) custom-call(bf16[400,256]{1,0:T(8,128)(2,1)S(1)} %attend.1.a0, bf16[400,256]{1,0:T(8,128)(2,1)S(1)} %collective-permute-done.7.a1, bf16[400,256]{1,0:T(8,128)(2,1)S(1)} %collective-permute-done.8.a2, bf16[400,256]{1,0:T(8,128)(2,1)S(1)} %collective-permute-done.9.a3, ...), custom_call_target="tpu_custom_call" | custom-call | flops 1677721600 | bytes 6291456 | tf_op jit(solution)/shard_map/feed_own/pallas_call | solution.py:433
  39.9 0.0 copy-start.7
  39.9 0.0 collective-permute-done.13.from_core
  39.9 0.1 fold.1
  40.0 1.1 %collective-permute-start.14 = (bf16[96,1024]{1,0:T(8,128)(2,1)S(1)}, bf16[96,1024]{1,0:T(8,128)(2,1)S(1)}, u32[]{:S(2)}, u32[]{:S(2)}) collective-permute-start(bf16[96,1024]{1,0:T(8,128)(2,1)S(1)} %fold.1), channel_id=1, source_target_pairs={{0,16},{8,24},{16,0},{24,8},{1,17},{9,25},{17,1},{25,9},{2,18},{10... | collective-permute-start | bytes 589832 | tf_op jit(solution)/shard_map/ppermute | solution.py:641
  41.1 6.1 %collective-permute-done.14.from_y = bf16[96,1024]{1,0:T(8,128)(2,1)S(1)} collective-permute-done((bf16[96,1024]{1,0:T(8,128)(2,1)S(1)}, bf16[96,1024]{1,0:T(8,128)(2,1)S(1)}, u32[]{:S(2)}, u32[]{:S(2)}) %collective-permute-start.14) | collective-permute-done | bytes 196640 | tf_op jit(solution)/shard_map/ppermute | solution.py:641
  47.2 0.5 project.1
  47.8 12.4 %all_to_all.14 = bf16[8,112,128]{2,1,0:T(8,128)(2,1)S(1)} all-to-all(bf16[8,112,128]{2,1,0:T(8,128)(2,1)S(1)} %get-tuple-element.24), channel_id=1, replica_groups=mesh['head'=4,'doc'=8] {'doc'}, dimensions={0} | all-to-all | bytes 458752 | tf_op jit(solution)/shard_map/all_to_all | solution.py:696
  60.1 5.8 %rate.1 = f32[8,4,8,128]{3,2,1,0:T(8,128)} custom-call(s32[64]{0:T(128)S(1)} %copy-done.7, bf16[896,128]{1,0:T(8,128)(2,1)S(1)} %bitcast.8, bf16[64,256,128]{2,1,0:T(8,128)(2,1)} %docs.1), custom_call_target="tpu_custom_call" | custom-call | tf_op jit(solution)/shard_map/rate/pallas_call | solution.py:698
  66.0 4.7 %all-to-all-start.1 = ((f32[32,8,128]{2,1,0:T(8,128)}), f32[32,8,128]{2,1,0:T(8,128)S(1)}, u32[]{:S(2)}, u32[]{:S(2)}) async-start(f32[32,8,128]{2,1,0:T(8,128)} %bitcast.5), calls=%async_computation.1 | async-start | bytes 262144 | tf_op jit(solution)/shard_map/all_to_all | solution.py:713
  70.7 0.3 collective-permute-start.15
  71.0 1.7 %collective-permute-start.16 = (bf16[96,128]{1,0:T(8,128)(2,1)S(1)}, bf16[96,128]{1,0:T(8,128)(2,1)S(1)}, u32[]{:S(2)}, u32[]{:S(2)}) collective-permute-start(bf16[96,128]{1,0:T(8,128)(2,1)S(1)} %get-tuple-element.25.refs_0_), channel_id=1, source_target_pairs={{0,16},{8,24},{16,0},{24,8},{1,17},{9,25},{17,1},{25,9},{2,18},{10... | collective-permute-start | bytes 73736 | tf_op jit(solution)/shard_map/ppermute | solution.py:641
  72.7 2.2 %collective-permute-done.16.refs_2_ = bf16[96,128]{1,0:T(8,128)(2,1)S(1)} collective-permute-done((bf16[96,128]{1,0:T(8,128)(2,1)S(1)}, bf16[96,128]{1,0:T(8,128)(2,1)S(1)}, u32[]{:S(2)}, u32[]{:S(2)}) %collective-permute-start.16) | collective-permute-done | bytes 24608 | tf_op jit(solution)/shard_map/ppermute | solution.py:641
  75.0 1.1 %collective-permute-done.17.refs_3_ = bf16[96,128]{1,0:T(8,128)(2,1)S(1)} collective-permute-done((bf16[96,128]{1,0:T(8,128)(2,1)S(1)}, bf16[96,128]{1,0:T(8,128)(2,1)S(1)}, u32[]{:S(2)}, u32[]{:S(2)}) %collective-permute-start.17) | collective-permute-done | bytes 24608 | tf_op jit(solution)/shard_map/ppermute | solution.py:641
  76.1 0.7 arrange.1
  76.7 2.2 %all-to-all-done.1 = f32[32,8,128]{2,1,0:T(8,128)S(1)} async-done(((f32[32,8,128]{2,1,0:T(8,128)}), f32[32,8,128]{2,1,0:T(8,128)S(1)}, u32[]{:S(2)}, u32[]{:S(2)}) %all-to-all-start.1) | async-done | bytes 131104 | tf_op jit(solution)/shard_map/all_to_all | solution.py:713
  78.9 0.8 %collect.1 = f32[8,12]{1,0:T(8,128)} custom-call(f32[8,4,8,128]{3,2,1,0:T(8,128)S(1)} %bitcast.9), custom_call_target="tpu_custom_call" | custom-call | tf_op jit(solution)/shard_map/collect/pallas_call | solution.py:726
  (22 shorter events, 0.0 us)
Async XLA Ops:
  0.6 7.1 %collective-permute-start.2 = (bf16[2,128,256]{2,1,0:T(8,128)(2,1)}, bf16[2,128,256]{2,1,0:T(8,128)(2,1)S(1)}, u32[]{:S(2)}, u32[]{:S(2)}) collective-permute-start(bf16[2,128,256]{2,1,0:T(8,128)(2,1)} %rest_0_.1), channel_id=1, source_target_pairs={{0,2},{1,3},{2,0},{3,1},{4,6},{5,7},{6,4},{7,5},{8,10},{9,11},{10,... | collective-permute-start | bytes 393224 | tf_op jit(solution)/shard_map/ppermute | solution.py:638
  3.7 12.6 %collective-permute-start = (bf16[2,128,256]{2,1,0:T(8,128)(2,1)}, bf16[2,128,256]{2,1,0:T(8,128)(2,1)S(1)}, u32[]{:S(2)}, u32[]{:S(2)}) collective-permute-start(bf16[2,128,256]{2,1,0:T(8,128)(2,1)} %rest_0_.1), channel_id=1, source_target_pairs={{0,6},{1,7},{2,4},{3,5},{4,2},{5,3},{6,0},{7,1},{8,14},{9,15},{10,... | collective-permute-start | bytes 393224 | tf_op jit(solution)/shard_map/ppermute | solution.py:638
  6.2 10.8 %collective-permute-start.1 = (bf16[2,128,256]{2,1,0:T(8,128)(2,1)}, bf16[2,128,256]{2,1,0:T(8,128)(2,1)S(1)}, u32[]{:S(2)}, u32[]{:S(2)}) collective-permute-start(bf16[2,128,256]{2,1,0:T(8,128)(2,1)} %rest_0_.1), channel_id=1, source_target_pairs={{0,1},{1,0},{2,3},{3,2},{4,5},{5,4},{6,7},{7,6},{8,9},{9,8},{10,11... | collective-permute-start | bytes 393224 | tf_op jit(solution)/shard_map/ppermute | solution.py:638
  7.7 14.9 %collective-permute-start.11 = (bf16[256,1024]{1,0:T(8,128)(2,1)}, bf16[256,1024]{1,0:T(8,128)(2,1)S(1)}, u32[]{:S(2)}, u32[]{:S(2)}) collective-permute-start(bf16[256,1024]{1,0:T(8,128)(2,1)} %w0.1), channel_id=1, source_target_pairs={{0,16},{8,24},{16,0},{24,8},{1,17},{9,25},{17,1},{25,9},{2,18},{10... | collective-permute-start | bytes 1572872 | tf_op jit(solution)/shard_map/ppermute | solution.py:641
  9.2 13.3 %collective-permute-start.3 = (bf16[2,128,256]{2,1,0:T(8,128)(2,1)}, bf16[2,128,256]{2,1,0:T(8,128)(2,1)S(1)}, u32[]{:S(2)}, u32[]{:S(2)}) collective-permute-start(bf16[2,128,256]{2,1,0:T(8,128)(2,1)} %rest_0_.1), channel_id=1, source_target_pairs={{0,3},{1,2},{2,1},{3,0},{4,7},{5,6},{6,5},{7,4},{8,11},{9,10},{10,... | collective-permute-start | bytes 393224 | tf_op jit(solution)/shard_map/ppermute | solution.py:638
  12.2 11.4 %collective-permute-start.4 = (bf16[2,128,256]{2,1,0:T(8,128)(2,1)}, bf16[2,128,256]{2,1,0:T(8,128)(2,1)S(1)}, u32[]{:S(2)}, u32[]{:S(2)}) collective-permute-start(bf16[2,128,256]{2,1,0:T(8,128)(2,1)} %rest_0_.1), channel_id=1, source_target_pairs={{0,4},{1,5},{2,6},{3,7},{4,0},{5,1},{6,2},{7,3},{8,12},{9,13},{10,... | collective-permute-start | bytes 393224 | tf_op jit(solution)/shard_map/ppermute | solution.py:638
  16.3 8.9 %collective-permute-start.5 = (bf16[2,128,256]{2,1,0:T(8,128)(2,1)}, bf16[2,128,256]{2,1,0:T(8,128)(2,1)S(1)}, u32[]{:S(2)}, u32[]{:S(2)}) collective-permute-start(bf16[2,128,256]{2,1,0:T(8,128)(2,1)} %rest_0_.1), channel_id=1, source_target_pairs={{0,5},{1,4},{2,7},{3,6},{4,1},{5,0},{6,3},{7,2},{8,13},{9,12},{10,... | collective-permute-start | bytes 393224 | tf_op jit(solution)/shard_map/ppermute | solution.py:638
  17.0 8.3 %collective-permute-start.6 = (bf16[2,128,256]{2,1,0:T(8,128)(2,1)S(1)}, bf16[2,128,256]{2,1,0:T(8,128)(2,1)S(1)}, u32[]{:S(2)}, u32[]{:S(2)}) collective-permute-start(bf16[2,128,256]{2,1,0:T(8,128)(2,1)S(1)} %collective-permute-done.rest_6_), channel_id=1, source_target_pairs={{0,1},{1,0},{2,3},{3,2},{4,5},{5,4},{6,7},{7,6},{8,9},{9,8},{10,11... | collective-permute-start | bytes 393224 | tf_op jit(solution)/shard_map/ppermute | solution.py:638
  17.8 4.7 %copy-start.3 = (bf16[256,1024]{1,0:T(8,128)(2,1)S(1)}, bf16[256,1024]{1,0:T(8,128)(2,1)}, u32[]{:S(2)}) copy-start(bf16[256,1024]{1,0:T(8,128)(2,1)} %w0.1) | copy-start | bytes 1572868
  17.8 7.4 %copy-start.8 = (bf16[2,128,256]{2,1,0:T(8,128)(2,1)S(1)}, bf16[2,128,256]{2,1,0:T(8,128)(2,1)}, u32[]{:S(2)}) copy-start(bf16[2,128,256]{2,1,0:T(8,128)(2,1)} %rest_0_.1) | copy-start | bytes 393220
  17.8 7.4 %copy-start.9 = (s32[12,8]{0,1:T(8,128)S(1)}, s32[12,8]{0,1:T(8,128)}, u32[]{:S(2)}) copy-start(s32[12,8]{0,1:T(8,128)} %param.27) | copy-start | bytes 1156
  17.8 7.4 %copy-start.10 = (s32[12]{0:T(128)S(1)}, s32[12]{0:T(128)}, u32[]{:S(2)}) copy-start(s32[12]{0:T(128)} %group_ids.1) | copy-start | bytes 148
  22.5 12.1 %collective-permute-start.10 = (bf16[256,1024]{1,0:T(8,128)(2,1)S(1)}, bf16[256,1024]{1,0:T(8,128)(2,1)S(1)}, u32[]{:S(2)}, u32[]{:S(2)}) collective-permute-start(bf16[256,1024]{1,0:T(8,128)(2,1)S(1)} %copy-done.3), channel_id=1, source_target_pairs={{0,8},{8,0},{16,24},{24,16},{1,9},{9,1},{17,25},{25,17},{2,10},{10... | collective-permute-start | bytes 1572872 | tf_op jit(solution)/shard_map/ppermute | solution.py:641
  22.6 13.5 %collective-permute-start.12 = (bf16[256,1024]{1,0:T(8,128)(2,1)S(1)}, bf16[256,1024]{1,0:T(8,128)(2,1)S(1)}, u32[]{:S(2)}, u32[]{:S(2)}) collective-permute-start(bf16[256,1024]{1,0:T(8,128)(2,1)S(1)} %collective-permute-done.11.w2), channel_id=1, source_target_pairs={{0,8},{8,0},{16,24},{24,16},{1,9},{9,1},{17,25},{25,17},{2,10},{10... | collective-permute-start | bytes 1572872 | tf_op jit(solution)/shard_map/ppermute | solution.py:641
  25.3 10.8 %copy-start = (bf16[1024,1024]{1,0:T(8,128)(2,1)S(1)}, bf16[1024,1024]{1,0:T(8,128)(2,1)}, u32[]{:S(2)}) copy-start(bf16[1024,1024]{1,0:T(8,128)(2,1)} %w_up.3) | copy-start | bytes 6291460
  25.3 10.8 %copy-start.1 = (bf16[1024,1024]{1,0:T(8,128)(2,1)S(1)}, bf16[1024,1024]{1,0:T(8,128)(2,1)}, u32[]{:S(2)}) copy-start(bf16[1024,1024]{1,0:T(8,128)(2,1)} %w_down.3) | copy-start | bytes 6291460
  25.3 10.7 %copy-start.2 = (bf16[384,1024]{1,0:T(8,128)(2,1)S(1)}, bf16[384,1024]{1,0:T(8,128)(2,1)}, u32[]{:S(2)}) copy-start(bf16[384,1024]{1,0:T(8,128)(2,1)} %tokens.3) | copy-start | bytes 2359300
  25.3 10.7 %copy-start.5 = (f32[1024]{0:T(1024)S(1)}, f32[1024]{0:T(1024)}, u32[]{:S(2)}) copy-start(f32[1024]{0:T(1024)} %param.19) | copy-start | bytes 12292
  28.8 5.8 %collective-permute-start.8 = (bf16[400,256]{1,0:T(8,128)(2,1)S(1)}, bf16[400,256]{1,0:T(8,128)(2,1)S(1)}, u32[]{:S(2)}, u32[]{:S(2)}) collective-permute-start(bf16[400,256]{1,0:T(8,128)(2,1)S(1)} %attend.1.a0), channel_id=1, source_target_pairs={{0,16},{8,24},{16,0},{24,8},{1,17},{9,25},{17,1},{25,9},{2,18},{10... | collective-permute-start | bytes 614408 | tf_op jit(solution)/shard_map/ppermute | solution.py:641
  29.8 4.7 %collective-permute-start.7 = (bf16[400,256]{1,0:T(8,128)(2,1)S(1)}, bf16[400,256]{1,0:T(8,128)(2,1)S(1)}, u32[]{:S(2)}, u32[]{:S(2)}) collective-permute-start(bf16[400,256]{1,0:T(8,128)(2,1)S(1)} %attend.1.a0), channel_id=1, source_target_pairs={{0,8},{8,0},{16,24},{24,16},{1,9},{9,1},{17,25},{25,17},{2,10},{10... | collective-permute-start | bytes 614408 | tf_op jit(solution)/shard_map/ppermute | solution.py:641
  34.6 1.5 %collective-permute-start.9 = (bf16[400,256]{1,0:T(8,128)(2,1)S(1)}, bf16[400,256]{1,0:T(8,128)(2,1)S(1)}, u32[]{:S(2)}, u32[]{:S(2)}) collective-permute-start(bf16[400,256]{1,0:T(8,128)(2,1)S(1)} %collective-permute-done.8.a2), channel_id=1, source_target_pairs={{0,8},{8,0},{16,24},{24,16},{1,9},{9,1},{17,25},{25,17},{2,10},{10... | collective-permute-start | bytes 614408 | tf_op jit(solution)/shard_map/ppermute | solution.py:641
  37.8 9.4 %copy-start.4 = (bf16[1024,128]{1,0:T(8,128)(2,1)S(1)}, bf16[1024,128]{1,0:T(8,128)(2,1)}, u32[]{:S(2)}) copy-start(bf16[1024,128]{1,0:T(8,128)(2,1)} %w_proj.1) | copy-start | bytes 786436
  37.8 9.4 %copy-start.6 = (f32[1024]{0:T(1024)S(1)}, f32[1024]{0:T(1024)}, u32[]{:S(2)}) copy-start(f32[1024]{0:T(1024)} %param.20) | copy-start | bytes 12292
  37.9 2.0 %collective-permute-start.13 = (bf16[192,1024]{1,0:T(8,128)(2,1)S(1)}, bf16[192,1024]{1,0:T(8,128)(2,1)S(1)}, u32[]{:S(2)}, u32[]{:S(2)}) collective-permute-start(bf16[192,1024]{1,0:T(8,128)(2,1)S(1)} %feed_other.1), channel_id=1, source_target_pairs={{0,8},{8,0},{16,24},{24,16},{1,9},{9,1},{17,25},{25,17},{2,10},{10... | collective-permute-start | bytes 1179656 | tf_op jit(solution)/shard_map/ppermute | solution.py:641
  39.9 20.2 %copy-start.7 = (s32[64]{0:T(128)S(1)}, s32[64]{0:T(128)}, u32[]{:S(2)}) copy-start(s32[64]{0:T(128)} %lengths.1) | copy-start | bytes 772
  40.0 7.3 %collective-permute-start.14 = (bf16[96,1024]{1,0:T(8,128)(2,1)S(1)}, bf16[96,1024]{1,0:T(8,128)(2,1)S(1)}, u32[]{:S(2)}, u32[]{:S(2)}) collective-permute-start(bf16[96,1024]{1,0:T(8,128)(2,1)S(1)} %fold.1), channel_id=1, source_target_pairs={{0,16},{8,24},{16,0},{24,8},{1,17},{9,25},{17,1},{25,9},{2,18},{10... | collective-permute-start | bytes 589832 | tf_op jit(solution)/shard_map/ppermute | solution.py:641
  66.0 13.0 %all-to-all-start.1 = ((f32[32,8,128]{2,1,0:T(8,128)}), f32[32,8,128]{2,1,0:T(8,128)S(1)}, u32[]{:S(2)}, u32[]{:S(2)}) async-start(f32[32,8,128]{2,1,0:T(8,128)} %bitcast.5), calls=%async_computation.1 | async-start | bytes 262144 | tf_op jit(solution)/shard_map/all_to_all | solution.py:713
  70.7 2.0 %collective-permute-start.15 = (bf16[96,128]{1,0:T(8,128)(2,1)S(1)}, bf16[96,128]{1,0:T(8,128)(2,1)S(1)}, u32[]{:S(2)}, u32[]{:S(2)}) collective-permute-start(bf16[96,128]{1,0:T(8,128)(2,1)S(1)} %get-tuple-element.25.refs_0_), channel_id=1, source_target_pairs={{0,8},{8,0},{16,24},{24,16},{1,9},{9,1},{17,25},{25,17},{2,10},{10... | collective-permute-start | bytes 73736 | tf_op jit(solution)/shard_map/ppermute | solution.py:641
  71.0 3.9 %collective-permute-start.16 = (bf16[96,128]{1,0:T(8,128)(2,1)S(1)}, bf16[96,128]{1,0:T(8,128)(2,1)S(1)}, u32[]{:S(2)}, u32[]{:S(2)}) collective-permute-start(bf16[96,128]{1,0:T(8,128)(2,1)S(1)} %get-tuple-element.25.refs_0_), channel_id=1, source_target_pairs={{0,16},{8,24},{16,0},{24,8},{1,17},{9,25},{17,1},{25,9},{2,18},{10... | collective-permute-start | bytes 73736 | tf_op jit(solution)/shard_map/ppermute | solution.py:641
  72.7 3.4 %collective-permute-start.17 = (bf16[96,128]{1,0:T(8,128)(2,1)S(1)}, bf16[96,128]{1,0:T(8,128)(2,1)S(1)}, u32[]{:S(2)}, u32[]{:S(2)}) collective-permute-start(bf16[96,128]{1,0:T(8,128)(2,1)S(1)} %get-tuple-element.25.refs_0_), channel_id=1, source_target_pairs={{0,24},{8,16},{16,8},{24,0},{1,25},{9,17},{17,9},{25,1},{2,26},{10... | collective-permute-start | bytes 73736 | tf_op jit(solution)/shard_map/ppermute | solution.py:641
